TPU v7x, 32 devices: a whole 2x2x4 slice. The times are simulated.
32 devices in a mesh: pb: 8 (over y, x, core), ha: 4 (over z).
Axes of the slice: x: 2, y: 2, z: 4, core: 2. Of those that a mesh axis runs over, the one named last changes fastest.
Arguments:
- main_query: bfloat16 [1024, 128, 576], P('pb', 'ha'), may hold values from -1.8 to 1.8
- latent: bfloat16 [1024, 576], P('pb'), may hold values from -6 to 6
- log_sums: float32 [1024, 128], P('pb', 'ha'), may hold values from 0 to 4
- window_start: int32 [1024], P('pb'), may hold values from 0 to 1022, as said below
- index_query: bfloat16 [1024, 64, 128], P('pb', 'ha'), may hold values from -0.6 to 0.6
- index_key: bfloat16 [1024, 128], P('pb'), may hold values from -4 to 4
- index_weight: float32 [1024, 64], P('pb', 'ha'), may hold values from -4 to 4
Outputs:
- index_query_grad: bfloat16 [1024, 64, 128], P('pb', 'ha')
- index_key_grad: bfloat16 [1024, 128], P('pb')
- index_weight_grad: float32 [1024, 64], P('pb', 'ha')
Inputs may be any that keep to these rules, and one draw needn't show every extreme that they name: window_start[0] is 0, window_start[t] is at most t - 1 for t >= 1, and window_start[1023] is 1022, so every query sees itself and, past the first, at least one earlier key.
All inputs are finite; a program needn't handle non-finite values.
Results may differ from a plain program's by a relative error of at most 0.0049.
Values may be sent and summed in bfloat16 or wider, within the bound.
No kernel may reach another device: no remote copies, remote signals or barrier semaphores. Data moves between devices by JAX's collectives and lax.ppermute only.
A program may use at most 64 MiB of HBM per device.

v0:
```python
import math

import jax
import jax.numpy as jnp
from jax import lax
from jax.sharding import PartitionSpec as P

main_scale = 192.0 ** (-0.5)
very_low = -1e30


def visible(window_start, positions, first_row, width):
    columns = first_row + jnp.arange(width, dtype=jnp.int32)
    return (columns[None, :] >= window_start[:, None]) & (columns[None, :] <= positions[:, None])


def on_device(main_query, latent, log_sums, window_start, index_query, index_key, index_weight):
    query_rows, head_count, latent_width = main_query.shape
    index_heads = index_query.shape[1]
    index_width = index_query.shape[2]
    tokens = query_rows * lax.axis_size("pb")
    positions = lax.axis_index("pb") * query_rows + jnp.arange(query_rows, dtype=jnp.int32)
    flat_query = main_query.reshape(query_rows * head_count, latent_width)
    flat_index = index_query.reshape(query_rows * index_heads, index_width)
    probs_part = jnp.zeros((query_rows, tokens), jnp.float32)
    logit_part = jnp.zeros((query_rows, tokens), jnp.float32)
    latent_piece = lax.all_gather(latent, "pb", axis=0, tiled=True)
    key_piece = lax.all_gather(index_key, "pb", axis=0, tiled=True)
    piece_rows = latent_piece.shape[0]
    block_size = math.gcd(piece_rows, 512)

    def one_block(block_index, partial_value):
        probs_inner, logit_inner = partial_value
        offset = block_index * block_size
        latent_block = lax.dynamic_slice_in_dim(latent_piece, offset, block_size, 0)
        key_block = lax.dynamic_slice_in_dim(key_piece, offset, block_size, 0)
        visible_mask = visible(window_start, positions, offset, block_size)
        scores = jnp.einsum(
            "rd,kd->rk", flat_query, latent_block, preferred_element_type=jnp.float32
        )
        scores = scores.reshape(query_rows, head_count, block_size) * main_scale
        head_mass = jnp.where(
            visible_mask, jnp.sum(jnp.exp(scores - log_sums[:, :, None]), axis=1), 0.0
        )
        active = jnp.einsum("rd,kd->rk", flat_index, key_block, preferred_element_type=jnp.float32)
        active = jnp.maximum(active.reshape(query_rows, index_heads, block_size), 0.0)
        logit_block = jnp.sum(index_weight[:, :, None] * active, axis=1)
        probs_inner = lax.dynamic_update_slice_in_dim(probs_inner, head_mass, offset, 1)
        logit_inner = lax.dynamic_update_slice_in_dim(logit_inner, logit_block, offset, 1)
        return (probs_inner, logit_inner)

    probs_part, logit_part = lax.fori_loop(
        0, piece_rows // block_size, one_block, (probs_part, logit_part)
    )
    probs_part, logit_part, keys_all = (probs_part, logit_part, key_piece)
    probs_all, logit_all = lax.psum((probs_part, logit_part), "ha")
    visible_all = visible(window_start, positions, 0, tokens)
    target = probs_all / jnp.sum(probs_all, axis=1, keepdims=True)
    masked = jnp.where(visible_all, logit_all, very_low)
    row_top = jnp.max(masked, axis=1, keepdims=True)
    expo = jnp.where(visible_all, jnp.exp(masked - row_top), 0.0)
    logit_grad = jnp.where(visible_all, expo / jnp.sum(expo, axis=1, keepdims=True) - target, 0.0)
    block_keys = math.gcd(tokens, 512)

    def back_block(block_index, partial_value):
        query_grad, weight_grad, key_grad = partial_value
        offset = block_index * block_keys
        key_block = lax.dynamic_slice_in_dim(keys_all, offset, block_keys, 0)
        grad_block = lax.dynamic_slice_in_dim(logit_grad, offset, block_keys, 1)
        active = jnp.einsum("rd,kd->rk", flat_index, key_block, preferred_element_type=jnp.float32)
        active = active.reshape(query_rows, index_heads, block_keys)
        weight_grad = weight_grad + jnp.sum(
            grad_block[:, None, :] * jnp.maximum(active, 0.0), axis=2
        )
        coeffs = jnp.where(
            active > 0.0, grad_block[:, None, :] * index_weight[:, :, None], 0.0
        ).astype(jnp.bfloat16)
        coeffs = coeffs.reshape(query_rows * index_heads, block_keys)
        query_grad = query_grad + jnp.dot(coeffs, key_block, preferred_element_type=jnp.float32)
        key_terms = jnp.einsum("rk,rd->kd", coeffs, flat_index, preferred_element_type=jnp.float32)
        key_grad = lax.dynamic_update_slice_in_dim(key_grad, key_terms, offset, 0)
        return (query_grad, weight_grad, key_grad)

    start_state = (
        jnp.zeros((query_rows * index_heads, index_width), jnp.float32),
        jnp.zeros((query_rows, index_heads), jnp.float32),
        jnp.zeros((tokens, index_width), jnp.float32),
    )
    query_grad, weight_grad, key_grad = lax.fori_loop(
        0, tokens // block_keys, back_block, start_state
    )
    key_share = lax.psum_scatter(key_grad, ("pb", "ha"), scatter_dimension=0, tiled=True).astype(
        jnp.bfloat16
    )
    key_output = lax.all_gather(key_share, "ha", axis=0, tiled=True)
    query_output = query_grad.astype(jnp.bfloat16).reshape(query_rows, index_heads, index_width)
    return (query_output, key_output, weight_grad)


def solution(mesh):
    return jax.shard_map(
        on_device,
        mesh=mesh,
        in_specs=(
            P("pb", "ha", None),
            P("pb", None),
            P("pb", "ha"),
            P("pb"),
            P("pb", "ha", None),
            P("pb", None),
            P("pb", "ha"),
        ),
        out_specs=(P("pb", "ha", None), P("pb", None), P("pb", "ha")),
        check_vma=False,
    )
```

profile of v0, /device:TPU:0, one launch (start us, length us, event | category | flops | bytes accessed | tf_op | source)
XLA Modules:
  0.0 351.2 jit_solution(8477494517470689985)
XLA Ops:
  9.8 9.1 %copy.23 = bf16[128,32,576]{2,1,0:T(8,128)(2,1)} copy(bf16[128,32,576]{0,2,1:T(8,128)(2,1)} %param.11) | data formatting | bytes 9437184 | tf_op args[0]
  19.0 10.8 %all_gather.9 = bf16[1024,128]{1,0:T(8,128)(2,1)S(1)} all-gather(bf16[128,128]{1,0:T(8,128)(2,1)S(1)} %copy-done.6), channel_id=1, replica_groups=mesh['pb'=8,'ha'=4] {'pb'}, dimensions={0}, use_global_device_ids=true | all-gather | bytes 294912 | tf_op jit(solution)/shard_map/all_gather | solution.py:28
  29.8 8.2 %all-gather.2.cloned.1.call-done = bf16[1024,576]{1,0:T(8,128)(2,1)} async-done(((bf16[128,576]{1,0:T(8,128)(2,1)}), bf16[1024,576]{1,0:T(8,128)(2,1)}) %all-gather.2.cloned.1.call-update) | async-done | bytes 1179664 | tf_op jit(solution)/shard_map/all_gather | solution.py:27
  38.1 67.9 %while.35 = (s32[]{:T(128)}, f32[128,1024]{1,0:T(8,128)S(1)}, f32[128,1024]{1,0:T(8,128)S(1)}, s32[128]{0:T(128)S(1)}, bf16[1024,576]{1,0:T(8,128)(2,1)}, /*inde...) while((s32[]{:T(128)}, f32[128,1024]{1,0:T(8,128)S(1)}, ...), condition=%wide.region_3.4_spmd.clone, body=%wide.region_0.3_spmd.clone.sunk | while | flops 2693923328 | bytes 58488528 | solution.py:52
  38.1 9.4 %multiply_bitcast_fusion.2 = f32[4096,512]{0,1:T(8,128)} fusion(bf16[4096,576]{1,0:T(8,128)(2,1)} %get-tuple-element.662, bf16[1024,576]{1,0:T(8,128)(2,1)} %get-tuple-element.661, s32[]{:T(128)S(6)} %select_n.73), kind=kOutput, calls=%fused_computation.2.clone.1 | convolution fusion | flops 2418016256 | bytes 14286852 | tf_op jit(solution)/shard_map/while/body/eval_jaxpr/rd,kd->rk/dot_general | solution.py:38
  47.5 9.0 %copy.32 = f32[4096,512]{1,0:T(8,128)} copy(f32[4096,512]{0,1:T(8,128)} %multiply_bitcast_fusion.2) | data formatting | bytes 16777216 | tf_op jit(solution)/shard_map/while/body/eval_jaxpr/mul | solution.py:41
  56.5 4.3 %exponential_reduce_fusion.2 = f32[128,512]{1,0:T(8,128)S(1)} fusion(f32[128,32]{1,0:T(8,128)S(1)} %get-tuple-element.663, f32[4096,512]{1,0:T(8,128)} %copy.32), kind=kLoop, calls=%fused_computation.1.clone.1 | loop fusion | flops 4128768 | bytes 8667136 | tf_op jit(solution)/shard_map/while/body/eval_jaxpr/reduce_sum | solution.py:43
  63.4 5.4 %copy.33 = f32[2048,512]{1,0:T(8,128)} copy(f32[2048,512]{0,1:T(8,128)} %maximum_bitcast_fusion.2) | data formatting | bytes 8388608 | tf_op jit(solution)/shard_map/while/body/eval_jaxpr/max | solution.py:46
  68.8 3.1 multiply_reduce_fusion.2
  72.0 9.4 %multiply_bitcast_fusion.2 = f32[4096,512]{0,1:T(8,128)} fusion(bf16[4096,576]{1,0:T(8,128)(2,1)} %get-tuple-element.662, bf16[1024,576]{1,0:T(8,128)(2,1)} %get-tuple-element.661, s32[]{:T(128)S(6)} %select_n.73), kind=kOutput, calls=%fused_computation.2.clone.1 | convolution fusion | flops 2418016256 | bytes 14286852 | tf_op jit(solution)/shard_map/while/body/eval_jaxpr/rd,kd->rk/dot_general | solution.py:38
  81.4 9.0 %copy.32 = f32[4096,512]{1,0:T(8,128)} copy(f32[4096,512]{0,1:T(8,128)} %multiply_bitcast_fusion.2) | data formatting | bytes 16777216 | tf_op jit(solution)/shard_map/while/body/eval_jaxpr/mul | solution.py:41
  90.4 4.3 %exponential_reduce_fusion.2 = f32[128,512]{1,0:T(8,128)S(1)} fusion(f32[128,32]{1,0:T(8,128)S(1)} %get-tuple-element.663, f32[4096,512]{1,0:T(8,128)} %copy.32), kind=kLoop, calls=%fused_computation.1.clone.1 | loop fusion | flops 4128768 | bytes 8667136 | tf_op jit(solution)/shard_map/while/body/eval_jaxpr/reduce_sum | solution.py:43
  94.7 2.7 maximum_bitcast_fusion.2
  97.4 5.4 %copy.33 = f32[2048,512]{1,0:T(8,128)} copy(f32[2048,512]{0,1:T(8,128)} %maximum_bitcast_fusion.2) | data formatting | bytes 8388608 | tf_op jit(solution)/shard_map/while/body/eval_jaxpr/max | solution.py:46
  102.7 3.1 multiply_reduce_fusion.2
  107.3 52.0 %all-reduce.3.cloned.1.call-done = (f32[128,1024]{1,0:T(8,128)}, f32[128,1024]{1,0:T(8,128)}) async-done(((f32[128,1024]{1,0:T(8,128)}, f32[128,1024]{1,0:T(8,128)}), (f32[128,1024]{1,0:T(8,128)}, f32[128,1024]{1,0:T(8,128)})) %all-reduce.3.cloned.1.call-update) | async-done | bytes 1048592 | tf_op jit(solution)/shard_map/psum | solution.py:56
  165.6 30.7 %while.36 = (s32[]{:T(128)}, f32[2048,128]{1,0:T(8,128)}, f32[128,16]{1,0:T(8,128)S(1)}, f32[1024,128]{1,0:T(8,128)}, bf16[1024,128]{1,0:T(8,128)(2,1)S(1)}, /*i...) while((s32[]{:T(128)}, f32[2048,128]{1,0:T(8,128)}, ...), condition=%wide.wide.region_11.12_spmd.clone, body=%wide.wide.region_9.11_spmd.clone.sunk | while | flops 813172736 | bytes 31777020 | solution.py:89
  168.1 5.5 %copy.34 = f32[2048,512]{0,1:T(8,128)} copy(f32[2048,512]{1,0:T(8,128)} %bitcast.54) | data formatting | bytes 8388608 | tf_op jit(solution)/shard_map/while/body/eval_jaxpr/mul | solution.py:76
  173.5 3.3 fusion.47
  182.8 5.5 %copy.34 = f32[2048,512]{0,1:T(8,128)} copy(f32[2048,512]{1,0:T(8,128)} %bitcast.54) | data formatting | bytes 8388608 | tf_op jit(solution)/shard_map/while/body/eval_jaxpr/mul | solution.py:76
  188.2 3.3 fusion.47
  191.5 3.1 convolution_add_fusion.3
  199.0 131.2 %reduce-scatter.2.cloned.1.call-done = f32[32,128]{1,0:T(8,128)} async-done(((f32[1024,128]{1,0:T(8,128)}), f32[32,128]{1,0:T(8,128)}) %reduce-scatter.2.cloned.1.call-update) | async-done | bytes 16400 | tf_op jit(solution)/shard_map/reduce_scatter | solution.py:92
  331.0 13.1 %all_gather.11 = bf16[128,128]{1,0:T(8,128)(2,1)S(1)} all-gather(bf16[32,128]{1,0:T(8,128)(2,1)S(1)} %convert_element_type.15), channel_id=1, replica_groups=mesh['pb'=8,'ha'=4] {'ha'}, dimensions={0}, use_global_device_ids=true | all-gather | bytes 40960 | tf_op jit(solution)/shard_map/all_gather | solution.py:95
  (64 shorter events, 27.3 us)
Async XLA Ops:
  7.2 30.8 %all-gather.2.cloned.1.call-start = ((), (), s32[]{:S(2)}) async-start(), calls=%async_computation.1 | async-start | bytes 1474560 | tf_op jit(solution)/shard_map/all_gather | solution.py:27
  8.9 150.4 %all-reduce.3.cloned.1.call-start = ((), (), s32[]{:S(2)}) async-start(), calls=%async_computation.3 | async-start | bytes 2097152 | tf_op jit(solution)/shard_map/psum | solution.py:56
  9.8 9.1 %copy-start.8 = (f32[128,32]{0,1:T(8,128)S(1)}, f32[128,32]{0,1:T(8,128)}, u32[]{:S(2)}) copy-start(f32[128,32]{0,1:T(8,128)} %param.13) | copy-start | bytes 49156
  9.8 9.2 %copy-start.6 = (bf16[128,128]{1,0:T(8,128)(2,1)S(1)}, bf16[128,128]{1,0:T(8,128)(2,1)}, u32[]{:S(2)}) copy-start(bf16[128,128]{1,0:T(8,128)(2,1)} %param.16) | copy-start | bytes 98308
  9.8 28.2 %copy-start = (bf16[128,16,128]{2,1,0:T(8,128)(2,1)S(1)}, bf16[128,16,128]{2,1,0:T(8,128)(2,1)}, u32[]{:S(2)}) copy-start(bf16[128,16,128]{2,1,0:T(8,128)(2,1)} %param.15) | copy-start | bytes 1572868
  9.8 28.2 %copy-start.7 = (s32[128]{0:T(128)S(1)}, s32[128]{0:T(128)}, u32[]{:S(2)}) copy-start(s32[128]{0:T(128)} %param.14) | copy-start | bytes 1540
  106.0 0.8 copy-start.4
  106.0 0.9 copy-start.5
  106.0 59.5 %copy-start.1 = (f32[128,16]{1,0:T(8,128)}, f32[128,16]{1,0:T(8,128)S(1)}, u32[]{:S(2)}) copy-start(f32[128,16]{1,0:T(8,128)S(1)} %get-tuple-element.727) | copy-start | bytes 24580
  107.0 223.3 %reduce-scatter.2.cloned.1.call-start = ((), (), s32[]{:S(2)}) async-start(), calls=%async_computation.2 | async-start | bytes 540672 | tf_op jit(solution)/shard_map/reduce_scatter | solution.py:92
  176.8 1.8 copy-start.2
  179.3 0.8 copy-start.3
  191.5 3.1 copy-start.2
  195.3 0.8 copy-start.3
Sparse Core Ops, SparseCore 0:
  10.5 27.4 all-gather.1
  107.1 52.1 all-reduce.2
  196.4 133.8 reduce-scatter.1
where the time goes:
time: 353 us; the launch traced here: 351 us
  waiting for transfers between devices  191 us (54%)
  local copies, waits for them, and re-layouts  61.3 us (17%)
  matrix products  36.9 us (10%)
  blocking collectives  23.9 us (7%)
  other arithmetic  23.2 us (7%)
  between operations  13.9 us (4%)
    reduce_scatter x1, waiting for transfers between devices, on_device(): lax.psum_scatter(key_grad, ('pb', 'ha'), scatter_dimension=0, tiled=True)  131 us
    psum x1, waiting for transfers between devices, on_device(): probs_all, logit_all = lax.psum((probs_part, logit_part), 'ha')  52 us
    dot_general x2, matrix products, one_block(): jnp.einsum('rd,kd->rk', flat_query, latent_block, preferred_element_type=...  18.8 us
    mul x2, local copies, waits for them, and re-layouts, one_block(): scores = scores.reshape(query_rows, head_count, block_size) * main_scale  18 us
    mul x5, local copies, waits for them, and re-layouts, back_block(): grad_block[:, None, :] * index_weight[:, :, None]  16 us
    unnamed x20, local copies, waits for them, and re-layouts  13.9 us
    all_gather x1, blocking collectives, on_device(): key_output = lax.all_gather(key_share, 'ha', axis=0, tiled=True)  13.1 us
    all_gather x1, blocking collectives, on_device(): key_piece = lax.all_gather(index_key, 'pb', axis=0, tiled=True)  10.8 us
  transfers between devices with their start and end apart: 3, of which 3 were waited for; matrix products, arithmetic and copies ran while one was open for 4% of the time, Pallas kernels for 0%

commit v1 on v0

v1 whole, which is shorter than its diff:
```python
import functools

import jax
import jax.numpy as jnp
from jax import lax
from jax.experimental import pallas as pl
from jax.experimental.pallas import tpu as pltpu
from jax.sharding import PartitionSpec as P

main_scale = 192.0 ** (-0.5)
log2e = 1.4426950408889634
very_low = -1e30
group = 4
VMEM = pl.BlockSpec(memory_space=pltpu.VMEM)


def params(**kwargs):
    return pltpu.CompilerParams(vmem_limit_bytes=48 * 1024 * 1024, **kwargs)


def visible_block(rel, rows, start_row):
    me = lax.axis_index("pb")
    keys = (me ^ rel) * rows + lax.broadcasted_iota(jnp.int32, (rows, rows), 0)
    queries = me * rows + lax.broadcasted_iota(jnp.int32, (rows, rows), 1)
    return (keys >= start_row) & (keys <= queries)


def pack_kernel(latent_ref, key_ref, out_ref):
    width = key_ref.shape[1]
    out_ref[:, :width] = key_ref[...]
    out_ref[:, width:] = latent_ref[...].T


def put_slices(outs, turned):
    me = lax.axis_index("ha")
    rows = outs[0].shape[0]
    for r, out in enumerate(outs):
        first = pl.multiple_of((me ^ r) * rows, rows)
        out[...] = turned[pl.ds(first, rows), :].astype(out.dtype)


def index_kernel(count, *refs):
    blocks = refs[:count]
    query_ref, weight_ref = refs[count : count + 2]
    outs = refs[count + 2 : -3]
    keys, total, turned = refs[-3:]
    rows = query_ref.shape[1]
    for k in range(count):
        keys[k * rows : (k + 1) * rows, :] = blocks[k][...]
    total[...] = jnp.zeros_like(total)

    def body(pair, carry):
        two = query_ref[pl.ds(2 * pair, 2)].reshape(2 * rows, -1)
        act = lax.dot_general(
            keys[...], two, (((1,), (1,)), ((), ())), preferred_element_type=jnp.float32
        )
        act = jnp.maximum(act, 0.0)
        total[...] += (
            act[:, :rows] * weight_ref[pl.ds(2 * pair, 1), :]
            + act[:, rows:] * weight_ref[pl.ds(2 * pair + 1, 1), :]
        )
        return carry

    lax.fori_loop(0, query_ref.shape[0] // 2, body, 0)
    for k in range(count):
        turned[:, k * rows : (k + 1) * rows] = total[k * rows : (k + 1) * rows, :].T
    put_slices(outs, turned)


def main_kernel(rels, *refs):
    count = len(rels)
    blocks = refs[:count]
    query_ref, sums_ref, start_ref = refs[count : count + 3]
    outs = refs[count + 3 : -3]
    keys, total, turned = refs[-3:]
    heads, width, rows = query_ref.shape
    step = pl.program_id(0)

    @pl.when(step == 0)
    def _():
        for k in range(count):
            block = blocks[k][...]
            keys[k * rows : (k + 1) * rows, :] = block[:, block.shape[1] - width :]
        total[...] = jnp.zeros_like(total)

    def body(pair, carry):
        two = jnp.concatenate([query_ref[2 * pair], query_ref[2 * pair + 1]], axis=1)
        scores = jnp.dot(keys[...], two, preferred_element_type=jnp.float32)
        first = jnp.exp2(
            scores[:, :rows] * (main_scale * log2e) - sums_ref[pl.ds(2 * pair, 1), :] * log2e
        )
        second = jnp.exp2(
            scores[:, rows:] * (main_scale * log2e) - sums_ref[pl.ds(2 * pair + 1, 1), :] * log2e
        )
        total[...] += first + second
        return carry

    lax.fori_loop(0, heads // 2, body, 0)

    @pl.when(step == pl.num_programs(0) - 1)
    def _():
        for k in range(count):
            seen = visible_block(rels[k], rows, start_ref[...])
            piece = jnp.where(seen, total[k * rows : (k + 1) * rows, :], 0.0)
            turned[:, k * rows : (k + 1) * rows] = piece.T
        put_slices(outs, turned)


def tree(values):
    while len(values) > 1:
        values = [values[i] + values[i + 1] for i in range(0, len(values), 2)]
    return values[0]


def grad_kernel(parts, chunks, *refs):
    logit_refs = refs[: parts * chunks]
    prob_refs = refs[parts * chunks : 2 * parts * chunks]
    start_ref, out_ref = refs[2 * parts * chunks :]
    rows = out_ref.shape[0]
    me = lax.axis_index("pb")
    first = lax.axis_index("ha") * rows
    starts = start_ref[pl.ds(pl.multiple_of(first, rows), rows), :]
    block = rows * parts

    def gather(some):
        return jnp.concatenate(
            [
                tree([some[c * parts + r][...].astype(jnp.float32) for r in range(parts)])
                for c in range(chunks)
            ],
            axis=1,
        )

    logits = gather(logit_refs)
    probs = gather(prob_refs)
    lanes = lax.broadcasted_iota(jnp.int32, logits.shape, 1)
    keys = ((lanes // block) ^ me) * block + lanes % block
    queries = me * block + first + lax.broadcasted_iota(jnp.int32, logits.shape, 0)
    seen = (keys >= starts) & (keys <= queries)
    target = probs / jnp.sum(probs, axis=1, keepdims=True)
    masked = jnp.where(seen, logits, very_low)
    expo = jnp.where(seen, jnp.exp(masked - jnp.max(masked, axis=1, keepdims=True)), 0.0)
    result = expo / jnp.sum(expo, axis=1, keepdims=True) - target
    out_ref[...] = jnp.where(seen, result, 0.0).astype(out_ref.dtype)


def back_kernel(parts, count, *refs):
    grad_refs = refs[:parts]
    blocks = refs[parts : parts + count]
    query_ref, weight_ref = refs[parts + count : parts + count + 2]
    query_out, weight_out = refs[parts + count + 2 : parts + count + 4]
    key_outs = refs[parts + count + 4 : parts + 2 * count + 4]
    keys, turned_keys, grad, grad_turned, key_total, query_total = refs[parts + 2 * count + 4 :]
    heads, rows, width = query_ref.shape
    me = lax.axis_index("ha")
    for r in range(parts):
        size = grad_refs[r].shape[0]
        grad[pl.ds(pl.multiple_of((me ^ r) * size, size), size), :] = grad_refs[r][...].astype(
            jnp.float32
        )
    for k in range(count):
        at = slice(k * rows, (k + 1) * rows)
        keys[at, :] = blocks[k][...]
        turned_keys[:, at] = blocks[k][...].T
        grad_turned[at, :] = grad[:, at].T
    key_total[...] = jnp.zeros_like(key_total)

    def body(pair, carry):
        two = query_ref[pl.ds(2 * pair, 2)].reshape(2 * rows, width)
        act = lax.dot_general(
            keys[...], two, (((1,), (1,)), ((), ())), preferred_element_type=jnp.float32
        )
        coeffs = []
        for half in range(2):
            head = 2 * pair + half
            mine = act[:, half * rows : (half + 1) * rows]
            g = grad_turned[...]
            weight_out[pl.ds(head, 1), :] = jnp.sum(
                g * jnp.maximum(mine, 0.0), axis=0, keepdims=True
            )
            coeffs.append(
                jnp.where(mine > 0.0, g * weight_ref[pl.ds(head, 1), :], 0.0).astype(jnp.bfloat16)
            )
        coeffs = jnp.concatenate(coeffs, axis=1)
        key_total[...] += jnp.dot(coeffs, two, preferred_element_type=jnp.float32)
        found = jnp.dot(turned_keys[...], coeffs, preferred_element_type=jnp.float32)
        for half in range(2):
            query_total[pl.ds(2 * pair + half, rows, stride=heads), :] = found[
                :, half * rows : (half + 1) * rows
            ].T
        return carry

    lax.fori_loop(0, heads // 2, body, 0)
    query_out[...] = query_total[...].astype(query_out.dtype)
    for k in range(count):
        key_outs[k][...] = key_total[k * rows : (k + 1) * rows, :].astype(key_outs[k].dtype)


def sum_kernel(*refs):
    out_ref = refs[-1]
    out_ref[...] = tree([ref[...].astype(jnp.float32) for ref in refs[:-1]]).astype(out_ref.dtype)


def on_device(main_query, latent, log_sums, window_start, index_query, index_key, index_weight):
    rows, head_count, width = main_query.shape
    index_heads, index_width = index_query.shape[1:]
    blocks = lax.axis_size("pb")
    parts = lax.axis_size("ha")
    share = rows // parts
    chunks = blocks // group
    span = group * rows

    def swap(value, axis, rel):
        size = lax.axis_size(axis)
        return lax.ppermute(value, axis, [(i, i ^ rel) for i in range(size)])

    packed = pl.pallas_call(
        pack_kernel,
        out_shape=jax.ShapeDtypeStruct((rows, index_width + width), jnp.bfloat16),
        in_specs=[VMEM, VMEM],
        out_specs=VMEM,
        compiler_params=params(),
    )(latent.T, index_key)
    held = [None] * blocks
    held[0] = packed
    held[1] = swap(packed, "pb", 1)
    for k in range(2, blocks, 2):
        held[k] = swap(packed, "pb", k)
        held[k + 1] = swap(held[k], "pb", 1)

    query_by_head = jnp.transpose(index_query, (1, 0, 2))
    weights = index_weight.T
    sums = log_sums.T
    start_row = window_start.reshape(1, rows)
    start_column = window_start.reshape(rows, 1)
    key_only = pl.BlockSpec((rows, index_width), lambda *_: (0, 0))

    logit_parts, prob_parts = [], []
    for c in range(chunks):
        rels = list(range(c * group, (c + 1) * group))
        mine = pl.pallas_call(
            functools.partial(index_kernel, group),
            grid=(1,),
            out_shape=[jax.ShapeDtypeStruct((share, span), jnp.float32)] * parts,
            in_specs=[key_only] * group + [VMEM, VMEM],
            out_specs=[VMEM] * parts,
            scratch_shapes=[
                pltpu.VMEM((span, index_width), jnp.bfloat16),
                pltpu.VMEM((span, rows), jnp.float32),
                pltpu.VMEM((rows, span), jnp.float32),
            ],
            compiler_params=params(),
            cost_estimate=pl.CostEstimate(
                flops=2 * span * rows * index_heads * index_width,
                bytes_accessed=2 * rows * index_heads * index_width,
                transcendentals=0,
            ),
        )(*[held[k] for k in rels], query_by_head, weights)
        logit_parts += [mine[0]] + [swap(mine[r], "ha", r) for r in range(1, parts)]
    per_step = min(8, head_count)
    for c in range(chunks):
        rels = list(range(c * group, (c + 1) * group))
        mine = pl.pallas_call(
            functools.partial(main_kernel, rels),
            grid=(head_count // per_step,),
            out_shape=[jax.ShapeDtypeStruct((share, span), jnp.bfloat16)] * parts,
            in_specs=[VMEM] * group
            + [
                pl.BlockSpec((per_step, width, rows), lambda i: (i, 0, 0)),
                pl.BlockSpec((per_step, rows), lambda i: (i, 0)),
                VMEM,
            ],
            out_specs=[VMEM] * parts,
            scratch_shapes=[
                pltpu.VMEM((span, width), jnp.bfloat16),
                pltpu.VMEM((span, rows), jnp.float32),
                pltpu.VMEM((rows, span), jnp.float32),
            ],
            compiler_params=params(),
            cost_estimate=pl.CostEstimate(
                flops=2 * span * rows * head_count * width,
                bytes_accessed=2 * rows * head_count * width,
                transcendentals=span * rows * head_count,
            ),
        )(*[held[k] for k in rels], jnp.transpose(main_query, (1, 2, 0)), sums, start_row)
        prob_parts += [mine[0]] + [swap(mine[r], "ha", r) for r in range(1, parts)]

    grad = pl.pallas_call(
        functools.partial(grad_kernel, parts, chunks),
        out_shape=jax.ShapeDtypeStruct((share, chunks * span), jnp.bfloat16),
        in_specs=[VMEM] * (2 * parts * chunks + 1),
        out_specs=VMEM,
        compiler_params=params(),
    )(*logit_parts, *prob_parts, start_column)
    grads = [grad] + [swap(grad, "ha", r) for r in range(1, parts)]

    tokens = blocks * rows
    found = pl.pallas_call(
        functools.partial(back_kernel, parts, blocks),
        grid=(1,),
        out_shape=[
            jax.ShapeDtypeStruct((rows * index_heads, index_width), jnp.bfloat16),
            jax.ShapeDtypeStruct((index_heads, rows), jnp.float32),
        ]
        + [jax.ShapeDtypeStruct((rows, index_width), jnp.bfloat16)] * blocks,
        in_specs=[VMEM] * parts + [key_only] * blocks + [VMEM, VMEM],
        out_specs=[VMEM] * (2 + blocks),
        scratch_shapes=[
            pltpu.VMEM((tokens, index_width), jnp.bfloat16),
            pltpu.VMEM((index_width, tokens), jnp.bfloat16),
            pltpu.VMEM((rows, tokens), jnp.float32),
            pltpu.VMEM((tokens, rows), jnp.float32),
            pltpu.VMEM((tokens, index_width), jnp.float32),
            pltpu.VMEM((rows * index_heads, index_width), jnp.float32),
        ],
        compiler_params=params(),
    )(*grads, *held, query_by_head, weights)
    query_grad, weight_grad = found[:2]
    terms = [found[2]] + [swap(found[2 + k], "pb", k) for k in range(1, blocks)]

    def add_up(values):
        return pl.pallas_call(
            sum_kernel,
            out_shape=jax.ShapeDtypeStruct(values[0].shape, jnp.bfloat16),
            in_specs=[VMEM] * len(values),
            out_specs=VMEM,
            compiler_params=params(),
        )(*values)

    mine = add_up(terms)
    key_grad = add_up([mine] + [swap(mine, "ha", r) for r in range(1, parts)])
    return (query_grad.reshape(index_query.shape), key_grad, weight_grad.T)


def solution(mesh):
    return jax.shard_map(
        on_device,
        mesh=mesh,
        in_specs=(
            P("pb", "ha", None),
            P("pb", None),
            P("pb", "ha"),
            P("pb"),
            P("pb", "ha", None),
            P("pb", None),
            P("pb", "ha"),
        ),
        out_specs=(P("pb", "ha", None), P("pb", None), P("pb", "ha")),
        check_vma=False,
    )
```

time: 353 us -> 93.9 us (0.27)
  waiting for transfers between devices: 191 us -> 23.5 us
  local copies, waits for them, and re-layouts: 61.3 us -> 6.67 us
  starting transfers between devices: 0.3 us -> 38.2 us
  matrix products: 36.9 us -> 0 us
  Pallas kernels: 0 us -> 24.4 us
  blocking collectives: 23.9 us -> 0 us
  other arithmetic: 23.2 us -> 0 us
  between operations: 13.9 us -> 0.79 us
    reduce_scatter x1 -> x0, waiting for transfers between devices: 131 us -> none  [on_device(): lax.psum_scatter(key_grad, ('pb', 'ha'), scatter_dimension=0, tiled=True)]
    psum x1 -> x0, waiting for transfers between devices: 52 us -> none  [on_device(): probs_all, logit_all = lax.psum((probs_part, logit_part), 'ha')]
    ppermute x0 -> x32, starting transfers between devices: none -> 38.2 us  [swap(): return lax.ppermute(value, axis, [(i, i ^ rel) for i in range(size)])]
    dot_general x10 -> x0, matrix products: 36.9 us -> none  [the longest x2 18.8 us: one_block(): jnp.einsum('rd,kd->rk', flat_query, latent_block, preferred_element_type=...]
    mul x7 -> x0, local copies, waits for them, and re-layouts: 33.9 us -> none  [the longest x2 18 us: one_block(): scores = scores.reshape(query_rows, head_count, block_size) * main_scale]
    pallas_call x0 -> x9, Pallas kernels: none -> 24.4 us  [the longest x2 12.9 us: on_device(): pl.pallas_call(functools.partial(main_kernel, rels), grid=(head_count //...]
    all_gather x2 -> x0, blocking collectives: 23.9 us -> none  [the longest x1 13.1 us: on_device(): key_output = lax.all_gather(key_share, 'ha', axis=0, tiled=True)]
    ppermute x0 -> x32, waiting for transfers between devices: none -> 23.5 us  [swap(): return lax.ppermute(value, axis, [(i, i ^ rel) for i in range(size)])]
  transfers between devices with their start and end apart: 3 -> 32, of which waited for: 3 -> 11; matrix products, arithmetic and copies ran while one was open for 4% -> 1% of each run, Pallas kernels for 0% -> 18%
where the time goes in v1:
time: 93.9 us; the launch traced here: 93.6 us
  starting transfers between devices  38.2 us (41%)
  Pallas kernels  24.4 us (26%)
  waiting for transfers between devices  23.5 us (25%)
  local copies, waits for them, and re-layouts  6.67 us (7%)
    ppermute x32, starting transfers between devices, swap(): return lax.ppermute(value, axis, [(i, i ^ rel) for i in range(size)])  38.2 us
    ppermute x32, waiting for transfers between devices, swap(): return lax.ppermute(value, axis, [(i, i ^ rel) for i in range(size)])  23.5 us
    pallas_call x2, Pallas kernels, on_device(): pl.pallas_call(functools.partial(main_kernel, rels), grid=(head_count //...  12.9 us
    unnamed x19, local copies, waits for them, and re-layouts  6.56 us
    pallas_call x1, Pallas kernels, on_device(): pl.pallas_call(functools.partial(back_kernel, parts, blocks), grid=(1,),...  6.4 us
    pallas_call x2, Pallas kernels, on_device(): pl.pallas_call(functools.partial(index_kernel, group), grid=(1,), out_sha...  4.08 us
  transfers between devices with their start and end apart: 32, of which 11 were waited for; matrix products, arithmetic and copies ran while one was open for 1% of the time, Pallas kernels for 18%

profile of v1, /device:TPU:0, one launch (start us, length us, event | category | flops | bytes accessed | tf_op | source)
XLA Modules:
  0.0 93.6 jit_solution(18045285493161192174)
XLA Ops:
  2.4 4.0 %collective-permute-start.8 = (bf16[128,704]{1,0:T(8,128)(2,1)S(1)}, bf16[128,704]{1,0:T(8,128)(2,1)S(1)}, u32[]{:S(2)}, u32[]{:S(2)}) collective-permute-start(bf16[128,704]{1,0:T(8,128)(2,1)S(1)} %shard_map.94.refs_0_.refs_4_), channel_id=1, source_target_pairs={{0,24},{4,28},{8,16},{12,20},{16,8},{20,12},{24,0},{28,4},{1,25},{... | collective-permute-start | bytes 540680 | tf_op jit(solution)/shard_map/ppermute | solution.py:215
  7.0 5.1 %collective-permute-done.8.refs_2_.refs_10_ = bf16[128,704]{1,0:T(8,128)(2,1)S(1)} collective-permute-done((bf16[128,704]{1,0:T(8,128)(2,1)S(1)}, bf16[128,704]{1,0:T(8,128)(2,1)S(1)}, u32[]{:S(2)}, u32[]{:S(2)}) %collective-permute-start.8) | collective-permute-done | bytes 180256 | tf_op jit(solution)/shard_map/ppermute | solution.py:215
  12.1 3.3 %collective-permute-done.6.refs_0_.refs_8_ = bf16[128,704]{1,0:T(8,128)(2,1)S(1)} collective-permute-done((bf16[128,704]{1,0:T(8,128)(2,1)S(1)}, bf16[128,704]{1,0:T(8,128)(2,1)S(1)}, u32[]{:S(2)}, u32[]{:S(2)}) %collective-permute-start.6) | collective-permute-done | bytes 180256 | tf_op jit(solution)/shard_map/ppermute | solution.py:215
  18.0 2.3 %copy-done.5 = bf16[128,32,576]{0,2,1:T(8,128)(2,1)S(1)} copy-done((bf16[128,32,576]{0,2,1:T(8,128)(2,1)S(1)}, bf16[128,32,576]{0,2,1:T(8,128)(2,1)}, u32[]{:S(2)}) %copy-start.5) | copy-done | bytes 4718616
  21.0 6.4 %shard_map.98 = (bf16[32,512]{1,0:T(8,128)(2,1)S(1)}, bf16[32,512]{1,0:T(8,128)(2,1)S(1)}, bf16[32,512]{1,0:T(8,128)(2,1)S(1)}, bf16[32,512]{1,0:T(8,128)(2,1)S(1)}) custom-call(bf16[128,704]{1,0:T(8,128)(2,1)S(1)} %collective-permute-done.6.refs_0_.refs_8_, bf16[128,704]{1,0:T(8,128)(2,1)S(1)} %collective-permute-done.7.refs_1_.refs_9_, ...), custom_call_target="tpu_custom_call" | custom-call | flops 2415919104 | bytes 4718592 | tf_op jit(solution)/shard_map/pallas_call | solution.py:263
  27.5 1.8 %collective-permute-start.16 = (bf16[32,512]{1,0:T(8,128)(2,1)S(1)}, bf16[32,512]{1,0:T(8,128)(2,1)S(1)}, u32[]{:S(2)}, u32[]{:S(2)}) collective-permute-start(bf16[32,512]{1,0:T(8,128)(2,1)S(1)} %get-tuple-element.42), channel_id=1, source_target_pairs={{0,1},{1,0},{2,3},{3,2},{4,5},{5,4},{6,7},{7,6},{8,9},{9,8},{10,11... | collective-permute-start | bytes 98312 | tf_op jit(solution)/shard_map/ppermute | solution.py:215
  29.3 2.6 %collective-permute-start.17 = (bf16[32,512]{1,0:T(8,128)(2,1)S(1)}, bf16[32,512]{1,0:T(8,128)(2,1)S(1)}, u32[]{:S(2)}, u32[]{:S(2)}) collective-permute-start(bf16[32,512]{1,0:T(8,128)(2,1)S(1)} %get-tuple-element.43), channel_id=1, source_target_pairs={{0,2},{1,3},{2,0},{3,1},{4,6},{5,7},{6,4},{7,5},{8,10},{9,11},{10,... | collective-permute-start | bytes 98312 | tf_op jit(solution)/shard_map/ppermute | solution.py:215
  31.9 2.0 %shard_map.96 = (f32[32,512]{1,0:T(8,128)S(1)}, f32[32,512]{1,0:T(8,128)S(1)}, f32[32,512]{1,0:T(8,128)S(1)}, f32[32,512]{1,0:T(8,128)S(1)}) custom-call(bf16[128,704]{1,0:T(8,128)(2,1)S(1)} %collective-permute-done.6.refs_0_.refs_8_, bf16[128,704]{1,0:T(8,128)(2,1)S(1)} %collective-permute-done.7.refs_1_.refs_9_, ...), custom_call_target="tpu_custom_call" | custom-call | flops 268435456 | bytes 524288 | tf_op jit(solution)/shard_map/pallas_call | solution.py:241
  34.9 6.5 %shard_map.97 = (bf16[32,512]{1,0:T(8,128)(2,1)S(1)}, bf16[32,512]{1,0:T(8,128)(2,1)S(1)}, bf16[32,512]{1,0:T(8,128)(2,1)S(1)}, bf16[32,512]{1,0:T(8,128)(2,1)S(1)}) custom-call(bf16[128,704]{1,0:T(8,128)(2,1)S(1)} %shard_map.94.refs_0_.refs_4_, bf16[128,704]{1,0:T(8,128)(2,1)S(1)} %collective-permute-done.refs_1_.refs_5_, ...), custom_call_target="tpu_custom_call" | custom-call | flops 2415919104 | bytes 4718592 | tf_op jit(solution)/shard_map/pallas_call | solution.py:263
  42.6 2.4 %collective-permute-start.14 = (bf16[32,512]{1,0:T(8,128)(2,1)S(1)}, bf16[32,512]{1,0:T(8,128)(2,1)S(1)}, u32[]{:S(2)}, u32[]{:S(2)}) collective-permute-start(bf16[32,512]{1,0:T(8,128)(2,1)S(1)} %get-tuple-element.39), channel_id=1, source_target_pairs={{0,2},{1,3},{2,0},{3,1},{4,6},{5,7},{6,4},{7,5},{8,10},{9,11},{10,... | collective-permute-start | bytes 98312 | tf_op jit(solution)/shard_map/ppermute | solution.py:215
  46.5 2.0 %shard_map.95 = (f32[32,512]{1,0:T(8,128)S(1)}, f32[32,512]{1,0:T(8,128)S(1)}, f32[32,512]{1,0:T(8,128)S(1)}, f32[32,512]{1,0:T(8,128)S(1)}) custom-call(bf16[128,704]{1,0:T(8,128)(2,1)S(1)} %shard_map.94.refs_0_.refs_4_, bf16[128,704]{1,0:T(8,128)(2,1)S(1)} %collective-permute-done.refs_1_.refs_5_, ...), custom_call_target="tpu_custom_call" | custom-call | flops 268435456 | bytes 524288 | tf_op jit(solution)/shard_map/pallas_call | solution.py:241
  48.6 2.0 %collective-permute-start.11 = (f32[32,512]{1,0:T(8,128)S(1)}, f32[32,512]{1,0:T(8,128)S(1)}, u32[]{:S(2)}, u32[]{:S(2)}) collective-permute-start(f32[32,512]{1,0:T(8,128)S(1)} %get-tuple-element.35), channel_id=1, source_target_pairs={{0,2},{1,3},{2,0},{3,1},{4,6},{5,7},{6,4},{7,5},{8,10},{9,11},{10,... | collective-permute-start | bytes 196616 | tf_op jit(solution)/shard_map/ppermute | solution.py:215
  52.1 2.9 %collective-permute-start.4 = (f32[32,512]{1,0:T(8,128)S(1)}, f32[32,512]{1,0:T(8,128)S(1)}, u32[]{:S(2)}, u32[]{:S(2)}) collective-permute-start(f32[32,512]{1,0:T(8,128)S(1)} %get-tuple-element.31), channel_id=1, source_target_pairs={{0,2},{1,3},{2,0},{3,1},{4,6},{5,7},{6,4},{7,5},{8,10},{9,11},{10,... | collective-permute-start | bytes 196616 | tf_op jit(solution)/shard_map/ppermute | solution.py:215
  56.0 1.6 %collective-permute-done.11.refs_6_ = f32[32,512]{1,0:T(8,128)S(1)} collective-permute-done((f32[32,512]{1,0:T(8,128)S(1)}, f32[32,512]{1,0:T(8,128)S(1)}, u32[]{:S(2)}, u32[]{:S(2)}) %collective-permute-start.11) | collective-permute-done | bytes 65568 | tf_op jit(solution)/shard_map/ppermute | solution.py:215
  57.7 3.8 %collective-permute-done.4.refs_2_ = f32[32,512]{1,0:T(8,128)S(1)} collective-permute-done((f32[32,512]{1,0:T(8,128)S(1)}, f32[32,512]{1,0:T(8,128)S(1)}, u32[]{:S(2)}, u32[]{:S(2)}) %collective-permute-start.4) | collective-permute-done | bytes 65568 | tf_op jit(solution)/shard_map/ppermute | solution.py:215
  61.8 2.4 %collective-permute-start.21 = (bf16[32,1024]{1,0:T(8,128)(2,1)S(1)}, bf16[32,1024]{1,0:T(8,128)(2,1)S(1)}, u32[]{:S(2)}, u32[]{:S(2)}) collective-permute-start(bf16[32,1024]{1,0:T(8,128)(2,1)S(1)} %shard_map.99.refs_0_), channel_id=1, source_target_pairs={{0,3},{1,2},{2,1},{3,0},{4,7},{5,6},{6,5},{7,4},{8,11},{9,10},{10,... | collective-permute-start | bytes 196616 | tf_op jit(solution)/shard_map/ppermute | solution.py:215
  64.6 1.7 %collective-permute-start.19 = (bf16[32,1024]{1,0:T(8,128)(2,1)S(1)}, bf16[32,1024]{1,0:T(8,128)(2,1)S(1)}, u32[]{:S(2)}, u32[]{:S(2)}) collective-permute-start(bf16[32,1024]{1,0:T(8,128)(2,1)S(1)} %shard_map.99.refs_0_), channel_id=1, source_target_pairs={{0,1},{1,0},{2,3},{3,2},{4,5},{5,4},{6,7},{7,6},{8,9},{9,8},{10,11... | collective-permute-start | bytes 196616 | tf_op jit(solution)/shard_map/ppermute | solution.py:215
  66.2 2.1 %collective-permute-done.21.refs_3_ = bf16[32,1024]{1,0:T(8,128)(2,1)S(1)} collective-permute-done((bf16[32,1024]{1,0:T(8,128)(2,1)S(1)}, bf16[32,1024]{1,0:T(8,128)(2,1)S(1)}, u32[]{:S(2)}, u32[]{:S(2)}) %collective-permute-start.21) | collective-permute-done | bytes 65568 | tf_op jit(solution)/shard_map/ppermute | solution.py:215
  68.4 1.6 %collective-permute-done.20.refs_2_ = bf16[32,1024]{1,0:T(8,128)(2,1)S(1)} collective-permute-done((bf16[32,1024]{1,0:T(8,128)(2,1)S(1)}, bf16[32,1024]{1,0:T(8,128)(2,1)S(1)}, u32[]{:S(2)}, u32[]{:S(2)}) %collective-permute-start.20) | collective-permute-done | bytes 65568 | tf_op jit(solution)/shard_map/ppermute | solution.py:215
  69.9 6.4 %shard_map.100 = (bf16[2048,128]{1,0:T(8,128)(2,1)}, f32[16,128]{1,0:T(8,128)}, bf16[128,128]{1,0:T(8,128)(2,1)S(1)}, bf16[128,128]{1,0:T(8,128)(2,1)S(1)}, bf16...) custom-call(bf16[32,1024]{1,0:T(8,128)(2,1)S(1)} %shard_map.99.refs_, ...), custom_call_target="tpu_custom_call" | custom-call | tf_op jit(solution)/shard_map/pallas_call | solution.py:298
  78.2 1.5 %collective-permute-start.25 = (bf16[128,128]{1,0:T(8,128)(2,1)S(1)}, bf16[128,128]{1,0:T(8,128)(2,1)S(1)}, u32[]{:S(2)}, u32[]{:S(2)}) collective-permute-start(bf16[128,128]{1,0:T(8,128)(2,1)S(1)} %get-tuple-element.50), channel_id=1, source_target_pairs={{0,16},{4,20},{8,24},{12,28},{16,0},{20,4},{24,8},{28,12},{1,17},{... | collective-permute-start | bytes 98312 | tf_op jit(solution)/shard_map/ppermute | solution.py:215
  79.8 1.7 %collective-permute-start.27 = (bf16[128,128]{1,0:T(8,128)(2,1)S(1)}, bf16[128,128]{1,0:T(8,128)(2,1)S(1)}, u32[]{:S(2)}, u32[]{:S(2)}) collective-permute-start(bf16[128,128]{1,0:T(8,128)(2,1)S(1)} %get-tuple-element.52), channel_id=1, source_target_pairs={{0,24},{4,28},{8,16},{12,20},{16,8},{20,12},{24,0},{28,4},{1,25},{... | collective-permute-start | bytes 98312 | tf_op jit(solution)/shard_map/ppermute | solution.py:215
  85.9 2.3 %collective-permute-start.31 = (bf16[128,128]{1,0:T(8,128)(2,1)S(1)}, bf16[128,128]{1,0:T(8,128)(2,1)S(1)}, u32[]{:S(2)}, u32[]{:S(2)}) collective-permute-start(bf16[128,128]{1,0:T(8,128)(2,1)S(1)} %shard_map.101.refs_0_), channel_id=1, source_target_pairs={{0,3},{1,2},{2,1},{3,0},{4,7},{5,6},{6,5},{7,4},{8,11},{9,10},{10,... | collective-permute-start | bytes 98312 | tf_op jit(solution)/shard_map/ppermute | solution.py:215
  88.1 2.2 %collective-permute-start.29 = (bf16[128,128]{1,0:T(8,128)(2,1)S(1)}, bf16[128,128]{1,0:T(8,128)(2,1)S(1)}, u32[]{:S(2)}, u32[]{:S(2)}) collective-permute-start(bf16[128,128]{1,0:T(8,128)(2,1)S(1)} %shard_map.101.refs_0_), channel_id=1, source_target_pairs={{0,1},{1,0},{2,3},{3,2},{4,5},{5,4},{6,7},{7,6},{8,9},{9,8},{10,11... | collective-permute-start | bytes 98312 | tf_op jit(solution)/shard_map/ppermute | solution.py:215
  (69 shorter events, 21.9 us)
Async XLA Ops:
  2.4 9.7 %collective-permute-start.8 = (bf16[128,704]{1,0:T(8,128)(2,1)S(1)}, bf16[128,704]{1,0:T(8,128)(2,1)S(1)}, u32[]{:S(2)}, u32[]{:S(2)}) collective-permute-start(bf16[128,704]{1,0:T(8,128)(2,1)S(1)} %shard_map.94.refs_0_.refs_4_), channel_id=1, source_target_pairs={{0,24},{4,28},{8,16},{12,20},{16,8},{20,12},{24,0},{28,4},{1,25},{... | collective-permute-start | bytes 540680 | tf_op jit(solution)/shard_map/ppermute | solution.py:215
  6.4 9.1 %collective-permute-start.6 = (bf16[128,704]{1,0:T(8,128)(2,1)S(1)}, bf16[128,704]{1,0:T(8,128)(2,1)S(1)}, u32[]{:S(2)}, u32[]{:S(2)}) collective-permute-start(bf16[128,704]{1,0:T(8,128)(2,1)S(1)} %shard_map.94.refs_0_.refs_4_), channel_id=1, source_target_pairs={{0,16},{4,20},{8,24},{12,28},{16,0},{20,4},{24,8},{28,12},{1,17},{... | collective-permute-start | bytes 540680 | tf_op jit(solution)/shard_map/ppermute | solution.py:215
  6.9 10.3 %collective-permute-start.1 = (bf16[128,704]{1,0:T(8,128)(2,1)S(1)}, bf16[128,704]{1,0:T(8,128)(2,1)S(1)}, u32[]{:S(2)}, u32[]{:S(2)}) collective-permute-start(bf16[128,704]{1,0:T(8,128)(2,1)S(1)} %shard_map.94.refs_0_.refs_4_), channel_id=1, source_target_pairs={{0,8},{4,12},{8,0},{12,4},{16,24},{20,28},{24,16},{28,20},{1,9},{5... | collective-permute-start | bytes 540680 | tf_op jit(solution)/shard_map/ppermute | solution.py:215
  12.1 5.1 %collective-permute-start.9 = (bf16[128,704]{1,0:T(8,128)(2,1)S(1)}, bf16[128,704]{1,0:T(8,128)(2,1)S(1)}, u32[]{:S(2)}, u32[]{:S(2)}) collective-permute-start(bf16[128,704]{1,0:T(8,128)(2,1)S(1)} %collective-permute-done.8.refs_2_.refs_10_), channel_id=1, source_target_pairs={{0,4},{4,0},{8,12},{12,8},{16,20},{20,16},{24,28},{28,24},{1,5},{5... | collective-permute-start | bytes 540680 | tf_op jit(solution)/shard_map/ppermute | solution.py:215
  15.5 18.5 %collective-permute-start = (bf16[128,704]{1,0:T(8,128)(2,1)S(1)}, bf16[128,704]{1,0:T(8,128)(2,1)S(1)}, u32[]{:S(2)}, u32[]{:S(2)}) collective-permute-start(bf16[128,704]{1,0:T(8,128)(2,1)S(1)} %shard_map.94.refs_0_.refs_4_), channel_id=1, source_target_pairs={{0,4},{4,0},{8,12},{12,8},{16,20},{20,16},{24,28},{28,24},{1,5},{5... | collective-permute-start | bytes 540680 | tf_op jit(solution)/shard_map/ppermute | solution.py:215
  17.2 17.7 %collective-permute-start.2 = (bf16[128,704]{1,0:T(8,128)(2,1)S(1)}, bf16[128,704]{1,0:T(8,128)(2,1)S(1)}, u32[]{:S(2)}, u32[]{:S(2)}) collective-permute-start(bf16[128,704]{1,0:T(8,128)(2,1)S(1)} %collective-permute-done.1.refs_2_.refs_6_), channel_id=1, source_target_pairs={{0,4},{4,0},{8,12},{12,8},{16,20},{20,16},{24,28},{28,24},{1,5},{5... | collective-permute-start | bytes 540680 | tf_op jit(solution)/shard_map/ppermute | solution.py:215
  27.5 15.2 %collective-permute-start.16 = (bf16[32,512]{1,0:T(8,128)(2,1)S(1)}, bf16[32,512]{1,0:T(8,128)(2,1)S(1)}, u32[]{:S(2)}, u32[]{:S(2)}) collective-permute-start(bf16[32,512]{1,0:T(8,128)(2,1)S(1)} %get-tuple-element.42), channel_id=1, source_target_pairs={{0,1},{1,0},{2,3},{3,2},{4,5},{5,4},{6,7},{7,6},{8,9},{9,8},{10,11... | collective-permute-start | bytes 98312 | tf_op jit(solution)/shard_map/ppermute | solution.py:215
  29.3 15.8 %collective-permute-start.17 = (bf16[32,512]{1,0:T(8,128)(2,1)S(1)}, bf16[32,512]{1,0:T(8,128)(2,1)S(1)}, u32[]{:S(2)}, u32[]{:S(2)}) collective-permute-start(bf16[32,512]{1,0:T(8,128)(2,1)S(1)} %get-tuple-element.43), channel_id=1, source_target_pairs={{0,2},{1,3},{2,0},{3,1},{4,6},{5,7},{6,4},{7,5},{8,10},{9,11},{10,... | collective-permute-start | bytes 98312 | tf_op jit(solution)/shard_map/ppermute | solution.py:215
  31.9 16.7 %collective-permute-start.18 = (bf16[32,512]{1,0:T(8,128)(2,1)S(1)}, bf16[32,512]{1,0:T(8,128)(2,1)S(1)}, u32[]{:S(2)}, u32[]{:S(2)}) collective-permute-start(bf16[32,512]{1,0:T(8,128)(2,1)S(1)} %get-tuple-element.44), channel_id=1, source_target_pairs={{0,3},{1,2},{2,1},{3,0},{4,7},{5,6},{6,5},{7,4},{8,11},{9,10},{10,... | collective-permute-start | bytes 98312 | tf_op jit(solution)/shard_map/ppermute | solution.py:215
  34.0 21.0 %collective-permute-start.10 = (f32[32,512]{1,0:T(8,128)S(1)}, f32[32,512]{1,0:T(8,128)S(1)}, u32[]{:S(2)}, u32[]{:S(2)}) collective-permute-start(f32[32,512]{1,0:T(8,128)S(1)} %get-tuple-element.34), channel_id=1, source_target_pairs={{0,1},{1,0},{2,3},{3,2},{4,5},{5,4},{6,7},{7,6},{8,9},{9,8},{10,11... | collective-permute-start | bytes 196616 | tf_op jit(solution)/shard_map/ppermute | solution.py:215
  41.4 9.2 %collective-permute-start.13 = (bf16[32,512]{1,0:T(8,128)(2,1)S(1)}, bf16[32,512]{1,0:T(8,128)(2,1)S(1)}, u32[]{:S(2)}, u32[]{:S(2)}) collective-permute-start(bf16[32,512]{1,0:T(8,128)(2,1)S(1)} %get-tuple-element.38), channel_id=1, source_target_pairs={{0,1},{1,0},{2,3},{3,2},{4,5},{5,4},{6,7},{7,6},{8,9},{9,8},{10,11... | collective-permute-start | bytes 98312 | tf_op jit(solution)/shard_map/ppermute | solution.py:215
  42.6 8.9 %collective-permute-start.14 = (bf16[32,512]{1,0:T(8,128)(2,1)S(1)}, bf16[32,512]{1,0:T(8,128)(2,1)S(1)}, u32[]{:S(2)}, u32[]{:S(2)}) collective-permute-start(bf16[32,512]{1,0:T(8,128)(2,1)S(1)} %get-tuple-element.39), channel_id=1, source_target_pairs={{0,2},{1,3},{2,0},{3,1},{4,6},{5,7},{6,4},{7,5},{8,10},{9,11},{10,... | collective-permute-start | bytes 98312 | tf_op jit(solution)/shard_map/ppermute | solution.py:215
  45.1 7.1 %collective-permute-start.15 = (bf16[32,512]{1,0:T(8,128)(2,1)S(1)}, bf16[32,512]{1,0:T(8,128)(2,1)S(1)}, u32[]{:S(2)}, u32[]{:S(2)}) collective-permute-start(bf16[32,512]{1,0:T(8,128)(2,1)S(1)} %get-tuple-element.40), channel_id=1, source_target_pairs={{0,3},{1,2},{2,1},{3,0},{4,7},{5,6},{6,5},{7,4},{8,11},{9,10},{10,... | collective-permute-start | bytes 98312 | tf_op jit(solution)/shard_map/ppermute | solution.py:215
  48.6 9.1 %collective-permute-start.11 = (f32[32,512]{1,0:T(8,128)S(1)}, f32[32,512]{1,0:T(8,128)S(1)}, u32[]{:S(2)}, u32[]{:S(2)}) collective-permute-start(f32[32,512]{1,0:T(8,128)S(1)} %get-tuple-element.35), channel_id=1, source_target_pairs={{0,2},{1,3},{2,0},{3,1},{4,6},{5,7},{6,4},{7,5},{8,10},{9,11},{10,... | collective-permute-start | bytes 196616 | tf_op jit(solution)/shard_map/ppermute | solution.py:215
  50.6 7.1 %collective-permute-start.12 = (f32[32,512]{1,0:T(8,128)S(1)}, f32[32,512]{1,0:T(8,128)S(1)}, u32[]{:S(2)}, u32[]{:S(2)}) collective-permute-start(f32[32,512]{1,0:T(8,128)S(1)} %get-tuple-element.36), channel_id=1, source_target_pairs={{0,3},{1,2},{2,1},{3,0},{4,7},{5,6},{6,5},{7,4},{8,11},{9,10},{10,... | collective-permute-start | bytes 196616 | tf_op jit(solution)/shard_map/ppermute | solution.py:215
  51.5 6.1 %collective-permute-start.3 = (f32[32,512]{1,0:T(8,128)S(1)}, f32[32,512]{1,0:T(8,128)S(1)}, u32[]{:S(2)}, u32[]{:S(2)}) collective-permute-start(f32[32,512]{1,0:T(8,128)S(1)} %get-tuple-element.30), channel_id=1, source_target_pairs={{0,1},{1,0},{2,3},{3,2},{4,5},{5,4},{6,7},{7,6},{8,9},{9,8},{10,11... | collective-permute-start | bytes 196616 | tf_op jit(solution)/shard_map/ppermute | solution.py:215
  52.1 9.3 %collective-permute-start.4 = (f32[32,512]{1,0:T(8,128)S(1)}, f32[32,512]{1,0:T(8,128)S(1)}, u32[]{:S(2)}, u32[]{:S(2)}) collective-permute-start(f32[32,512]{1,0:T(8,128)S(1)} %get-tuple-element.31), channel_id=1, source_target_pairs={{0,2},{1,3},{2,0},{3,1},{4,6},{5,7},{6,4},{7,5},{8,10},{9,11},{10,... | collective-permute-start | bytes 196616 | tf_op jit(solution)/shard_map/ppermute | solution.py:215
  55.0 6.5 %collective-permute-start.5 = (f32[32,512]{1,0:T(8,128)S(1)}, f32[32,512]{1,0:T(8,128)S(1)}, u32[]{:S(2)}, u32[]{:S(2)}) collective-permute-start(f32[32,512]{1,0:T(8,128)S(1)} %get-tuple-element.32), channel_id=1, source_target_pairs={{0,3},{1,2},{2,1},{3,0},{4,7},{5,6},{6,5},{7,4},{8,11},{9,10},{10,... | collective-permute-start | bytes 196616 | tf_op jit(solution)/shard_map/ppermute | solution.py:215
  61.8 6.6 %collective-permute-start.21 = (bf16[32,1024]{1,0:T(8,128)(2,1)S(1)}, bf16[32,1024]{1,0:T(8,128)(2,1)S(1)}, u32[]{:S(2)}, u32[]{:S(2)}) collective-permute-start(bf16[32,1024]{1,0:T(8,128)(2,1)S(1)} %shard_map.99.refs_0_), channel_id=1, source_target_pairs={{0,3},{1,2},{2,1},{3,0},{4,7},{5,6},{6,5},{7,4},{8,11},{9,10},{10,... | collective-permute-start | bytes 196616 | tf_op jit(solution)/shard_map/ppermute | solution.py:215
  64.2 5.7 %collective-permute-start.20 = (bf16[32,1024]{1,0:T(8,128)(2,1)S(1)}, bf16[32,1024]{1,0:T(8,128)(2,1)S(1)}, u32[]{:S(2)}, u32[]{:S(2)}) collective-permute-start(bf16[32,1024]{1,0:T(8,128)(2,1)S(1)} %shard_map.99.refs_0_), channel_id=1, source_target_pairs={{0,2},{1,3},{2,0},{3,1},{4,6},{5,7},{6,4},{7,5},{8,10},{9,11},{10,... | collective-permute-start | bytes 196616 | tf_op jit(solution)/shard_map/ppermute | solution.py:215
  64.6 5.4 %collective-permute-start.19 = (bf16[32,1024]{1,0:T(8,128)(2,1)S(1)}, bf16[32,1024]{1,0:T(8,128)(2,1)S(1)}, u32[]{:S(2)}, u32[]{:S(2)}) collective-permute-start(bf16[32,1024]{1,0:T(8,128)(2,1)S(1)} %shard_map.99.refs_0_), channel_id=1, source_target_pairs={{0,1},{1,0},{2,3},{3,2},{4,5},{5,4},{6,7},{7,6},{8,9},{9,8},{10,11... | collective-permute-start | bytes 196616 | tf_op jit(solution)/shard_map/ppermute | solution.py:215
  76.3 5.2 %collective-permute-start.23 = (bf16[128,128]{1,0:T(8,128)(2,1)S(1)}, bf16[128,128]{1,0:T(8,128)(2,1)S(1)}, u32[]{:S(2)}, u32[]{:S(2)}) collective-permute-start(bf16[128,128]{1,0:T(8,128)(2,1)S(1)} %get-tuple-element.48), channel_id=1, source_target_pairs={{0,8},{4,12},{8,0},{12,4},{16,24},{20,28},{24,16},{28,20},{1,9},{5... | collective-permute-start | bytes 98312 | tf_op jit(solution)/shard_map/ppermute | solution.py:215
  79.8 4.8 %collective-permute-start.27 = (bf16[128,128]{1,0:T(8,128)(2,1)S(1)}, bf16[128,128]{1,0:T(8,128)(2,1)S(1)}, u32[]{:S(2)}, u32[]{:S(2)}) collective-permute-start(bf16[128,128]{1,0:T(8,128)(2,1)S(1)} %get-tuple-element.52), channel_id=1, source_target_pairs={{0,24},{4,28},{8,16},{12,20},{16,8},{20,12},{24,0},{28,4},{1,25},{... | collective-permute-start | bytes 98312 | tf_op jit(solution)/shard_map/ppermute | solution.py:215
  85.9 5.8 %collective-permute-start.31 = (bf16[128,128]{1,0:T(8,128)(2,1)S(1)}, bf16[128,128]{1,0:T(8,128)(2,1)S(1)}, u32[]{:S(2)}, u32[]{:S(2)}) collective-permute-start(bf16[128,128]{1,0:T(8,128)(2,1)S(1)} %shard_map.101.refs_0_), channel_id=1, source_target_pairs={{0,3},{1,2},{2,1},{3,0},{4,7},{5,6},{6,5},{7,4},{8,11},{9,10},{10,... | collective-permute-start | bytes 98312 | tf_op jit(solution)/shard_map/ppermute | solution.py:215
  (17 other events, 101.8 us)

commit v2 on v0

v2 whole, which is shorter than its diff:
```python
import functools

import jax
import jax.numpy as jnp
from jax import lax
from jax.experimental import pallas as pl
from jax.experimental.pallas import tpu as pltpu
from jax.sharding import PartitionSpec as P

main_scale = 192.0 ** (-0.5)
log2e = 1.4426950408889634
very_low = -1e30
LANES = 128
TAIL = 16
f32, bf16 = jnp.float32, jnp.bfloat16


def params():
    return pltpu.CompilerParams(vmem_limit_bytes=48 * 1024 * 1024)


def whole(value):
    zeros = (0,) * len(value.shape)
    return pl.BlockSpec(value.shape, lambda *_: zeros)


def call(kernel, outs, values, scratch=(), specs=None, cost=None):
    many = isinstance(outs, list)
    found = pl.pallas_call(
        kernel,
        grid=(1,),
        out_shape=outs,
        in_specs=specs or [whole(v) for v in values],
        out_specs=[whole(o) for o in outs] if many else whole(outs),
        scratch_shapes=list(scratch),
        compiler_params=params(),
        cost_estimate=cost,
    )(*values)
    return list(found) if many else found


def tree(values):
    while len(values) > 1:
        values = [values[i] + values[i + 1] for i in range(0, len(values), 2)]
    return values[0]


def terms_of(value, count):
    found = []
    for _ in range(count):
        term = value.astype(bf16)
        found.append(term)
        value = value - term.astype(f32)
    return found


def pack_kernel(latent_ref, key_ref, query_ref, weight_ref, packed_ref, *outs):
    width = key_ref.shape[1]
    packed_ref[:, :width] = key_ref[...]
    packed_ref[:, width:] = latent_ref[...].T
    me = lax.axis_index("ha")
    heads = weight_ref.shape[0]
    rows = outs[0].shape[0] - 3 * TAIL
    split = terms_of(weight_ref[...], 3)
    for r, out in enumerate(outs):
        first = pl.multiple_of((me ^ r) * rows, rows)
        out[:rows, :] = query_ref[pl.ds(first, rows), :]
        for i in range(3):
            at = rows + i * TAIL
            if heads < TAIL:
                out[at : at + TAIL, :] = jnp.zeros((TAIL, LANES), bf16)
            out[at : at + heads, :] = split[i]


def own_lanes(value, share):
    me = lax.axis_index("ha")
    value = pltpu.roll(value, lax.rem(LANES - me * share, LANES), 1)
    lanes = lax.broadcasted_iota(jnp.int32, value.shape, 1)
    value = jnp.where(lanes < share, value, jnp.zeros_like(value))
    shift = share
    while shift < LANES:
        value = value + pltpu.roll(value, shift, 1)
        shift *= 2
    return value


def main_kernel(rels, earlier, *refs):
    count = len(rels)
    blocks = refs[:count]
    query_hbm, sums_ref, start_ref = refs[count : count + 3]
    before = refs[count + 3 : count + 3 + earlier]
    outs = refs[count + 3 + earlier : -6]
    keys, query, total, turned, sems, _ = refs[-6:]
    heads, width, rows = query.shape
    pieces = sems.shape[0]
    per = heads // pieces
    copies = [
        pltpu.make_async_copy(
            query_hbm.at[pl.ds(i * per, per)], query.at[pl.ds(i * per, per)], sems.at[i]
        )
        for i in range(pieces)
    ]
    for copy in copies:
        copy.start()
    for k in range(count):
        block = blocks[k][...]
        keys[k * rows : (k + 1) * rows, :] = block[:, block.shape[1] - width :]
    total[...] = jnp.zeros_like(total)

    for i in range(pieces):
        copies[i].wait()
        for pair in range(i * per // 2, (i + 1) * per // 2):
            two = jnp.concatenate([query[2 * pair], query[2 * pair + 1]], axis=1)
            scores = jnp.dot(keys[...], two, preferred_element_type=f32)
            parts = [
                jnp.exp2(
                    scores[:, half * rows : (half + 1) * rows] * (main_scale * log2e)
                    - sums_ref[2 * pair + half : 2 * pair + half + 1, :] * log2e
                )
                for half in range(2)
            ]
            total[...] += parts[0] + parts[1]

    me = lax.axis_index("pb")
    kept = turned.shape[1] - count * rows
    at = 0
    for ref in before:
        turned[:, at : at + ref.shape[1]] = ref[...].astype(f32)
        at += ref.shape[1]
    for k in range(count):
        key = (me ^ rels[k]) * rows + lax.broadcasted_iota(jnp.int32, (rows, rows), 0)
        mine = me * rows + lax.broadcasted_iota(jnp.int32, (rows, rows), 1)
        seen = (key >= start_ref[...]) & (key <= mine)
        piece = jnp.where(seen, total[k * rows : (k + 1) * rows, :], 0.0)
        turned[:, kept + k * rows : kept + (k + 1) * rows] = piece.T
    if len(outs) == 1:
        outs[0][...] = turned[...].astype(bf16)
    else:
        me = lax.axis_index("ha")
        share = outs[0].shape[0]
        for r, out in enumerate(outs):
            first = pl.multiple_of((me ^ r) * share, share)
            out[...] = turned[pl.ds(first, share), :].astype(bf16)


def index_kernel(share, count, parts, heads, *refs):
    blocks = refs[:count]
    messages = refs[count : count + parts]
    start_ref, prob_ref, queries_ref, weights_ref, keys, wide, total = refs[count + parts :]
    rows, width = blocks[0].shape
    for k in range(count):
        keys[k * rows : (k + 1) * rows, :] = blocks[k][...]
    own = share * heads
    repeats = LANES // share
    group = lax.broadcasted_iota(jnp.int32, (1, LANES), 1) // share
    row_of = []
    for r in range(parts):
        wide[...] = messages[r][:own, :].astype(f32)
        for j in range(heads):
            first = (r * heads + j) * share
            queries_ref[first : first + share, :] = wide[
                pl.ds(j, share, stride=heads), :
            ].astype(bf16)
        weight = tree_of_three(messages[r], own)
        weight = own_lanes(weight, share)
        row_of += [weight[j : j + 1, :] for j in range(heads)]
    weights_ref[...] = jnp.zeros_like(weights_ref)
    for g in range(len(row_of) // repeats):
        row = row_of[g * repeats]
        for i in range(1, repeats):
            row = jnp.where(group == i, row_of[g * repeats + i], row)
        weights_ref[g : g + 1, :] = row
    total[...] = jnp.zeros_like(total)
    for g in range(0, len(row_of) // repeats, 2):
        two = queries_ref[g * LANES : (g + 2) * LANES, :]
        act = lax.dot_general(
            keys[...], two, (((1,), (1,)), ((), ())), preferred_element_type=f32
        )
        act = jnp.maximum(act, 0.0)
        total[...] += (
            act[:, :LANES] * weights_ref[g : g + 1, :]
            + act[:, LANES:] * weights_ref[g + 1 : g + 2, :]
        )

    me = lax.axis_index("pb")
    lane = lax.broadcasted_iota(jnp.int32, (rows, LANES), 1) % share
    mine = me * rows + lax.axis_index("ha") * share + lane
    start = own_lanes(jnp.broadcast_to(start_ref[...], (8, LANES)), share)[:1, :]
    top = jnp.full((1, LANES), very_low, f32)
    masks = []
    for k in range(count):
        at = slice(k * rows, (k + 1) * rows)
        key = (me ^ k) * rows + lax.broadcasted_iota(jnp.int32, (rows, LANES), 0)
        seen = (key >= start) & (key <= mine)
        value = total[at, :]
        shift = share
        while shift < LANES:
            value = value + pltpu.roll(value, shift, 1)
            shift *= 2
        value = jnp.where(seen, value, very_low)
        total[at, :] = value
        top = jnp.maximum(top, jnp.max(value, axis=0, keepdims=True))
        masks.append(seen)
    mass = jnp.zeros((1, LANES), f32)
    for k in range(count):
        at = slice(k * rows, (k + 1) * rows)
        value = jnp.where(masks[k], jnp.exp(total[at, :] - top), 0.0)
        prob_ref[at, :] = value
        mass = mass + jnp.sum(value, axis=0, keepdims=True)
    prob_ref[...] = prob_ref[...] * (1.0 / mass)


def tree_of_three(ref, at):
    parts = [ref[at + i * TAIL : at + (i + 1) * TAIL, :].astype(f32) for i in range(3)]
    return parts[0] + (parts[1] + parts[2])


def back_kernel(share, count, parts, heads, *refs):
    mass_refs = refs[:parts]
    blocks = refs[parts : parts + count]
    prob_ref, queries_ref, weights_ref = refs[parts + count : parts + count + 3]
    outs = refs[parts + count + 3 : -6]
    even_ref, odd_ref = outs[:2]
    messages = outs[2:]
    keys, turned_keys, grad, key_total, query_total, weight_total = refs[-6:]
    rows, width = blocks[0].shape
    repeats = LANES // share
    mass = tree([ref[...].astype(f32) for ref in mass_refs])
    for k in range(count):
        at = slice(k * rows, (k + 1) * rows)
        keys[at, :] = blocks[k][...]
        turned_keys[:, at] = blocks[k][...].T
        grad[at, :] = jnp.concatenate([mass[:, at]] * repeats, axis=0).T
    total = jnp.sum(grad[...], axis=0, keepdims=True)
    grad[...] = prob_ref[...] - grad[...] / total
    key_total[...] = jnp.zeros_like(key_total)
    weight_total[...] = jnp.zeros_like(weight_total)
    all_heads = parts * heads
    for g in range(0, all_heads // repeats, 2):
        two = queries_ref[g * LANES : (g + 2) * LANES, :]
        act = lax.dot_general(
            keys[...], two, (((1,), (1,)), ((), ())), preferred_element_type=f32
        )
        coeffs = []
        for half in range(2):
            mine = act[:, half * LANES : (half + 1) * LANES]
            lean = grad[...]
            weight_total[g + half : g + half + 1, :] = jnp.sum(
                lean * jnp.maximum(mine, 0.0), axis=0, keepdims=True
            )
            coeffs.append(
                jnp.where(
                    mine > 0.0, lean * weights_ref[g + half : g + half + 1, :], 0.0
                ).astype(bf16)
            )
        coeffs = jnp.concatenate(coeffs, axis=1)
        key_total[...] += jnp.dot(coeffs, two, preferred_element_type=f32)
        found = jnp.dot(turned_keys[...], coeffs, preferred_element_type=f32)
        found = jnp.concatenate([found[:, :LANES].T, found[:, LANES:].T], axis=0)
        for i in range(2 * repeats):
            head = g * repeats + i
            first = (head // heads) * heads * share + head % heads
            query_total[pl.ds(first, share, stride=heads), :] = found[
                i * share : (i + 1) * share, :
            ]
    own = share * heads
    split = terms_of(weight_total[...], 2)
    for r in range(parts):
        messages[r][:own, :] = query_total[r * own : (r + 1) * own, :].astype(bf16)
        for i in range(2):
            messages[r][own + i * TAIL : own + (i + 1) * TAIL, :] = split[i]
    for i in range(count // 2):
        at = slice(i * rows, (i + 1) * rows)
        even_ref[at, :] = key_total[2 * i * rows : (2 * i + 1) * rows, :]
        odd_ref[at, :] = key_total[(2 * i + 1) * rows : (2 * i + 2) * rows, :]


def pair_kernel(mine_ref, other_ref, own_ref, *outs):
    rows = own_ref.shape[0]
    own_ref[...] = mine_ref[:rows, :] + other_ref[:rows, :]
    for i, out in enumerate(outs):
        at = slice((i + 1) * rows, (i + 2) * rows)
        out[...] = (mine_ref[at, :] + other_ref[at, :]).astype(out.dtype)


def sum_kernel(*refs):
    out_ref = refs[-1]
    out_ref[...] = tree([ref[...].astype(f32) for ref in refs[:-1]]).astype(out_ref.dtype)


def finish_kernel(share, heads, *refs):
    messages = refs[:-2]
    query_out, weight_out = refs[-2:]
    me = lax.axis_index("ha")
    own = share * heads
    total = jnp.zeros((heads, LANES), f32)
    lanes = lax.broadcasted_iota(jnp.int32, (heads, LANES), 1)
    for r, message in enumerate(messages):
        first = pl.multiple_of((me ^ r) * own, own)
        query_out[pl.ds(first, own), :] = message[:own, :]
        value = message[own : own + TAIL, :].astype(f32) + message[
            own + TAIL : own + 2 * TAIL, :
        ].astype(f32)
        rolled = {}
        found = []
        for j in range(heads):
            column = (r * heads + j) * share
            row, lane = column // LANES, column % LANES
            if lane not in rolled:
                rolled[lane] = pltpu.roll(value, LANES - lane, 1) if lane else value
            found.append(rolled[lane][row : row + 1, :])
        piece = jnp.where(lanes < share, jnp.concatenate(found, axis=0), 0.0)
        total = total + pltpu.roll(piece, (me ^ r) * share, 1)
    weight_out[...] = total


def on_device(main_query, latent, log_sums, window_start, index_query, index_key, index_weight):
    rows, head_count, width = main_query.shape
    heads, index_width = index_query.shape[1:]
    blocks = lax.axis_size("pb")
    parts = lax.axis_size("ha")
    share = rows // parts
    tokens = blocks * rows
    own = share * heads
    columns = share * heads * parts
    shape = jax.ShapeDtypeStruct

    def swap(value, axis, rel):
        size = lax.axis_size(axis)
        return lax.ppermute(value, axis, [(i, i ^ rel) for i in range(size)])

    start_row = window_start.reshape(1, rows)
    key_only = pl.BlockSpec((rows, index_width), lambda *_: (0, 0))

    packed, *asked = call(
        pack_kernel,
        [shape((rows, index_width + width), bf16)]
        + [shape((own + 3 * TAIL, index_width), bf16)] * parts,
        (latent.T, index_key, index_query.reshape(rows * heads, index_width), index_weight.T),
    )
    held = [None] * blocks
    held[0] = packed
    held[1] = swap(packed, "pb", 1)
    for k in range(2, blocks, 2):
        held[k] = swap(packed, "pb", k)
        held[k + 1] = swap(held[k], "pb", 1)
    asked = [asked[0]] + [swap(asked[r], "ha", r) for r in range(1, parts)]

    queries = jnp.transpose(main_query, (1, 2, 0))
    sums = log_sums.T
    chunks = [[0, 1]] + [list(range(k, min(k + 4, blocks))) for k in range(2, blocks, 4)]
    pieces = max(1, head_count // 8)
    mass = []
    for rels in chunks:
        last = rels is chunks[-1]
        span = len(rels) * rows
        outs = [shape((share, tokens), bf16)] * parts if last else [shape((rows, span), bf16)]
        before = mass if last else []
        values = [held[k] for k in rels] + [queries, sums, start_row] + before
        specs = [whole(v) for v in values]
        specs[len(rels)] = pl.BlockSpec(memory_space=pltpu.HBM)
        found = call(
            functools.partial(main_kernel, rels, len(before)),
            outs,
            values,
            [
                pltpu.VMEM((span, width), bf16),
                pltpu.VMEM((head_count, width, rows), bf16),
                pltpu.VMEM((span, rows), f32),
                pltpu.VMEM((rows, tokens if last else span), f32),
                pltpu.SemaphoreType.DMA((pieces,)),
                pltpu.VMEM((8, LANES), f32),
            ],
            specs,
            pl.CostEstimate(
                flops=2 * span * rows * head_count * width,
                bytes_accessed=2 * rows * head_count * width,
                transcendentals=span * rows * head_count,
            ),
        )
        mass = found if last else mass + found
    first, key_block = lax.optimization_barrier((mass[0], held[0]))
    mass = [first] + [swap(mass[r], "ha", r) for r in range(1, parts)]
    key_blocks = [key_block] + held[1:]

    probs, query_rows, weight_rows = call(
        functools.partial(index_kernel, share, blocks, parts, heads),
        [
            shape((tokens, LANES), f32),
            shape((columns, index_width), bf16),
            shape((TAIL, LANES), f32),
        ],
        key_blocks + asked + [start_row],
        [
            pltpu.VMEM((tokens, index_width), bf16),
            pltpu.VMEM((own, index_width), f32),
            pltpu.VMEM((tokens, LANES), f32),
        ],
        [key_only] * blocks + [whole(v) for v in asked + [start_row]],
        pl.CostEstimate(
            flops=2 * tokens * columns * index_width,
            bytes_accessed=2 * columns * index_width,
            transcendentals=tokens * LANES,
        ),
    )

    even, odd, *answers = call(
        functools.partial(back_kernel, share, blocks, parts, heads),
        [shape((tokens // 2, index_width), f32)] * 2
        + [shape((own + 2 * TAIL, index_width), bf16)] * parts,
        mass + key_blocks + [probs, query_rows, weight_rows],
        [
            pltpu.VMEM((tokens, index_width), bf16),
            pltpu.VMEM((index_width, tokens), bf16),
            pltpu.VMEM((tokens, LANES), f32),
            pltpu.VMEM((tokens, index_width), f32),
            pltpu.VMEM((columns, index_width), f32),
            pltpu.VMEM((TAIL, LANES), f32),
        ],
        [whole(v) for v in mass]
        + [key_only] * blocks
        + [whole(v) for v in (probs, query_rows, weight_rows)],
        pl.CostEstimate(
            flops=6 * tokens * columns * index_width,
            bytes_accessed=2 * columns * index_width,
            transcendentals=0,
        ),
    )
    odd = swap(odd, "pb", 1)
    term = shape((rows, index_width), f32)
    half = shape((rows, index_width), bf16)
    mine, *others = call(pair_kernel, [term] + [half] * (blocks // 2 - 1), (even, odd))
    others = [swap(value, "pb", 2 * (i + 1)) for i, value in enumerate(others)]
    mine = call(sum_kernel, half, [mine] + others)
    key_grad = call(sum_kernel, half, [mine] + [swap(mine, "ha", r) for r in range(1, parts)])

    answers = [answers[0]] + [swap(answers[r], "ha", r) for r in range(1, parts)]
    query_grad, weight_grad = call(
        functools.partial(finish_kernel, share, heads),
        [shape((rows * heads, index_width), bf16), shape((heads, rows), f32)],
        answers,
    )
    return (query_grad.reshape(index_query.shape), key_grad, weight_grad.T)


def solution(mesh):
    return jax.shard_map(
        on_device,
        mesh=mesh,
        in_specs=(
            P("pb", "ha", None),
            P("pb", None),
            P("pb", "ha"),
            P("pb"),
            P("pb", "ha", None),
            P("pb", None),
            P("pb", "ha"),
        ),
        out_specs=(P("pb", "ha", None), P("pb", None), P("pb", "ha")),
        check_vma=False,
    )
```

time: 353 us -> 71.3 us (0.20)
  waiting for transfers between devices: 191 us -> 17.1 us
  local copies, waits for them, and re-layouts: 61.3 us -> 7.11 us
  matrix products: 36.9 us -> 0 us
  starting transfers between devices: 0.3 us -> 26 us
  blocking collectives: 23.9 us -> 0 us
  other arithmetic: 23.2 us -> 0 us
  Pallas kernels: 0 us -> 19.9 us
  between operations: 13.9 us -> 0.76 us
    reduce_scatter x1 -> x0, waiting for transfers between devices: 131 us -> none  [on_device(): lax.psum_scatter(key_grad, ('pb', 'ha'), scatter_dimension=0, tiled=True)]
    psum x1 -> x0, waiting for transfers between devices: 52 us -> none  [on_device(): probs_all, logit_all = lax.psum((probs_part, logit_part), 'ha')]
    dot_general x10 -> x0, matrix products: 36.9 us -> none  [the longest x2 18.8 us: one_block(): jnp.einsum('rd,kd->rk', flat_query, latent_block, preferred_element_type=...]
    mul x7 -> x0, local copies, waits for them, and re-layouts: 33.9 us -> none  [the longest x2 18 us: one_block(): scores = scores.reshape(query_rows, head_count, block_size) * main_scale]
    ppermute x0 -> x23, starting transfers between devices: none -> 26 us  [swap(): return lax.ppermute(value, axis, [(i, i ^ rel) for i in range(size)])]
    all_gather x2 -> x0, blocking collectives: 23.9 us -> none  [the longest x1 13.1 us: on_device(): key_output = lax.all_gather(key_share, 'ha', axis=0, tiled=True)]
    pallas_call x0 -> x10, Pallas kernels: none -> 19.9 us  [call(): pl.pallas_call(kernel, grid=(1,), out_shape=outs, in_specs=specs or [whol...]
    reduce_sum x6 -> x0, other arithmetic: 17.3 us -> none  [the longest x2 8.62 us: one_block(): jnp.sum(jnp.exp(scores - log_sums[:, :, None]), axis=1)]
  transfers between devices with their start and end apart: 3 -> 23, of which waited for: 3 -> 9; matrix products, arithmetic and copies ran while one was open for 4% -> 0% of each run, Pallas kernels for 0% -> 21%
where the time goes in v2:
time: 71.3 us; the launch traced here: 70.9 us
  starting transfers between devices  26 us (36%)
  Pallas kernels  19.9 us (28%)
  waiting for transfers between devices  17.1 us (24%)
  local copies, waits for them, and re-layouts  7.11 us (10%)
  between operations  0.76 us (1%)
    ppermute x23, starting transfers between devices, swap(): return lax.ppermute(value, axis, [(i, i ^ rel) for i in range(size)])  26 us
    pallas_call x10, Pallas kernels, call(): pl.pallas_call(kernel, grid=(1,), out_shape=outs, in_specs=specs or [whol...  19.9 us
    ppermute x23, waiting for transfers between devices, swap(): return lax.ppermute(value, axis, [(i, i ^ rel) for i in range(size)])  17.1 us
    unnamed x16, local copies, waits for them, and re-layouts  7.11 us
  transfers between devices with their start and end apart: 23, of which 9 were waited for; matrix products, arithmetic and copies ran while one was open for 0% of the time, Pallas kernels for 21%

profile of v2, /device:TPU:0, one launch (start us, length us, event | category | flops | bytes accessed | tf_op | source)
XLA Modules:
  0.0 70.9 jit_solution(6606510293999832359)
XLA Ops:
  4.1 3.0 %collective-permute-start.5 = (bf16[128,704]{1,0:T(8,128)(2,1)S(1)}, bf16[128,704]{1,0:T(8,128)(2,1)S(1)}, u32[]{:S(2)}, u32[]{:S(2)}) collective-permute-start(bf16[128,704]{1,0:T(8,128)(2,1)S(1)} %get-tuple-element.35.refs_0_.refs_4_), channel_id=1, source_target_pairs={{0,16},{4,20},{8,24},{12,28},{16,0},{20,4},{24,8},{28,12},{1,17},{... | collective-permute-start | bytes 540680 | tf_op jit(solution)/shard_map/ppermute | solution.py:330
  7.2 1.5 %collective-permute-start.3 = (bf16[128,704]{1,0:T(8,128)(2,1)S(1)}, bf16[128,704]{1,0:T(8,128)(2,1)S(1)}, u32[]{:S(2)}, u32[]{:S(2)}) collective-permute-start(bf16[128,704]{1,0:T(8,128)(2,1)S(1)} %get-tuple-element.35.refs_0_.refs_4_), channel_id=1, source_target_pairs={{0,8},{4,12},{8,0},{12,4},{16,24},{20,28},{24,16},{28,20},{1,9},{5... | collective-permute-start | bytes 540680 | tf_op jit(solution)/shard_map/ppermute | solution.py:330
  8.7 3.4 %collective-permute-done.5.refs_2_.refs_4_.refs_8_ = bf16[128,704]{1,0:T(8,128)(2,1)S(1)} collective-permute-done((bf16[128,704]{1,0:T(8,128)(2,1)S(1)}, bf16[128,704]{1,0:T(8,128)(2,1)S(1)}, u32[]{:S(2)}, u32[]{:S(2)}) %collective-permute-start.5) | collective-permute-done | bytes 180256 | tf_op jit(solution)/shard_map/ppermute | solution.py:330
  12.1 2.9 %collective-permute-done.3.refs_0_.refs_2_.refs_6_ = bf16[128,704]{1,0:T(8,128)(2,1)S(1)} collective-permute-done((bf16[128,704]{1,0:T(8,128)(2,1)S(1)}, bf16[128,704]{1,0:T(8,128)(2,1)S(1)}, u32[]{:S(2)}, u32[]{:S(2)}) %collective-permute-start.3) | collective-permute-done | bytes 180256 | tf_op jit(solution)/shard_map/ppermute | solution.py:330
  15.0 1.6 %collective-permute-start.10 = (bf16[560,128]{1,0:T(8,128)(2,1)S(1)}, bf16[560,128]{1,0:T(8,128)(2,1)S(1)}, u32[]{:S(2)}, u32[]{:S(2)}) collective-permute-start(bf16[560,128]{1,0:T(8,128)(2,1)S(1)} %get-tuple-element.37), channel_id=1, source_target_pairs={{0,1},{1,0},{2,3},{3,2},{4,5},{5,4},{6,7},{7,6},{8,9},{9,8},{10,11... | collective-permute-start | bytes 430088 | tf_op jit(solution)/shard_map/ppermute | solution.py:330
  16.6 2.6 %collective-permute-start.11 = (bf16[560,128]{1,0:T(8,128)(2,1)S(1)}, bf16[560,128]{1,0:T(8,128)(2,1)S(1)}, u32[]{:S(2)}, u32[]{:S(2)}) collective-permute-start(bf16[560,128]{1,0:T(8,128)(2,1)S(1)} %get-tuple-element.38), channel_id=1, source_target_pairs={{0,2},{1,3},{2,0},{3,1},{4,6},{5,7},{6,4},{7,5},{8,10},{9,11},{10,... | collective-permute-start | bytes 430088 | tf_op jit(solution)/shard_map/ppermute | solution.py:330
  19.2 2.3 %copy-done = bf16[128,32,576]{0,2,1:T(8,128)(2,1)S(1)} copy-done((bf16[128,32,576]{0,2,1:T(8,128)(2,1)S(1)}, bf16[128,32,576]{0,2,1:T(8,128)(2,1)}, u32[]{:S(2)}) %copy-start) | copy-done | bytes 4718616
  22.9 3.5 %shard_map.95.refs_5_ = bf16[128,256]{1,0:T(8,128)(2,1)S(1)} custom-call(bf16[128,704]{1,0:T(8,128)(2,1)S(1)} %get-tuple-element.35.refs_0_.refs_4_, bf16[128,704]{1,0:T(8,128)(2,1)S(1)} %collective-permute-done.2.refs_1_.refs_5_, bf16[32,576,128]{2,1,0:T(8,128)(2,1)S(1)} %bitcast.8, f32[32,128]{1,0:T(8,128)S(1)} %bitcast.13, s32[1,128]{1,0:T(1,128)S(1)} %bitcast.17), custom_call_target="tpu_custom_call" | custom-call | flops 1207959552 | bytes 4718592 | tf_op jit(solution)/shard_map/pallas_call | solution.py:29
  26.7 5.2 %shard_map.96.refs_6_ = bf16[128,512]{1,0:T(8,128)(2,1)S(1)} custom-call(bf16[128,704]{1,0:T(8,128)(2,1)S(1)} %collective-permute-done.3.refs_0_.refs_2_.refs_6_, bf16[128,704]{1,0:T(8,128)(2,1)S(1)} %collective-permute-done.4.refs_1_.refs_3_.refs_7_, bf16[128,704]{1,0:T(8,128)(2,1)S(1)} %collective-permute-done.5.refs_2_.refs_4_.refs_8_, ...), custom_call_target="tpu_custom_call" | custom-call | flops 2415919104 | bytes 4718592 | tf_op jit(solution)/shard_map/pallas_call | solution.py:29
  31.9 3.7 %shard_map.97 = (bf16[32,1024]{1,0:T(8,128)(2,1)S(1)}, bf16[32,1024]{1,0:T(8,128)(2,1)S(1)}, bf16[32,1024]{1,0:T(8,128)(2,1)S(1)}, bf16[32,1024]{1,0:T(8,128)(2,1)S(1)}) custom-call(bf16[128,704]{1,0:T(8,128)(2,1)S(1)} %collective-permute-done.refs_0_.refs_6_.refs_10_, bf16[128,704]{1,0:T(8,128)(2,1)S(1)} %collective-permute-done.1.refs_1_.refs_7_.refs_11_, ...), custom_call_target="tpu_custom_call" | custom-call | flops 1207959552 | bytes 4718592 | tf_op jit(solution)/shard_map/pallas_call | solution.py:29
  36.3 3.5 %collective-permute-start.8 = (bf16[32,1024]{1,0:T(8,128)(2,1)S(1)}, bf16[32,1024]{1,0:T(8,128)(2,1)S(1)}, u32[]{:S(2)}, u32[]{:S(2)}) collective-permute-start(bf16[32,1024]{1,0:T(8,128)(2,1)S(1)} %get-tuple-element.33), channel_id=1, source_target_pairs={{0,2},{1,3},{2,0},{3,1},{4,6},{5,7},{6,4},{7,5},{8,10},{9,11},{10,... | collective-permute-start | bytes 196616 | tf_op jit(solution)/shard_map/ppermute | solution.py:330
  40.0 1.9 %shard_map.98 = (f32[1024,128]{1,0:T(8,128)S(1)}, bf16[2048,128]{1,0:T(8,128)(2,1)S(1)}, f32[16,128]{1,0:T(8,128)S(1)}) custom-call(bf16[128,704]{1,0:T(8,128)(2,1)S(1)} %get-tuple-element.35.refs_0_.refs_4_, bf16[128,704]{1,0:T(8,128)(2,1)S(1)} %collective-permute-done.2.refs_1_.refs_5_, ...), custom_call_target="tpu_custom_call" | custom-call | flops 536870912 | bytes 524288 | tf_op jit(solution)/shard_map/pallas_call | solution.py:29
  41.9 2.1 %collective-permute-done.8.refs_2_ = bf16[32,1024]{1,0:T(8,128)(2,1)S(1)} collective-permute-done((bf16[32,1024]{1,0:T(8,128)(2,1)S(1)}, bf16[32,1024]{1,0:T(8,128)(2,1)S(1)}, u32[]{:S(2)}, u32[]{:S(2)}) %collective-permute-start.8) | collective-permute-done | bytes 65568 | tf_op jit(solution)/shard_map/ppermute | solution.py:330
  44.0 1.9 %collective-permute-done.9.refs_3_ = bf16[32,1024]{1,0:T(8,128)(2,1)S(1)} collective-permute-done((bf16[32,1024]{1,0:T(8,128)(2,1)S(1)}, bf16[32,1024]{1,0:T(8,128)(2,1)S(1)}, u32[]{:S(2)}, u32[]{:S(2)}) %collective-permute-start.9) | collective-permute-done | bytes 65568 | tf_op jit(solution)/shard_map/ppermute | solution.py:330
  45.9 4.0 %shard_map.99 = (f32[512,128]{1,0:T(8,128)S(1)}, f32[512,128]{1,0:T(8,128)S(1)}, bf16[544,128]{1,0:T(8,128)(2,1)S(1)}, bf16[544,128]{1,0:T(8,128)(2,1)S(1)}, bf1...) custom-call(bf16[32,1024]{1,0:T(8,128)(2,1)S(1)} %get-tuple-element.31.refs_0_, ...), custom_call_target="tpu_custom_call" | custom-call | flops 1610612736 | bytes 524288 | tf_op jit(solution)/shard_map/pallas_call | solution.py:29
  50.0 1.2 %collective-permute-start.13 = (bf16[544,128]{1,0:T(8,128)(2,1)S(1)}, bf16[544,128]{1,0:T(8,128)(2,1)S(1)}, u32[]{:S(2)}, u32[]{:S(2)}) collective-permute-start(bf16[544,128]{1,0:T(8,128)(2,1)S(1)} %get-tuple-element.44), channel_id=1, source_target_pairs={{0,1},{1,0},{2,3},{3,2},{4,5},{5,4},{6,7},{7,6},{8,9},{9,8},{10,11... | collective-permute-start | bytes 417800 | tf_op jit(solution)/shard_map/ppermute | solution.py:330
  51.2 1.5 %collective-permute-start.14 = (bf16[544,128]{1,0:T(8,128)(2,1)S(1)}, bf16[544,128]{1,0:T(8,128)(2,1)S(1)}, u32[]{:S(2)}, u32[]{:S(2)}) collective-permute-start(bf16[544,128]{1,0:T(8,128)(2,1)S(1)} %get-tuple-element.45), channel_id=1, source_target_pairs={{0,2},{1,3},{2,0},{3,1},{4,6},{5,7},{6,4},{7,5},{8,10},{9,11},{10,... | collective-permute-start | bytes 417800 | tf_op jit(solution)/shard_map/ppermute | solution.py:330
  52.7 1.8 %collective-permute-start.15 = (bf16[544,128]{1,0:T(8,128)(2,1)S(1)}, bf16[544,128]{1,0:T(8,128)(2,1)S(1)}, u32[]{:S(2)}, u32[]{:S(2)}) collective-permute-start(bf16[544,128]{1,0:T(8,128)(2,1)S(1)} %get-tuple-element.46), channel_id=1, source_target_pairs={{0,3},{1,2},{2,1},{3,0},{4,7},{5,6},{6,5},{7,4},{8,11},{9,10},{10,... | collective-permute-start | bytes 417800 | tf_op jit(solution)/shard_map/ppermute | solution.py:330
  54.5 1.6 %collective-permute-start.17 = (bf16[128,128]{1,0:T(8,128)(2,1)S(1)}, bf16[128,128]{1,0:T(8,128)(2,1)S(1)}, u32[]{:S(2)}, u32[]{:S(2)}) collective-permute-start(bf16[128,128]{1,0:T(8,128)(2,1)S(1)} %get-tuple-element.51), channel_id=1, source_target_pairs={{0,8},{4,12},{8,0},{12,4},{16,24},{20,28},{24,16},{28,20},{1,9},{5... | collective-permute-start | bytes 98312 | tf_op jit(solution)/shard_map/ppermute | solution.py:330
  56.6 1.9 %collective-permute-done.17.refs_1_ = bf16[128,128]{1,0:T(8,128)(2,1)S(1)} collective-permute-done((bf16[128,128]{1,0:T(8,128)(2,1)S(1)}, bf16[128,128]{1,0:T(8,128)(2,1)S(1)}, u32[]{:S(2)}, u32[]{:S(2)}) %collective-permute-start.17) | collective-permute-done | bytes 32800 | tf_op jit(solution)/shard_map/ppermute | solution.py:330
  58.5 1.4 %collective-permute-start.19 = (bf16[128,128]{1,0:T(8,128)(2,1)S(1)}, bf16[128,128]{1,0:T(8,128)(2,1)S(1)}, u32[]{:S(2)}, u32[]{:S(2)}) collective-permute-start(bf16[128,128]{1,0:T(8,128)(2,1)S(1)} %get-tuple-element.53), channel_id=1, source_target_pairs={{0,24},{4,28},{8,16},{12,20},{16,8},{20,12},{24,0},{28,4},{1,25},{... | collective-permute-start | bytes 98312 | tf_op jit(solution)/shard_map/ppermute | solution.py:330
  60.0 3.3 %collective-permute-done.19.refs_3_ = bf16[128,128]{1,0:T(8,128)(2,1)S(1)} collective-permute-done((bf16[128,128]{1,0:T(8,128)(2,1)S(1)}, bf16[128,128]{1,0:T(8,128)(2,1)S(1)}, u32[]{:S(2)}, u32[]{:S(2)}) %collective-permute-start.19) | collective-permute-done | bytes 32800 | tf_op jit(solution)/shard_map/ppermute | solution.py:330
  63.3 2.1 %collective-permute-start.22 = (bf16[128,128]{1,0:T(8,128)(2,1)S(1)}, bf16[128,128]{1,0:T(8,128)(2,1)S(1)}, u32[]{:S(2)}, u32[]{:S(2)}) collective-permute-start(bf16[128,128]{1,0:T(8,128)(2,1)S(1)} %shard_map.102.refs_0_), channel_id=1, source_target_pairs={{0,3},{1,2},{2,1},{3,0},{4,7},{5,6},{6,5},{7,4},{8,11},{9,10},{10,... | collective-permute-start | bytes 98312 | tf_op jit(solution)/shard_map/ppermute | solution.py:330
  65.4 2.3 %collective-permute-start.20 = (bf16[128,128]{1,0:T(8,128)(2,1)S(1)}, bf16[128,128]{1,0:T(8,128)(2,1)S(1)}, u32[]{:S(2)}, u32[]{:S(2)}) collective-permute-start(bf16[128,128]{1,0:T(8,128)(2,1)S(1)} %shard_map.102.refs_0_), channel_id=1, source_target_pairs={{0,1},{1,0},{2,3},{3,2},{4,5},{5,4},{6,7},{7,6},{8,9},{9,8},{10,11... | collective-permute-start | bytes 98312 | tf_op jit(solution)/shard_map/ppermute | solution.py:330
  (48 shorter events, 10.0 us)
Async XLA Ops:
  4.1 7.9 %collective-permute-start.5 = (bf16[128,704]{1,0:T(8,128)(2,1)S(1)}, bf16[128,704]{1,0:T(8,128)(2,1)S(1)}, u32[]{:S(2)}, u32[]{:S(2)}) collective-permute-start(bf16[128,704]{1,0:T(8,128)(2,1)S(1)} %get-tuple-element.35.refs_0_.refs_4_), channel_id=1, source_target_pairs={{0,16},{4,20},{8,24},{12,28},{16,0},{20,4},{24,8},{28,12},{1,17},{... | collective-permute-start | bytes 540680 | tf_op jit(solution)/shard_map/ppermute | solution.py:330
  7.2 7.8 %collective-permute-start.3 = (bf16[128,704]{1,0:T(8,128)(2,1)S(1)}, bf16[128,704]{1,0:T(8,128)(2,1)S(1)}, u32[]{:S(2)}, u32[]{:S(2)}) collective-permute-start(bf16[128,704]{1,0:T(8,128)(2,1)S(1)} %get-tuple-element.35.refs_0_.refs_4_), channel_id=1, source_target_pairs={{0,8},{4,12},{8,0},{12,4},{16,24},{20,28},{24,16},{28,20},{1,9},{5... | collective-permute-start | bytes 540680 | tf_op jit(solution)/shard_map/ppermute | solution.py:330
  8.7 7.9 %collective-permute-start.2 = (bf16[128,704]{1,0:T(8,128)(2,1)S(1)}, bf16[128,704]{1,0:T(8,128)(2,1)S(1)}, u32[]{:S(2)}, u32[]{:S(2)}) collective-permute-start(bf16[128,704]{1,0:T(8,128)(2,1)S(1)} %get-tuple-element.35.refs_0_.refs_4_), channel_id=1, source_target_pairs={{0,4},{4,0},{8,12},{12,8},{16,20},{20,16},{24,28},{28,24},{1,5},{5... | collective-permute-start | bytes 540680 | tf_op jit(solution)/shard_map/ppermute | solution.py:330
  8.7 17.7 %collective-permute-start = (bf16[128,704]{1,0:T(8,128)(2,1)S(1)}, bf16[128,704]{1,0:T(8,128)(2,1)S(1)}, u32[]{:S(2)}, u32[]{:S(2)}) collective-permute-start(bf16[128,704]{1,0:T(8,128)(2,1)S(1)} %get-tuple-element.35.refs_0_.refs_4_), channel_id=1, source_target_pairs={{0,24},{4,28},{8,16},{12,20},{16,8},{20,12},{24,0},{28,4},{1,25},{... | collective-permute-start | bytes 540680 | tf_op jit(solution)/shard_map/ppermute | solution.py:330
  12.1 14.6 %collective-permute-start.6 = (bf16[128,704]{1,0:T(8,128)(2,1)S(1)}, bf16[128,704]{1,0:T(8,128)(2,1)S(1)}, u32[]{:S(2)}, u32[]{:S(2)}) collective-permute-start(bf16[128,704]{1,0:T(8,128)(2,1)S(1)} %collective-permute-done.5.refs_2_.refs_4_.refs_8_), channel_id=1, source_target_pairs={{0,4},{4,0},{8,12},{12,8},{16,20},{20,16},{24,28},{28,24},{1,5},{5... | collective-permute-start | bytes 540680 | tf_op jit(solution)/shard_map/ppermute | solution.py:330
  15.0 11.7 %collective-permute-start.4 = (bf16[128,704]{1,0:T(8,128)(2,1)S(1)}, bf16[128,704]{1,0:T(8,128)(2,1)S(1)}, u32[]{:S(2)}, u32[]{:S(2)}) collective-permute-start(bf16[128,704]{1,0:T(8,128)(2,1)S(1)} %collective-permute-done.3.refs_0_.refs_2_.refs_6_), channel_id=1, source_target_pairs={{0,4},{4,0},{8,12},{12,8},{16,20},{20,16},{24,28},{28,24},{1,5},{5... | collective-permute-start | bytes 540680 | tf_op jit(solution)/shard_map/ppermute | solution.py:330
  15.0 24.8 %collective-permute-start.10 = (bf16[560,128]{1,0:T(8,128)(2,1)S(1)}, bf16[560,128]{1,0:T(8,128)(2,1)S(1)}, u32[]{:S(2)}, u32[]{:S(2)}) collective-permute-start(bf16[560,128]{1,0:T(8,128)(2,1)S(1)} %get-tuple-element.37), channel_id=1, source_target_pairs={{0,1},{1,0},{2,3},{3,2},{4,5},{5,4},{6,7},{7,6},{8,9},{9,8},{10,11... | collective-permute-start | bytes 430088 | tf_op jit(solution)/shard_map/ppermute | solution.py:330
  16.6 23.4 %collective-permute-start.11 = (bf16[560,128]{1,0:T(8,128)(2,1)S(1)}, bf16[560,128]{1,0:T(8,128)(2,1)S(1)}, u32[]{:S(2)}, u32[]{:S(2)}) collective-permute-start(bf16[560,128]{1,0:T(8,128)(2,1)S(1)} %get-tuple-element.38), channel_id=1, source_target_pairs={{0,2},{1,3},{2,0},{3,1},{4,6},{5,7},{6,4},{7,5},{8,10},{9,11},{10,... | collective-permute-start | bytes 430088 | tf_op jit(solution)/shard_map/ppermute | solution.py:330
  22.9 3.8 %copy-start.1 = (bf16[128,32,576]{0,2,1:T(8,128)(2,1)S(1)}, bf16[128,32,576]{0,2,1:T(8,128)(2,1)}, u32[]{:S(2)}) copy-start(bf16[128,32,576]{0,2,1:T(8,128)(2,1)} %param.7) | copy-start | bytes 14155780
  26.4 13.6 %collective-permute-start.12 = (bf16[560,128]{1,0:T(8,128)(2,1)S(1)}, bf16[560,128]{1,0:T(8,128)(2,1)S(1)}, u32[]{:S(2)}, u32[]{:S(2)}) collective-permute-start(bf16[560,128]{1,0:T(8,128)(2,1)S(1)} %get-tuple-element.39), channel_id=1, source_target_pairs={{0,3},{1,2},{2,1},{3,0},{4,7},{5,6},{6,5},{7,4},{8,11},{9,10},{10,... | collective-permute-start | bytes 430088 | tf_op jit(solution)/shard_map/ppermute | solution.py:330
  26.7 5.2 %collective-permute-start.1 = (bf16[128,704]{1,0:T(8,128)(2,1)S(1)}, bf16[128,704]{1,0:T(8,128)(2,1)S(1)}, u32[]{:S(2)}, u32[]{:S(2)}) collective-permute-start(bf16[128,704]{1,0:T(8,128)(2,1)S(1)} %collective-permute-done.refs_0_.refs_6_.refs_10_), channel_id=1, source_target_pairs={{0,4},{4,0},{8,12},{12,8},{16,20},{20,16},{24,28},{28,24},{1,5},{5... | collective-permute-start | bytes 540680 | tf_op jit(solution)/shard_map/ppermute | solution.py:330
  35.6 6.4 %collective-permute-start.7 = (bf16[32,1024]{1,0:T(8,128)(2,1)S(1)}, bf16[32,1024]{1,0:T(8,128)(2,1)S(1)}, u32[]{:S(2)}, u32[]{:S(2)}) collective-permute-start(bf16[32,1024]{1,0:T(8,128)(2,1)S(1)} %get-tuple-element.32), channel_id=1, source_target_pairs={{0,1},{1,0},{2,3},{3,2},{4,5},{5,4},{6,7},{7,6},{8,9},{9,8},{10,11... | collective-permute-start | bytes 196616 | tf_op jit(solution)/shard_map/ppermute | solution.py:330
  36.3 7.7 %collective-permute-start.8 = (bf16[32,1024]{1,0:T(8,128)(2,1)S(1)}, bf16[32,1024]{1,0:T(8,128)(2,1)S(1)}, u32[]{:S(2)}, u32[]{:S(2)}) collective-permute-start(bf16[32,1024]{1,0:T(8,128)(2,1)S(1)} %get-tuple-element.33), channel_id=1, source_target_pairs={{0,2},{1,3},{2,0},{3,1},{4,6},{5,7},{6,4},{7,5},{8,10},{9,11},{10,... | collective-permute-start | bytes 196616 | tf_op jit(solution)/shard_map/ppermute | solution.py:330
  39.8 6.1 %collective-permute-start.9 = (bf16[32,1024]{1,0:T(8,128)(2,1)S(1)}, bf16[32,1024]{1,0:T(8,128)(2,1)S(1)}, u32[]{:S(2)}, u32[]{:S(2)}) collective-permute-start(bf16[32,1024]{1,0:T(8,128)(2,1)S(1)} %get-tuple-element.34), channel_id=1, source_target_pairs={{0,3},{1,2},{2,1},{3,0},{4,7},{5,6},{6,5},{7,4},{8,11},{9,10},{10,... | collective-permute-start | bytes 196616 | tf_op jit(solution)/shard_map/ppermute | solution.py:330
  49.9 4.5 %collective-permute-start.16 = (f32[512,128]{1,0:T(8,128)S(1)}, f32[512,128]{1,0:T(8,128)S(1)}, u32[]{:S(2)}, u32[]{:S(2)}) collective-permute-start(f32[512,128]{1,0:T(8,128)S(1)} %get-tuple-element.49), channel_id=1, source_target_pairs={{0,4},{4,0},{8,12},{12,8},{16,20},{20,16},{24,28},{28,24},{1,5},{5... | collective-permute-start | bytes 786440 | tf_op jit(solution)/shard_map/ppermute | solution.py:330
  50.0 15.4 %collective-permute-start.13 = (bf16[544,128]{1,0:T(8,128)(2,1)S(1)}, bf16[544,128]{1,0:T(8,128)(2,1)S(1)}, u32[]{:S(2)}, u32[]{:S(2)}) collective-permute-start(bf16[544,128]{1,0:T(8,128)(2,1)S(1)} %get-tuple-element.44), channel_id=1, source_target_pairs={{0,1},{1,0},{2,3},{3,2},{4,5},{5,4},{6,7},{7,6},{8,9},{9,8},{10,11... | collective-permute-start | bytes 417800 | tf_op jit(solution)/shard_map/ppermute | solution.py:330
  51.2 16.6 %collective-permute-start.14 = (bf16[544,128]{1,0:T(8,128)(2,1)S(1)}, bf16[544,128]{1,0:T(8,128)(2,1)S(1)}, u32[]{:S(2)}, u32[]{:S(2)}) collective-permute-start(bf16[544,128]{1,0:T(8,128)(2,1)S(1)} %get-tuple-element.45), channel_id=1, source_target_pairs={{0,2},{1,3},{2,0},{3,1},{4,6},{5,7},{6,4},{7,5},{8,10},{9,11},{10,... | collective-permute-start | bytes 417800 | tf_op jit(solution)/shard_map/ppermute | solution.py:330
  52.7 15.1 %collective-permute-start.15 = (bf16[544,128]{1,0:T(8,128)(2,1)S(1)}, bf16[544,128]{1,0:T(8,128)(2,1)S(1)}, u32[]{:S(2)}, u32[]{:S(2)}) collective-permute-start(bf16[544,128]{1,0:T(8,128)(2,1)S(1)} %get-tuple-element.46), channel_id=1, source_target_pairs={{0,3},{1,2},{2,1},{3,0},{4,7},{5,6},{6,5},{7,4},{8,11},{9,10},{10,... | collective-permute-start | bytes 417800 | tf_op jit(solution)/shard_map/ppermute | solution.py:330
  54.5 4.0 %collective-permute-start.17 = (bf16[128,128]{1,0:T(8,128)(2,1)S(1)}, bf16[128,128]{1,0:T(8,128)(2,1)S(1)}, u32[]{:S(2)}, u32[]{:S(2)}) collective-permute-start(bf16[128,128]{1,0:T(8,128)(2,1)S(1)} %get-tuple-element.51), channel_id=1, source_target_pairs={{0,8},{4,12},{8,0},{12,4},{16,24},{20,28},{24,16},{28,20},{1,9},{5... | collective-permute-start | bytes 98312 | tf_op jit(solution)/shard_map/ppermute | solution.py:330
  56.1 3.9 %collective-permute-start.18 = (bf16[128,128]{1,0:T(8,128)(2,1)S(1)}, bf16[128,128]{1,0:T(8,128)(2,1)S(1)}, u32[]{:S(2)}, u32[]{:S(2)}) collective-permute-start(bf16[128,128]{1,0:T(8,128)(2,1)S(1)} %get-tuple-element.52), channel_id=1, source_target_pairs={{0,16},{4,20},{8,24},{12,28},{16,0},{20,4},{24,8},{28,12},{1,17},{... | collective-permute-start | bytes 98312 | tf_op jit(solution)/shard_map/ppermute | solution.py:330
  58.5 4.8 %collective-permute-start.19 = (bf16[128,128]{1,0:T(8,128)(2,1)S(1)}, bf16[128,128]{1,0:T(8,128)(2,1)S(1)}, u32[]{:S(2)}, u32[]{:S(2)}) collective-permute-start(bf16[128,128]{1,0:T(8,128)(2,1)S(1)} %get-tuple-element.53), channel_id=1, source_target_pairs={{0,24},{4,28},{8,16},{12,20},{16,8},{20,12},{24,0},{28,4},{1,25},{... | collective-permute-start | bytes 98312 | tf_op jit(solution)/shard_map/ppermute | solution.py:330
  63.3 5.8 %collective-permute-start.22 = (bf16[128,128]{1,0:T(8,128)(2,1)S(1)}, bf16[128,128]{1,0:T(8,128)(2,1)S(1)}, u32[]{:S(2)}, u32[]{:S(2)}) collective-permute-start(bf16[128,128]{1,0:T(8,128)(2,1)S(1)} %shard_map.102.refs_0_), channel_id=1, source_target_pairs={{0,3},{1,2},{2,1},{3,0},{4,7},{5,6},{6,5},{7,4},{8,11},{9,10},{10,... | collective-permute-start | bytes 98312 | tf_op jit(solution)/shard_map/ppermute | solution.py:330
  65.4 4.8 %collective-permute-start.21 = (bf16[128,128]{1,0:T(8,128)(2,1)S(1)}, bf16[128,128]{1,0:T(8,128)(2,1)S(1)}, u32[]{:S(2)}, u32[]{:S(2)}) collective-permute-start(bf16[128,128]{1,0:T(8,128)(2,1)S(1)} %shard_map.102.refs_0_), channel_id=1, source_target_pairs={{0,2},{1,3},{2,0},{3,1},{4,6},{5,7},{6,4},{7,5},{8,10},{9,11},{10,... | collective-permute-start | bytes 98312 | tf_op jit(solution)/shard_map/ppermute | solution.py:330
  65.4 4.8 %collective-permute-start.20 = (bf16[128,128]{1,0:T(8,128)(2,1)S(1)}, bf16[128,128]{1,0:T(8,128)(2,1)S(1)}, u32[]{:S(2)}, u32[]{:S(2)}) collective-permute-start(bf16[128,128]{1,0:T(8,128)(2,1)S(1)} %shard_map.102.refs_0_), channel_id=1, source_target_pairs={{0,1},{1,0},{2,3},{3,2},{4,5},{5,4},{6,7},{7,6},{8,9},{9,8},{10,11... | collective-permute-start | bytes 98312 | tf_op jit(solution)/shard_map/ppermute | solution.py:330
  (7 other events, 7.1 us)

commit v3 on v2

--- a/solution.py
+++ b/solution.py
@@ -15,8 +15,8 @@
 f32, bf16 = jnp.float32, jnp.bfloat16
 
 
-def params():
-    return pltpu.CompilerParams(vmem_limit_bytes=48 * 1024 * 1024)
+def params(mega=48):
+    return pltpu.CompilerParams(vmem_limit_bytes=mega * 1024 * 1024)
 
 
 def whole(value):
@@ -24,7 +24,7 @@
     return pl.BlockSpec(value.shape, lambda *_: zeros)
 
 
-def call(kernel, outs, values, scratch=(), specs=None, cost=None):
+def call(kernel, outs, values, scratch=(), specs=None, cost=None, mega=48):
     many = isinstance(outs, list)
     found = pl.pallas_call(
         kernel,
@@ -33,7 +33,7 @@
         in_specs=specs or [whole(v) for v in values],
         out_specs=[whole(o) for o in outs] if many else whole(outs),
         scratch_shapes=list(scratch),
-        compiler_params=params(),
+        compiler_params=params(mega),
         cost_estimate=cost,
     )(*values)
     return list(found) if many else found
@@ -54,10 +54,13 @@
     return found
 
 
-def pack_kernel(latent_ref, key_ref, query_ref, weight_ref, packed_ref, *outs):
+def pack_kernel(latent_ref, key_ref, packed_ref):
     width = key_ref.shape[1]
     packed_ref[:, :width] = key_ref[...]
     packed_ref[:, width:] = latent_ref[...].T
+
+
+def ask_kernel(query_ref, weight_ref, *outs):
     me = lax.axis_index("ha")
     heads = weight_ref.shape[0]
     rows = outs[0].shape[0] - 3 * TAIL
@@ -109,17 +112,17 @@
 
     for i in range(pieces):
         copies[i].wait()
-        for pair in range(i * per // 2, (i + 1) * per // 2):
-            two = jnp.concatenate([query[2 * pair], query[2 * pair + 1]], axis=1)
-            scores = jnp.dot(keys[...], two, preferred_element_type=f32)
+        for head in range(i * per, (i + 1) * per, 4):
+            four = jnp.concatenate([query[head + n] for n in range(4)], axis=1)
+            scores = jnp.dot(keys[...], four, preferred_element_type=f32)
             parts = [
                 jnp.exp2(
-                    scores[:, half * rows : (half + 1) * rows] * (main_scale * log2e)
-                    - sums_ref[2 * pair + half : 2 * pair + half + 1, :] * log2e
+                    scores[:, n * rows : (n + 1) * rows] * (main_scale * log2e)
+                    - sums_ref[head + n : head + n + 1, :] * log2e
                 )
-                for half in range(2)
+                for n in range(4)
             ]
-            total[...] += parts[0] + parts[1]
+            total[...] += tree(parts)
 
     me = lax.axis_index("pb")
     kept = turned.shape[1] - count * rows
@@ -215,28 +218,11 @@
     return parts[0] + (parts[1] + parts[2])
 
 
-def back_kernel(share, count, parts, heads, *refs):
-    mass_refs = refs[:parts]
-    blocks = refs[parts : parts + count]
-    prob_ref, queries_ref, weights_ref = refs[parts + count : parts + count + 3]
-    outs = refs[parts + count + 3 : -6]
-    even_ref, odd_ref = outs[:2]
-    messages = outs[2:]
-    keys, turned_keys, grad, key_total, query_total, weight_total = refs[-6:]
-    rows, width = blocks[0].shape
+def back_heads(span, share, heads, keys, turned_keys, grad, queries_ref, weights_ref, totals):
+    key_total, query_total, weight_total = totals
     repeats = LANES // share
-    mass = tree([ref[...].astype(f32) for ref in mass_refs])
-    for k in range(count):
-        at = slice(k * rows, (k + 1) * rows)
-        keys[at, :] = blocks[k][...]
-        turned_keys[:, at] = blocks[k][...].T
-        grad[at, :] = jnp.concatenate([mass[:, at]] * repeats, axis=0).T
-    total = jnp.sum(grad[...], axis=0, keepdims=True)
-    grad[...] = prob_ref[...] - grad[...] / total
-    key_total[...] = jnp.zeros_like(key_total)
-    weight_total[...] = jnp.zeros_like(weight_total)
-    all_heads = parts * heads
-    for g in range(0, all_heads // repeats, 2):
+    base = span[0] * LANES
+    for g in range(span[0], span[1], 2):
         two = queries_ref[g * LANES : (g + 2) * LANES, :]
         act = lax.dot_general(
             keys[...], two, (((1,), (1,)), ((), ())), preferred_element_type=f32
@@ -259,16 +245,58 @@
         found = jnp.concatenate([found[:, :LANES].T, found[:, LANES:].T], axis=0)
         for i in range(2 * repeats):
             head = g * repeats + i
-            first = (head // heads) * heads * share + head % heads
+            first = (head // heads) * heads * share + head % heads - base
             query_total[pl.ds(first, share, stride=heads), :] = found[
                 i * share : (i + 1) * share, :
             ]
+
+
+def put_answers(share, heads, messages, query_total, weight_total):
     own = share * heads
     split = terms_of(weight_total[...], 2)
-    for r in range(parts):
-        messages[r][:own, :] = query_total[r * own : (r + 1) * own, :].astype(bf16)
+    for r, message in enumerate(messages):
+        message[:own, :] = query_total[r * own : (r + 1) * own, :].astype(bf16)
         for i in range(2):
-            messages[r][own + i * TAIL : own + (i + 1) * TAIL, :] = split[i]
+            message[own + i * TAIL : own + (i + 1) * TAIL, :] = split[i]
+
+
+def far_kernel(span, share, count, parts, heads, *refs):
+    mass_refs = refs[:parts]
+    blocks = refs[parts : parts + count]
+    prob_ref, queries_ref, weights_ref, grad, key_total = refs[parts + count : parts + count + 5]
+    messages = refs[parts + count + 5 : -4]
+    keys, turned_keys, query_total, weight_total = refs[-4:]
+    rows = blocks[0].shape[0]
+    mass = tree([ref[...].astype(f32) for ref in mass_refs])
+    for k in range(count):
+        at = slice(k * rows, (k + 1) * rows)
+        keys[at, :] = blocks[k][...]
+        turned_keys[:, at] = blocks[k][...].T
+        grad[at, :] = jnp.concatenate([mass[:, at]] * (LANES // share), axis=0).T
+    total = jnp.sum(grad[...], axis=0, keepdims=True)
+    grad[...] = prob_ref[...] - grad[...] / total
+    key_total[...] = jnp.zeros_like(key_total)
+    weight_total[...] = jnp.zeros_like(weight_total)
+    totals = (key_total, query_total, weight_total)
+    back_heads(span, share, heads, keys, turned_keys, grad, queries_ref, weights_ref, totals)
+    put_answers(share, heads, messages, query_total, weight_total)
+
+
+def near_kernel(span, share, count, heads, *refs):
+    blocks = refs[:count]
+    queries_ref, weights_ref, grad, key_before, even_ref, odd_ref = refs[count : count + 6]
+    messages = refs[count + 6 : -5]
+    keys, turned_keys, key_total, query_total, weight_total = refs[-5:]
+    rows = blocks[0].shape[0]
+    for k in range(count):
+        at = slice(k * rows, (k + 1) * rows)
+        keys[at, :] = blocks[k][...]
+        turned_keys[:, at] = blocks[k][...].T
+    key_total[...] = key_before[...]
+    weight_total[...] = jnp.zeros_like(weight_total)
+    totals = (key_total, query_total, weight_total)
+    back_heads(span, share, heads, keys, turned_keys, grad, queries_ref, weights_ref, totals)
+    put_answers(share, heads, messages, query_total, weight_total)
     for i in range(count // 2):
         at = slice(i * rows, (i + 1) * rows)
         even_ref[at, :] = key_total[2 * i * rows : (2 * i + 1) * rows, :]
@@ -332,11 +360,8 @@
     start_row = window_start.reshape(1, rows)
     key_only = pl.BlockSpec((rows, index_width), lambda *_: (0, 0))
 
-    packed, *asked = call(
-        pack_kernel,
-        [shape((rows, index_width + width), bf16)]
-        + [shape((own + 3 * TAIL, index_width), bf16)] * parts,
-        (latent.T, index_key, index_query.reshape(rows * heads, index_width), index_weight.T),
+    packed = call(
+        pack_kernel, shape((rows, index_width + width), bf16), (latent.T, index_key)
     )
     held = [None] * blocks
     held[0] = packed
@@ -344,6 +369,11 @@
     for k in range(2, blocks, 2):
         held[k] = swap(packed, "pb", k)
         held[k + 1] = swap(held[k], "pb", 1)
+    asked = call(
+        ask_kernel,
+        [shape((own + 3 * TAIL, index_width), bf16)] * parts,
+        (index_query.reshape(rows * heads, index_width), index_weight.T),
+    )
     asked = [asked[0]] + [swap(asked[r], "ha", r) for r in range(1, parts)]
 
     queries = jnp.transpose(main_query, (1, 2, 0))
@@ -377,6 +407,7 @@
                 bytes_accessed=2 * rows * head_count * width,
                 transcendentals=span * rows * head_count,
             ),
+            60,
         )
         mass = found if last else mass + found
     first, key_block = lax.optimization_barrier((mass[0], held[0]))
@@ -404,36 +435,47 @@
         ),
     )
 
-    even, odd, *answers = call(
-        functools.partial(back_kernel, share, blocks, parts, heads),
-        [shape((tokens // 2, index_width), f32)] * 2
-        + [shape((own + 2 * TAIL, index_width), bf16)] * parts,
-        mass + key_blocks + [probs, query_rows, weight_rows],
-        [
-            pltpu.VMEM((tokens, index_width), bf16),
-            pltpu.VMEM((index_width, tokens), bf16),
-            pltpu.VMEM((tokens, LANES), f32),
-            pltpu.VMEM((tokens, index_width), f32),
-            pltpu.VMEM((columns, index_width), f32),
-            pltpu.VMEM((TAIL, LANES), f32),
-        ],
-        [whole(v) for v in mass]
-        + [key_only] * blocks
-        + [whole(v) for v in (probs, query_rows, weight_rows)],
-        pl.CostEstimate(
-            flops=6 * tokens * columns * index_width,
-            bytes_accessed=2 * columns * index_width,
-            transcendentals=0,
-        ),
+    groups = columns // LANES
+    message = shape((own + 2 * TAIL, index_width), bf16)
+    cost = pl.CostEstimate(
+        flops=3 * tokens * columns * index_width,
+        bytes_accessed=2 * columns * index_width,
+        transcendentals=0,
+    )
+    scratch = [
+        pltpu.VMEM((tokens, index_width), bf16),
+        pltpu.VMEM((index_width, tokens), bf16),
+        pltpu.VMEM((columns // 2, index_width), f32),
+        pltpu.VMEM((TAIL, LANES), f32),
+    ]
+    others = [probs, query_rows, weight_rows]
+    grad, key_part, *far = call(
+        functools.partial(far_kernel, (groups // 2, groups), share, blocks, parts, heads),
+        [shape((tokens, LANES), f32), shape((tokens, index_width), f32)] + [message] * (parts // 2),
+        mass + key_blocks + others,
+        scratch,
+        [whole(v) for v in mass] + [key_only] * blocks + [whole(v) for v in others],
+        cost,
+    )
+    others = [query_rows, weight_rows, grad, key_part]
+    even, odd, *near = call(
+        functools.partial(near_kernel, (0, groups // 2), share, blocks, heads),
+        [shape((tokens // 2, index_width), f32)] * 2 + [message] * (parts // 2),
+        key_blocks + others,
+        scratch[:2] + [pltpu.VMEM((tokens, index_width), f32)] + scratch[2:],
+        [key_only] * blocks + [whole(v) for v in others],
+        cost,
     )
     odd = swap(odd, "pb", 1)
     term = shape((rows, index_width), f32)
     half = shape((rows, index_width), bf16)
     mine, *others = call(pair_kernel, [term] + [half] * (blocks // 2 - 1), (even, odd))
+    mine, near = lax.optimization_barrier((mine, near))
     others = [swap(value, "pb", 2 * (i + 1)) for i, value in enumerate(others)]
     mine = call(sum_kernel, half, [mine] + others)
     key_grad = call(sum_kernel, half, [mine] + [swap(mine, "ha", r) for r in range(1, parts)])
 
+    answers = near + far
     answers = [answers[0]] + [swap(answers[r], "ha", r) for r in range(1, parts)]
     query_grad, weight_grad = call(
         functools.partial(finish_kernel, share, heads),

time: 71.3 us -> 80.2 us (1.12)
  Pallas kernels: 19.9 us -> 26.3 us
  waiting for transfers between devices: 17.1 us -> 20.7 us
  starting transfers between devices: 26 us -> 23.6 us
  local copies, waits for them, and re-layouts: 7.11 us -> 8.2 us
    pallas_call x10 -> x12, Pallas kernels: 19.9 us -> 26.3 us  [call(): pl.pallas_call(kernel, grid=(1,), out_shape=outs, in_specs=specs or [whol...]
    ppermute x23, waiting for transfers between devices: 17.1 us -> 20.7 us  [swap(): return lax.ppermute(value, axis, [(i, i ^ rel) for i in range(size)])]
    ppermute x23, starting transfers between devices: 26 us -> 23.6 us  [swap(): return lax.ppermute(value, axis, [(i, i ^ rel) for i in range(size)])]
    unnamed x16 -> x44, local copies, waits for them, and re-layouts: 7.11 us -> 8.2 us
  transfers between devices with their start and end apart: 23 -> 23, of which waited for: 9 -> 10; matrix products, arithmetic and copies ran while one was open for 0% -> 0% of each run, Pallas kernels for 21% -> 26%
where the time goes in v3:
time: 80.2 us; the launch traced here: 79.7 us
  Pallas kernels  26.3 us (33%)
  starting transfers between devices  23.6 us (29%)
  waiting for transfers between devices  20.7 us (26%)
  local copies, waits for them, and re-layouts  8.2 us (10%)
  between operations  0.94 us (1%)
    pallas_call x12, Pallas kernels, call(): pl.pallas_call(kernel, grid=(1,), out_shape=outs, in_specs=specs or [whol...  26.3 us
    ppermute x23, starting transfers between devices, swap(): return lax.ppermute(value, axis, [(i, i ^ rel) for i in range(size)])  23.6 us
    ppermute x23, waiting for transfers between devices, swap(): return lax.ppermute(value, axis, [(i, i ^ rel) for i in range(size)])  20.7 us
    unnamed x44, local copies, waits for them, and re-layouts  8.2 us
  transfers between devices with their start and end apart: 23, of which 10 were waited for; matrix products, arithmetic and copies ran while one was open for 0% of the time, Pallas kernels for 26%

profile of v3, /device:TPU:0, one launch (start us, length us, event | category | flops | bytes accessed | tf_op | source)
XLA Modules:
  0.0 79.7 jit_solution(13765156676356817953)
XLA Ops:
  2.4 3.0 %collective-permute-start.5 = (bf16[128,704]{1,0:T(8,128)(2,1)S(1)}, bf16[128,704]{1,0:T(8,128)(2,1)S(1)}, u32[]{:S(2)}, u32[]{:S(2)}) collective-permute-start(bf16[128,704]{1,0:T(8,128)(2,1)S(1)} %shard_map.94.refs_0_.refs_4_), channel_id=1, source_target_pairs={{0,16},{4,20},{8,24},{12,28},{16,0},{20,4},{24,8},{28,12},{1,17},{... | collective-permute-start | bytes 540680 | tf_op jit(solution)/shard_map/ppermute | solution.py:358
  5.5 1.5 %collective-permute-start.3 = (bf16[128,704]{1,0:T(8,128)(2,1)S(1)}, bf16[128,704]{1,0:T(8,128)(2,1)S(1)}, u32[]{:S(2)}, u32[]{:S(2)}) collective-permute-start(bf16[128,704]{1,0:T(8,128)(2,1)S(1)} %shard_map.94.refs_0_.refs_4_), channel_id=1, source_target_pairs={{0,8},{4,12},{8,0},{12,4},{16,24},{20,28},{24,16},{28,20},{1,9},{5... | collective-permute-start | bytes 540680 | tf_op jit(solution)/shard_map/ppermute | solution.py:358
  7.0 3.4 %collective-permute-done.5.refs_2_.refs_4_.refs_8_ = bf16[128,704]{1,0:T(8,128)(2,1)S(1)} collective-permute-done((bf16[128,704]{1,0:T(8,128)(2,1)S(1)}, bf16[128,704]{1,0:T(8,128)(2,1)S(1)}, u32[]{:S(2)}, u32[]{:S(2)}) %collective-permute-start.5) | collective-permute-done | bytes 180256 | tf_op jit(solution)/shard_map/ppermute | solution.py:358
  10.4 2.9 %collective-permute-done.3.refs_0_.refs_2_.refs_6_ = bf16[128,704]{1,0:T(8,128)(2,1)S(1)} collective-permute-done((bf16[128,704]{1,0:T(8,128)(2,1)S(1)}, bf16[128,704]{1,0:T(8,128)(2,1)S(1)}, u32[]{:S(2)}, u32[]{:S(2)}) %collective-permute-start.3) | collective-permute-done | bytes 180256 | tf_op jit(solution)/shard_map/ppermute | solution.py:358
  13.3 1.1 %copy-done.16 = bf16[128,16,128]{2,1,0:T(8,128)(2,1)S(1)} copy-done((bf16[128,16,128]{2,1,0:T(8,128)(2,1)S(1)}, bf16[128,16,128]{2,1,0:T(8,128)(2,1)}, u32[]{:S(2)}) %copy-start.16) | copy-done | bytes 524312
  15.1 1.6 %collective-permute-start.7 = (bf16[560,128]{1,0:T(8,128)(2,1)S(1)}, bf16[560,128]{1,0:T(8,128)(2,1)S(1)}, u32[]{:S(2)}, u32[]{:S(2)}) collective-permute-start(bf16[560,128]{1,0:T(8,128)(2,1)S(1)} %get-tuple-element.36), channel_id=1, source_target_pairs={{0,1},{1,0},{2,3},{3,2},{4,5},{5,4},{6,7},{7,6},{8,9},{9,8},{10,11... | collective-permute-start | bytes 430088 | tf_op jit(solution)/shard_map/ppermute | solution.py:358
  16.8 2.6 %collective-permute-start.8 = (bf16[560,128]{1,0:T(8,128)(2,1)S(1)}, bf16[560,128]{1,0:T(8,128)(2,1)S(1)}, u32[]{:S(2)}, u32[]{:S(2)}) collective-permute-start(bf16[560,128]{1,0:T(8,128)(2,1)S(1)} %get-tuple-element.37), channel_id=1, source_target_pairs={{0,2},{1,3},{2,0},{3,1},{4,6},{5,7},{6,4},{7,5},{8,10},{9,11},{10,... | collective-permute-start | bytes 430088 | tf_op jit(solution)/shard_map/ppermute | solution.py:358
  19.4 5.4 %shard_map.95.refs_5_ = bf16[128,256]{1,0:T(8,128)(2,1)} custom-call(bf16[128,704]{1,0:T(8,128)(2,1)} %copy-done, bf16[128,704]{1,0:T(8,128)(2,1)} %copy-done.6, bf16[32,576,128]{2,1,0:T(8,128)(2,1)} %bitcast.15, f32[32,128]{1,0:T(8,128)} %bitcast.18, s32[1,128]{1,0:T(1,128)} %bitcast.11), custom_call_target="tpu_custom_call" | custom-call | flops 1207959552 | bytes 4718592 | tf_op jit(solution)/shard_map/pallas_call | solution.py:29
  26.8 7.3 %shard_map.96.refs_6_ = bf16[128,512]{1,0:T(8,128)(2,1)} custom-call(bf16[128,704]{1,0:T(8,128)(2,1)} %copy-done.10, bf16[128,704]{1,0:T(8,128)(2,1)} %copy-done.14, bf16[128,704]{1,0:T(8,128)(2,1)} %copy-done.8, bf16[128,704]{1,0:T(8,128)(2,1)} %copy-done.12, bf16[32,576,128]{2,1,0:T(8,128)(2,1)} %bitcast.16, f32[32,128]{1,0:T(8,128)} %bitcast.19, ...), custom_call_target="tpu_custom_call" | custom-call | flops 2415919104 | bytes 4718592 | tf_op jit(solution)/shard_map/pallas_call | solution.py:29
  34.8 5.6 %shard_map.97 = (bf16[32,1024]{1,0:T(8,128)(2,1)}, bf16[32,1024]{1,0:T(8,128)(2,1)}, bf16[32,1024]{1,0:T(8,128)(2,1)}, bf16[32,1024]{1,0:T(8,128)(2,1)}) custom-call(bf16[128,704]{1,0:T(8,128)(2,1)} %copy-done.2, bf16[128,704]{1,0:T(8,128)(2,1)} %copy-done.4, bf16[32,576,128]{2,1,0:T(8,128)(2,1)} %bitcast.17, f32[32,128]{1,0:T(8,128)} %bitcast.20, ...), custom_call_target="tpu_custom_call" | custom-call | flops 1207959552 | bytes 4718592 | tf_op jit(solution)/shard_map/pallas_call | solution.py:29
  41.2 3.1 %collective-permute-start.11 = (bf16[32,1024]{1,0:T(8,128)(2,1)}, bf16[32,1024]{1,0:T(8,128)(2,1)S(1)}, u32[]{:S(2)}, u32[]{:S(2)}) collective-permute-start(bf16[32,1024]{1,0:T(8,128)(2,1)} %get-tuple-element.43), channel_id=1, source_target_pairs={{0,2},{1,3},{2,0},{3,1},{4,6},{5,7},{6,4},{7,5},{8,10},{9,11},{10,... | collective-permute-start | bytes 196616 | tf_op jit(solution)/shard_map/ppermute | solution.py:358
  46.8 1.9 %shard_map.99 = (f32[1024,128]{1,0:T(8,128)S(1)}, bf16[2048,128]{1,0:T(8,128)(2,1)S(1)}, f32[16,128]{1,0:T(8,128)S(1)}) custom-call(bf16[128,704]{1,0:T(8,128)(2,1)S(1)} %copy-done.1, bf16[128,704]{1,0:T(8,128)(2,1)S(1)} %copy-done.7, bf16[128,704]{1,0:T(8,128)(2,1)S(1)} %copy-done.11, bf16[128,704]{1,0:T(8,128)(2,1)S(1)} %copy-done.15, ...), custom_call_target="tpu_custom_call" | custom-call | flops 536870912 | bytes 524288 | tf_op jit(solution)/shard_map/pallas_call | solution.py:29
  49.1 1.5 %collective-permute-done.12.refs_3_ = bf16[32,1024]{1,0:T(8,128)(2,1)S(1)} collective-permute-done((bf16[32,1024]{1,0:T(8,128)(2,1)}, bf16[32,1024]{1,0:T(8,128)(2,1)S(1)}, u32[]{:S(2)}, u32[]{:S(2)}) %collective-permute-start.12) | collective-permute-done | bytes 65568 | tf_op jit(solution)/shard_map/ppermute | solution.py:358
  51.5 2.3 %shard_map.100 = (f32[1024,128]{1,0:T(8,128)S(1)}, f32[1024,128]{1,0:T(8,128)S(1)}, bf16[544,128]{1,0:T(8,128)(2,1)S(1)}, bf16[544,128]{1,0:T(8,128)(2,1)S(1)}) custom-call(bf16[32,1024]{1,0:T(8,128)(2,1)S(1)} %copy-done.21, bf16[32,1024]{1,0:T(8,128)(2,1)S(1)} %collective-permute-done.10.refs_1_, bf16[32,1024]{1,0:T(8,128)(2,1)S(1)} %collective-permute-done.11.refs_2_, ...), custom_call_target="tpu_custom_call" | custom-call | flops 805306368 | bytes 524288 | tf_op jit(solution)/shard_map/pallas_call | solution.py:29
  53.8 2.0 %shard_map.101 = (f32[512,128]{1,0:T(8,128)S(1)}, f32[512,128]{1,0:T(8,128)S(1)}, bf16[544,128]{1,0:T(8,128)(2,1)S(1)}, bf16[544,128]{1,0:T(8,128)(2,1)S(1)}) custom-call(bf16[128,704]{1,0:T(8,128)(2,1)S(1)} %copy-done.1, bf16[128,704]{1,0:T(8,128)(2,1)S(1)} %copy-done.7, bf16[128,704]{1,0:T(8,128)(2,1)S(1)} %copy-done.11, bf16[128,704]{1,0:T(8,128)(2,1)S(1)} %copy-done.15, ...), custom_call_target="tpu_custom_call" | custom-call | flops 805306368 | bytes 524288 | tf_op jit(solution)/shard_map/pallas_call | solution.py:29
  55.9 1.6 %collective-permute-start.15 = (bf16[544,128]{1,0:T(8,128)(2,1)S(1)}, bf16[544,128]{1,0:T(8,128)(2,1)S(1)}, u32[]{:S(2)}, u32[]{:S(2)}) collective-permute-start(bf16[544,128]{1,0:T(8,128)(2,1)S(1)} %get-tuple-element.55), channel_id=1, source_target_pairs={{0,2},{1,3},{2,0},{3,1},{4,6},{5,7},{6,4},{7,5},{8,10},{9,11},{10,... | collective-permute-start | bytes 417800 | tf_op jit(solution)/shard_map/ppermute | solution.py:358
  58.3 1.3 %collective-permute-start.14 = (bf16[544,128]{1,0:T(8,128)(2,1)S(1)}, bf16[544,128]{1,0:T(8,128)(2,1)S(1)}, u32[]{:S(2)}, u32[]{:S(2)}) collective-permute-start(bf16[544,128]{1,0:T(8,128)(2,1)S(1)} %get-tuple-element.54), channel_id=1, source_target_pairs={{0,1},{1,0},{2,3},{3,2},{4,5},{5,4},{6,7},{7,6},{8,9},{9,8},{10,11... | collective-permute-start | bytes 417800 | tf_op jit(solution)/shard_map/ppermute | solution.py:358
  59.6 1.5 %collective-permute-start.17 = (bf16[128,128]{1,0:T(8,128)(2,1)S(1)}, bf16[128,128]{1,0:T(8,128)(2,1)S(1)}, u32[]{:S(2)}, u32[]{:S(2)}) collective-permute-start(bf16[128,128]{1,0:T(8,128)(2,1)S(1)} %get-tuple-element.59), channel_id=1, source_target_pairs={{0,8},{4,12},{8,0},{12,4},{16,24},{20,28},{24,16},{28,20},{1,9},{5... | collective-permute-start | bytes 98312 | tf_op jit(solution)/shard_map/ppermute | solution.py:358
  61.6 1.9 %collective-permute-done.17.refs_1_ = bf16[128,128]{1,0:T(8,128)(2,1)S(1)} collective-permute-done((bf16[128,128]{1,0:T(8,128)(2,1)S(1)}, bf16[128,128]{1,0:T(8,128)(2,1)S(1)}, u32[]{:S(2)}, u32[]{:S(2)}) %collective-permute-start.17) | collective-permute-done | bytes 32800 | tf_op jit(solution)/shard_map/ppermute | solution.py:358
  63.5 1.4 %collective-permute-start.19 = (bf16[128,128]{1,0:T(8,128)(2,1)S(1)}, bf16[128,128]{1,0:T(8,128)(2,1)S(1)}, u32[]{:S(2)}, u32[]{:S(2)}) collective-permute-start(bf16[128,128]{1,0:T(8,128)(2,1)S(1)} %get-tuple-element.61), channel_id=1, source_target_pairs={{0,24},{4,28},{8,16},{12,20},{16,8},{20,12},{24,0},{28,4},{1,25},{... | collective-permute-start | bytes 98312 | tf_op jit(solution)/shard_map/ppermute | solution.py:358
  65.0 3.3 %collective-permute-done.19.refs_3_ = bf16[128,128]{1,0:T(8,128)(2,1)S(1)} collective-permute-done((bf16[128,128]{1,0:T(8,128)(2,1)S(1)}, bf16[128,128]{1,0:T(8,128)(2,1)S(1)}, u32[]{:S(2)}, u32[]{:S(2)}) %collective-permute-start.19) | collective-permute-done | bytes 32800 | tf_op jit(solution)/shard_map/ppermute | solution.py:358
  68.4 2.0 %collective-permute-start.22 = (bf16[128,128]{1,0:T(8,128)(2,1)S(1)}, bf16[128,128]{1,0:T(8,128)(2,1)S(1)}, u32[]{:S(2)}, u32[]{:S(2)}) collective-permute-start(bf16[128,128]{1,0:T(8,128)(2,1)S(1)} %shard_map.104.refs_0_), channel_id=1, source_target_pairs={{0,3},{1,2},{2,1},{3,0},{4,7},{5,6},{6,5},{7,4},{8,11},{9,10},{10,... | collective-permute-start | bytes 98312 | tf_op jit(solution)/shard_map/ppermute | solution.py:358
  70.9 3.3 %collective-permute-done.22.refs_3_ = bf16[128,128]{1,0:T(8,128)(2,1)S(1)} collective-permute-done((bf16[128,128]{1,0:T(8,128)(2,1)S(1)}, bf16[128,128]{1,0:T(8,128)(2,1)S(1)}, u32[]{:S(2)}, u32[]{:S(2)}) %collective-permute-start.22) | collective-permute-done | bytes 32800 | tf_op jit(solution)/shard_map/ppermute | solution.py:358
  75.2 3.0 %collective-permute-done.20.refs_1_ = bf16[128,128]{1,0:T(8,128)(2,1)S(1)} collective-permute-done((bf16[128,128]{1,0:T(8,128)(2,1)S(1)}, bf16[128,128]{1,0:T(8,128)(2,1)S(1)}, u32[]{:S(2)}, u32[]{:S(2)}) %collective-permute-start.20) | collective-permute-done | bytes 32800 | tf_op jit(solution)/shard_map/ppermute | solution.py:358
  (78 shorter events, 14.0 us)
Async XLA Ops:
  2.4 17.0 %copy-start = (bf16[128,704]{1,0:T(8,128)(2,1)}, bf16[128,704]{1,0:T(8,128)(2,1)S(1)}, u32[]{:S(2)}) copy-start(bf16[128,704]{1,0:T(8,128)(2,1)S(1)} %shard_map.94.refs_0_.refs_4_) | copy-start | bytes 540676
  2.4 7.9 %collective-permute-start.5 = (bf16[128,704]{1,0:T(8,128)(2,1)S(1)}, bf16[128,704]{1,0:T(8,128)(2,1)S(1)}, u32[]{:S(2)}, u32[]{:S(2)}) collective-permute-start(bf16[128,704]{1,0:T(8,128)(2,1)S(1)} %shard_map.94.refs_0_.refs_4_), channel_id=1, source_target_pairs={{0,16},{4,20},{8,24},{12,28},{16,0},{20,4},{24,8},{28,12},{1,17},{... | collective-permute-start | bytes 540680 | tf_op jit(solution)/shard_map/ppermute | solution.py:358
  5.5 7.8 %collective-permute-start.3 = (bf16[128,704]{1,0:T(8,128)(2,1)S(1)}, bf16[128,704]{1,0:T(8,128)(2,1)S(1)}, u32[]{:S(2)}, u32[]{:S(2)}) collective-permute-start(bf16[128,704]{1,0:T(8,128)(2,1)S(1)} %shard_map.94.refs_0_.refs_4_), channel_id=1, source_target_pairs={{0,8},{4,12},{8,0},{12,4},{16,24},{20,28},{24,16},{28,20},{1,9},{5... | collective-permute-start | bytes 540680 | tf_op jit(solution)/shard_map/ppermute | solution.py:358
  6.9 9.8 %collective-permute-start.2 = (bf16[128,704]{1,0:T(8,128)(2,1)S(1)}, bf16[128,704]{1,0:T(8,128)(2,1)S(1)}, u32[]{:S(2)}, u32[]{:S(2)}) collective-permute-start(bf16[128,704]{1,0:T(8,128)(2,1)S(1)} %shard_map.94.refs_0_.refs_4_), channel_id=1, source_target_pairs={{0,4},{4,0},{8,12},{12,8},{16,20},{20,16},{24,28},{28,24},{1,5},{5... | collective-permute-start | bytes 540680 | tf_op jit(solution)/shard_map/ppermute | solution.py:358
  6.9 17.8 %collective-permute-start = (bf16[128,704]{1,0:T(8,128)(2,1)S(1)}, bf16[128,704]{1,0:T(8,128)(2,1)S(1)}, u32[]{:S(2)}, u32[]{:S(2)}) collective-permute-start(bf16[128,704]{1,0:T(8,128)(2,1)S(1)} %shard_map.94.refs_0_.refs_4_), channel_id=1, source_target_pairs={{0,24},{4,28},{8,16},{12,20},{16,8},{20,12},{24,0},{28,4},{1,25},{... | collective-permute-start | bytes 540680 | tf_op jit(solution)/shard_map/ppermute | solution.py:358
  10.4 15.1 %collective-permute-start.6 = (bf16[128,704]{1,0:T(8,128)(2,1)S(1)}, bf16[128,704]{1,0:T(8,128)(2,1)S(1)}, u32[]{:S(2)}, u32[]{:S(2)}) collective-permute-start(bf16[128,704]{1,0:T(8,128)(2,1)S(1)} %collective-permute-done.5.refs_2_.refs_4_.refs_8_), channel_id=1, source_target_pairs={{0,4},{4,0},{8,12},{12,8},{16,20},{20,16},{24,28},{28,24},{1,5},{5... | collective-permute-start | bytes 540680 | tf_op jit(solution)/shard_map/ppermute | solution.py:358
  13.3 12.2 %collective-permute-start.4 = (bf16[128,704]{1,0:T(8,128)(2,1)S(1)}, bf16[128,704]{1,0:T(8,128)(2,1)S(1)}, u32[]{:S(2)}, u32[]{:S(2)}) collective-permute-start(bf16[128,704]{1,0:T(8,128)(2,1)S(1)} %collective-permute-done.3.refs_0_.refs_2_.refs_6_), channel_id=1, source_target_pairs={{0,4},{4,0},{8,12},{12,8},{16,20},{20,16},{24,28},{28,24},{1,5},{5... | collective-permute-start | bytes 540680 | tf_op jit(solution)/shard_map/ppermute | solution.py:358
  15.1 29.2 %collective-permute-start.7 = (bf16[560,128]{1,0:T(8,128)(2,1)S(1)}, bf16[560,128]{1,0:T(8,128)(2,1)S(1)}, u32[]{:S(2)}, u32[]{:S(2)}) collective-permute-start(bf16[560,128]{1,0:T(8,128)(2,1)S(1)} %get-tuple-element.36), channel_id=1, source_target_pairs={{0,1},{1,0},{2,3},{3,2},{4,5},{5,4},{6,7},{7,6},{8,9},{9,8},{10,11... | collective-permute-start | bytes 430088 | tf_op jit(solution)/shard_map/ppermute | solution.py:358
  16.8 28.1 %collective-permute-start.8 = (bf16[560,128]{1,0:T(8,128)(2,1)S(1)}, bf16[560,128]{1,0:T(8,128)(2,1)S(1)}, u32[]{:S(2)}, u32[]{:S(2)}) collective-permute-start(bf16[560,128]{1,0:T(8,128)(2,1)S(1)} %get-tuple-element.37), channel_id=1, source_target_pairs={{0,2},{1,3},{2,0},{3,1},{4,6},{5,7},{6,4},{7,5},{8,10},{9,11},{10,... | collective-permute-start | bytes 430088 | tf_op jit(solution)/shard_map/ppermute | solution.py:358
  24.8 20.1 %collective-permute-start.9 = (bf16[560,128]{1,0:T(8,128)(2,1)S(1)}, bf16[560,128]{1,0:T(8,128)(2,1)S(1)}, u32[]{:S(2)}, u32[]{:S(2)}) collective-permute-start(bf16[560,128]{1,0:T(8,128)(2,1)S(1)} %get-tuple-element.38), channel_id=1, source_target_pairs={{0,3},{1,2},{2,1},{3,0},{4,7},{5,6},{6,5},{7,4},{8,11},{9,10},{10,... | collective-permute-start | bytes 430088 | tf_op jit(solution)/shard_map/ppermute | solution.py:358
  25.4 8.7 %collective-permute-start.1 = (bf16[128,704]{1,0:T(8,128)(2,1)S(1)}, bf16[128,704]{1,0:T(8,128)(2,1)S(1)}, u32[]{:S(2)}, u32[]{:S(2)}) collective-permute-start(bf16[128,704]{1,0:T(8,128)(2,1)S(1)} %collective-permute-done.refs_0_.refs_6_.refs_10_), channel_id=1, source_target_pairs={{0,4},{4,0},{8,12},{12,8},{16,20},{20,16},{24,28},{28,24},{1,5},{5... | collective-permute-start | bytes 540680 | tf_op jit(solution)/shard_map/ppermute | solution.py:358
  40.5 8.3 %collective-permute-start.10 = (bf16[32,1024]{1,0:T(8,128)(2,1)}, bf16[32,1024]{1,0:T(8,128)(2,1)S(1)}, u32[]{:S(2)}, u32[]{:S(2)}) collective-permute-start(bf16[32,1024]{1,0:T(8,128)(2,1)} %get-tuple-element.42), channel_id=1, source_target_pairs={{0,1},{1,0},{2,3},{3,2},{4,5},{5,4},{6,7},{7,6},{8,9},{9,8},{10,11... | collective-permute-start | bytes 196616 | tf_op jit(solution)/shard_map/ppermute | solution.py:358
  41.2 7.9 %collective-permute-start.11 = (bf16[32,1024]{1,0:T(8,128)(2,1)}, bf16[32,1024]{1,0:T(8,128)(2,1)S(1)}, u32[]{:S(2)}, u32[]{:S(2)}) collective-permute-start(bf16[32,1024]{1,0:T(8,128)(2,1)} %get-tuple-element.43), channel_id=1, source_target_pairs={{0,2},{1,3},{2,0},{3,1},{4,6},{5,7},{6,4},{7,5},{8,10},{9,11},{10,... | collective-permute-start | bytes 196616 | tf_op jit(solution)/shard_map/ppermute | solution.py:358
  44.4 6.3 %collective-permute-start.12 = (bf16[32,1024]{1,0:T(8,128)(2,1)}, bf16[32,1024]{1,0:T(8,128)(2,1)S(1)}, u32[]{:S(2)}, u32[]{:S(2)}) collective-permute-start(bf16[32,1024]{1,0:T(8,128)(2,1)} %get-tuple-element.44), channel_id=1, source_target_pairs={{0,3},{1,2},{2,1},{3,0},{4,7},{5,6},{6,5},{7,4},{8,11},{9,10},{10,... | collective-permute-start | bytes 196616 | tf_op jit(solution)/shard_map/ppermute | solution.py:358
  55.9 2.4 %collective-permute-start.13 = (f32[512,128]{1,0:T(8,128)S(1)}, f32[512,128]{1,0:T(8,128)S(1)}, u32[]{:S(2)}, u32[]{:S(2)}) collective-permute-start(f32[512,128]{1,0:T(8,128)S(1)} %get-tuple-element.49), channel_id=1, source_target_pairs={{0,4},{4,0},{8,12},{12,8},{16,20},{20,16},{24,28},{28,24},{1,5},{5... | collective-permute-start | bytes 786440 | tf_op jit(solution)/shard_map/ppermute | solution.py:358
  55.9 22.9 %collective-permute-start.15 = (bf16[544,128]{1,0:T(8,128)(2,1)S(1)}, bf16[544,128]{1,0:T(8,128)(2,1)S(1)}, u32[]{:S(2)}, u32[]{:S(2)}) collective-permute-start(bf16[544,128]{1,0:T(8,128)(2,1)S(1)} %get-tuple-element.55), channel_id=1, source_target_pairs={{0,2},{1,3},{2,0},{3,1},{4,6},{5,7},{6,4},{7,5},{8,10},{9,11},{10,... | collective-permute-start | bytes 417800 | tf_op jit(solution)/shard_map/ppermute | solution.py:358
  57.5 21.3 %collective-permute-start.16 = (bf16[544,128]{1,0:T(8,128)(2,1)S(1)}, bf16[544,128]{1,0:T(8,128)(2,1)S(1)}, u32[]{:S(2)}, u32[]{:S(2)}) collective-permute-start(bf16[544,128]{1,0:T(8,128)(2,1)S(1)} %get-tuple-element.56), channel_id=1, source_target_pairs={{0,3},{1,2},{2,1},{3,0},{4,7},{5,6},{6,5},{7,4},{8,11},{9,10},{10,... | collective-permute-start | bytes 417800 | tf_op jit(solution)/shard_map/ppermute | solution.py:358
  58.3 20.5 %collective-permute-start.14 = (bf16[544,128]{1,0:T(8,128)(2,1)S(1)}, bf16[544,128]{1,0:T(8,128)(2,1)S(1)}, u32[]{:S(2)}, u32[]{:S(2)}) collective-permute-start(bf16[544,128]{1,0:T(8,128)(2,1)S(1)} %get-tuple-element.54), channel_id=1, source_target_pairs={{0,1},{1,0},{2,3},{3,2},{4,5},{5,4},{6,7},{7,6},{8,9},{9,8},{10,11... | collective-permute-start | bytes 417800 | tf_op jit(solution)/shard_map/ppermute | solution.py:358
  59.6 3.9 %collective-permute-start.17 = (bf16[128,128]{1,0:T(8,128)(2,1)S(1)}, bf16[128,128]{1,0:T(8,128)(2,1)S(1)}, u32[]{:S(2)}, u32[]{:S(2)}) collective-permute-start(bf16[128,128]{1,0:T(8,128)(2,1)S(1)} %get-tuple-element.59), channel_id=1, source_target_pairs={{0,8},{4,12},{8,0},{12,4},{16,24},{20,28},{24,16},{28,20},{1,9},{5... | collective-permute-start | bytes 98312 | tf_op jit(solution)/shard_map/ppermute | solution.py:358
  61.1 3.9 %collective-permute-start.18 = (bf16[128,128]{1,0:T(8,128)(2,1)S(1)}, bf16[128,128]{1,0:T(8,128)(2,1)S(1)}, u32[]{:S(2)}, u32[]{:S(2)}) collective-permute-start(bf16[128,128]{1,0:T(8,128)(2,1)S(1)} %get-tuple-element.60), channel_id=1, source_target_pairs={{0,16},{4,20},{8,24},{12,28},{16,0},{20,4},{24,8},{28,12},{1,17},{... | collective-permute-start | bytes 98312 | tf_op jit(solution)/shard_map/ppermute | solution.py:358
  63.5 4.8 %collective-permute-start.19 = (bf16[128,128]{1,0:T(8,128)(2,1)S(1)}, bf16[128,128]{1,0:T(8,128)(2,1)S(1)}, u32[]{:S(2)}, u32[]{:S(2)}) collective-permute-start(bf16[128,128]{1,0:T(8,128)(2,1)S(1)} %get-tuple-element.61), channel_id=1, source_target_pairs={{0,24},{4,28},{8,16},{12,20},{16,8},{20,12},{24,0},{28,4},{1,25},{... | collective-permute-start | bytes 98312 | tf_op jit(solution)/shard_map/ppermute | solution.py:358
  68.4 5.9 %collective-permute-start.22 = (bf16[128,128]{1,0:T(8,128)(2,1)S(1)}, bf16[128,128]{1,0:T(8,128)(2,1)S(1)}, u32[]{:S(2)}, u32[]{:S(2)}) collective-permute-start(bf16[128,128]{1,0:T(8,128)(2,1)S(1)} %shard_map.104.refs_0_), channel_id=1, source_target_pairs={{0,3},{1,2},{2,1},{3,0},{4,7},{5,6},{6,5},{7,4},{8,11},{9,10},{10,... | collective-permute-start | bytes 98312 | tf_op jit(solution)/shard_map/ppermute | solution.py:358
  70.4 4.8 %collective-permute-start.21 = (bf16[128,128]{1,0:T(8,128)(2,1)S(1)}, bf16[128,128]{1,0:T(8,128)(2,1)S(1)}, u32[]{:S(2)}, u32[]{:S(2)}) collective-permute-start(bf16[128,128]{1,0:T(8,128)(2,1)S(1)} %shard_map.104.refs_0_), channel_id=1, source_target_pairs={{0,2},{1,3},{2,0},{3,1},{4,6},{5,7},{6,4},{7,5},{8,10},{9,11},{10,... | collective-permute-start | bytes 98312 | tf_op jit(solution)/shard_map/ppermute | solution.py:358
  74.2 3.9 %collective-permute-start.20 = (bf16[128,128]{1,0:T(8,128)(2,1)S(1)}, bf16[128,128]{1,0:T(8,128)(2,1)S(1)}, u32[]{:S(2)}, u32[]{:S(2)}) collective-permute-start(bf16[128,128]{1,0:T(8,128)(2,1)S(1)} %shard_map.104.refs_0_), channel_id=1, source_target_pairs={{0,1},{1,0},{2,3},{3,2},{4,5},{5,4},{6,7},{7,6},{8,9},{9,8},{10,11... | collective-permute-start | bytes 98312 | tf_op jit(solution)/shard_map/ppermute | solution.py:358
  (21 other events, 123.5 us)

commit v4 on v2

--- a/solution.py
+++ b/solution.py
@@ -16,7 +16,7 @@
 
 
 def params():
-    return pltpu.CompilerParams(vmem_limit_bytes=48 * 1024 * 1024)
+    return pltpu.CompilerParams(vmem_limit_bytes=24 * 1024 * 1024)
 
 
 def whole(value):
@@ -54,10 +54,13 @@
     return found
 
 
-def pack_kernel(latent_ref, key_ref, query_ref, weight_ref, packed_ref, *outs):
+def pack_kernel(latent_ref, key_ref, packed_ref):
     width = key_ref.shape[1]
     packed_ref[:, :width] = key_ref[...]
     packed_ref[:, width:] = latent_ref[...].T
+
+
+def ask_kernel(query_ref, weight_ref, *outs):
     me = lax.axis_index("ha")
     heads = weight_ref.shape[0]
     rows = outs[0].shape[0] - 3 * TAIL
@@ -87,39 +90,27 @@
 def main_kernel(rels, earlier, *refs):
     count = len(rels)
     blocks = refs[:count]
-    query_hbm, sums_ref, start_ref = refs[count : count + 3]
+    query, sums_ref, start_ref = refs[count : count + 3]
     before = refs[count + 3 : count + 3 + earlier]
-    outs = refs[count + 3 + earlier : -6]
-    keys, query, total, turned, sems, _ = refs[-6:]
+    outs = refs[count + 3 + earlier : -3]
+    keys, total, turned = refs[-3:]
     heads, width, rows = query.shape
-    pieces = sems.shape[0]
-    per = heads // pieces
-    copies = [
-        pltpu.make_async_copy(
-            query_hbm.at[pl.ds(i * per, per)], query.at[pl.ds(i * per, per)], sems.at[i]
-        )
-        for i in range(pieces)
-    ]
-    for copy in copies:
-        copy.start()
     for k in range(count):
         block = blocks[k][...]
         keys[k * rows : (k + 1) * rows, :] = block[:, block.shape[1] - width :]
     total[...] = jnp.zeros_like(total)
 
-    for i in range(pieces):
-        copies[i].wait()
-        for pair in range(i * per // 2, (i + 1) * per // 2):
-            two = jnp.concatenate([query[2 * pair], query[2 * pair + 1]], axis=1)
-            scores = jnp.dot(keys[...], two, preferred_element_type=f32)
-            parts = [
-                jnp.exp2(
-                    scores[:, half * rows : (half + 1) * rows] * (main_scale * log2e)
-                    - sums_ref[2 * pair + half : 2 * pair + half + 1, :] * log2e
-                )
-                for half in range(2)
-            ]
-            total[...] += parts[0] + parts[1]
+    for head in range(0, heads, 2):
+        two = jnp.concatenate([query[head], query[head + 1]], axis=1)
+        scores = jnp.dot(keys[...], two, preferred_element_type=f32)
+        parts = [
+            jnp.exp2(
+                scores[:, half * rows : (half + 1) * rows] * (main_scale * log2e)
+                - sums_ref[head + half : head + half + 1, :] * log2e
+            )
+            for half in range(2)
+        ]
+        total[...] += parts[0] + parts[1]
 
     me = lax.axis_index("pb")
     kept = turned.shape[1] - count * rows
@@ -332,24 +323,29 @@
     start_row = window_start.reshape(1, rows)
     key_only = pl.BlockSpec((rows, index_width), lambda *_: (0, 0))
 
-    packed, *asked = call(
+    packed = call(
         pack_kernel,
-        [shape((rows, index_width + width), bf16)]
-        + [shape((own + 3 * TAIL, index_width), bf16)] * parts,
-        (latent.T, index_key, index_query.reshape(rows * heads, index_width), index_weight.T),
-    )
+        shape((rows, index_width + width), bf16),
+        (latent.T, index_key),
+        cost=pl.CostEstimate(flops=0, bytes_accessed=1 << 24, transcendentals=0),
+    )
+    asked = call(
+        ask_kernel,
+        [shape((own + 3 * TAIL, index_width), bf16)] * parts,
+        (index_query.reshape(rows * heads, index_width), index_weight.T),
+    )
+    queries = jnp.transpose(main_query, (1, 2, 0))
+    sums = log_sums.T
     held = [None] * blocks
     held[0] = packed
     held[1] = swap(packed, "pb", 1)
     for k in range(2, blocks, 2):
         held[k] = swap(packed, "pb", k)
-        held[k + 1] = swap(held[k], "pb", 1)
-    asked = [asked[0]] + [swap(asked[r], "ha", r) for r in range(1, parts)]
-
-    queries = jnp.transpose(main_query, (1, 2, 0))
-    sums = log_sums.T
+    ready = lax.optimization_barrier((asked[0], held[1]))
+    asked = [ready[0]] + [swap(asked[r], "ha", r) for r in range(1, parts)]
+    held[1] = ready[1]
+
     chunks = [[0, 1]] + [list(range(k, min(k + 4, blocks))) for k in range(2, blocks, 4)]
-    pieces = max(1, head_count // 8)
     mass = []
     for rels in chunks:
         last = rels is chunks[-1]
@@ -358,18 +354,15 @@
         before = mass if last else []
         values = [held[k] for k in rels] + [queries, sums, start_row] + before
         specs = [whole(v) for v in values]
-        specs[len(rels)] = pl.BlockSpec(memory_space=pltpu.HBM)
+        specs[len(rels)] = pl.BlockSpec(memory_space=pltpu.VMEM)
         found = call(
             functools.partial(main_kernel, rels, len(before)),
             outs,
             values,
             [
                 pltpu.VMEM((span, width), bf16),
-                pltpu.VMEM((head_count, width, rows), bf16),
                 pltpu.VMEM((span, rows), f32),
                 pltpu.VMEM((rows, tokens if last else span), f32),
-                pltpu.SemaphoreType.DMA((pieces,)),
-                pltpu.VMEM((8, LANES), f32),
             ],
             specs,
             pl.CostEstimate(
@@ -379,6 +372,13 @@
             ),
         )
         mass = found if last else mass + found
+        if rels is chunks[0]:
+            even = list(range(2, blocks, 2))
+            ready = lax.optimization_barrier((found[0], [held[k] for k in even]))
+            mass = [ready[0]]
+            for k, block in zip(even, ready[1]):
+                held[k] = block
+                held[k + 1] = swap(block, "pb", 1)
     first, key_block = lax.optimization_barrier((mass[0], held[0]))
     mass = [first] + [swap(mass[r], "ha", r) for r in range(1, parts)]
     key_blocks = [key_block] + held[1:]

time: 71.3 us -> 64.8 us (0.909)
  Pallas kernels: 19.9 us -> 15.1 us
  waiting for transfers between devices: 17.1 us -> 14.5 us
  starting transfers between devices: 26 us -> 26.9 us
    pallas_call x10 -> x11, Pallas kernels: 19.9 us -> 15.1 us  [call(): pl.pallas_call(kernel, grid=(1,), out_shape=outs, in_specs=specs or [whol...]
    ppermute x23, waiting for transfers between devices: 17.1 us -> 14.5 us  [swap(): return lax.ppermute(value, axis, [(i, i ^ rel) for i in range(size)])]
    ppermute x23, starting transfers between devices: 26 us -> 26.9 us  [swap(): return lax.ppermute(value, axis, [(i, i ^ rel) for i in range(size)])]
    unnamed x16 -> x20, local copies, waits for them, and re-layouts: 7.11 us -> 7.12 us
  transfers between devices with their start and end apart: 23 -> 23, of which waited for: 9 -> 8; matrix products, arithmetic and copies ran while one was open for 0% -> 0% of each run, Pallas kernels for 21% -> 16%
where the time goes in v4:
time: 64.8 us; the launch traced here: 64.5 us
  starting transfers between devices  26.9 us (42%)
  Pallas kernels  15.1 us (23%)
  waiting for transfers between devices  14.5 us (22%)
  local copies, waits for them, and re-layouts  7.12 us (11%)
  between operations  0.8 us (1%)
    ppermute x23, starting transfers between devices, swap(): return lax.ppermute(value, axis, [(i, i ^ rel) for i in range(size)])  26.9 us
    pallas_call x11, Pallas kernels, call(): pl.pallas_call(kernel, grid=(1,), out_shape=outs, in_specs=specs or [whol...  15.1 us
    ppermute x23, waiting for transfers between devices, swap(): return lax.ppermute(value, axis, [(i, i ^ rel) for i in range(size)])  14.5 us
    unnamed x20, local copies, waits for them, and re-layouts  7.12 us
  transfers between devices with their start and end apart: 23, of which 8 were waited for; matrix products, arithmetic and copies ran while one was open for 0% of the time, Pallas kernels for 16%

profile of v4, /device:TPU:0, one launch (start us, length us, event | category | flops | bytes accessed | tf_op | source)
XLA Modules:
  0.0 64.5 jit_solution(6796050095505127264)
XLA Ops:
  2.9 3.5 %collective-permute-start.3 = (bf16[128,704]{1,0:T(8,128)(2,1)S(1)}, bf16[128,704]{1,0:T(8,128)(2,1)S(1)}, u32[]{:S(2)}, u32[]{:S(2)}) collective-permute-start(bf16[128,704]{1,0:T(8,128)(2,1)S(1)} %shard_map.94.refs_0_.refs_4_), channel_id=1, source_target_pairs={{0,24},{4,28},{8,16},{12,20},{16,8},{20,12},{24,0},{28,4},{1,25},{... | collective-permute-start | bytes 540680 | tf_op jit(solution)/shard_map/ppermute | solution.py:321
  7.1 1.0 %copy-done.2 = bf16[128,16,128]{2,1,0:T(8,128)(2,1)S(1)} copy-done((bf16[128,16,128]{2,1,0:T(8,128)(2,1)S(1)}, bf16[128,16,128]{2,1,0:T(8,128)(2,1)}, u32[]{:S(2)}) %copy-start.2) | copy-done | bytes 524312
  8.9 2.3 %copy-done = bf16[128,32,576]{0,2,1:T(8,128)(2,1)S(1)} copy-done((bf16[128,32,576]{0,2,1:T(8,128)(2,1)S(1)}, bf16[128,32,576]{0,2,1:T(8,128)(2,1)}, u32[]{:S(2)}) %copy-start) | copy-done | bytes 4718616
  12.6 1.9 %shard_map.96.refs_5_ = bf16[128,256]{1,0:T(8,128)(2,1)S(1)} custom-call(bf16[128,704]{1,0:T(8,128)(2,1)S(1)} %shard_map.94.refs_0_.refs_4_, bf16[128,704]{1,0:T(8,128)(2,1)S(1)} %collective-permute-done.refs_1_.refs_5_, bf16[32,576,128]{2,1,0:T(8,128)(2,1)S(1)} %bitcast.8, f32[32,128]{1,0:T(8,128)S(1)} %bitcast.13, s32[1,128]{1,0:T(1,128)S(1)} %bitcast.17), custom_call_target="tpu_custom_call" | custom-call | flops 1207959552 | bytes 4718592 | tf_op jit(solution)/shard_map/pallas_call | solution.py:29
  14.5 1.6 %collective-permute-done.2.refs_2_.refs_4_.refs_8_ = bf16[128,704]{1,0:T(8,128)(2,1)S(1)} collective-permute-done((bf16[128,704]{1,0:T(8,128)(2,1)S(1)}, bf16[128,704]{1,0:T(8,128)(2,1)S(1)}, u32[]{:S(2)}, u32[]{:S(2)}) %collective-permute-start.2) | collective-permute-done | bytes 180256 | tf_op jit(solution)/shard_map/ppermute | solution.py:321
  17.0 1.6 %collective-permute-start.10 = (bf16[560,128]{1,0:T(8,128)(2,1)S(1)}, bf16[560,128]{1,0:T(8,128)(2,1)S(1)}, u32[]{:S(2)}, u32[]{:S(2)}) collective-permute-start(bf16[560,128]{1,0:T(8,128)(2,1)S(1)} %get-tuple-element.47), channel_id=1, source_target_pairs={{0,1},{1,0},{2,3},{3,2},{4,5},{5,4},{6,7},{7,6},{8,9},{9,8},{10,11... | collective-permute-start | bytes 430088 | tf_op jit(solution)/shard_map/ppermute | solution.py:321
  18.6 2.6 %collective-permute-start.11 = (bf16[560,128]{1,0:T(8,128)(2,1)S(1)}, bf16[560,128]{1,0:T(8,128)(2,1)S(1)}, u32[]{:S(2)}, u32[]{:S(2)}) collective-permute-start(bf16[560,128]{1,0:T(8,128)(2,1)S(1)} %get-tuple-element.48), channel_id=1, source_target_pairs={{0,2},{1,3},{2,0},{3,1},{4,6},{5,7},{6,4},{7,5},{8,10},{9,11},{10,... | collective-permute-start | bytes 430088 | tf_op jit(solution)/shard_map/ppermute | solution.py:321
  21.4 3.6 %shard_map.97.refs_6_ = bf16[128,512]{1,0:T(8,128)(2,1)S(1)} custom-call(bf16[128,704]{1,0:T(8,128)(2,1)S(1)} %collective-permute-done.1.refs_0_.refs_2_.refs_6_, bf16[128,704]{1,0:T(8,128)(2,1)S(1)} %collective-permute-done.5.refs_1_.refs_3_.refs_7_, bf16[128,704]{1,0:T(8,128)(2,1)S(1)} %collective-permute-done.2.refs_2_.refs_4_.refs_8_, ...), custom_call_target="tpu_custom_call" | custom-call | flops 2415919104 | bytes 4718592 | tf_op jit(solution)/shard_map/pallas_call | solution.py:29
  25.0 1.9 %shard_map.98 = (bf16[32,1024]{1,0:T(8,128)(2,1)S(1)}, bf16[32,1024]{1,0:T(8,128)(2,1)S(1)}, bf16[32,1024]{1,0:T(8,128)(2,1)S(1)}, bf16[32,1024]{1,0:T(8,128)(2,1)S(1)}) custom-call(bf16[128,704]{1,0:T(8,128)(2,1)S(1)} %collective-permute-done.3.refs_0_.refs_6_.refs_10_, bf16[128,704]{1,0:T(8,128)(2,1)S(1)} %collective-permute-done.4.refs_1_.refs_7_.refs_11_, ...), custom_call_target="tpu_custom_call" | custom-call | flops 1207959552 | bytes 4718592 | tf_op jit(solution)/shard_map/pallas_call | solution.py:29
  27.7 3.5 %collective-permute-start.8 = (bf16[32,1024]{1,0:T(8,128)(2,1)S(1)}, bf16[32,1024]{1,0:T(8,128)(2,1)S(1)}, u32[]{:S(2)}, u32[]{:S(2)}) collective-permute-start(bf16[32,1024]{1,0:T(8,128)(2,1)S(1)} %get-tuple-element.43), channel_id=1, source_target_pairs={{0,2},{1,3},{2,0},{3,1},{4,6},{5,7},{6,4},{7,5},{8,10},{9,11},{10,... | collective-permute-start | bytes 196616 | tf_op jit(solution)/shard_map/ppermute | solution.py:321
  32.3 1.9 %shard_map.99 = (f32[1024,128]{1,0:T(8,128)S(1)}, bf16[2048,128]{1,0:T(8,128)(2,1)S(1)}, f32[16,128]{1,0:T(8,128)S(1)}) custom-call(bf16[128,704]{1,0:T(8,128)(2,1)S(1)} %shard_map.94.refs_0_.refs_4_, bf16[128,704]{1,0:T(8,128)(2,1)S(1)} %collective-permute-done.refs_1_.refs_5_, bf16[128,704]{1,0:T(8,128)(2,1)S(1)} %collective-permute-done.1.refs_0_.refs_2_.refs_6_, ...), custom_call_target="tpu_custom_call" | custom-call | flops 536870912 | bytes 524288 | tf_op jit(solution)/shard_map/pallas_call | solution.py:29
  34.2 4.8 %collective-permute-done.8.refs_2_ = bf16[32,1024]{1,0:T(8,128)(2,1)S(1)} collective-permute-done((bf16[32,1024]{1,0:T(8,128)(2,1)S(1)}, bf16[32,1024]{1,0:T(8,128)(2,1)S(1)}, u32[]{:S(2)}, u32[]{:S(2)}) %collective-permute-start.8) | collective-permute-done | bytes 65568 | tf_op jit(solution)/shard_map/ppermute | solution.py:321
  39.0 4.0 %shard_map.100 = (f32[512,128]{1,0:T(8,128)S(1)}, f32[512,128]{1,0:T(8,128)S(1)}, bf16[544,128]{1,0:T(8,128)(2,1)S(1)}, bf16[544,128]{1,0:T(8,128)(2,1)S(1)}, bf...) custom-call(bf16[32,1024]{1,0:T(8,128)(2,1)S(1)} %get-tuple-element.41.refs_0_, ...), custom_call_target="tpu_custom_call" | custom-call | flops 1610612736 | bytes 524288 | tf_op jit(solution)/shard_map/pallas_call | solution.py:29
  43.1 1.7 %collective-permute-start.13 = (bf16[544,128]{1,0:T(8,128)(2,1)S(1)}, bf16[544,128]{1,0:T(8,128)(2,1)S(1)}, u32[]{:S(2)}, u32[]{:S(2)}) collective-permute-start(bf16[544,128]{1,0:T(8,128)(2,1)S(1)} %get-tuple-element.54), channel_id=1, source_target_pairs={{0,1},{1,0},{2,3},{3,2},{4,5},{5,4},{6,7},{7,6},{8,9},{9,8},{10,11... | collective-permute-start | bytes 417800 | tf_op jit(solution)/shard_map/ppermute | solution.py:321
  44.9 1.4 %collective-permute-start.14 = (bf16[544,128]{1,0:T(8,128)(2,1)S(1)}, bf16[544,128]{1,0:T(8,128)(2,1)S(1)}, u32[]{:S(2)}, u32[]{:S(2)}) collective-permute-start(bf16[544,128]{1,0:T(8,128)(2,1)S(1)} %get-tuple-element.55), channel_id=1, source_target_pairs={{0,2},{1,3},{2,0},{3,1},{4,6},{5,7},{6,4},{7,5},{8,10},{9,11},{10,... | collective-permute-start | bytes 417800 | tf_op jit(solution)/shard_map/ppermute | solution.py:321
  46.2 1.4 %collective-permute-start.15 = (bf16[544,128]{1,0:T(8,128)(2,1)S(1)}, bf16[544,128]{1,0:T(8,128)(2,1)S(1)}, u32[]{:S(2)}, u32[]{:S(2)}) collective-permute-start(bf16[544,128]{1,0:T(8,128)(2,1)S(1)} %get-tuple-element.56), channel_id=1, source_target_pairs={{0,3},{1,2},{2,1},{3,0},{4,7},{5,6},{6,5},{7,4},{8,11},{9,10},{10,... | collective-permute-start | bytes 417800 | tf_op jit(solution)/shard_map/ppermute | solution.py:321
  47.6 1.6 %collective-permute-start.17 = (bf16[128,128]{1,0:T(8,128)(2,1)S(1)}, bf16[128,128]{1,0:T(8,128)(2,1)S(1)}, u32[]{:S(2)}, u32[]{:S(2)}) collective-permute-start(bf16[128,128]{1,0:T(8,128)(2,1)S(1)} %get-tuple-element.61), channel_id=1, source_target_pairs={{0,8},{4,12},{8,0},{12,4},{16,24},{20,28},{24,16},{28,20},{1,9},{5... | collective-permute-start | bytes 98312 | tf_op jit(solution)/shard_map/ppermute | solution.py:321
  49.9 1.7 %collective-permute-done.17.refs_1_ = bf16[128,128]{1,0:T(8,128)(2,1)S(1)} collective-permute-done((bf16[128,128]{1,0:T(8,128)(2,1)S(1)}, bf16[128,128]{1,0:T(8,128)(2,1)S(1)}, u32[]{:S(2)}, u32[]{:S(2)}) %collective-permute-start.17) | collective-permute-done | bytes 32800 | tf_op jit(solution)/shard_map/ppermute | solution.py:321
  51.6 1.6 %collective-permute-start.19 = (bf16[128,128]{1,0:T(8,128)(2,1)S(1)}, bf16[128,128]{1,0:T(8,128)(2,1)S(1)}, u32[]{:S(2)}, u32[]{:S(2)}) collective-permute-start(bf16[128,128]{1,0:T(8,128)(2,1)S(1)} %get-tuple-element.63), channel_id=1, source_target_pairs={{0,24},{4,28},{8,16},{12,20},{16,8},{20,12},{24,0},{28,4},{1,25},{... | collective-permute-start | bytes 98312 | tf_op jit(solution)/shard_map/ppermute | solution.py:321
  53.3 3.2 %collective-permute-done.19.refs_3_ = bf16[128,128]{1,0:T(8,128)(2,1)S(1)} collective-permute-done((bf16[128,128]{1,0:T(8,128)(2,1)S(1)}, bf16[128,128]{1,0:T(8,128)(2,1)S(1)}, u32[]{:S(2)}, u32[]{:S(2)}) %collective-permute-start.19) | collective-permute-done | bytes 32800 | tf_op jit(solution)/shard_map/ppermute | solution.py:321
  56.5 2.5 %collective-permute-start.22 = (bf16[128,128]{1,0:T(8,128)(2,1)S(1)}, bf16[128,128]{1,0:T(8,128)(2,1)S(1)}, u32[]{:S(2)}, u32[]{:S(2)}) collective-permute-start(bf16[128,128]{1,0:T(8,128)(2,1)S(1)} %shard_map.103.refs_0_), channel_id=1, source_target_pairs={{0,3},{1,2},{2,1},{3,0},{4,7},{5,6},{6,5},{7,4},{8,11},{9,10},{10,... | collective-permute-start | bytes 98312 | tf_op jit(solution)/shard_map/ppermute | solution.py:321
  59.0 1.9 %collective-permute-start.20 = (bf16[128,128]{1,0:T(8,128)(2,1)S(1)}, bf16[128,128]{1,0:T(8,128)(2,1)S(1)}, u32[]{:S(2)}, u32[]{:S(2)}) collective-permute-start(bf16[128,128]{1,0:T(8,128)(2,1)S(1)} %shard_map.103.refs_0_), channel_id=1, source_target_pairs={{0,1},{1,0},{2,3},{3,2},{4,5},{5,4},{6,7},{7,6},{8,9},{9,8},{10,11... | collective-permute-start | bytes 98312 | tf_op jit(solution)/shard_map/ppermute | solution.py:321
  60.9 0.9 %shard_map.101 = (bf16[2048,128]{1,0:T(8,128)(2,1)}, f32[16,128]{1,0:T(8,128)}) custom-call(bf16[544,128]{1,0:T(8,128)(2,1)S(1)} %get-tuple-element.53.refs_0_, bf16[544,128]{1,0:T(8,128)(2,1)S(1)} %collective-permute-done.13.refs_1_, bf16[544,128]{1,0:T(8,128)(2,1)S(1)} %collective-permute-done.14.refs_2_, bf16[544,128]{1,0:T(8,128)(2,1)S(1)} %collective-permute-done.15.refs_3_), custom_call_target="tpu_custom_call" | custom-call | tf_op jit(solution)/shard_map/pallas_call | solution.py:29
  62.3 1.5 %collective-permute-done.21.refs_2_ = bf16[128,128]{1,0:T(8,128)(2,1)S(1)} collective-permute-done((bf16[128,128]{1,0:T(8,128)(2,1)S(1)}, bf16[128,128]{1,0:T(8,128)(2,1)S(1)}, u32[]{:S(2)}, u32[]{:S(2)}) %collective-permute-start.21) | collective-permute-done | bytes 32800 | tf_op jit(solution)/shard_map/ppermute | solution.py:321
  (53 shorter events, 9.9 us)
Async XLA Ops:
  0.6 20.8 %copy-start.9 = (s32[128]{0:T(128)S(1)}, s32[128]{0:T(128)}, u32[]{:S(2)}) copy-start(s32[128]{0:T(128)} %param.10) | copy-start | bytes 1540
  2.4 6.5 %collective-permute-start = (bf16[128,704]{1,0:T(8,128)(2,1)S(1)}, bf16[128,704]{1,0:T(8,128)(2,1)S(1)}, u32[]{:S(2)}, u32[]{:S(2)}) collective-permute-start(bf16[128,704]{1,0:T(8,128)(2,1)S(1)} %shard_map.94.refs_0_.refs_4_), channel_id=1, source_target_pairs={{0,4},{4,0},{8,12},{12,8},{16,20},{20,16},{24,28},{28,24},{1,5},{5... | collective-permute-start | bytes 540680 | tf_op jit(solution)/shard_map/ppermute | solution.py:321
  2.9 11.6 %collective-permute-start.3 = (bf16[128,704]{1,0:T(8,128)(2,1)S(1)}, bf16[128,704]{1,0:T(8,128)(2,1)S(1)}, u32[]{:S(2)}, u32[]{:S(2)}) collective-permute-start(bf16[128,704]{1,0:T(8,128)(2,1)S(1)} %shard_map.94.refs_0_.refs_4_), channel_id=1, source_target_pairs={{0,24},{4,28},{8,16},{12,20},{16,8},{20,12},{24,0},{28,4},{1,25},{... | collective-permute-start | bytes 540680 | tf_op jit(solution)/shard_map/ppermute | solution.py:321
  6.5 9.7 %collective-permute-start.2 = (bf16[128,704]{1,0:T(8,128)(2,1)S(1)}, bf16[128,704]{1,0:T(8,128)(2,1)S(1)}, u32[]{:S(2)}, u32[]{:S(2)}) collective-permute-start(bf16[128,704]{1,0:T(8,128)(2,1)S(1)} %shard_map.94.refs_0_.refs_4_), channel_id=1, source_target_pairs={{0,16},{4,20},{8,24},{12,28},{16,0},{20,4},{24,8},{28,12},{1,17},{... | collective-permute-start | bytes 540680 | tf_op jit(solution)/shard_map/ppermute | solution.py:321
  7.0 9.5 %collective-permute-start.1 = (bf16[128,704]{1,0:T(8,128)(2,1)S(1)}, bf16[128,704]{1,0:T(8,128)(2,1)S(1)}, u32[]{:S(2)}, u32[]{:S(2)}) collective-permute-start(bf16[128,704]{1,0:T(8,128)(2,1)S(1)} %shard_map.94.refs_0_.refs_4_), channel_id=1, source_target_pairs={{0,8},{4,12},{8,0},{12,4},{16,24},{20,28},{24,16},{28,20},{1,9},{5... | collective-permute-start | bytes 540680 | tf_op jit(solution)/shard_map/ppermute | solution.py:321
  16.5 4.9 %collective-permute-start.5 = (bf16[128,704]{1,0:T(8,128)(2,1)S(1)}, bf16[128,704]{1,0:T(8,128)(2,1)S(1)}, u32[]{:S(2)}, u32[]{:S(2)}) collective-permute-start(bf16[128,704]{1,0:T(8,128)(2,1)S(1)} %collective-permute-done.1.refs_0_.refs_2_.refs_6_), channel_id=1, source_target_pairs={{0,4},{4,0},{8,12},{12,8},{16,20},{20,16},{24,28},{28,24},{1,5},{5... | collective-permute-start | bytes 540680 | tf_op jit(solution)/shard_map/ppermute | solution.py:321
  16.5 4.9 %collective-permute-start.6 = (bf16[128,704]{1,0:T(8,128)(2,1)S(1)}, bf16[128,704]{1,0:T(8,128)(2,1)S(1)}, u32[]{:S(2)}, u32[]{:S(2)}) collective-permute-start(bf16[128,704]{1,0:T(8,128)(2,1)S(1)} %collective-permute-done.2.refs_2_.refs_4_.refs_8_), channel_id=1, source_target_pairs={{0,4},{4,0},{8,12},{12,8},{16,20},{20,16},{24,28},{28,24},{1,5},{5... | collective-permute-start | bytes 540680 | tf_op jit(solution)/shard_map/ppermute | solution.py:321
  17.0 14.2 %collective-permute-start.10 = (bf16[560,128]{1,0:T(8,128)(2,1)S(1)}, bf16[560,128]{1,0:T(8,128)(2,1)S(1)}, u32[]{:S(2)}, u32[]{:S(2)}) collective-permute-start(bf16[560,128]{1,0:T(8,128)(2,1)S(1)} %get-tuple-element.47), channel_id=1, source_target_pairs={{0,1},{1,0},{2,3},{3,2},{4,5},{5,4},{6,7},{7,6},{8,9},{9,8},{10,11... | collective-permute-start | bytes 430088 | tf_op jit(solution)/shard_map/ppermute | solution.py:321
  18.6 13.7 %collective-permute-start.11 = (bf16[560,128]{1,0:T(8,128)(2,1)S(1)}, bf16[560,128]{1,0:T(8,128)(2,1)S(1)}, u32[]{:S(2)}, u32[]{:S(2)}) collective-permute-start(bf16[560,128]{1,0:T(8,128)(2,1)S(1)} %get-tuple-element.48), channel_id=1, source_target_pairs={{0,2},{1,3},{2,0},{3,1},{4,6},{5,7},{6,4},{7,5},{8,10},{9,11},{10,... | collective-permute-start | bytes 430088 | tf_op jit(solution)/shard_map/ppermute | solution.py:321
  21.2 11.1 %collective-permute-start.12 = (bf16[560,128]{1,0:T(8,128)(2,1)S(1)}, bf16[560,128]{1,0:T(8,128)(2,1)S(1)}, u32[]{:S(2)}, u32[]{:S(2)}) collective-permute-start(bf16[560,128]{1,0:T(8,128)(2,1)S(1)} %get-tuple-element.49), channel_id=1, source_target_pairs={{0,3},{1,2},{2,1},{3,0},{4,7},{5,6},{6,5},{7,4},{8,11},{9,10},{10,... | collective-permute-start | bytes 430088 | tf_op jit(solution)/shard_map/ppermute | solution.py:321
  21.4 3.6 %collective-permute-start.4 = (bf16[128,704]{1,0:T(8,128)(2,1)S(1)}, bf16[128,704]{1,0:T(8,128)(2,1)S(1)}, u32[]{:S(2)}, u32[]{:S(2)}) collective-permute-start(bf16[128,704]{1,0:T(8,128)(2,1)S(1)} %collective-permute-done.3.refs_0_.refs_6_.refs_10_), channel_id=1, source_target_pairs={{0,4},{4,0},{8,12},{12,8},{16,20},{20,16},{24,28},{28,24},{1,5},{5... | collective-permute-start | bytes 540680 | tf_op jit(solution)/shard_map/ppermute | solution.py:321
  27.0 7.2 %collective-permute-start.7 = (bf16[32,1024]{1,0:T(8,128)(2,1)S(1)}, bf16[32,1024]{1,0:T(8,128)(2,1)S(1)}, u32[]{:S(2)}, u32[]{:S(2)}) collective-permute-start(bf16[32,1024]{1,0:T(8,128)(2,1)S(1)} %get-tuple-element.42), channel_id=1, source_target_pairs={{0,1},{1,0},{2,3},{3,2},{4,5},{5,4},{6,7},{7,6},{8,9},{9,8},{10,11... | collective-permute-start | bytes 196616 | tf_op jit(solution)/shard_map/ppermute | solution.py:321
  27.7 11.3 %collective-permute-start.8 = (bf16[32,1024]{1,0:T(8,128)(2,1)S(1)}, bf16[32,1024]{1,0:T(8,128)(2,1)S(1)}, u32[]{:S(2)}, u32[]{:S(2)}) collective-permute-start(bf16[32,1024]{1,0:T(8,128)(2,1)S(1)} %get-tuple-element.43), channel_id=1, source_target_pairs={{0,2},{1,3},{2,0},{3,1},{4,6},{5,7},{6,4},{7,5},{8,10},{9,11},{10,... | collective-permute-start | bytes 196616 | tf_op jit(solution)/shard_map/ppermute | solution.py:321
  31.2 7.8 %collective-permute-start.9 = (bf16[32,1024]{1,0:T(8,128)(2,1)S(1)}, bf16[32,1024]{1,0:T(8,128)(2,1)S(1)}, u32[]{:S(2)}, u32[]{:S(2)}) collective-permute-start(bf16[32,1024]{1,0:T(8,128)(2,1)S(1)} %get-tuple-element.44), channel_id=1, source_target_pairs={{0,3},{1,2},{2,1},{3,0},{4,7},{5,6},{6,5},{7,4},{8,11},{9,10},{10,... | collective-permute-start | bytes 196616 | tf_op jit(solution)/shard_map/ppermute | solution.py:321
  43.1 4.5 %collective-permute-start.16 = (f32[512,128]{1,0:T(8,128)S(1)}, f32[512,128]{1,0:T(8,128)S(1)}, u32[]{:S(2)}, u32[]{:S(2)}) collective-permute-start(f32[512,128]{1,0:T(8,128)S(1)} %get-tuple-element.59), channel_id=1, source_target_pairs={{0,4},{4,0},{8,12},{12,8},{16,20},{20,16},{24,28},{28,24},{1,5},{5... | collective-permute-start | bytes 786440 | tf_op jit(solution)/shard_map/ppermute | solution.py:321
  43.1 15.9 %collective-permute-start.13 = (bf16[544,128]{1,0:T(8,128)(2,1)S(1)}, bf16[544,128]{1,0:T(8,128)(2,1)S(1)}, u32[]{:S(2)}, u32[]{:S(2)}) collective-permute-start(bf16[544,128]{1,0:T(8,128)(2,1)S(1)} %get-tuple-element.54), channel_id=1, source_target_pairs={{0,1},{1,0},{2,3},{3,2},{4,5},{5,4},{6,7},{7,6},{8,9},{9,8},{10,11... | collective-permute-start | bytes 417800 | tf_op jit(solution)/shard_map/ppermute | solution.py:321
  44.9 16.1 %collective-permute-start.14 = (bf16[544,128]{1,0:T(8,128)(2,1)S(1)}, bf16[544,128]{1,0:T(8,128)(2,1)S(1)}, u32[]{:S(2)}, u32[]{:S(2)}) collective-permute-start(bf16[544,128]{1,0:T(8,128)(2,1)S(1)} %get-tuple-element.55), channel_id=1, source_target_pairs={{0,2},{1,3},{2,0},{3,1},{4,6},{5,7},{6,4},{7,5},{8,10},{9,11},{10,... | collective-permute-start | bytes 417800 | tf_op jit(solution)/shard_map/ppermute | solution.py:321
  46.2 14.7 %collective-permute-start.15 = (bf16[544,128]{1,0:T(8,128)(2,1)S(1)}, bf16[544,128]{1,0:T(8,128)(2,1)S(1)}, u32[]{:S(2)}, u32[]{:S(2)}) collective-permute-start(bf16[544,128]{1,0:T(8,128)(2,1)S(1)} %get-tuple-element.56), channel_id=1, source_target_pairs={{0,3},{1,2},{2,1},{3,0},{4,7},{5,6},{6,5},{7,4},{8,11},{9,10},{10,... | collective-permute-start | bytes 417800 | tf_op jit(solution)/shard_map/ppermute | solution.py:321
  47.6 4.0 %collective-permute-start.17 = (bf16[128,128]{1,0:T(8,128)(2,1)S(1)}, bf16[128,128]{1,0:T(8,128)(2,1)S(1)}, u32[]{:S(2)}, u32[]{:S(2)}) collective-permute-start(bf16[128,128]{1,0:T(8,128)(2,1)S(1)} %get-tuple-element.61), channel_id=1, source_target_pairs={{0,8},{4,12},{8,0},{12,4},{16,24},{20,28},{24,16},{28,20},{1,9},{5... | collective-permute-start | bytes 98312 | tf_op jit(solution)/shard_map/ppermute | solution.py:321
  49.2 4.1 %collective-permute-start.18 = (bf16[128,128]{1,0:T(8,128)(2,1)S(1)}, bf16[128,128]{1,0:T(8,128)(2,1)S(1)}, u32[]{:S(2)}, u32[]{:S(2)}) collective-permute-start(bf16[128,128]{1,0:T(8,128)(2,1)S(1)} %get-tuple-element.62), channel_id=1, source_target_pairs={{0,16},{4,20},{8,24},{12,28},{16,0},{20,4},{24,8},{28,12},{1,17},{... | collective-permute-start | bytes 98312 | tf_op jit(solution)/shard_map/ppermute | solution.py:321
  51.6 4.8 %collective-permute-start.19 = (bf16[128,128]{1,0:T(8,128)(2,1)S(1)}, bf16[128,128]{1,0:T(8,128)(2,1)S(1)}, u32[]{:S(2)}, u32[]{:S(2)}) collective-permute-start(bf16[128,128]{1,0:T(8,128)(2,1)S(1)} %get-tuple-element.63), channel_id=1, source_target_pairs={{0,24},{4,28},{8,16},{12,20},{16,8},{20,12},{24,0},{28,4},{1,25},{... | collective-permute-start | bytes 98312 | tf_op jit(solution)/shard_map/ppermute | solution.py:321
  56.5 5.9 %collective-permute-start.22 = (bf16[128,128]{1,0:T(8,128)(2,1)S(1)}, bf16[128,128]{1,0:T(8,128)(2,1)S(1)}, u32[]{:S(2)}, u32[]{:S(2)}) collective-permute-start(bf16[128,128]{1,0:T(8,128)(2,1)S(1)} %shard_map.103.refs_0_), channel_id=1, source_target_pairs={{0,3},{1,2},{2,1},{3,0},{4,7},{5,6},{6,5},{7,4},{8,11},{9,10},{10,... | collective-permute-start | bytes 98312 | tf_op jit(solution)/shard_map/ppermute | solution.py:321
  59.0 4.8 %collective-permute-start.21 = (bf16[128,128]{1,0:T(8,128)(2,1)S(1)}, bf16[128,128]{1,0:T(8,128)(2,1)S(1)}, u32[]{:S(2)}, u32[]{:S(2)}) collective-permute-start(bf16[128,128]{1,0:T(8,128)(2,1)S(1)} %shard_map.103.refs_0_), channel_id=1, source_target_pairs={{0,2},{1,3},{2,0},{3,1},{4,6},{5,7},{6,4},{7,5},{8,10},{9,11},{10,... | collective-permute-start | bytes 98312 | tf_op jit(solution)/shard_map/ppermute | solution.py:321
  59.0 4.8 %collective-permute-start.20 = (bf16[128,128]{1,0:T(8,128)(2,1)S(1)}, bf16[128,128]{1,0:T(8,128)(2,1)S(1)}, u32[]{:S(2)}, u32[]{:S(2)}) collective-permute-start(bf16[128,128]{1,0:T(8,128)(2,1)S(1)} %shard_map.103.refs_0_), channel_id=1, source_target_pairs={{0,1},{1,0},{2,3},{3,2},{4,5},{5,4},{6,7},{7,6},{8,9},{9,8},{10,11... | collective-permute-start | bytes 98312 | tf_op jit(solution)/shard_map/ppermute | solution.py:321
  (9 other events, 35.0 us)

commit v5 on v4

--- a/solution.py
+++ b/solution.py
@@ -15,8 +15,8 @@
 f32, bf16 = jnp.float32, jnp.bfloat16
 
 
-def params():
-    return pltpu.CompilerParams(vmem_limit_bytes=24 * 1024 * 1024)
+def params(mega=24):
+    return pltpu.CompilerParams(vmem_limit_bytes=mega * 1024 * 1024)
 
 
 def whole(value):
@@ -24,7 +24,7 @@
     return pl.BlockSpec(value.shape, lambda *_: zeros)
 
 
-def call(kernel, outs, values, scratch=(), specs=None, cost=None):
+def call(kernel, outs, values, scratch=(), specs=None, cost=None, mega=24):
     many = isinstance(outs, list)
     found = pl.pallas_call(
         kernel,
@@ -33,7 +33,7 @@
         in_specs=specs or [whole(v) for v in values],
         out_specs=[whole(o) for o in outs] if many else whole(outs),
         scratch_shapes=list(scratch),
-        compiler_params=params(),
+        compiler_params=params(mega),
         cost_estimate=cost,
     )(*values)
     return list(found) if many else found
@@ -54,13 +54,10 @@
     return found
 
 
-def pack_kernel(latent_ref, key_ref, packed_ref):
+def pack_kernel(latent_ref, key_ref, query_ref, weight_ref, packed_ref, *outs):
     width = key_ref.shape[1]
     packed_ref[:, :width] = key_ref[...]
     packed_ref[:, width:] = latent_ref[...].T
-
-
-def ask_kernel(query_ref, weight_ref, *outs):
     me = lax.axis_index("ha")
     heads = weight_ref.shape[0]
     rows = outs[0].shape[0] - 3 * TAIL
@@ -266,17 +263,15 @@
         odd_ref[at, :] = key_total[(2 * i + 1) * rows : (2 * i + 2) * rows, :]
 
 
-def pair_kernel(mine_ref, other_ref, own_ref, *outs):
-    rows = own_ref.shape[0]
-    own_ref[...] = mine_ref[:rows, :] + other_ref[:rows, :]
-    for i, out in enumerate(outs):
-        at = slice((i + 1) * rows, (i + 2) * rows)
-        out[...] = (mine_ref[at, :] + other_ref[at, :]).astype(out.dtype)
-
-
-def sum_kernel(*refs):
-    out_ref = refs[-1]
-    out_ref[...] = tree([ref[...].astype(f32) for ref in refs[:-1]]).astype(out_ref.dtype)
+def halve_kernel(*refs):
+    mine_ref, other_ref, keep_ref = refs[:3]
+    rows = LANES
+    for i in range(mine_ref.shape[0] // rows):
+        at = slice(i * rows, (i + 1) * rows)
+        value = mine_ref[at, :].astype(f32) + other_ref[at, :].astype(f32)
+        out = refs[3] if i % 2 else keep_ref
+        to = slice(i // 2 * rows, (i // 2 + 1) * rows)
+        out[to, :] = value.astype(out.dtype)
 
 
 def finish_kernel(share, heads, *refs):
@@ -323,27 +318,24 @@
     start_row = window_start.reshape(1, rows)
     key_only = pl.BlockSpec((rows, index_width), lambda *_: (0, 0))
 
-    packed = call(
+    packed, *asked = call(
         pack_kernel,
-        shape((rows, index_width + width), bf16),
-        (latent.T, index_key),
-        cost=pl.CostEstimate(flops=0, bytes_accessed=1 << 24, transcendentals=0),
-    )
-    asked = call(
-        ask_kernel,
-        [shape((own + 3 * TAIL, index_width), bf16)] * parts,
-        (index_query.reshape(rows * heads, index_width), index_weight.T),
+        [shape((rows, index_width + width), bf16)]
+        + [shape((own + 3 * TAIL, index_width), bf16)] * parts,
+        (latent.T, index_key, index_query.reshape(rows * heads, index_width), index_weight.T),
+        mega=64,
     )
     queries = jnp.transpose(main_query, (1, 2, 0))
     sums = log_sums.T
-    held = [None] * blocks
-    held[0] = packed
+    held = [packed] + [None] * (blocks - 1)
     held[1] = swap(packed, "pb", 1)
     for k in range(2, blocks, 2):
         held[k] = swap(packed, "pb", k)
-    ready = lax.optimization_barrier((asked[0], held[1]))
-    asked = [ready[0]] + [swap(asked[r], "ha", r) for r in range(1, parts)]
-    held[1] = ready[1]
+    asked[2] = swap(asked[2], "ha", 2)
+    held[1], asked[1] = lax.optimization_barrier((held[1], asked[1]))
+    asked[1] = swap(asked[1], "ha", 1)
+    held[1], asked[1], asked[2:] = lax.optimization_barrier((held[1], asked[1], asked[2:]))
+    asked[3:] = [swap(asked[r], "ha", r) for r in range(3, parts)]
 
     chunks = [[0, 1]] + [list(range(k, min(k + 4, blocks))) for k in range(2, blocks, 4)]
     mass = []
@@ -427,12 +419,16 @@
         ),
     )
     odd = swap(odd, "pb", 1)
-    term = shape((rows, index_width), f32)
-    half = shape((rows, index_width), bf16)
-    mine, *others = call(pair_kernel, [term] + [half] * (blocks // 2 - 1), (even, odd))
-    others = [swap(value, "pb", 2 * (i + 1)) for i, value in enumerate(others)]
-    mine = call(sum_kernel, half, [mine] + others)
-    key_grad = call(sum_kernel, half, [mine] + [swap(mine, "ha", r) for r in range(1, parts)])
+    mine, other, rel = even, odd, 2
+    while mine.shape[0] > rows:
+        half = (mine.shape[0] // 2, index_width)
+        mine, other = call(halve_kernel, [shape(half, f32), shape(half, bf16)], (mine, other))
+        other = swap(other, "pb", rel)
+        rel *= 2
+    for r in [1 << i for i in range(parts.bit_length() - 1)]:
+        mine = call(halve_kernel, shape((rows, index_width), bf16), (mine, other))
+        other = swap(mine, "ha", r)
+    key_grad = call(halve_kernel, shape((rows, index_width), bf16), (mine, other))
 
     answers = [answers[0]] + [swap(answers[r], "ha", r) for r in range(1, parts)]
     query_grad, weight_grad = call(

time: 64.8 us -> 66.4 us (1.025)
  waiting for transfers between devices: 14.5 us -> 17.3 us
  local copies, waits for them, and re-layouts: 7.12 us -> 4.65 us
  Pallas kernels: 15.1 us -> 16.9 us
    ppermute x23 -> x21, waiting for transfers between devices: 14.5 us -> 17.3 us  [swap(): return lax.ppermute(value, axis, [(i, i ^ rel) for i in range(size)])]
    unnamed x20 -> x14, local copies, waits for them, and re-layouts: 7.12 us -> 4.65 us
    pallas_call x11 -> x12, Pallas kernels: 15.1 us -> 16.9 us  [call(): pl.pallas_call(kernel, grid=(1,), out_shape=outs, in_specs=specs or [whol...]
    ppermute x23 -> x21, starting transfers between devices: 26.9 us -> 26.5 us  [swap(): return lax.ppermute(value, axis, [(i, i ^ rel) for i in range(size)])]
  transfers between devices with their start and end apart: 23 -> 21, of which waited for: 8 -> 8; matrix products, arithmetic and copies ran while one was open for 0% -> 0% of each run, Pallas kernels for 16% -> 15%
where the time goes in v5:
time: 66.4 us; the launch traced here: 66.1 us
  starting transfers between devices  26.5 us (40%)
  waiting for transfers between devices  17.3 us (26%)
  Pallas kernels  16.9 us (25%)
  local copies, waits for them, and re-layouts  4.65 us (7%)
  between operations  0.78 us (1%)
    ppermute x21, starting transfers between devices, swap(): return lax.ppermute(value, axis, [(i, i ^ rel) for i in range(size)])  26.5 us
    ppermute x21, waiting for transfers between devices, swap(): return lax.ppermute(value, axis, [(i, i ^ rel) for i in range(size)])  17.3 us
    pallas_call x12, Pallas kernels, call(): pl.pallas_call(kernel, grid=(1,), out_shape=outs, in_specs=specs or [whol...  16.9 us
    unnamed x14, local copies, waits for them, and re-layouts  4.65 us
  transfers between devices with their start and end apart: 21, of which 8 were waited for; matrix products, arithmetic and copies ran while one was open for 0% of the time, Pallas kernels for 15%

profile of v5, /device:TPU:0, one launch (start us, length us, event | category | flops | bytes accessed | tf_op | source)
XLA Modules:
  0.0 66.1 jit_solution(17375324629443188522)
XLA Ops:
  0.6 2.0 %shard_map.94 = (bf16[128,704]{1,0:T(8,128)(2,1)}, bf16[560,128]{1,0:T(8,128)(2,1)}, bf16[560,128]{1,0:T(8,128)(2,1)}, bf16[560,128]{1,0:T(8,128)(2,1)}, bf16[560,128]{1,0:T(8,128)(2,1)}) custom-call(bf16[576,128]{1,0:T(8,128)(2,1)} %bitcast.19, bf16[128,128]{1,0:T(8,128)(2,1)} %key_ref.1, bf16[2048,128]{1,0:T(8,128)(2,1)} %bitcast.18, f32[16,128]{1,0:T(8,128)} %bitcast.20), custom_call_target="tpu_custom_call" | custom-call | tf_op jit(solution)/shard_map/pallas_call | solution.py:29
  3.1 3.6 %collective-permute-start.2 = (bf16[560,128]{1,0:T(8,128)(2,1)}, bf16[560,128]{1,0:T(8,128)(2,1)S(1)}, u32[]{:S(2)}, u32[]{:S(2)}) collective-permute-start(bf16[560,128]{1,0:T(8,128)(2,1)} %get-tuple-element.43), channel_id=1, source_target_pairs={{0,2},{1,3},{2,0},{3,1},{4,6},{5,7},{6,4},{7,5},{8,10},{9,11},{10,... | collective-permute-start | bytes 430088 | tf_op jit(solution)/shard_map/ppermute | solution.py:316
  6.8 1.6 %collective-permute-start.1 = (bf16[560,128]{1,0:T(8,128)(2,1)}, bf16[560,128]{1,0:T(8,128)(2,1)S(1)}, u32[]{:S(2)}, u32[]{:S(2)}) collective-permute-start(bf16[560,128]{1,0:T(8,128)(2,1)} %get-tuple-element.42), channel_id=1, source_target_pairs={{0,1},{1,0},{2,3},{3,2},{4,5},{5,4},{6,7},{7,6},{8,9},{9,8},{10,11... | collective-permute-start | bytes 430088 | tf_op jit(solution)/shard_map/ppermute | solution.py:316
  8.3 2.4 %collective-permute-start.5 = (bf16[128,704]{1,0:T(8,128)(2,1)}, bf16[128,704]{1,0:T(8,128)(2,1)S(1)}, u32[]{:S(2)}, u32[]{:S(2)}) collective-permute-start(bf16[128,704]{1,0:T(8,128)(2,1)} %get-tuple-element.55.refs_0_.refs_4_), channel_id=1, source_target_pairs={{0,24},{4,28},{8,16},{12,20},{16,8},{20,12},{24,0},{28,4},{1,25},{... | collective-permute-start | bytes 540680 | tf_op jit(solution)/shard_map/ppermute | solution.py:316
  11.8 2.7 %collective-permute-done.2.refs_10_ = bf16[560,128]{1,0:T(8,128)(2,1)S(1)} collective-permute-done((bf16[560,128]{1,0:T(8,128)(2,1)}, bf16[560,128]{1,0:T(8,128)(2,1)S(1)}, u32[]{:S(2)}, u32[]{:S(2)}) %collective-permute-start.2) | collective-permute-done | bytes 143392 | tf_op jit(solution)/shard_map/ppermute | solution.py:316
  14.7 2.3 %copy-done = bf16[128,32,576]{0,2,1:T(8,128)(2,1)S(1)} copy-done((bf16[128,32,576]{0,2,1:T(8,128)(2,1)S(1)}, bf16[128,32,576]{0,2,1:T(8,128)(2,1)}, u32[]{:S(2)}) %copy-start) | copy-done | bytes 4718616
  19.4 1.9 %shard_map.95.refs_5_ = bf16[128,256]{1,0:T(8,128)(2,1)S(1)} custom-call(bf16[128,704]{1,0:T(8,128)(2,1)S(1)} %copy-done.2, bf16[128,704]{1,0:T(8,128)(2,1)S(1)} %collective-permute-done.refs_1_.refs_5_, bf16[32,576,128]{2,1,0:T(8,128)(2,1)S(1)} %bitcast.8, f32[32,128]{1,0:T(8,128)S(1)} %bitcast.11, s32[1,128]{1,0:T(1,128)S(1)} %bitcast.14), custom_call_target="tpu_custom_call" | custom-call | flops 1207959552 | bytes 4718592 | tf_op jit(solution)/shard_map/pallas_call | solution.py:29
  21.9 3.7 %collective-permute-start.12 = (bf16[560,128]{1,0:T(8,128)(2,1)S(1)}, bf16[560,128]{1,0:T(8,128)(2,1)S(1)}, u32[]{:S(2)}, u32[]{:S(2)}) collective-permute-start(bf16[560,128]{1,0:T(8,128)(2,1)S(1)} %copy-done.6), channel_id=1, source_target_pairs={{0,3},{1,2},{2,1},{3,0},{4,7},{5,6},{6,5},{7,4},{8,11},{9,10},{10,... | collective-permute-start | bytes 430088 | tf_op jit(solution)/shard_map/ppermute | solution.py:316
  25.6 3.6 %shard_map.96.refs_6_ = bf16[128,512]{1,0:T(8,128)(2,1)S(1)} custom-call(bf16[128,704]{1,0:T(8,128)(2,1)S(1)} %collective-permute-done.3.refs_0_.refs_2_.refs_6_, bf16[128,704]{1,0:T(8,128)(2,1)S(1)} %collective-permute-done.7.refs_1_.refs_3_.refs_7_, bf16[128,704]{1,0:T(8,128)(2,1)S(1)} %collective-permute-done.4.refs_2_.refs_4_.refs_8_, ...), custom_call_target="tpu_custom_call" | custom-call | flops 2415919104 | bytes 4718592 | tf_op jit(solution)/shard_map/pallas_call | solution.py:29
  29.2 1.9 %shard_map.97 = (bf16[32,1024]{1,0:T(8,128)(2,1)S(1)}, bf16[32,1024]{1,0:T(8,128)(2,1)S(1)}, bf16[32,1024]{1,0:T(8,128)(2,1)S(1)}, bf16[32,1024]{1,0:T(8,128)(2,1)S(1)}) custom-call(bf16[128,704]{1,0:T(8,128)(2,1)S(1)} %collective-permute-done.5.refs_0_.refs_6_.refs_10_, bf16[128,704]{1,0:T(8,128)(2,1)S(1)} %collective-permute-done.6.refs_1_.refs_7_.refs_11_, ...), custom_call_target="tpu_custom_call" | custom-call | flops 1207959552 | bytes 4718592 | tf_op jit(solution)/shard_map/pallas_call | solution.py:29
  31.2 1.7 %collective-permute-start.10 = (bf16[32,1024]{1,0:T(8,128)(2,1)S(1)}, bf16[32,1024]{1,0:T(8,128)(2,1)S(1)}, u32[]{:S(2)}, u32[]{:S(2)}) collective-permute-start(bf16[32,1024]{1,0:T(8,128)(2,1)S(1)} %get-tuple-element.53), channel_id=1, source_target_pairs={{0,2},{1,3},{2,0},{3,1},{4,6},{5,7},{6,4},{7,5},{8,10},{9,11},{10,... | collective-permute-start | bytes 196616 | tf_op jit(solution)/shard_map/ppermute | solution.py:316
  32.9 2.6 %collective-permute-start.11 = (bf16[32,1024]{1,0:T(8,128)(2,1)S(1)}, bf16[32,1024]{1,0:T(8,128)(2,1)S(1)}, u32[]{:S(2)}, u32[]{:S(2)}) collective-permute-start(bf16[32,1024]{1,0:T(8,128)(2,1)S(1)} %get-tuple-element.54), channel_id=1, source_target_pairs={{0,3},{1,2},{2,1},{3,0},{4,7},{5,6},{6,5},{7,4},{8,11},{9,10},{10,... | collective-permute-start | bytes 196616 | tf_op jit(solution)/shard_map/ppermute | solution.py:316
  35.6 1.9 %shard_map.98 = (f32[1024,128]{1,0:T(8,128)S(1)}, bf16[2048,128]{1,0:T(8,128)(2,1)S(1)}, f32[16,128]{1,0:T(8,128)S(1)}) custom-call(bf16[128,704]{1,0:T(8,128)(2,1)S(1)} %copy-done.2, bf16[128,704]{1,0:T(8,128)(2,1)S(1)} %collective-permute-done.refs_1_.refs_5_, bf16[128,704]{1,0:T(8,128)(2,1)S(1)} %collective-permute-done.3.refs_0_.refs_2_.refs_6_, ...), custom_call_target="tpu_custom_call" | custom-call | flops 536870912 | bytes 524288 | tf_op jit(solution)/shard_map/pallas_call | solution.py:29
  37.5 2.4 %collective-permute-done.10.refs_2_ = bf16[32,1024]{1,0:T(8,128)(2,1)S(1)} collective-permute-done((bf16[32,1024]{1,0:T(8,128)(2,1)S(1)}, bf16[32,1024]{1,0:T(8,128)(2,1)S(1)}, u32[]{:S(2)}, u32[]{:S(2)}) %collective-permute-start.10) | collective-permute-done | bytes 65568 | tf_op jit(solution)/shard_map/ppermute | solution.py:316
  39.9 4.0 %shard_map.99 = (f32[512,128]{1,0:T(8,128)S(1)}, f32[512,128]{1,0:T(8,128)S(1)}, bf16[544,128]{1,0:T(8,128)(2,1)S(1)}, bf16[544,128]{1,0:T(8,128)(2,1)S(1)}, bf1...) custom-call(bf16[32,1024]{1,0:T(8,128)(2,1)S(1)} %get-tuple-element.51.refs_0_, ...), custom_call_target="tpu_custom_call" | custom-call | flops 1610612736 | bytes 524288 | tf_op jit(solution)/shard_map/pallas_call | solution.py:29
  44.0 1.5 %collective-permute-done.16.refs_1_ = f32[512,128]{1,0:T(8,128)S(1)} collective-permute-done((f32[512,128]{1,0:T(8,128)S(1)}, f32[512,128]{1,0:T(8,128)S(1)}, u32[]{:S(2)}, u32[]{:S(2)}) %collective-permute-start.16) | collective-permute-done | bytes 262176 | tf_op jit(solution)/shard_map/ppermute | solution.py:316
  45.5 1.6 %collective-permute-start.17 = (bf16[256,128]{1,0:T(8,128)(2,1)S(1)}, bf16[256,128]{1,0:T(8,128)(2,1)S(1)}, u32[]{:S(2)}, u32[]{:S(2)}) collective-permute-start(bf16[256,128]{1,0:T(8,128)(2,1)S(1)} %get-tuple-element.71), channel_id=1, source_target_pairs={{0,8},{4,12},{8,0},{12,4},{16,24},{20,28},{24,16},{28,20},{1,9},{5... | collective-permute-start | bytes 196616 | tf_op jit(solution)/shard_map/ppermute | solution.py:316
  47.1 1.6 %collective-permute-start.13 = (bf16[544,128]{1,0:T(8,128)(2,1)S(1)}, bf16[544,128]{1,0:T(8,128)(2,1)S(1)}, u32[]{:S(2)}, u32[]{:S(2)}) collective-permute-start(bf16[544,128]{1,0:T(8,128)(2,1)S(1)} %get-tuple-element.64), channel_id=1, source_target_pairs={{0,1},{1,0},{2,3},{3,2},{4,5},{5,4},{6,7},{7,6},{8,9},{9,8},{10,11... | collective-permute-start | bytes 417800 | tf_op jit(solution)/shard_map/ppermute | solution.py:316
  49.4 2.0 %collective-permute-start.15 = (bf16[544,128]{1,0:T(8,128)(2,1)S(1)}, bf16[544,128]{1,0:T(8,128)(2,1)S(1)}, u32[]{:S(2)}, u32[]{:S(2)}) collective-permute-start(bf16[544,128]{1,0:T(8,128)(2,1)S(1)} %get-tuple-element.66), channel_id=1, source_target_pairs={{0,3},{1,2},{2,1},{3,0},{4,7},{5,6},{6,5},{7,4},{8,11},{9,10},{10,... | collective-permute-start | bytes 417800 | tf_op jit(solution)/shard_map/ppermute | solution.py:316
  51.5 1.6 %collective-permute-start.18 = (bf16[128,128]{1,0:T(8,128)(2,1)S(1)}, bf16[128,128]{1,0:T(8,128)(2,1)S(1)}, u32[]{:S(2)}, u32[]{:S(2)}) collective-permute-start(bf16[128,128]{1,0:T(8,128)(2,1)S(1)} %get-tuple-element.73), channel_id=1, source_target_pairs={{0,16},{4,20},{8,24},{12,28},{16,0},{20,4},{24,8},{28,12},{1,17},{... | collective-permute-start | bytes 98312 | tf_op jit(solution)/shard_map/ppermute | solution.py:316
  53.1 2.4 %collective-permute-done.18.refs_1_ = bf16[128,128]{1,0:T(8,128)(2,1)S(1)} collective-permute-done((bf16[128,128]{1,0:T(8,128)(2,1)S(1)}, bf16[128,128]{1,0:T(8,128)(2,1)S(1)}, u32[]{:S(2)}, u32[]{:S(2)}) %collective-permute-start.18) | collective-permute-done | bytes 32800 | tf_op jit(solution)/shard_map/ppermute | solution.py:316
  56.2 4.2 %collective-permute-done.19.refs_1_ = bf16[128,128]{1,0:T(8,128)(2,1)S(1)} collective-permute-done((bf16[128,128]{1,0:T(8,128)(2,1)S(1)}, bf16[128,128]{1,0:T(8,128)(2,1)S(1)}, u32[]{:S(2)}, u32[]{:S(2)}) %collective-permute-start.19) | collective-permute-done | bytes 32800 | tf_op jit(solution)/shard_map/ppermute | solution.py:316
  60.8 0.9 %collective-permute-done.14.refs_2_ = bf16[544,128]{1,0:T(8,128)(2,1)S(1)} collective-permute-done((bf16[544,128]{1,0:T(8,128)(2,1)S(1)}, bf16[544,128]{1,0:T(8,128)(2,1)S(1)}, u32[]{:S(2)}, u32[]{:S(2)}) %collective-permute-start.14) | collective-permute-done | bytes 139296 | tf_op jit(solution)/shard_map/ppermute | solution.py:316
  62.6 2.9 %collective-permute-done.20.refs_1_ = bf16[128,128]{1,0:T(8,128)(2,1)S(1)} collective-permute-done((bf16[128,128]{1,0:T(8,128)(2,1)S(1)}, bf16[128,128]{1,0:T(8,128)(2,1)S(1)}, u32[]{:S(2)}, u32[]{:S(2)}) %collective-permute-start.20) | collective-permute-done | bytes 32800 | tf_op jit(solution)/shard_map/ppermute | solution.py:316
  (44 shorter events, 8.1 us)
Async XLA Ops:
  2.7 4.1 %collective-permute-start = (bf16[128,704]{1,0:T(8,128)(2,1)}, bf16[128,704]{1,0:T(8,128)(2,1)S(1)}, u32[]{:S(2)}, u32[]{:S(2)}) collective-permute-start(bf16[128,704]{1,0:T(8,128)(2,1)} %get-tuple-element.55.refs_0_.refs_4_), channel_id=1, source_target_pairs={{0,4},{4,0},{8,12},{12,8},{16,20},{20,16},{24,28},{28,24},{1,5},{5... | collective-permute-start | bytes 540680 | tf_op jit(solution)/shard_map/ppermute | solution.py:316
  3.1 11.4 %collective-permute-start.2 = (bf16[560,128]{1,0:T(8,128)(2,1)}, bf16[560,128]{1,0:T(8,128)(2,1)S(1)}, u32[]{:S(2)}, u32[]{:S(2)}) collective-permute-start(bf16[560,128]{1,0:T(8,128)(2,1)} %get-tuple-element.43), channel_id=1, source_target_pairs={{0,2},{1,3},{2,0},{3,1},{4,6},{5,7},{6,4},{7,5},{8,10},{9,11},{10,... | collective-permute-start | bytes 430088 | tf_op jit(solution)/shard_map/ppermute | solution.py:316
  6.8 7.9 %collective-permute-start.1 = (bf16[560,128]{1,0:T(8,128)(2,1)}, bf16[560,128]{1,0:T(8,128)(2,1)S(1)}, u32[]{:S(2)}, u32[]{:S(2)}) collective-permute-start(bf16[560,128]{1,0:T(8,128)(2,1)} %get-tuple-element.42), channel_id=1, source_target_pairs={{0,1},{1,0},{2,3},{3,2},{4,5},{5,4},{6,7},{7,6},{8,9},{9,8},{10,11... | collective-permute-start | bytes 430088 | tf_op jit(solution)/shard_map/ppermute | solution.py:316
  8.3 12.9 %collective-permute-start.5 = (bf16[128,704]{1,0:T(8,128)(2,1)}, bf16[128,704]{1,0:T(8,128)(2,1)S(1)}, u32[]{:S(2)}, u32[]{:S(2)}) collective-permute-start(bf16[128,704]{1,0:T(8,128)(2,1)} %get-tuple-element.55.refs_0_.refs_4_), channel_id=1, source_target_pairs={{0,24},{4,28},{8,16},{12,20},{16,8},{20,12},{24,0},{28,4},{1,25},{... | collective-permute-start | bytes 540680 | tf_op jit(solution)/shard_map/ppermute | solution.py:316
  10.8 10.5 %collective-permute-start.4 = (bf16[128,704]{1,0:T(8,128)(2,1)}, bf16[128,704]{1,0:T(8,128)(2,1)S(1)}, u32[]{:S(2)}, u32[]{:S(2)}) collective-permute-start(bf16[128,704]{1,0:T(8,128)(2,1)} %get-tuple-element.55.refs_0_.refs_4_), channel_id=1, source_target_pairs={{0,16},{4,20},{8,24},{12,28},{16,0},{20,4},{24,8},{28,12},{1,17},{... | collective-permute-start | bytes 540680 | tf_op jit(solution)/shard_map/ppermute | solution.py:316
  11.3 10.0 %collective-permute-start.3 = (bf16[128,704]{1,0:T(8,128)(2,1)}, bf16[128,704]{1,0:T(8,128)(2,1)S(1)}, u32[]{:S(2)}, u32[]{:S(2)}) collective-permute-start(bf16[128,704]{1,0:T(8,128)(2,1)} %get-tuple-element.55.refs_0_.refs_4_), channel_id=1, source_target_pairs={{0,8},{4,12},{8,0},{12,4},{16,24},{20,28},{24,16},{28,20},{1,9},{5... | collective-permute-start | bytes 540680 | tf_op jit(solution)/shard_map/ppermute | solution.py:316
  19.4 2.5 %copy-start.6 = (bf16[560,128]{1,0:T(8,128)(2,1)S(1)}, bf16[560,128]{1,0:T(8,128)(2,1)}, u32[]{:S(2)}) copy-start(bf16[560,128]{1,0:T(8,128)(2,1)} %get-tuple-element.59) | copy-start | bytes 430084
  19.4 6.2 %copy-start.1 = (bf16[128,32,576]{0,2,1:T(8,128)(2,1)S(1)}, bf16[128,32,576]{0,2,1:T(8,128)(2,1)}, u32[]{:S(2)}) copy-start(bf16[128,32,576]{0,2,1:T(8,128)(2,1)} %param.7) | copy-start | bytes 14155780
  21.3 4.3 %collective-permute-start.7 = (bf16[128,704]{1,0:T(8,128)(2,1)S(1)}, bf16[128,704]{1,0:T(8,128)(2,1)S(1)}, u32[]{:S(2)}, u32[]{:S(2)}) collective-permute-start(bf16[128,704]{1,0:T(8,128)(2,1)S(1)} %collective-permute-done.3.refs_0_.refs_2_.refs_6_), channel_id=1, source_target_pairs={{0,4},{4,0},{8,12},{12,8},{16,20},{20,16},{24,28},{28,24},{1,5},{5... | collective-permute-start | bytes 540680 | tf_op jit(solution)/shard_map/ppermute | solution.py:316
  21.4 4.2 %collective-permute-start.8 = (bf16[128,704]{1,0:T(8,128)(2,1)S(1)}, bf16[128,704]{1,0:T(8,128)(2,1)S(1)}, u32[]{:S(2)}, u32[]{:S(2)}) collective-permute-start(bf16[128,704]{1,0:T(8,128)(2,1)S(1)} %collective-permute-done.4.refs_2_.refs_4_.refs_8_), channel_id=1, source_target_pairs={{0,4},{4,0},{8,12},{12,8},{16,20},{20,16},{24,28},{28,24},{1,5},{5... | collective-permute-start | bytes 540680 | tf_op jit(solution)/shard_map/ppermute | solution.py:316
  21.9 13.7 %collective-permute-start.12 = (bf16[560,128]{1,0:T(8,128)(2,1)S(1)}, bf16[560,128]{1,0:T(8,128)(2,1)S(1)}, u32[]{:S(2)}, u32[]{:S(2)}) collective-permute-start(bf16[560,128]{1,0:T(8,128)(2,1)S(1)} %copy-done.6), channel_id=1, source_target_pairs={{0,3},{1,2},{2,1},{3,0},{4,7},{5,6},{6,5},{7,4},{8,11},{9,10},{10,... | collective-permute-start | bytes 430088 | tf_op jit(solution)/shard_map/ppermute | solution.py:316
  25.6 3.6 %collective-permute-start.6 = (bf16[128,704]{1,0:T(8,128)(2,1)S(1)}, bf16[128,704]{1,0:T(8,128)(2,1)S(1)}, u32[]{:S(2)}, u32[]{:S(2)}) collective-permute-start(bf16[128,704]{1,0:T(8,128)(2,1)S(1)} %collective-permute-done.5.refs_0_.refs_6_.refs_10_), channel_id=1, source_target_pairs={{0,4},{4,0},{8,12},{12,8},{16,20},{20,16},{24,28},{28,24},{1,5},{5... | collective-permute-start | bytes 540680 | tf_op jit(solution)/shard_map/ppermute | solution.py:316
  29.2 6.4 %copy-start.3 = (bf16[560,128]{1,0:T(8,128)(2,1)S(1)}, bf16[560,128]{1,0:T(8,128)(2,1)}, u32[]{:S(2)}) copy-start(bf16[560,128]{1,0:T(8,128)(2,1)} %get-tuple-element.56.refs_8_) | copy-start | bytes 430084
  31.1 6.4 %collective-permute-start.9 = (bf16[32,1024]{1,0:T(8,128)(2,1)S(1)}, bf16[32,1024]{1,0:T(8,128)(2,1)S(1)}, u32[]{:S(2)}, u32[]{:S(2)}) collective-permute-start(bf16[32,1024]{1,0:T(8,128)(2,1)S(1)} %get-tuple-element.52), channel_id=1, source_target_pairs={{0,1},{1,0},{2,3},{3,2},{4,5},{5,4},{6,7},{7,6},{8,9},{9,8},{10,11... | collective-permute-start | bytes 196616 | tf_op jit(solution)/shard_map/ppermute | solution.py:316
  31.2 8.7 %collective-permute-start.10 = (bf16[32,1024]{1,0:T(8,128)(2,1)S(1)}, bf16[32,1024]{1,0:T(8,128)(2,1)S(1)}, u32[]{:S(2)}, u32[]{:S(2)}) collective-permute-start(bf16[32,1024]{1,0:T(8,128)(2,1)S(1)} %get-tuple-element.53), channel_id=1, source_target_pairs={{0,2},{1,3},{2,0},{3,1},{4,6},{5,7},{6,4},{7,5},{8,10},{9,11},{10,... | collective-permute-start | bytes 196616 | tf_op jit(solution)/shard_map/ppermute | solution.py:316
  32.9 7.0 %collective-permute-start.11 = (bf16[32,1024]{1,0:T(8,128)(2,1)S(1)}, bf16[32,1024]{1,0:T(8,128)(2,1)S(1)}, u32[]{:S(2)}, u32[]{:S(2)}) collective-permute-start(bf16[32,1024]{1,0:T(8,128)(2,1)S(1)} %get-tuple-element.54), channel_id=1, source_target_pairs={{0,3},{1,2},{2,1},{3,0},{4,7},{5,6},{6,5},{7,4},{8,11},{9,10},{10,... | collective-permute-start | bytes 196616 | tf_op jit(solution)/shard_map/ppermute | solution.py:316
  43.9 1.6 %collective-permute-start.16 = (f32[512,128]{1,0:T(8,128)S(1)}, f32[512,128]{1,0:T(8,128)S(1)}, u32[]{:S(2)}, u32[]{:S(2)}) collective-permute-start(f32[512,128]{1,0:T(8,128)S(1)} %get-tuple-element.69), channel_id=1, source_target_pairs={{0,4},{4,0},{8,12},{12,8},{16,20},{20,16},{24,28},{28,24},{1,5},{5... | collective-permute-start | bytes 786440 | tf_op jit(solution)/shard_map/ppermute | solution.py:316
  45.5 5.9 %collective-permute-start.17 = (bf16[256,128]{1,0:T(8,128)(2,1)S(1)}, bf16[256,128]{1,0:T(8,128)(2,1)S(1)}, u32[]{:S(2)}, u32[]{:S(2)}) collective-permute-start(bf16[256,128]{1,0:T(8,128)(2,1)S(1)} %get-tuple-element.71), channel_id=1, source_target_pairs={{0,8},{4,12},{8,0},{12,4},{16,24},{20,28},{24,16},{28,20},{1,9},{5... | collective-permute-start | bytes 196616 | tf_op jit(solution)/shard_map/ppermute | solution.py:316
  47.1 13.7 %collective-permute-start.13 = (bf16[544,128]{1,0:T(8,128)(2,1)S(1)}, bf16[544,128]{1,0:T(8,128)(2,1)S(1)}, u32[]{:S(2)}, u32[]{:S(2)}) collective-permute-start(bf16[544,128]{1,0:T(8,128)(2,1)S(1)} %get-tuple-element.64), channel_id=1, source_target_pairs={{0,1},{1,0},{2,3},{3,2},{4,5},{5,4},{6,7},{7,6},{8,9},{9,8},{10,11... | collective-permute-start | bytes 417800 | tf_op jit(solution)/shard_map/ppermute | solution.py:316
  48.7 13.0 %collective-permute-start.14 = (bf16[544,128]{1,0:T(8,128)(2,1)S(1)}, bf16[544,128]{1,0:T(8,128)(2,1)S(1)}, u32[]{:S(2)}, u32[]{:S(2)}) collective-permute-start(bf16[544,128]{1,0:T(8,128)(2,1)S(1)} %get-tuple-element.65), channel_id=1, source_target_pairs={{0,2},{1,3},{2,0},{3,1},{4,6},{5,7},{6,4},{7,5},{8,10},{9,11},{10,... | collective-permute-start | bytes 417800 | tf_op jit(solution)/shard_map/ppermute | solution.py:316
  49.4 12.3 %collective-permute-start.15 = (bf16[544,128]{1,0:T(8,128)(2,1)S(1)}, bf16[544,128]{1,0:T(8,128)(2,1)S(1)}, u32[]{:S(2)}, u32[]{:S(2)}) collective-permute-start(bf16[544,128]{1,0:T(8,128)(2,1)S(1)} %get-tuple-element.66), channel_id=1, source_target_pairs={{0,3},{1,2},{2,1},{3,0},{4,7},{5,6},{6,5},{7,4},{8,11},{9,10},{10,... | collective-permute-start | bytes 417800 | tf_op jit(solution)/shard_map/ppermute | solution.py:316
  51.5 4.0 %collective-permute-start.18 = (bf16[128,128]{1,0:T(8,128)(2,1)S(1)}, bf16[128,128]{1,0:T(8,128)(2,1)S(1)}, u32[]{:S(2)}, u32[]{:S(2)}) collective-permute-start(bf16[128,128]{1,0:T(8,128)(2,1)S(1)} %get-tuple-element.73), channel_id=1, source_target_pairs={{0,16},{4,20},{8,24},{12,28},{16,0},{20,4},{24,8},{28,12},{1,17},{... | collective-permute-start | bytes 98312 | tf_op jit(solution)/shard_map/ppermute | solution.py:316
  55.5 5.0 %collective-permute-start.19 = (bf16[128,128]{1,0:T(8,128)(2,1)S(1)}, bf16[128,128]{1,0:T(8,128)(2,1)S(1)}, u32[]{:S(2)}, u32[]{:S(2)}) collective-permute-start(bf16[128,128]{1,0:T(8,128)(2,1)S(1)} %shard_map.103.refs_0_), channel_id=1, source_target_pairs={{0,1},{1,0},{2,3},{3,2},{4,5},{5,4},{6,7},{7,6},{8,9},{9,8},{10,11... | collective-permute-start | bytes 98312 | tf_op jit(solution)/shard_map/ppermute | solution.py:316
  60.5 5.0 %collective-permute-start.20 = (bf16[128,128]{1,0:T(8,128)(2,1)S(1)}, bf16[128,128]{1,0:T(8,128)(2,1)S(1)}, u32[]{:S(2)}, u32[]{:S(2)}) collective-permute-start(bf16[128,128]{1,0:T(8,128)(2,1)S(1)} %shard_map.104.refs_0_), channel_id=1, source_target_pairs={{0,2},{1,3},{2,0},{3,1},{4,6},{5,7},{6,4},{7,5},{8,10},{9,11},{10,... | collective-permute-start | bytes 98312 | tf_op jit(solution)/shard_map/ppermute | solution.py:316
  (4 other events, 4.6 us)

commit v6 on v4

--- a/solution.py
+++ b/solution.py
@@ -266,17 +266,15 @@
         odd_ref[at, :] = key_total[(2 * i + 1) * rows : (2 * i + 2) * rows, :]
 
 
-def pair_kernel(mine_ref, other_ref, own_ref, *outs):
-    rows = own_ref.shape[0]
-    own_ref[...] = mine_ref[:rows, :] + other_ref[:rows, :]
-    for i, out in enumerate(outs):
-        at = slice((i + 1) * rows, (i + 2) * rows)
-        out[...] = (mine_ref[at, :] + other_ref[at, :]).astype(out.dtype)
-
-
-def sum_kernel(*refs):
-    out_ref = refs[-1]
-    out_ref[...] = tree([ref[...].astype(f32) for ref in refs[:-1]]).astype(out_ref.dtype)
+def halve_kernel(*refs):
+    mine_ref, other_ref, keep_ref = refs[:3]
+    rows = LANES
+    for i in range(mine_ref.shape[0] // rows):
+        at = slice(i * rows, (i + 1) * rows)
+        value = mine_ref[at, :].astype(f32) + other_ref[at, :].astype(f32)
+        out = refs[3] if i % 2 else keep_ref
+        to = slice(i // 2 * rows, (i // 2 + 1) * rows)
+        out[to, :] = value.astype(out.dtype)
 
 
 def finish_kernel(share, heads, *refs):
@@ -427,14 +425,19 @@
         ),
     )
     odd = swap(odd, "pb", 1)
-    term = shape((rows, index_width), f32)
-    half = shape((rows, index_width), bf16)
-    mine, *others = call(pair_kernel, [term] + [half] * (blocks // 2 - 1), (even, odd))
-    others = [swap(value, "pb", 2 * (i + 1)) for i, value in enumerate(others)]
-    mine = call(sum_kernel, half, [mine] + others)
-    key_grad = call(sum_kernel, half, [mine] + [swap(mine, "ha", r) for r in range(1, parts)])
-
     answers = [answers[0]] + [swap(answers[r], "ha", r) for r in range(1, parts)]
+    mine, other, rel = even, odd, 2
+    while mine.shape[0] > rows:
+        half = (mine.shape[0] // 2, index_width)
+        mine, other = call(halve_kernel, [shape(half, f32), shape(half, bf16)], (mine, other))
+        other = swap(other, "pb", rel)
+        rel *= 2
+    other, answers = lax.optimization_barrier((other, answers))
+    for r in [1 << i for i in range(parts.bit_length() - 1)]:
+        mine = call(halve_kernel, shape((rows, index_width), bf16), (mine, other))
+        other = swap(mine, "ha", r)
+    key_grad = call(halve_kernel, shape((rows, index_width), bf16), (mine, other))
+
     query_grad, weight_grad = call(
         functools.partial(finish_kernel, share, heads),
         [shape((rows * heads, index_width), bf16), shape((heads, rows), f32)],

time: 64.8 us -> 69 us (1.065)
  waiting for transfers between devices: 14.5 us -> 18.1 us
    ppermute x23 -> x21, waiting for transfers between devices: 14.5 us -> 18.1 us  [swap(): return lax.ppermute(value, axis, [(i, i ^ rel) for i in range(size)])]
    ppermute x23 -> x21, starting transfers between devices: 26.9 us -> 27.5 us  [swap(): return lax.ppermute(value, axis, [(i, i ^ rel) for i in range(size)])]
    pallas_call x11 -> x13, Pallas kernels: 15.1 us -> 15.1 us  [call(): pl.pallas_call(kernel, grid=(1,), out_shape=outs, in_specs=specs or [whol...]
  transfers between devices with their start and end apart: 23 -> 21, of which waited for: 8 -> 8; matrix products, arithmetic and copies ran while one was open for 0% -> 0% of each run, Pallas kernels for 16% -> 15%
where the time goes in v6:
time: 69 us; the launch traced here: 68.6 us
  starting transfers between devices  27.5 us (40%)
  waiting for transfers between devices  18.1 us (26%)
  Pallas kernels  15.1 us (22%)
  local copies, waits for them, and re-layouts  7.12 us (10%)
  between operations  0.8 us (1%)
    ppermute x21, starting transfers between devices, swap(): return lax.ppermute(value, axis, [(i, i ^ rel) for i in range(size)])  27.5 us
    ppermute x21, waiting for transfers between devices, swap(): return lax.ppermute(value, axis, [(i, i ^ rel) for i in range(size)])  18.1 us
    pallas_call x13, Pallas kernels, call(): pl.pallas_call(kernel, grid=(1,), out_shape=outs, in_specs=specs or [whol...  15.1 us
    unnamed x20, local copies, waits for them, and re-layouts  7.12 us
  transfers between devices with their start and end apart: 21, of which 8 were waited for; matrix products, arithmetic and copies ran while one was open for 0% of the time, Pallas kernels for 15%

profile of v6, /device:TPU:0, one launch (start us, length us, event | category | flops | bytes accessed | tf_op | source)
XLA Modules:
  0.0 68.6 jit_solution(12402479696809956244)
XLA Ops:
  2.9 3.5 %collective-permute-start.3 = (bf16[128,704]{1,0:T(8,128)(2,1)S(1)}, bf16[128,704]{1,0:T(8,128)(2,1)S(1)}, u32[]{:S(2)}, u32[]{:S(2)}) collective-permute-start(bf16[128,704]{1,0:T(8,128)(2,1)S(1)} %shard_map.94.refs_0_.refs_4_), channel_id=1, source_target_pairs={{0,24},{4,28},{8,16},{12,20},{16,8},{20,12},{24,0},{28,4},{1,25},{... | collective-permute-start | bytes 540680 | tf_op jit(solution)/shard_map/ppermute | solution.py:319
  7.1 1.0 %copy-done.2 = bf16[128,16,128]{2,1,0:T(8,128)(2,1)S(1)} copy-done((bf16[128,16,128]{2,1,0:T(8,128)(2,1)S(1)}, bf16[128,16,128]{2,1,0:T(8,128)(2,1)}, u32[]{:S(2)}) %copy-start.2) | copy-done | bytes 524312
  8.9 2.3 %copy-done = bf16[128,32,576]{0,2,1:T(8,128)(2,1)S(1)} copy-done((bf16[128,32,576]{0,2,1:T(8,128)(2,1)S(1)}, bf16[128,32,576]{0,2,1:T(8,128)(2,1)}, u32[]{:S(2)}) %copy-start) | copy-done | bytes 4718616
  12.6 1.9 %shard_map.96.refs_5_ = bf16[128,256]{1,0:T(8,128)(2,1)S(1)} custom-call(bf16[128,704]{1,0:T(8,128)(2,1)S(1)} %shard_map.94.refs_0_.refs_4_, bf16[128,704]{1,0:T(8,128)(2,1)S(1)} %collective-permute-done.refs_1_.refs_5_, bf16[32,576,128]{2,1,0:T(8,128)(2,1)S(1)} %bitcast.8, f32[32,128]{1,0:T(8,128)S(1)} %bitcast.13, s32[1,128]{1,0:T(1,128)S(1)} %bitcast.17), custom_call_target="tpu_custom_call" | custom-call | flops 1207959552 | bytes 4718592 | tf_op jit(solution)/shard_map/pallas_call | solution.py:29
  14.5 1.6 %collective-permute-done.2.refs_2_.refs_4_.refs_8_ = bf16[128,704]{1,0:T(8,128)(2,1)S(1)} collective-permute-done((bf16[128,704]{1,0:T(8,128)(2,1)S(1)}, bf16[128,704]{1,0:T(8,128)(2,1)S(1)}, u32[]{:S(2)}, u32[]{:S(2)}) %collective-permute-start.2) | collective-permute-done | bytes 180256 | tf_op jit(solution)/shard_map/ppermute | solution.py:319
  17.0 1.6 %collective-permute-start.10 = (bf16[560,128]{1,0:T(8,128)(2,1)S(1)}, bf16[560,128]{1,0:T(8,128)(2,1)S(1)}, u32[]{:S(2)}, u32[]{:S(2)}) collective-permute-start(bf16[560,128]{1,0:T(8,128)(2,1)S(1)} %get-tuple-element.52), channel_id=1, source_target_pairs={{0,1},{1,0},{2,3},{3,2},{4,5},{5,4},{6,7},{7,6},{8,9},{9,8},{10,11... | collective-permute-start | bytes 430088 | tf_op jit(solution)/shard_map/ppermute | solution.py:319
  18.6 2.6 %collective-permute-start.11 = (bf16[560,128]{1,0:T(8,128)(2,1)S(1)}, bf16[560,128]{1,0:T(8,128)(2,1)S(1)}, u32[]{:S(2)}, u32[]{:S(2)}) collective-permute-start(bf16[560,128]{1,0:T(8,128)(2,1)S(1)} %get-tuple-element.53), channel_id=1, source_target_pairs={{0,2},{1,3},{2,0},{3,1},{4,6},{5,7},{6,4},{7,5},{8,10},{9,11},{10,... | collective-permute-start | bytes 430088 | tf_op jit(solution)/shard_map/ppermute | solution.py:319
  21.4 3.6 %shard_map.97.refs_6_ = bf16[128,512]{1,0:T(8,128)(2,1)S(1)} custom-call(bf16[128,704]{1,0:T(8,128)(2,1)S(1)} %collective-permute-done.1.refs_0_.refs_2_.refs_6_, bf16[128,704]{1,0:T(8,128)(2,1)S(1)} %collective-permute-done.5.refs_1_.refs_3_.refs_7_, bf16[128,704]{1,0:T(8,128)(2,1)S(1)} %collective-permute-done.2.refs_2_.refs_4_.refs_8_, ...), custom_call_target="tpu_custom_call" | custom-call | flops 2415919104 | bytes 4718592 | tf_op jit(solution)/shard_map/pallas_call | solution.py:29
  25.0 1.9 %shard_map.98 = (bf16[32,1024]{1,0:T(8,128)(2,1)S(1)}, bf16[32,1024]{1,0:T(8,128)(2,1)S(1)}, bf16[32,1024]{1,0:T(8,128)(2,1)S(1)}, bf16[32,1024]{1,0:T(8,128)(2,1)S(1)}) custom-call(bf16[128,704]{1,0:T(8,128)(2,1)S(1)} %collective-permute-done.3.refs_0_.refs_6_.refs_10_, bf16[128,704]{1,0:T(8,128)(2,1)S(1)} %collective-permute-done.4.refs_1_.refs_7_.refs_11_, ...), custom_call_target="tpu_custom_call" | custom-call | flops 1207959552 | bytes 4718592 | tf_op jit(solution)/shard_map/pallas_call | solution.py:29
  27.7 3.5 %collective-permute-start.8 = (bf16[32,1024]{1,0:T(8,128)(2,1)S(1)}, bf16[32,1024]{1,0:T(8,128)(2,1)S(1)}, u32[]{:S(2)}, u32[]{:S(2)}) collective-permute-start(bf16[32,1024]{1,0:T(8,128)(2,1)S(1)} %get-tuple-element.48), channel_id=1, source_target_pairs={{0,2},{1,3},{2,0},{3,1},{4,6},{5,7},{6,4},{7,5},{8,10},{9,11},{10,... | collective-permute-start | bytes 196616 | tf_op jit(solution)/shard_map/ppermute | solution.py:319
  32.3 1.9 %shard_map.99 = (f32[1024,128]{1,0:T(8,128)S(1)}, bf16[2048,128]{1,0:T(8,128)(2,1)S(1)}, f32[16,128]{1,0:T(8,128)S(1)}) custom-call(bf16[128,704]{1,0:T(8,128)(2,1)S(1)} %shard_map.94.refs_0_.refs_4_, bf16[128,704]{1,0:T(8,128)(2,1)S(1)} %collective-permute-done.refs_1_.refs_5_, bf16[128,704]{1,0:T(8,128)(2,1)S(1)} %collective-permute-done.1.refs_0_.refs_2_.refs_6_, ...), custom_call_target="tpu_custom_call" | custom-call | flops 536870912 | bytes 524288 | tf_op jit(solution)/shard_map/pallas_call | solution.py:29
  34.2 4.8 %collective-permute-done.8.refs_2_ = bf16[32,1024]{1,0:T(8,128)(2,1)S(1)} collective-permute-done((bf16[32,1024]{1,0:T(8,128)(2,1)S(1)}, bf16[32,1024]{1,0:T(8,128)(2,1)S(1)}, u32[]{:S(2)}, u32[]{:S(2)}) %collective-permute-start.8) | collective-permute-done | bytes 65568 | tf_op jit(solution)/shard_map/ppermute | solution.py:319
  39.0 4.0 %shard_map.100 = (f32[512,128]{1,0:T(8,128)S(1)}, f32[512,128]{1,0:T(8,128)S(1)}, bf16[544,128]{1,0:T(8,128)(2,1)S(1)}, bf16[544,128]{1,0:T(8,128)(2,1)S(1)}, bf...) custom-call(bf16[32,1024]{1,0:T(8,128)(2,1)S(1)} %get-tuple-element.46.refs_0_, ...), custom_call_target="tpu_custom_call" | custom-call | flops 1610612736 | bytes 524288 | tf_op jit(solution)/shard_map/pallas_call | solution.py:29
  43.2 1.7 %collective-permute-start.16 = (bf16[544,128]{1,0:T(8,128)(2,1)S(1)}, bf16[544,128]{1,0:T(8,128)(2,1)S(1)}, u32[]{:S(2)}, u32[]{:S(2)}) collective-permute-start(bf16[544,128]{1,0:T(8,128)(2,1)S(1)} %get-tuple-element.64), channel_id=1, source_target_pairs={{0,1},{1,0},{2,3},{3,2},{4,5},{5,4},{6,7},{7,6},{8,9},{9,8},{10,11... | collective-permute-start | bytes 417800 | tf_op jit(solution)/shard_map/ppermute | solution.py:319
  44.9 1.4 %collective-permute-start.17 = (bf16[544,128]{1,0:T(8,128)(2,1)S(1)}, bf16[544,128]{1,0:T(8,128)(2,1)S(1)}, u32[]{:S(2)}, u32[]{:S(2)}) collective-permute-start(bf16[544,128]{1,0:T(8,128)(2,1)S(1)} %get-tuple-element.65), channel_id=1, source_target_pairs={{0,2},{1,3},{2,0},{3,1},{4,6},{5,7},{6,4},{7,5},{8,10},{9,11},{10,... | collective-permute-start | bytes 417800 | tf_op jit(solution)/shard_map/ppermute | solution.py:319
  46.3 1.4 %collective-permute-start.18 = (bf16[544,128]{1,0:T(8,128)(2,1)S(1)}, bf16[544,128]{1,0:T(8,128)(2,1)S(1)}, u32[]{:S(2)}, u32[]{:S(2)}) collective-permute-start(bf16[544,128]{1,0:T(8,128)(2,1)S(1)} %get-tuple-element.66), channel_id=1, source_target_pairs={{0,3},{1,2},{2,1},{3,0},{4,7},{5,6},{6,5},{7,4},{8,11},{9,10},{10,... | collective-permute-start | bytes 417800 | tf_op jit(solution)/shard_map/ppermute | solution.py:319
  47.7 1.6 %collective-permute-start.14 = (bf16[256,128]{1,0:T(8,128)(2,1)S(1)}, bf16[256,128]{1,0:T(8,128)(2,1)S(1)}, u32[]{:S(2)}, u32[]{:S(2)}) collective-permute-start(bf16[256,128]{1,0:T(8,128)(2,1)S(1)} %get-tuple-element.61), channel_id=1, source_target_pairs={{0,8},{4,12},{8,0},{12,4},{16,24},{20,28},{24,16},{28,20},{1,9},{5... | collective-permute-start | bytes 196616 | tf_op jit(solution)/shard_map/ppermute | solution.py:319
  49.2 2.8 %collective-permute-done.14.refs_1_ = bf16[256,128]{1,0:T(8,128)(2,1)S(1)} collective-permute-done((bf16[256,128]{1,0:T(8,128)(2,1)S(1)}, bf16[256,128]{1,0:T(8,128)(2,1)S(1)}, u32[]{:S(2)}, u32[]{:S(2)}) %collective-permute-start.14) | collective-permute-done | bytes 65568 | tf_op jit(solution)/shard_map/ppermute | solution.py:319
  52.0 1.5 %collective-permute-start.15 = (bf16[128,128]{1,0:T(8,128)(2,1)S(1)}, bf16[128,128]{1,0:T(8,128)(2,1)S(1)}, u32[]{:S(2)}, u32[]{:S(2)}) collective-permute-start(bf16[128,128]{1,0:T(8,128)(2,1)S(1)} %get-tuple-element.62), channel_id=1, source_target_pairs={{0,16},{4,20},{8,24},{12,28},{16,0},{20,4},{24,8},{28,12},{1,17},{... | collective-permute-start | bytes 98312 | tf_op jit(solution)/shard_map/ppermute | solution.py:319
  53.5 4.8 %collective-permute-done.17.refs_2_ = bf16[544,128]{1,0:T(8,128)(2,1)S(1)} collective-permute-done((bf16[544,128]{1,0:T(8,128)(2,1)S(1)}, bf16[544,128]{1,0:T(8,128)(2,1)S(1)}, u32[]{:S(2)}, u32[]{:S(2)}) %collective-permute-start.17) | collective-permute-done | bytes 139296 | tf_op jit(solution)/shard_map/ppermute | solution.py:319
  58.3 2.8 %collective-permute-start.19 = (bf16[128,128]{1,0:T(8,128)(2,1)S(1)}, bf16[128,128]{1,0:T(8,128)(2,1)S(1)}, u32[]{:S(2)}, u32[]{:S(2)}) collective-permute-start(bf16[128,128]{1,0:T(8,128)(2,1)S(1)} %shard_map.104.refs_0_), channel_id=1, source_target_pairs={{0,1},{1,0},{2,3},{3,2},{4,5},{5,4},{6,7},{7,6},{8,9},{9,8},{10,11... | collective-permute-start | bytes 98312 | tf_op jit(solution)/shard_map/ppermute | solution.py:319
  61.2 1.9 %collective-permute-done.19.refs_1_ = bf16[128,128]{1,0:T(8,128)(2,1)S(1)} collective-permute-done((bf16[128,128]{1,0:T(8,128)(2,1)S(1)}, bf16[128,128]{1,0:T(8,128)(2,1)S(1)}, u32[]{:S(2)}, u32[]{:S(2)}) %collective-permute-start.19) | collective-permute-done | bytes 32800 | tf_op jit(solution)/shard_map/ppermute | solution.py:319
  63.1 3.0 %collective-permute-start.20 = (bf16[128,128]{1,0:T(8,128)(2,1)S(1)}, bf16[128,128]{1,0:T(8,128)(2,1)S(1)}, u32[]{:S(2)}, u32[]{:S(2)}) collective-permute-start(bf16[128,128]{1,0:T(8,128)(2,1)S(1)} %shard_map.105.refs_0_), channel_id=1, source_target_pairs={{0,2},{1,3},{2,0},{3,1},{4,6},{5,7},{6,4},{7,5},{8,10},{9,11},{10,... | collective-permute-start | bytes 98312 | tf_op jit(solution)/shard_map/ppermute | solution.py:319
  67.0 1.0 %collective-permute-done.20.refs_1_ = bf16[128,128]{1,0:T(8,128)(2,1)S(1)} collective-permute-done((bf16[128,128]{1,0:T(8,128)(2,1)S(1)}, bf16[128,128]{1,0:T(8,128)(2,1)S(1)}, u32[]{:S(2)}, u32[]{:S(2)}) %collective-permute-start.20) | collective-permute-done | bytes 32800 | tf_op jit(solution)/shard_map/ppermute | solution.py:319
  (51 shorter events, 9.6 us)
Async XLA Ops:
  0.6 20.8 %copy-start.9 = (s32[128]{0:T(128)S(1)}, s32[128]{0:T(128)}, u32[]{:S(2)}) copy-start(s32[128]{0:T(128)} %param.10) | copy-start | bytes 1540
  2.3 19.1 %copy-start.5 = (f32[128,32]{0,1:T(8,128)S(1)}, f32[128,32]{0,1:T(8,128)}, u32[]{:S(2)}) copy-start(f32[128,32]{0,1:T(8,128)} %param.9) | copy-start | bytes 49156
  2.4 6.5 %collective-permute-start = (bf16[128,704]{1,0:T(8,128)(2,1)S(1)}, bf16[128,704]{1,0:T(8,128)(2,1)S(1)}, u32[]{:S(2)}, u32[]{:S(2)}) collective-permute-start(bf16[128,704]{1,0:T(8,128)(2,1)S(1)} %shard_map.94.refs_0_.refs_4_), channel_id=1, source_target_pairs={{0,4},{4,0},{8,12},{12,8},{16,20},{20,16},{24,28},{28,24},{1,5},{5... | collective-permute-start | bytes 540680 | tf_op jit(solution)/shard_map/ppermute | solution.py:319
  2.9 11.6 %collective-permute-start.3 = (bf16[128,704]{1,0:T(8,128)(2,1)S(1)}, bf16[128,704]{1,0:T(8,128)(2,1)S(1)}, u32[]{:S(2)}, u32[]{:S(2)}) collective-permute-start(bf16[128,704]{1,0:T(8,128)(2,1)S(1)} %shard_map.94.refs_0_.refs_4_), channel_id=1, source_target_pairs={{0,24},{4,28},{8,16},{12,20},{16,8},{20,12},{24,0},{28,4},{1,25},{... | collective-permute-start | bytes 540680 | tf_op jit(solution)/shard_map/ppermute | solution.py:319
  6.5 9.7 %collective-permute-start.2 = (bf16[128,704]{1,0:T(8,128)(2,1)S(1)}, bf16[128,704]{1,0:T(8,128)(2,1)S(1)}, u32[]{:S(2)}, u32[]{:S(2)}) collective-permute-start(bf16[128,704]{1,0:T(8,128)(2,1)S(1)} %shard_map.94.refs_0_.refs_4_), channel_id=1, source_target_pairs={{0,16},{4,20},{8,24},{12,28},{16,0},{20,4},{24,8},{28,12},{1,17},{... | collective-permute-start | bytes 540680 | tf_op jit(solution)/shard_map/ppermute | solution.py:319
  7.0 9.5 %collective-permute-start.1 = (bf16[128,704]{1,0:T(8,128)(2,1)S(1)}, bf16[128,704]{1,0:T(8,128)(2,1)S(1)}, u32[]{:S(2)}, u32[]{:S(2)}) collective-permute-start(bf16[128,704]{1,0:T(8,128)(2,1)S(1)} %shard_map.94.refs_0_.refs_4_), channel_id=1, source_target_pairs={{0,8},{4,12},{8,0},{12,4},{16,24},{20,28},{24,16},{28,20},{1,9},{5... | collective-permute-start | bytes 540680 | tf_op jit(solution)/shard_map/ppermute | solution.py:319
  12.6 8.8 %copy-start.1 = (bf16[128,32,576]{0,2,1:T(8,128)(2,1)S(1)}, bf16[128,32,576]{0,2,1:T(8,128)(2,1)}, u32[]{:S(2)}) copy-start(bf16[128,32,576]{0,2,1:T(8,128)(2,1)} %param.7) | copy-start | bytes 14155780
  16.5 4.9 %collective-permute-start.5 = (bf16[128,704]{1,0:T(8,128)(2,1)S(1)}, bf16[128,704]{1,0:T(8,128)(2,1)S(1)}, u32[]{:S(2)}, u32[]{:S(2)}) collective-permute-start(bf16[128,704]{1,0:T(8,128)(2,1)S(1)} %collective-permute-done.1.refs_0_.refs_2_.refs_6_), channel_id=1, source_target_pairs={{0,4},{4,0},{8,12},{12,8},{16,20},{20,16},{24,28},{28,24},{1,5},{5... | collective-permute-start | bytes 540680 | tf_op jit(solution)/shard_map/ppermute | solution.py:319
  16.5 4.9 %collective-permute-start.6 = (bf16[128,704]{1,0:T(8,128)(2,1)S(1)}, bf16[128,704]{1,0:T(8,128)(2,1)S(1)}, u32[]{:S(2)}, u32[]{:S(2)}) collective-permute-start(bf16[128,704]{1,0:T(8,128)(2,1)S(1)} %collective-permute-done.2.refs_2_.refs_4_.refs_8_), channel_id=1, source_target_pairs={{0,4},{4,0},{8,12},{12,8},{16,20},{20,16},{24,28},{28,24},{1,5},{5... | collective-permute-start | bytes 540680 | tf_op jit(solution)/shard_map/ppermute | solution.py:319
  17.0 14.2 %collective-permute-start.10 = (bf16[560,128]{1,0:T(8,128)(2,1)S(1)}, bf16[560,128]{1,0:T(8,128)(2,1)S(1)}, u32[]{:S(2)}, u32[]{:S(2)}) collective-permute-start(bf16[560,128]{1,0:T(8,128)(2,1)S(1)} %get-tuple-element.52), channel_id=1, source_target_pairs={{0,1},{1,0},{2,3},{3,2},{4,5},{5,4},{6,7},{7,6},{8,9},{9,8},{10,11... | collective-permute-start | bytes 430088 | tf_op jit(solution)/shard_map/ppermute | solution.py:319
  18.6 13.7 %collective-permute-start.11 = (bf16[560,128]{1,0:T(8,128)(2,1)S(1)}, bf16[560,128]{1,0:T(8,128)(2,1)S(1)}, u32[]{:S(2)}, u32[]{:S(2)}) collective-permute-start(bf16[560,128]{1,0:T(8,128)(2,1)S(1)} %get-tuple-element.53), channel_id=1, source_target_pairs={{0,2},{1,3},{2,0},{3,1},{4,6},{5,7},{6,4},{7,5},{8,10},{9,11},{10,... | collective-permute-start | bytes 430088 | tf_op jit(solution)/shard_map/ppermute | solution.py:319
  21.2 11.1 %collective-permute-start.12 = (bf16[560,128]{1,0:T(8,128)(2,1)S(1)}, bf16[560,128]{1,0:T(8,128)(2,1)S(1)}, u32[]{:S(2)}, u32[]{:S(2)}) collective-permute-start(bf16[560,128]{1,0:T(8,128)(2,1)S(1)} %get-tuple-element.54), channel_id=1, source_target_pairs={{0,3},{1,2},{2,1},{3,0},{4,7},{5,6},{6,5},{7,4},{8,11},{9,10},{10,... | collective-permute-start | bytes 430088 | tf_op jit(solution)/shard_map/ppermute | solution.py:319
  21.4 3.6 %collective-permute-start.4 = (bf16[128,704]{1,0:T(8,128)(2,1)S(1)}, bf16[128,704]{1,0:T(8,128)(2,1)S(1)}, u32[]{:S(2)}, u32[]{:S(2)}) collective-permute-start(bf16[128,704]{1,0:T(8,128)(2,1)S(1)} %collective-permute-done.3.refs_0_.refs_6_.refs_10_), channel_id=1, source_target_pairs={{0,4},{4,0},{8,12},{12,8},{16,20},{20,16},{24,28},{28,24},{1,5},{5... | collective-permute-start | bytes 540680 | tf_op jit(solution)/shard_map/ppermute | solution.py:319
  27.0 7.2 %collective-permute-start.7 = (bf16[32,1024]{1,0:T(8,128)(2,1)S(1)}, bf16[32,1024]{1,0:T(8,128)(2,1)S(1)}, u32[]{:S(2)}, u32[]{:S(2)}) collective-permute-start(bf16[32,1024]{1,0:T(8,128)(2,1)S(1)} %get-tuple-element.47), channel_id=1, source_target_pairs={{0,1},{1,0},{2,3},{3,2},{4,5},{5,4},{6,7},{7,6},{8,9},{9,8},{10,11... | collective-permute-start | bytes 196616 | tf_op jit(solution)/shard_map/ppermute | solution.py:319
  27.7 11.3 %collective-permute-start.8 = (bf16[32,1024]{1,0:T(8,128)(2,1)S(1)}, bf16[32,1024]{1,0:T(8,128)(2,1)S(1)}, u32[]{:S(2)}, u32[]{:S(2)}) collective-permute-start(bf16[32,1024]{1,0:T(8,128)(2,1)S(1)} %get-tuple-element.48), channel_id=1, source_target_pairs={{0,2},{1,3},{2,0},{3,1},{4,6},{5,7},{6,4},{7,5},{8,10},{9,11},{10,... | collective-permute-start | bytes 196616 | tf_op jit(solution)/shard_map/ppermute | solution.py:319
  31.2 7.8 %collective-permute-start.9 = (bf16[32,1024]{1,0:T(8,128)(2,1)S(1)}, bf16[32,1024]{1,0:T(8,128)(2,1)S(1)}, u32[]{:S(2)}, u32[]{:S(2)}) collective-permute-start(bf16[32,1024]{1,0:T(8,128)(2,1)S(1)} %get-tuple-element.49), channel_id=1, source_target_pairs={{0,3},{1,2},{2,1},{3,0},{4,7},{5,6},{6,5},{7,4},{8,11},{9,10},{10,... | collective-permute-start | bytes 196616 | tf_op jit(solution)/shard_map/ppermute | solution.py:319
  43.1 4.5 %collective-permute-start.13 = (f32[512,128]{1,0:T(8,128)S(1)}, f32[512,128]{1,0:T(8,128)S(1)}, u32[]{:S(2)}, u32[]{:S(2)}) collective-permute-start(f32[512,128]{1,0:T(8,128)S(1)} %get-tuple-element.59), channel_id=1, source_target_pairs={{0,4},{4,0},{8,12},{12,8},{16,20},{20,16},{24,28},{28,24},{1,5},{5... | collective-permute-start | bytes 786440 | tf_op jit(solution)/shard_map/ppermute | solution.py:319
  43.2 10.4 %collective-permute-start.16 = (bf16[544,128]{1,0:T(8,128)(2,1)S(1)}, bf16[544,128]{1,0:T(8,128)(2,1)S(1)}, u32[]{:S(2)}, u32[]{:S(2)}) collective-permute-start(bf16[544,128]{1,0:T(8,128)(2,1)S(1)} %get-tuple-element.64), channel_id=1, source_target_pairs={{0,1},{1,0},{2,3},{3,2},{4,5},{5,4},{6,7},{7,6},{8,9},{9,8},{10,11... | collective-permute-start | bytes 417800 | tf_op jit(solution)/shard_map/ppermute | solution.py:319
  44.9 13.4 %collective-permute-start.17 = (bf16[544,128]{1,0:T(8,128)(2,1)S(1)}, bf16[544,128]{1,0:T(8,128)(2,1)S(1)}, u32[]{:S(2)}, u32[]{:S(2)}) collective-permute-start(bf16[544,128]{1,0:T(8,128)(2,1)S(1)} %get-tuple-element.65), channel_id=1, source_target_pairs={{0,2},{1,3},{2,0},{3,1},{4,6},{5,7},{6,4},{7,5},{8,10},{9,11},{10,... | collective-permute-start | bytes 417800 | tf_op jit(solution)/shard_map/ppermute | solution.py:319
  46.3 12.0 %collective-permute-start.18 = (bf16[544,128]{1,0:T(8,128)(2,1)S(1)}, bf16[544,128]{1,0:T(8,128)(2,1)S(1)}, u32[]{:S(2)}, u32[]{:S(2)}) collective-permute-start(bf16[544,128]{1,0:T(8,128)(2,1)S(1)} %get-tuple-element.66), channel_id=1, source_target_pairs={{0,3},{1,2},{2,1},{3,0},{4,7},{5,6},{6,5},{7,4},{8,11},{9,10},{10,... | collective-permute-start | bytes 417800 | tf_op jit(solution)/shard_map/ppermute | solution.py:319
  47.7 4.3 %collective-permute-start.14 = (bf16[256,128]{1,0:T(8,128)(2,1)S(1)}, bf16[256,128]{1,0:T(8,128)(2,1)S(1)}, u32[]{:S(2)}, u32[]{:S(2)}) collective-permute-start(bf16[256,128]{1,0:T(8,128)(2,1)S(1)} %get-tuple-element.61), channel_id=1, source_target_pairs={{0,8},{4,12},{8,0},{12,4},{16,24},{20,28},{24,16},{28,20},{1,9},{5... | collective-permute-start | bytes 196616 | tf_op jit(solution)/shard_map/ppermute | solution.py:319
  52.0 6.3 %collective-permute-start.15 = (bf16[128,128]{1,0:T(8,128)(2,1)S(1)}, bf16[128,128]{1,0:T(8,128)(2,1)S(1)}, u32[]{:S(2)}, u32[]{:S(2)}) collective-permute-start(bf16[128,128]{1,0:T(8,128)(2,1)S(1)} %get-tuple-element.62), channel_id=1, source_target_pairs={{0,16},{4,20},{8,24},{12,28},{16,0},{20,4},{24,8},{28,12},{1,17},{... | collective-permute-start | bytes 98312 | tf_op jit(solution)/shard_map/ppermute | solution.py:319
  58.3 4.7 %collective-permute-start.19 = (bf16[128,128]{1,0:T(8,128)(2,1)S(1)}, bf16[128,128]{1,0:T(8,128)(2,1)S(1)}, u32[]{:S(2)}, u32[]{:S(2)}) collective-permute-start(bf16[128,128]{1,0:T(8,128)(2,1)S(1)} %shard_map.104.refs_0_), channel_id=1, source_target_pairs={{0,1},{1,0},{2,3},{3,2},{4,5},{5,4},{6,7},{7,6},{8,9},{9,8},{10,11... | collective-permute-start | bytes 98312 | tf_op jit(solution)/shard_map/ppermute | solution.py:319
  63.1 4.9 %collective-permute-start.20 = (bf16[128,128]{1,0:T(8,128)(2,1)S(1)}, bf16[128,128]{1,0:T(8,128)(2,1)S(1)}, u32[]{:S(2)}, u32[]{:S(2)}) collective-permute-start(bf16[128,128]{1,0:T(8,128)(2,1)S(1)} %shard_map.105.refs_0_), channel_id=1, source_target_pairs={{0,2},{1,3},{2,0},{3,1},{4,6},{5,7},{6,4},{7,5},{8,10},{9,11},{10,... | collective-permute-start | bytes 98312 | tf_op jit(solution)/shard_map/ppermute | solution.py:319
  (7 other events, 7.1 us)

commit v7 on v4

--- a/solution.py
+++ b/solution.py
@@ -11,6 +11,7 @@
 log2e = 1.4426950408889634
 very_low = -1e30
 LANES = 128
+FILL = 10
 TAIL = 16
 f32, bf16 = jnp.float32, jnp.bfloat16
 
@@ -366,7 +367,7 @@
             ],
             specs,
             pl.CostEstimate(
-                flops=2 * span * rows * head_count * width,
+                flops=2 * span * rows * head_count * width * (FILL if rels is chunks[0] else 1),
                 bytes_accessed=2 * rows * head_count * width,
                 transcendentals=span * rows * head_count,
             ),
@@ -374,8 +375,9 @@
         mass = found if last else mass + found
         if rels is chunks[0]:
             even = list(range(2, blocks, 2))
-            ready = lax.optimization_barrier((found[0], [held[k] for k in even]))
+            ready = lax.optimization_barrier((found[0], [held[k] for k in even], asked[1:3]))
             mass = [ready[0]]
+            asked[1:3] = ready[2]
             for k, block in zip(even, ready[1]):
                 held[k] = block
                 held[k + 1] = swap(block, "pb", 1)
@@ -430,11 +432,14 @@
     term = shape((rows, index_width), f32)
     half = shape((rows, index_width), bf16)
     mine, *others = call(pair_kernel, [term] + [half] * (blocks // 2 - 1), (even, odd))
-    others = [swap(value, "pb", 2 * (i + 1)) for i, value in enumerate(others)]
+    answers = [answers[0]] + [swap(answers[r], "ha", r) for r in range(1, parts)]
+    for i, value in enumerate(others):
+        if i == len(others) - 1:
+            value, answers[1] = lax.optimization_barrier((value, answers[1]))
+        others[i] = swap(value, "pb", 2 * (i + 1))
     mine = call(sum_kernel, half, [mine] + others)
     key_grad = call(sum_kernel, half, [mine] + [swap(mine, "ha", r) for r in range(1, parts)])
 
-    answers = [answers[0]] + [swap(answers[r], "ha", r) for r in range(1, parts)]
     query_grad, weight_grad = call(
         functools.partial(finish_kernel, share, heads),
         [shape((rows * heads, index_width), bf16), shape((heads, rows), f32)],

time: 64.8 us -> 64.7 us (level)
  waiting for transfers between devices: 14.5 us -> 12 us
  starting transfers between devices: 26.9 us -> 29.3 us
    ppermute x23, waiting for transfers between devices: 14.5 us -> 12 us  [swap(): return lax.ppermute(value, axis, [(i, i ^ rel) for i in range(size)])]
    ppermute x23, starting transfers between devices: 26.9 us -> 29.3 us  [swap(): return lax.ppermute(value, axis, [(i, i ^ rel) for i in range(size)])]
    unnamed x20 -> x18, local copies, waits for them, and re-layouts: 7.12 us -> 7.11 us
where the time goes in v7:
time: 64.7 us; the launch traced here: 64.3 us
  starting transfers between devices  29.3 us (45%)
  Pallas kernels  15.1 us (23%)
  waiting for transfers between devices  12 us (19%)
  local copies, waits for them, and re-layouts  7.11 us (11%)
  between operations  0.78 us (1%)
    ppermute x23, starting transfers between devices, swap(): return lax.ppermute(value, axis, [(i, i ^ rel) for i in range(size)])  29.3 us
    pallas_call x11, Pallas kernels, call(): pl.pallas_call(kernel, grid=(1,), out_shape=outs, in_specs=specs or [whol...  15.1 us
    ppermute x23, waiting for transfers between devices, swap(): return lax.ppermute(value, axis, [(i, i ^ rel) for i in range(size)])  12 us
    unnamed x18, local copies, waits for them, and re-layouts  7.11 us
  transfers between devices with their start and end apart: 23, of which 8 were waited for; matrix products, arithmetic and copies ran while one was open for 0% of the time, Pallas kernels for 16%

profile of v7, /device:TPU:0, one launch (start us, length us, event | category | flops | bytes accessed | tf_op | source)
XLA Modules:
  0.0 64.3 jit_solution(9827223987844424801)
XLA Ops:
  2.9 3.5 %collective-permute-start.3 = (bf16[128,704]{1,0:T(8,128)(2,1)S(1)}, bf16[128,704]{1,0:T(8,128)(2,1)S(1)}, u32[]{:S(2)}, u32[]{:S(2)}) collective-permute-start(bf16[128,704]{1,0:T(8,128)(2,1)S(1)} %shard_map.94.refs_0_.refs_4_), channel_id=1, source_target_pairs={{0,24},{4,28},{8,16},{12,20},{16,8},{20,12},{24,0},{28,4},{1,25},{... | collective-permute-start | bytes 540680 | tf_op jit(solution)/shard_map/ppermute | solution.py:322
  7.1 1.0 %copy-done.2 = bf16[128,16,128]{2,1,0:T(8,128)(2,1)S(1)} copy-done((bf16[128,16,128]{2,1,0:T(8,128)(2,1)S(1)}, bf16[128,16,128]{2,1,0:T(8,128)(2,1)}, u32[]{:S(2)}) %copy-start.2) | copy-done | bytes 524312
  8.9 2.0 %collective-permute-start.4 = (bf16[560,128]{1,0:T(8,128)(2,1)S(1)}, bf16[560,128]{1,0:T(8,128)(2,1)S(1)}, u32[]{:S(2)}, u32[]{:S(2)}) collective-permute-start(bf16[560,128]{1,0:T(8,128)(2,1)S(1)} %get-tuple-element.40), channel_id=1, source_target_pairs={{0,1},{1,0},{2,3},{3,2},{4,5},{5,4},{6,7},{7,6},{8,9},{9,8},{10,11... | collective-permute-start | bytes 430088 | tf_op jit(solution)/shard_map/ppermute | solution.py:322
  10.9 2.6 %collective-permute-start.5 = (bf16[560,128]{1,0:T(8,128)(2,1)S(1)}, bf16[560,128]{1,0:T(8,128)(2,1)S(1)}, u32[]{:S(2)}, u32[]{:S(2)}) collective-permute-start(bf16[560,128]{1,0:T(8,128)(2,1)S(1)} %get-tuple-element.41), channel_id=1, source_target_pairs={{0,2},{1,3},{2,0},{3,1},{4,6},{5,7},{6,4},{7,5},{8,10},{9,11},{10,... | collective-permute-start | bytes 430088 | tf_op jit(solution)/shard_map/ppermute | solution.py:322
  13.5 2.3 %copy-done = bf16[128,32,576]{0,2,1:T(8,128)(2,1)S(1)} copy-done((bf16[128,32,576]{0,2,1:T(8,128)(2,1)S(1)}, bf16[128,32,576]{0,2,1:T(8,128)(2,1)}, u32[]{:S(2)}) %copy-start) | copy-done | bytes 4718616
  17.2 1.9 %shard_map.96.refs_5_ = bf16[128,256]{1,0:T(8,128)(2,1)S(1)} custom-call(bf16[128,704]{1,0:T(8,128)(2,1)S(1)} %shard_map.94.refs_0_.refs_4_, bf16[128,704]{1,0:T(8,128)(2,1)S(1)} %collective-permute-done.refs_1_.refs_5_, bf16[32,576,128]{2,1,0:T(8,128)(2,1)S(1)} %bitcast.8, f32[32,128]{1,0:T(8,128)S(1)} %bitcast.13, s32[1,128]{1,0:T(1,128)S(1)} %bitcast.17), custom_call_target="tpu_custom_call" | custom-call | flops 12079595520 | bytes 4718592 | tf_op jit(solution)/shard_map/pallas_call | solution.py:30
  20.5 2.5 %collective-permute-start.12 = (bf16[560,128]{1,0:T(8,128)(2,1)S(1)}, bf16[560,128]{1,0:T(8,128)(2,1)S(1)}, u32[]{:S(2)}, u32[]{:S(2)}) collective-permute-start(bf16[560,128]{1,0:T(8,128)(2,1)S(1)} %get-tuple-element.55), channel_id=1, source_target_pairs={{0,3},{1,2},{2,1},{3,0},{4,7},{5,6},{6,5},{7,4},{8,11},{9,10},{10,... | collective-permute-start | bytes 430088 | tf_op jit(solution)/shard_map/ppermute | solution.py:322
  23.0 3.6 %shard_map.97.refs_6_ = bf16[128,512]{1,0:T(8,128)(2,1)S(1)} custom-call(bf16[128,704]{1,0:T(8,128)(2,1)S(1)} %collective-permute-done.1.refs_0_.refs_2_.refs_6_, bf16[128,704]{1,0:T(8,128)(2,1)S(1)} %collective-permute-done.7.refs_1_.refs_3_.refs_7_, bf16[128,704]{1,0:T(8,128)(2,1)S(1)} %collective-permute-done.2.refs_2_.refs_4_.refs_8_, ...), custom_call_target="tpu_custom_call" | custom-call | flops 2415919104 | bytes 4718592 | tf_op jit(solution)/shard_map/pallas_call | solution.py:30
  26.6 1.9 %shard_map.98 = (bf16[32,1024]{1,0:T(8,128)(2,1)S(1)}, bf16[32,1024]{1,0:T(8,128)(2,1)S(1)}, bf16[32,1024]{1,0:T(8,128)(2,1)S(1)}, bf16[32,1024]{1,0:T(8,128)(2,1)S(1)}) custom-call(bf16[128,704]{1,0:T(8,128)(2,1)S(1)} %collective-permute-done.3.refs_0_.refs_6_.refs_10_, bf16[128,704]{1,0:T(8,128)(2,1)S(1)} %collective-permute-done.6.refs_1_.refs_7_.refs_11_, ...), custom_call_target="tpu_custom_call" | custom-call | flops 1207959552 | bytes 4718592 | tf_op jit(solution)/shard_map/pallas_call | solution.py:30
  28.7 1.9 %collective-permute-start.10 = (bf16[32,1024]{1,0:T(8,128)(2,1)S(1)}, bf16[32,1024]{1,0:T(8,128)(2,1)S(1)}, u32[]{:S(2)}, u32[]{:S(2)}) collective-permute-start(bf16[32,1024]{1,0:T(8,128)(2,1)S(1)} %get-tuple-element.49), channel_id=1, source_target_pairs={{0,2},{1,3},{2,0},{3,1},{4,6},{5,7},{6,4},{7,5},{8,10},{9,11},{10,... | collective-permute-start | bytes 196616 | tf_op jit(solution)/shard_map/ppermute | solution.py:322
  30.6 2.5 %collective-permute-start.11 = (bf16[32,1024]{1,0:T(8,128)(2,1)S(1)}, bf16[32,1024]{1,0:T(8,128)(2,1)S(1)}, u32[]{:S(2)}, u32[]{:S(2)}) collective-permute-start(bf16[32,1024]{1,0:T(8,128)(2,1)S(1)} %get-tuple-element.50), channel_id=1, source_target_pairs={{0,3},{1,2},{2,1},{3,0},{4,7},{5,6},{6,5},{7,4},{8,11},{9,10},{10,... | collective-permute-start | bytes 196616 | tf_op jit(solution)/shard_map/ppermute | solution.py:322
  33.0 1.9 %shard_map.99 = (f32[1024,128]{1,0:T(8,128)S(1)}, bf16[2048,128]{1,0:T(8,128)(2,1)S(1)}, f32[16,128]{1,0:T(8,128)S(1)}) custom-call(bf16[128,704]{1,0:T(8,128)(2,1)S(1)} %shard_map.94.refs_0_.refs_4_, bf16[128,704]{1,0:T(8,128)(2,1)S(1)} %collective-permute-done.refs_1_.refs_5_, bf16[128,704]{1,0:T(8,128)(2,1)S(1)} %collective-permute-done.1.refs_0_.refs_2_.refs_6_, ...), custom_call_target="tpu_custom_call" | custom-call | flops 536870912 | bytes 524288 | tf_op jit(solution)/shard_map/pallas_call | solution.py:30
  35.0 2.4 %collective-permute-done.10.refs_2_ = bf16[32,1024]{1,0:T(8,128)(2,1)S(1)} collective-permute-done((bf16[32,1024]{1,0:T(8,128)(2,1)S(1)}, bf16[32,1024]{1,0:T(8,128)(2,1)S(1)}, u32[]{:S(2)}, u32[]{:S(2)}) %collective-permute-start.10) | collective-permute-done | bytes 65568 | tf_op jit(solution)/shard_map/ppermute | solution.py:322
  37.4 4.0 %shard_map.100 = (f32[512,128]{1,0:T(8,128)S(1)}, f32[512,128]{1,0:T(8,128)S(1)}, bf16[544,128]{1,0:T(8,128)(2,1)S(1)}, bf16[544,128]{1,0:T(8,128)(2,1)S(1)}, bf...) custom-call(bf16[32,1024]{1,0:T(8,128)(2,1)S(1)} %get-tuple-element.47.refs_0_, ...), custom_call_target="tpu_custom_call" | custom-call | flops 1610612736 | bytes 524288 | tf_op jit(solution)/shard_map/pallas_call | solution.py:30
  41.5 1.6 %collective-permute-start.14 = (bf16[544,128]{1,0:T(8,128)(2,1)S(1)}, bf16[544,128]{1,0:T(8,128)(2,1)S(1)}, u32[]{:S(2)}, u32[]{:S(2)}) collective-permute-start(bf16[544,128]{1,0:T(8,128)(2,1)S(1)} %get-tuple-element.63), channel_id=1, source_target_pairs={{0,1},{1,0},{2,3},{3,2},{4,5},{5,4},{6,7},{7,6},{8,9},{9,8},{10,11... | collective-permute-start | bytes 417800 | tf_op jit(solution)/shard_map/ppermute | solution.py:322
  43.9 2.0 %collective-permute-start.16 = (bf16[544,128]{1,0:T(8,128)(2,1)S(1)}, bf16[544,128]{1,0:T(8,128)(2,1)S(1)}, u32[]{:S(2)}, u32[]{:S(2)}) collective-permute-start(bf16[544,128]{1,0:T(8,128)(2,1)S(1)} %get-tuple-element.66), channel_id=1, source_target_pairs={{0,3},{1,2},{2,1},{3,0},{4,7},{5,6},{6,5},{7,4},{8,11},{9,10},{10,... | collective-permute-start | bytes 417800 | tf_op jit(solution)/shard_map/ppermute | solution.py:322
  46.0 3.4 %collective-permute-done.14.refs_1_ = bf16[544,128]{1,0:T(8,128)(2,1)S(1)} collective-permute-done((bf16[544,128]{1,0:T(8,128)(2,1)S(1)}, bf16[544,128]{1,0:T(8,128)(2,1)S(1)}, u32[]{:S(2)}, u32[]{:S(2)}) %collective-permute-start.14) | collective-permute-done | bytes 139296 | tf_op jit(solution)/shard_map/ppermute | solution.py:322
  49.3 2.4 %collective-permute-start.19 = (bf16[128,128]{1,0:T(8,128)(2,1)S(1)}, bf16[128,128]{1,0:T(8,128)(2,1)S(1)}, u32[]{:S(2)}, u32[]{:S(2)}) collective-permute-start(bf16[128,128]{1,0:T(8,128)(2,1)S(1)} %get-tuple-element.71), channel_id=1, source_target_pairs={{0,24},{4,28},{8,16},{12,20},{16,8},{20,12},{24,0},{28,4},{1,25},{... | collective-permute-start | bytes 98312 | tf_op jit(solution)/shard_map/ppermute | solution.py:322
  52.8 1.4 %collective-permute-done.19.refs_3_ = bf16[128,128]{1,0:T(8,128)(2,1)S(1)} collective-permute-done((bf16[128,128]{1,0:T(8,128)(2,1)S(1)}, bf16[128,128]{1,0:T(8,128)(2,1)S(1)}, u32[]{:S(2)}, u32[]{:S(2)}) %collective-permute-start.19) | collective-permute-done | bytes 32800 | tf_op jit(solution)/shard_map/ppermute | solution.py:322
  54.2 1.4 %collective-permute-done.17.refs_1_ = bf16[128,128]{1,0:T(8,128)(2,1)S(1)} collective-permute-done((bf16[128,128]{1,0:T(8,128)(2,1)S(1)}, bf16[128,128]{1,0:T(8,128)(2,1)S(1)}, u32[]{:S(2)}, u32[]{:S(2)}) %collective-permute-start.17) | collective-permute-done | bytes 32800 | tf_op jit(solution)/shard_map/ppermute | solution.py:322
  56.2 2.6 %collective-permute-start.22 = (bf16[128,128]{1,0:T(8,128)(2,1)S(1)}, bf16[128,128]{1,0:T(8,128)(2,1)S(1)}, u32[]{:S(2)}, u32[]{:S(2)}) collective-permute-start(bf16[128,128]{1,0:T(8,128)(2,1)S(1)} %shard_map.103.refs_0_), channel_id=1, source_target_pairs={{0,3},{1,2},{2,1},{3,0},{4,7},{5,6},{6,5},{7,4},{8,11},{9,10},{10,... | collective-permute-start | bytes 98312 | tf_op jit(solution)/shard_map/ppermute | solution.py:322
  58.8 1.9 %collective-permute-start.20 = (bf16[128,128]{1,0:T(8,128)(2,1)S(1)}, bf16[128,128]{1,0:T(8,128)(2,1)S(1)}, u32[]{:S(2)}, u32[]{:S(2)}) collective-permute-start(bf16[128,128]{1,0:T(8,128)(2,1)S(1)} %shard_map.103.refs_0_), channel_id=1, source_target_pairs={{0,1},{1,0},{2,3},{3,2},{4,5},{5,4},{6,7},{7,6},{8,9},{9,8},{10,11... | collective-permute-start | bytes 98312 | tf_op jit(solution)/shard_map/ppermute | solution.py:322
  60.7 0.9 %shard_map.102 = (bf16[2048,128]{1,0:T(8,128)(2,1)}, f32[16,128]{1,0:T(8,128)}) custom-call(bf16[544,128]{1,0:T(8,128)(2,1)S(1)} %get-tuple-element.59.refs_0_, bf16[544,128]{1,0:T(8,128)(2,1)S(1)} %collective-permute-done.14.refs_1_, bf16[544,128]{1,0:T(8,128)(2,1)S(1)} %collective-permute-done.15.refs_2_, bf16[544,128]{1,0:T(8,128)(2,1)S(1)} %collective-permute-done.16.refs_3_), custom_call_target="tpu_custom_call" | custom-call | tf_op jit(solution)/shard_map/pallas_call | solution.py:30
  62.4 1.3 %collective-permute-done.21.refs_2_ = bf16[128,128]{1,0:T(8,128)(2,1)S(1)} collective-permute-done((bf16[128,128]{1,0:T(8,128)(2,1)S(1)}, bf16[128,128]{1,0:T(8,128)(2,1)S(1)}, u32[]{:S(2)}, u32[]{:S(2)}) %collective-permute-start.21) | collective-permute-done | bytes 32800 | tf_op jit(solution)/shard_map/ppermute | solution.py:322
  (51 shorter events, 10.4 us)
Async XLA Ops:
  2.4 8.5 %collective-permute-start = (bf16[128,704]{1,0:T(8,128)(2,1)S(1)}, bf16[128,704]{1,0:T(8,128)(2,1)S(1)}, u32[]{:S(2)}, u32[]{:S(2)}) collective-permute-start(bf16[128,704]{1,0:T(8,128)(2,1)S(1)} %shard_map.94.refs_0_.refs_4_), channel_id=1, source_target_pairs={{0,4},{4,0},{8,12},{12,8},{16,20},{20,16},{24,28},{28,24},{1,5},{5... | collective-permute-start | bytes 540680 | tf_op jit(solution)/shard_map/ppermute | solution.py:322
  2.9 17.0 %collective-permute-start.3 = (bf16[128,704]{1,0:T(8,128)(2,1)S(1)}, bf16[128,704]{1,0:T(8,128)(2,1)S(1)}, u32[]{:S(2)}, u32[]{:S(2)}) collective-permute-start(bf16[128,704]{1,0:T(8,128)(2,1)S(1)} %shard_map.94.refs_0_.refs_4_), channel_id=1, source_target_pairs={{0,24},{4,28},{8,16},{12,20},{16,8},{20,12},{24,0},{28,4},{1,25},{... | collective-permute-start | bytes 540680 | tf_op jit(solution)/shard_map/ppermute | solution.py:322
  6.4 13.5 %collective-permute-start.2 = (bf16[128,704]{1,0:T(8,128)(2,1)S(1)}, bf16[128,704]{1,0:T(8,128)(2,1)S(1)}, u32[]{:S(2)}, u32[]{:S(2)}) collective-permute-start(bf16[128,704]{1,0:T(8,128)(2,1)S(1)} %shard_map.94.refs_0_.refs_4_), channel_id=1, source_target_pairs={{0,16},{4,20},{8,24},{12,28},{16,0},{20,4},{24,8},{28,12},{1,17},{... | collective-permute-start | bytes 540680 | tf_op jit(solution)/shard_map/ppermute | solution.py:322
  7.0 13.0 %collective-permute-start.1 = (bf16[128,704]{1,0:T(8,128)(2,1)S(1)}, bf16[128,704]{1,0:T(8,128)(2,1)S(1)}, u32[]{:S(2)}, u32[]{:S(2)}) collective-permute-start(bf16[128,704]{1,0:T(8,128)(2,1)S(1)} %shard_map.94.refs_0_.refs_4_), channel_id=1, source_target_pairs={{0,8},{4,12},{8,0},{12,4},{16,24},{20,28},{24,16},{28,20},{1,9},{5... | collective-permute-start | bytes 540680 | tf_op jit(solution)/shard_map/ppermute | solution.py:322
  8.9 10.3 %collective-permute-start.4 = (bf16[560,128]{1,0:T(8,128)(2,1)S(1)}, bf16[560,128]{1,0:T(8,128)(2,1)S(1)}, u32[]{:S(2)}, u32[]{:S(2)}) collective-permute-start(bf16[560,128]{1,0:T(8,128)(2,1)S(1)} %get-tuple-element.40), channel_id=1, source_target_pairs={{0,1},{1,0},{2,3},{3,2},{4,5},{5,4},{6,7},{7,6},{8,9},{9,8},{10,11... | collective-permute-start | bytes 430088 | tf_op jit(solution)/shard_map/ppermute | solution.py:322
  10.9 9.0 %collective-permute-start.5 = (bf16[560,128]{1,0:T(8,128)(2,1)S(1)}, bf16[560,128]{1,0:T(8,128)(2,1)S(1)}, u32[]{:S(2)}, u32[]{:S(2)}) collective-permute-start(bf16[560,128]{1,0:T(8,128)(2,1)S(1)} %get-tuple-element.41), channel_id=1, source_target_pairs={{0,2},{1,3},{2,0},{3,1},{4,6},{5,7},{6,4},{7,5},{8,10},{9,11},{10,... | collective-permute-start | bytes 430088 | tf_op jit(solution)/shard_map/ppermute | solution.py:322
  17.2 5.8 %copy-start.6 = (f32[128,32]{0,1:T(8,128)S(1)}, f32[128,32]{0,1:T(8,128)}, u32[]{:S(2)}) copy-start(f32[128,32]{0,1:T(8,128)} %param.9) | copy-start | bytes 49156
  19.9 3.1 %collective-permute-start.7 = (bf16[128,704]{1,0:T(8,128)(2,1)S(1)}, bf16[128,704]{1,0:T(8,128)(2,1)S(1)}, u32[]{:S(2)}, u32[]{:S(2)}) collective-permute-start(bf16[128,704]{1,0:T(8,128)(2,1)S(1)} %collective-permute-done.1.refs_0_.refs_2_.refs_6_), channel_id=1, source_target_pairs={{0,4},{4,0},{8,12},{12,8},{16,20},{20,16},{24,28},{28,24},{1,5},{5... | collective-permute-start | bytes 540680 | tf_op jit(solution)/shard_map/ppermute | solution.py:322
  20.0 3.0 %collective-permute-start.8 = (bf16[128,704]{1,0:T(8,128)(2,1)S(1)}, bf16[128,704]{1,0:T(8,128)(2,1)S(1)}, u32[]{:S(2)}, u32[]{:S(2)}) collective-permute-start(bf16[128,704]{1,0:T(8,128)(2,1)S(1)} %collective-permute-done.2.refs_2_.refs_4_.refs_8_), channel_id=1, source_target_pairs={{0,4},{4,0},{8,12},{12,8},{16,20},{20,16},{24,28},{28,24},{1,5},{5... | collective-permute-start | bytes 540680 | tf_op jit(solution)/shard_map/ppermute | solution.py:322
  20.5 12.5 %collective-permute-start.12 = (bf16[560,128]{1,0:T(8,128)(2,1)S(1)}, bf16[560,128]{1,0:T(8,128)(2,1)S(1)}, u32[]{:S(2)}, u32[]{:S(2)}) collective-permute-start(bf16[560,128]{1,0:T(8,128)(2,1)S(1)} %get-tuple-element.55), channel_id=1, source_target_pairs={{0,3},{1,2},{2,1},{3,0},{4,7},{5,6},{6,5},{7,4},{8,11},{9,10},{10,... | collective-permute-start | bytes 430088 | tf_op jit(solution)/shard_map/ppermute | solution.py:322
  23.0 3.6 %collective-permute-start.6 = (bf16[128,704]{1,0:T(8,128)(2,1)S(1)}, bf16[128,704]{1,0:T(8,128)(2,1)S(1)}, u32[]{:S(2)}, u32[]{:S(2)}) collective-permute-start(bf16[128,704]{1,0:T(8,128)(2,1)S(1)} %collective-permute-done.3.refs_0_.refs_6_.refs_10_), channel_id=1, source_target_pairs={{0,4},{4,0},{8,12},{12,8},{16,20},{20,16},{24,28},{28,24},{1,5},{5... | collective-permute-start | bytes 540680 | tf_op jit(solution)/shard_map/ppermute | solution.py:322
  28.6 6.4 %collective-permute-start.9 = (bf16[32,1024]{1,0:T(8,128)(2,1)S(1)}, bf16[32,1024]{1,0:T(8,128)(2,1)S(1)}, u32[]{:S(2)}, u32[]{:S(2)}) collective-permute-start(bf16[32,1024]{1,0:T(8,128)(2,1)S(1)} %get-tuple-element.48), channel_id=1, source_target_pairs={{0,1},{1,0},{2,3},{3,2},{4,5},{5,4},{6,7},{7,6},{8,9},{9,8},{10,11... | collective-permute-start | bytes 196616 | tf_op jit(solution)/shard_map/ppermute | solution.py:322
  28.7 8.7 %collective-permute-start.10 = (bf16[32,1024]{1,0:T(8,128)(2,1)S(1)}, bf16[32,1024]{1,0:T(8,128)(2,1)S(1)}, u32[]{:S(2)}, u32[]{:S(2)}) collective-permute-start(bf16[32,1024]{1,0:T(8,128)(2,1)S(1)} %get-tuple-element.49), channel_id=1, source_target_pairs={{0,2},{1,3},{2,0},{3,1},{4,6},{5,7},{6,4},{7,5},{8,10},{9,11},{10,... | collective-permute-start | bytes 196616 | tf_op jit(solution)/shard_map/ppermute | solution.py:322
  30.6 6.8 %collective-permute-start.11 = (bf16[32,1024]{1,0:T(8,128)(2,1)S(1)}, bf16[32,1024]{1,0:T(8,128)(2,1)S(1)}, u32[]{:S(2)}, u32[]{:S(2)}) collective-permute-start(bf16[32,1024]{1,0:T(8,128)(2,1)S(1)} %get-tuple-element.50), channel_id=1, source_target_pairs={{0,3},{1,2},{2,1},{3,0},{4,7},{5,6},{6,5},{7,4},{8,11},{9,10},{10,... | collective-permute-start | bytes 196616 | tf_op jit(solution)/shard_map/ppermute | solution.py:322
  41.4 4.5 %collective-permute-start.13 = (f32[512,128]{1,0:T(8,128)S(1)}, f32[512,128]{1,0:T(8,128)S(1)}, u32[]{:S(2)}, u32[]{:S(2)}) collective-permute-start(f32[512,128]{1,0:T(8,128)S(1)} %get-tuple-element.61), channel_id=1, source_target_pairs={{0,4},{4,0},{8,12},{12,8},{16,20},{20,16},{24,28},{28,24},{1,5},{5... | collective-permute-start | bytes 786440 | tf_op jit(solution)/shard_map/ppermute | solution.py:322
  41.5 7.9 %collective-permute-start.14 = (bf16[544,128]{1,0:T(8,128)(2,1)S(1)}, bf16[544,128]{1,0:T(8,128)(2,1)S(1)}, u32[]{:S(2)}, u32[]{:S(2)}) collective-permute-start(bf16[544,128]{1,0:T(8,128)(2,1)S(1)} %get-tuple-element.63), channel_id=1, source_target_pairs={{0,1},{1,0},{2,3},{3,2},{4,5},{5,4},{6,7},{7,6},{8,9},{9,8},{10,11... | collective-permute-start | bytes 417800 | tf_op jit(solution)/shard_map/ppermute | solution.py:322
  43.1 17.6 %collective-permute-start.15 = (bf16[544,128]{1,0:T(8,128)(2,1)S(1)}, bf16[544,128]{1,0:T(8,128)(2,1)S(1)}, u32[]{:S(2)}, u32[]{:S(2)}) collective-permute-start(bf16[544,128]{1,0:T(8,128)(2,1)S(1)} %get-tuple-element.65), channel_id=1, source_target_pairs={{0,2},{1,3},{2,0},{3,1},{4,6},{5,7},{6,4},{7,5},{8,10},{9,11},{10,... | collective-permute-start | bytes 417800 | tf_op jit(solution)/shard_map/ppermute | solution.py:322
  43.9 16.8 %collective-permute-start.16 = (bf16[544,128]{1,0:T(8,128)(2,1)S(1)}, bf16[544,128]{1,0:T(8,128)(2,1)S(1)}, u32[]{:S(2)}, u32[]{:S(2)}) collective-permute-start(bf16[544,128]{1,0:T(8,128)(2,1)S(1)} %get-tuple-element.66), channel_id=1, source_target_pairs={{0,3},{1,2},{2,1},{3,0},{4,7},{5,6},{6,5},{7,4},{8,11},{9,10},{10,... | collective-permute-start | bytes 417800 | tf_op jit(solution)/shard_map/ppermute | solution.py:322
  49.3 4.9 %collective-permute-start.19 = (bf16[128,128]{1,0:T(8,128)(2,1)S(1)}, bf16[128,128]{1,0:T(8,128)(2,1)S(1)}, u32[]{:S(2)}, u32[]{:S(2)}) collective-permute-start(bf16[128,128]{1,0:T(8,128)(2,1)S(1)} %get-tuple-element.71), channel_id=1, source_target_pairs={{0,24},{4,28},{8,16},{12,20},{16,8},{20,12},{24,0},{28,4},{1,25},{... | collective-permute-start | bytes 98312 | tf_op jit(solution)/shard_map/ppermute | solution.py:322
  51.8 3.9 %collective-permute-start.17 = (bf16[128,128]{1,0:T(8,128)(2,1)S(1)}, bf16[128,128]{1,0:T(8,128)(2,1)S(1)}, u32[]{:S(2)}, u32[]{:S(2)}) collective-permute-start(bf16[128,128]{1,0:T(8,128)(2,1)S(1)} %get-tuple-element.69), channel_id=1, source_target_pairs={{0,8},{4,12},{8,0},{12,4},{16,24},{20,28},{24,16},{28,20},{1,9},{5... | collective-permute-start | bytes 98312 | tf_op jit(solution)/shard_map/ppermute | solution.py:322
  52.3 3.9 %collective-permute-start.18 = (bf16[128,128]{1,0:T(8,128)(2,1)S(1)}, bf16[128,128]{1,0:T(8,128)(2,1)S(1)}, u32[]{:S(2)}, u32[]{:S(2)}) collective-permute-start(bf16[128,128]{1,0:T(8,128)(2,1)S(1)} %get-tuple-element.70), channel_id=1, source_target_pairs={{0,16},{4,20},{8,24},{12,28},{16,0},{20,4},{24,8},{28,12},{1,17},{... | collective-permute-start | bytes 98312 | tf_op jit(solution)/shard_map/ppermute | solution.py:322
  56.2 6.1 %collective-permute-start.22 = (bf16[128,128]{1,0:T(8,128)(2,1)S(1)}, bf16[128,128]{1,0:T(8,128)(2,1)S(1)}, u32[]{:S(2)}, u32[]{:S(2)}) collective-permute-start(bf16[128,128]{1,0:T(8,128)(2,1)S(1)} %shard_map.103.refs_0_), channel_id=1, source_target_pairs={{0,3},{1,2},{2,1},{3,0},{4,7},{5,6},{6,5},{7,4},{8,11},{9,10},{10,... | collective-permute-start | bytes 98312 | tf_op jit(solution)/shard_map/ppermute | solution.py:322
  58.8 4.8 %collective-permute-start.21 = (bf16[128,128]{1,0:T(8,128)(2,1)S(1)}, bf16[128,128]{1,0:T(8,128)(2,1)S(1)}, u32[]{:S(2)}, u32[]{:S(2)}) collective-permute-start(bf16[128,128]{1,0:T(8,128)(2,1)S(1)} %shard_map.103.refs_0_), channel_id=1, source_target_pairs={{0,2},{1,3},{2,0},{3,1},{4,6},{5,7},{6,4},{7,5},{8,10},{9,11},{10,... | collective-permute-start | bytes 98312 | tf_op jit(solution)/shard_map/ppermute | solution.py:322
  58.8 4.8 %collective-permute-start.20 = (bf16[128,128]{1,0:T(8,128)(2,1)S(1)}, bf16[128,128]{1,0:T(8,128)(2,1)S(1)}, u32[]{:S(2)}, u32[]{:S(2)}) collective-permute-start(bf16[128,128]{1,0:T(8,128)(2,1)S(1)} %shard_map.103.refs_0_), channel_id=1, source_target_pairs={{0,1},{1,0},{2,3},{3,2},{4,5},{5,4},{6,7},{7,6},{8,9},{9,8},{10,11... | collective-permute-start | bytes 98312 | tf_op jit(solution)/shard_map/ppermute | solution.py:322
  (8 other events, 12.9 us)

commit v8 on v4

--- a/solution.py
+++ b/solution.py
@@ -11,6 +11,7 @@
 log2e = 1.4426950408889634
 very_low = -1e30
 LANES = 128
+FILL = 10
 TAIL = 16
 f32, bf16 = jnp.float32, jnp.bfloat16
 
@@ -366,7 +367,7 @@
             ],
             specs,
             pl.CostEstimate(
-                flops=2 * span * rows * head_count * width,
+                flops=2 * span * rows * head_count * width * (FILL if rels is chunks[0] else 1),
                 bytes_accessed=2 * rows * head_count * width,
                 transcendentals=span * rows * head_count,
             ),
@@ -374,8 +375,9 @@
         mass = found if last else mass + found
         if rels is chunks[0]:
             even = list(range(2, blocks, 2))
-            ready = lax.optimization_barrier((found[0], [held[k] for k in even]))
+            ready = lax.optimization_barrier((found[0], [held[k] for k in even], asked[1:3]))
             mass = [ready[0]]
+            asked[1:3] = ready[2]
             for k, block in zip(even, ready[1]):
                 held[k] = block
                 held[k + 1] = swap(block, "pb", 1)

time: 64.8 us -> 62.6 us (0.966)
  waiting for transfers between devices: 14.5 us -> 7.91 us
  starting transfers between devices: 26.9 us -> 31.3 us
    ppermute x23, waiting for transfers between devices: 14.5 us -> 7.91 us  [swap(): return lax.ppermute(value, axis, [(i, i ^ rel) for i in range(size)])]
    ppermute x23, starting transfers between devices: 26.9 us -> 31.3 us  [swap(): return lax.ppermute(value, axis, [(i, i ^ rel) for i in range(size)])]
    unnamed x20 -> x18, local copies, waits for them, and re-layouts: 7.12 us -> 7.11 us
  transfers between devices with their start and end apart: 23 -> 23, of which waited for: 8 -> 6; matrix products, arithmetic and copies ran while one was open for 0% -> 0% of each run, Pallas kernels for 16% -> 17%
where the time goes in v8:
time: 62.6 us; the launch traced here: 62.2 us
  starting transfers between devices  31.3 us (50%)
  Pallas kernels  15.1 us (24%)
  waiting for transfers between devices  7.91 us (13%)
  local copies, waits for them, and re-layouts  7.11 us (11%)
  between operations  0.78 us (1%)
    ppermute x23, starting transfers between devices, swap(): return lax.ppermute(value, axis, [(i, i ^ rel) for i in range(size)])  31.3 us
    pallas_call x11, Pallas kernels, call(): pl.pallas_call(kernel, grid=(1,), out_shape=outs, in_specs=specs or [whol...  15.1 us
    ppermute x23, waiting for transfers between devices, swap(): return lax.ppermute(value, axis, [(i, i ^ rel) for i in range(size)])  7.91 us
    unnamed x18, local copies, waits for them, and re-layouts  7.11 us
  transfers between devices with their start and end apart: 23, of which 6 were waited for; matrix products, arithmetic and copies ran while one was open for 0% of the time, Pallas kernels for 17%

profile of v8, /device:TPU:0, one launch (start us, length us, event | category | flops | bytes accessed | tf_op | source)
XLA Modules:
  0.0 62.2 jit_solution(8769771559991402975)
XLA Ops:
  2.9 3.5 %collective-permute-start.3 = (bf16[128,704]{1,0:T(8,128)(2,1)S(1)}, bf16[128,704]{1,0:T(8,128)(2,1)S(1)}, u32[]{:S(2)}, u32[]{:S(2)}) collective-permute-start(bf16[128,704]{1,0:T(8,128)(2,1)S(1)} %shard_map.94.refs_0_.refs_4_), channel_id=1, source_target_pairs={{0,24},{4,28},{8,16},{12,20},{16,8},{20,12},{24,0},{28,4},{1,25},{... | collective-permute-start | bytes 540680 | tf_op jit(solution)/shard_map/ppermute | solution.py:322
  7.1 1.0 %copy-done.2 = bf16[128,16,128]{2,1,0:T(8,128)(2,1)S(1)} copy-done((bf16[128,16,128]{2,1,0:T(8,128)(2,1)S(1)}, bf16[128,16,128]{2,1,0:T(8,128)(2,1)}, u32[]{:S(2)}) %copy-start.2) | copy-done | bytes 524312
  8.9 2.0 %collective-permute-start.4 = (bf16[560,128]{1,0:T(8,128)(2,1)S(1)}, bf16[560,128]{1,0:T(8,128)(2,1)S(1)}, u32[]{:S(2)}, u32[]{:S(2)}) collective-permute-start(bf16[560,128]{1,0:T(8,128)(2,1)S(1)} %get-tuple-element.38), channel_id=1, source_target_pairs={{0,1},{1,0},{2,3},{3,2},{4,5},{5,4},{6,7},{7,6},{8,9},{9,8},{10,11... | collective-permute-start | bytes 430088 | tf_op jit(solution)/shard_map/ppermute | solution.py:322
  10.9 2.6 %collective-permute-start.5 = (bf16[560,128]{1,0:T(8,128)(2,1)S(1)}, bf16[560,128]{1,0:T(8,128)(2,1)S(1)}, u32[]{:S(2)}, u32[]{:S(2)}) collective-permute-start(bf16[560,128]{1,0:T(8,128)(2,1)S(1)} %get-tuple-element.39), channel_id=1, source_target_pairs={{0,2},{1,3},{2,0},{3,1},{4,6},{5,7},{6,4},{7,5},{8,10},{9,11},{10,... | collective-permute-start | bytes 430088 | tf_op jit(solution)/shard_map/ppermute | solution.py:322
  13.5 2.3 %copy-done = bf16[128,32,576]{0,2,1:T(8,128)(2,1)S(1)} copy-done((bf16[128,32,576]{0,2,1:T(8,128)(2,1)S(1)}, bf16[128,32,576]{0,2,1:T(8,128)(2,1)}, u32[]{:S(2)}) %copy-start) | copy-done | bytes 4718616
  17.2 1.9 %shard_map.96.refs_5_ = bf16[128,256]{1,0:T(8,128)(2,1)S(1)} custom-call(bf16[128,704]{1,0:T(8,128)(2,1)S(1)} %shard_map.94.refs_0_.refs_4_, bf16[128,704]{1,0:T(8,128)(2,1)S(1)} %collective-permute-done.refs_1_.refs_5_, bf16[32,576,128]{2,1,0:T(8,128)(2,1)S(1)} %bitcast.8, f32[32,128]{1,0:T(8,128)S(1)} %bitcast.13, s32[1,128]{1,0:T(1,128)S(1)} %bitcast.17), custom_call_target="tpu_custom_call" | custom-call | flops 12079595520 | bytes 4718592 | tf_op jit(solution)/shard_map/pallas_call | solution.py:30
  20.5 2.5 %collective-permute-start.12 = (bf16[560,128]{1,0:T(8,128)(2,1)S(1)}, bf16[560,128]{1,0:T(8,128)(2,1)S(1)}, u32[]{:S(2)}, u32[]{:S(2)}) collective-permute-start(bf16[560,128]{1,0:T(8,128)(2,1)S(1)} %get-tuple-element.53), channel_id=1, source_target_pairs={{0,3},{1,2},{2,1},{3,0},{4,7},{5,6},{6,5},{7,4},{8,11},{9,10},{10,... | collective-permute-start | bytes 430088 | tf_op jit(solution)/shard_map/ppermute | solution.py:322
  23.0 3.6 %shard_map.97.refs_6_ = bf16[128,512]{1,0:T(8,128)(2,1)S(1)} custom-call(bf16[128,704]{1,0:T(8,128)(2,1)S(1)} %collective-permute-done.1.refs_0_.refs_2_.refs_6_, bf16[128,704]{1,0:T(8,128)(2,1)S(1)} %collective-permute-done.7.refs_1_.refs_3_.refs_7_, bf16[128,704]{1,0:T(8,128)(2,1)S(1)} %collective-permute-done.2.refs_2_.refs_4_.refs_8_, ...), custom_call_target="tpu_custom_call" | custom-call | flops 2415919104 | bytes 4718592 | tf_op jit(solution)/shard_map/pallas_call | solution.py:30
  26.6 1.9 %shard_map.98 = (bf16[32,1024]{1,0:T(8,128)(2,1)S(1)}, bf16[32,1024]{1,0:T(8,128)(2,1)S(1)}, bf16[32,1024]{1,0:T(8,128)(2,1)S(1)}, bf16[32,1024]{1,0:T(8,128)(2,1)S(1)}) custom-call(bf16[128,704]{1,0:T(8,128)(2,1)S(1)} %collective-permute-done.3.refs_0_.refs_6_.refs_10_, bf16[128,704]{1,0:T(8,128)(2,1)S(1)} %collective-permute-done.6.refs_1_.refs_7_.refs_11_, ...), custom_call_target="tpu_custom_call" | custom-call | flops 1207959552 | bytes 4718592 | tf_op jit(solution)/shard_map/pallas_call | solution.py:30
  28.7 1.9 %collective-permute-start.10 = (bf16[32,1024]{1,0:T(8,128)(2,1)S(1)}, bf16[32,1024]{1,0:T(8,128)(2,1)S(1)}, u32[]{:S(2)}, u32[]{:S(2)}) collective-permute-start(bf16[32,1024]{1,0:T(8,128)(2,1)S(1)} %get-tuple-element.47), channel_id=1, source_target_pairs={{0,2},{1,3},{2,0},{3,1},{4,6},{5,7},{6,4},{7,5},{8,10},{9,11},{10,... | collective-permute-start | bytes 196616 | tf_op jit(solution)/shard_map/ppermute | solution.py:322
  30.6 2.5 %collective-permute-start.11 = (bf16[32,1024]{1,0:T(8,128)(2,1)S(1)}, bf16[32,1024]{1,0:T(8,128)(2,1)S(1)}, u32[]{:S(2)}, u32[]{:S(2)}) collective-permute-start(bf16[32,1024]{1,0:T(8,128)(2,1)S(1)} %get-tuple-element.48), channel_id=1, source_target_pairs={{0,3},{1,2},{2,1},{3,0},{4,7},{5,6},{6,5},{7,4},{8,11},{9,10},{10,... | collective-permute-start | bytes 196616 | tf_op jit(solution)/shard_map/ppermute | solution.py:322
  33.0 1.9 %shard_map.99 = (f32[1024,128]{1,0:T(8,128)S(1)}, bf16[2048,128]{1,0:T(8,128)(2,1)S(1)}, f32[16,128]{1,0:T(8,128)S(1)}) custom-call(bf16[128,704]{1,0:T(8,128)(2,1)S(1)} %shard_map.94.refs_0_.refs_4_, bf16[128,704]{1,0:T(8,128)(2,1)S(1)} %collective-permute-done.refs_1_.refs_5_, bf16[128,704]{1,0:T(8,128)(2,1)S(1)} %collective-permute-done.1.refs_0_.refs_2_.refs_6_, ...), custom_call_target="tpu_custom_call" | custom-call | flops 536870912 | bytes 524288 | tf_op jit(solution)/shard_map/pallas_call | solution.py:30
  35.0 2.4 %collective-permute-done.10.refs_2_ = bf16[32,1024]{1,0:T(8,128)(2,1)S(1)} collective-permute-done((bf16[32,1024]{1,0:T(8,128)(2,1)S(1)}, bf16[32,1024]{1,0:T(8,128)(2,1)S(1)}, u32[]{:S(2)}, u32[]{:S(2)}) %collective-permute-start.10) | collective-permute-done | bytes 65568 | tf_op jit(solution)/shard_map/ppermute | solution.py:322
  37.4 4.0 %shard_map.100 = (f32[512,128]{1,0:T(8,128)S(1)}, f32[512,128]{1,0:T(8,128)S(1)}, bf16[544,128]{1,0:T(8,128)(2,1)S(1)}, bf16[544,128]{1,0:T(8,128)(2,1)S(1)}, bf...) custom-call(bf16[32,1024]{1,0:T(8,128)(2,1)S(1)} %get-tuple-element.45.refs_0_, ...), custom_call_target="tpu_custom_call" | custom-call | flops 1610612736 | bytes 524288 | tf_op jit(solution)/shard_map/pallas_call | solution.py:30
  41.5 1.6 %collective-permute-start.13 = (bf16[544,128]{1,0:T(8,128)(2,1)S(1)}, bf16[544,128]{1,0:T(8,128)(2,1)S(1)}, u32[]{:S(2)}, u32[]{:S(2)}) collective-permute-start(bf16[544,128]{1,0:T(8,128)(2,1)S(1)} %get-tuple-element.58), channel_id=1, source_target_pairs={{0,1},{1,0},{2,3},{3,2},{4,5},{5,4},{6,7},{7,6},{8,9},{9,8},{10,11... | collective-permute-start | bytes 417800 | tf_op jit(solution)/shard_map/ppermute | solution.py:322
  43.9 2.0 %collective-permute-start.15 = (bf16[544,128]{1,0:T(8,128)(2,1)S(1)}, bf16[544,128]{1,0:T(8,128)(2,1)S(1)}, u32[]{:S(2)}, u32[]{:S(2)}) collective-permute-start(bf16[544,128]{1,0:T(8,128)(2,1)S(1)} %get-tuple-element.60), channel_id=1, source_target_pairs={{0,3},{1,2},{2,1},{3,0},{4,7},{5,6},{6,5},{7,4},{8,11},{9,10},{10,... | collective-permute-start | bytes 417800 | tf_op jit(solution)/shard_map/ppermute | solution.py:322
  46.0 1.6 %collective-permute-start.17 = (bf16[128,128]{1,0:T(8,128)(2,1)S(1)}, bf16[128,128]{1,0:T(8,128)(2,1)S(1)}, u32[]{:S(2)}, u32[]{:S(2)}) collective-permute-start(bf16[128,128]{1,0:T(8,128)(2,1)S(1)} %get-tuple-element.65), channel_id=1, source_target_pairs={{0,8},{4,12},{8,0},{12,4},{16,24},{20,28},{24,16},{28,20},{1,9},{5... | collective-permute-start | bytes 98312 | tf_op jit(solution)/shard_map/ppermute | solution.py:322
  47.5 1.5 %collective-permute-start.18 = (bf16[128,128]{1,0:T(8,128)(2,1)S(1)}, bf16[128,128]{1,0:T(8,128)(2,1)S(1)}, u32[]{:S(2)}, u32[]{:S(2)}) collective-permute-start(bf16[128,128]{1,0:T(8,128)(2,1)S(1)} %get-tuple-element.66), channel_id=1, source_target_pairs={{0,16},{4,20},{8,24},{12,28},{16,0},{20,4},{24,8},{28,12},{1,17},{... | collective-permute-start | bytes 98312 | tf_op jit(solution)/shard_map/ppermute | solution.py:322
  49.0 0.9 %collective-permute-done.17.refs_1_ = bf16[128,128]{1,0:T(8,128)(2,1)S(1)} collective-permute-done((bf16[128,128]{1,0:T(8,128)(2,1)S(1)}, bf16[128,128]{1,0:T(8,128)(2,1)S(1)}, u32[]{:S(2)}, u32[]{:S(2)}) %collective-permute-start.17) | collective-permute-done | bytes 32800 | tf_op jit(solution)/shard_map/ppermute | solution.py:322
  49.9 2.4 %collective-permute-start.19 = (bf16[128,128]{1,0:T(8,128)(2,1)S(1)}, bf16[128,128]{1,0:T(8,128)(2,1)S(1)}, u32[]{:S(2)}, u32[]{:S(2)}) collective-permute-start(bf16[128,128]{1,0:T(8,128)(2,1)S(1)} %get-tuple-element.67), channel_id=1, source_target_pairs={{0,24},{4,28},{8,16},{12,20},{16,8},{20,12},{24,0},{28,4},{1,25},{... | collective-permute-start | bytes 98312 | tf_op jit(solution)/shard_map/ppermute | solution.py:322
  52.4 2.4 %collective-permute-done.19.refs_3_ = bf16[128,128]{1,0:T(8,128)(2,1)S(1)} collective-permute-done((bf16[128,128]{1,0:T(8,128)(2,1)S(1)}, bf16[128,128]{1,0:T(8,128)(2,1)S(1)}, u32[]{:S(2)}, u32[]{:S(2)}) %collective-permute-start.19) | collective-permute-done | bytes 32800 | tf_op jit(solution)/shard_map/ppermute | solution.py:322
  54.8 1.8 %collective-permute-start.22 = (bf16[128,128]{1,0:T(8,128)(2,1)S(1)}, bf16[128,128]{1,0:T(8,128)(2,1)S(1)}, u32[]{:S(2)}, u32[]{:S(2)}) collective-permute-start(bf16[128,128]{1,0:T(8,128)(2,1)S(1)} %shard_map.103.refs_0_), channel_id=1, source_target_pairs={{0,3},{1,2},{2,1},{3,0},{4,7},{5,6},{6,5},{7,4},{8,11},{9,10},{10,... | collective-permute-start | bytes 98312 | tf_op jit(solution)/shard_map/ppermute | solution.py:322
  57.0 2.3 %collective-permute-start.20 = (bf16[128,128]{1,0:T(8,128)(2,1)S(1)}, bf16[128,128]{1,0:T(8,128)(2,1)S(1)}, u32[]{:S(2)}, u32[]{:S(2)}) collective-permute-start(bf16[128,128]{1,0:T(8,128)(2,1)S(1)} %shard_map.103.refs_0_), channel_id=1, source_target_pairs={{0,1},{1,0},{2,3},{3,2},{4,5},{5,4},{6,7},{7,6},{8,9},{9,8},{10,11... | collective-permute-start | bytes 98312 | tf_op jit(solution)/shard_map/ppermute | solution.py:322
  59.2 0.9 %shard_map.101 = (bf16[2048,128]{1,0:T(8,128)(2,1)}, f32[16,128]{1,0:T(8,128)}) custom-call(bf16[544,128]{1,0:T(8,128)(2,1)S(1)} %get-tuple-element.57.refs_0_, bf16[544,128]{1,0:T(8,128)(2,1)S(1)} %collective-permute-done.13.refs_1_, bf16[544,128]{1,0:T(8,128)(2,1)S(1)} %collective-permute-done.14.refs_2_, bf16[544,128]{1,0:T(8,128)(2,1)S(1)} %collective-permute-done.15.refs_3_), custom_call_target="tpu_custom_call" | custom-call | tf_op jit(solution)/shard_map/pallas_call | solution.py:30
  (51 shorter events, 9.8 us)
Async XLA Ops:
  2.4 8.5 %collective-permute-start = (bf16[128,704]{1,0:T(8,128)(2,1)S(1)}, bf16[128,704]{1,0:T(8,128)(2,1)S(1)}, u32[]{:S(2)}, u32[]{:S(2)}) collective-permute-start(bf16[128,704]{1,0:T(8,128)(2,1)S(1)} %shard_map.94.refs_0_.refs_4_), channel_id=1, source_target_pairs={{0,4},{4,0},{8,12},{12,8},{16,20},{20,16},{24,28},{28,24},{1,5},{5... | collective-permute-start | bytes 540680 | tf_op jit(solution)/shard_map/ppermute | solution.py:322
  2.9 17.0 %collective-permute-start.3 = (bf16[128,704]{1,0:T(8,128)(2,1)S(1)}, bf16[128,704]{1,0:T(8,128)(2,1)S(1)}, u32[]{:S(2)}, u32[]{:S(2)}) collective-permute-start(bf16[128,704]{1,0:T(8,128)(2,1)S(1)} %shard_map.94.refs_0_.refs_4_), channel_id=1, source_target_pairs={{0,24},{4,28},{8,16},{12,20},{16,8},{20,12},{24,0},{28,4},{1,25},{... | collective-permute-start | bytes 540680 | tf_op jit(solution)/shard_map/ppermute | solution.py:322
  6.4 13.5 %collective-permute-start.2 = (bf16[128,704]{1,0:T(8,128)(2,1)S(1)}, bf16[128,704]{1,0:T(8,128)(2,1)S(1)}, u32[]{:S(2)}, u32[]{:S(2)}) collective-permute-start(bf16[128,704]{1,0:T(8,128)(2,1)S(1)} %shard_map.94.refs_0_.refs_4_), channel_id=1, source_target_pairs={{0,16},{4,20},{8,24},{12,28},{16,0},{20,4},{24,8},{28,12},{1,17},{... | collective-permute-start | bytes 540680 | tf_op jit(solution)/shard_map/ppermute | solution.py:322
  7.0 13.0 %collective-permute-start.1 = (bf16[128,704]{1,0:T(8,128)(2,1)S(1)}, bf16[128,704]{1,0:T(8,128)(2,1)S(1)}, u32[]{:S(2)}, u32[]{:S(2)}) collective-permute-start(bf16[128,704]{1,0:T(8,128)(2,1)S(1)} %shard_map.94.refs_0_.refs_4_), channel_id=1, source_target_pairs={{0,8},{4,12},{8,0},{12,4},{16,24},{20,28},{24,16},{28,20},{1,9},{5... | collective-permute-start | bytes 540680 | tf_op jit(solution)/shard_map/ppermute | solution.py:322
  8.9 10.3 %collective-permute-start.4 = (bf16[560,128]{1,0:T(8,128)(2,1)S(1)}, bf16[560,128]{1,0:T(8,128)(2,1)S(1)}, u32[]{:S(2)}, u32[]{:S(2)}) collective-permute-start(bf16[560,128]{1,0:T(8,128)(2,1)S(1)} %get-tuple-element.38), channel_id=1, source_target_pairs={{0,1},{1,0},{2,3},{3,2},{4,5},{5,4},{6,7},{7,6},{8,9},{9,8},{10,11... | collective-permute-start | bytes 430088 | tf_op jit(solution)/shard_map/ppermute | solution.py:322
  10.9 9.0 %collective-permute-start.5 = (bf16[560,128]{1,0:T(8,128)(2,1)S(1)}, bf16[560,128]{1,0:T(8,128)(2,1)S(1)}, u32[]{:S(2)}, u32[]{:S(2)}) collective-permute-start(bf16[560,128]{1,0:T(8,128)(2,1)S(1)} %get-tuple-element.39), channel_id=1, source_target_pairs={{0,2},{1,3},{2,0},{3,1},{4,6},{5,7},{6,4},{7,5},{8,10},{9,11},{10,... | collective-permute-start | bytes 430088 | tf_op jit(solution)/shard_map/ppermute | solution.py:322
  17.2 5.8 %copy-start.6 = (f32[128,32]{0,1:T(8,128)S(1)}, f32[128,32]{0,1:T(8,128)}, u32[]{:S(2)}) copy-start(f32[128,32]{0,1:T(8,128)} %param.9) | copy-start | bytes 49156
  19.9 3.1 %collective-permute-start.7 = (bf16[128,704]{1,0:T(8,128)(2,1)S(1)}, bf16[128,704]{1,0:T(8,128)(2,1)S(1)}, u32[]{:S(2)}, u32[]{:S(2)}) collective-permute-start(bf16[128,704]{1,0:T(8,128)(2,1)S(1)} %collective-permute-done.1.refs_0_.refs_2_.refs_6_), channel_id=1, source_target_pairs={{0,4},{4,0},{8,12},{12,8},{16,20},{20,16},{24,28},{28,24},{1,5},{5... | collective-permute-start | bytes 540680 | tf_op jit(solution)/shard_map/ppermute | solution.py:322
  20.0 3.0 %collective-permute-start.8 = (bf16[128,704]{1,0:T(8,128)(2,1)S(1)}, bf16[128,704]{1,0:T(8,128)(2,1)S(1)}, u32[]{:S(2)}, u32[]{:S(2)}) collective-permute-start(bf16[128,704]{1,0:T(8,128)(2,1)S(1)} %collective-permute-done.2.refs_2_.refs_4_.refs_8_), channel_id=1, source_target_pairs={{0,4},{4,0},{8,12},{12,8},{16,20},{20,16},{24,28},{28,24},{1,5},{5... | collective-permute-start | bytes 540680 | tf_op jit(solution)/shard_map/ppermute | solution.py:322
  20.5 12.5 %collective-permute-start.12 = (bf16[560,128]{1,0:T(8,128)(2,1)S(1)}, bf16[560,128]{1,0:T(8,128)(2,1)S(1)}, u32[]{:S(2)}, u32[]{:S(2)}) collective-permute-start(bf16[560,128]{1,0:T(8,128)(2,1)S(1)} %get-tuple-element.53), channel_id=1, source_target_pairs={{0,3},{1,2},{2,1},{3,0},{4,7},{5,6},{6,5},{7,4},{8,11},{9,10},{10,... | collective-permute-start | bytes 430088 | tf_op jit(solution)/shard_map/ppermute | solution.py:322
  23.0 3.6 %collective-permute-start.6 = (bf16[128,704]{1,0:T(8,128)(2,1)S(1)}, bf16[128,704]{1,0:T(8,128)(2,1)S(1)}, u32[]{:S(2)}, u32[]{:S(2)}) collective-permute-start(bf16[128,704]{1,0:T(8,128)(2,1)S(1)} %collective-permute-done.3.refs_0_.refs_6_.refs_10_), channel_id=1, source_target_pairs={{0,4},{4,0},{8,12},{12,8},{16,20},{20,16},{24,28},{28,24},{1,5},{5... | collective-permute-start | bytes 540680 | tf_op jit(solution)/shard_map/ppermute | solution.py:322
  28.6 6.4 %collective-permute-start.9 = (bf16[32,1024]{1,0:T(8,128)(2,1)S(1)}, bf16[32,1024]{1,0:T(8,128)(2,1)S(1)}, u32[]{:S(2)}, u32[]{:S(2)}) collective-permute-start(bf16[32,1024]{1,0:T(8,128)(2,1)S(1)} %get-tuple-element.46), channel_id=1, source_target_pairs={{0,1},{1,0},{2,3},{3,2},{4,5},{5,4},{6,7},{7,6},{8,9},{9,8},{10,11... | collective-permute-start | bytes 196616 | tf_op jit(solution)/shard_map/ppermute | solution.py:322
  28.7 8.7 %collective-permute-start.10 = (bf16[32,1024]{1,0:T(8,128)(2,1)S(1)}, bf16[32,1024]{1,0:T(8,128)(2,1)S(1)}, u32[]{:S(2)}, u32[]{:S(2)}) collective-permute-start(bf16[32,1024]{1,0:T(8,128)(2,1)S(1)} %get-tuple-element.47), channel_id=1, source_target_pairs={{0,2},{1,3},{2,0},{3,1},{4,6},{5,7},{6,4},{7,5},{8,10},{9,11},{10,... | collective-permute-start | bytes 196616 | tf_op jit(solution)/shard_map/ppermute | solution.py:322
  30.6 6.8 %collective-permute-start.11 = (bf16[32,1024]{1,0:T(8,128)(2,1)S(1)}, bf16[32,1024]{1,0:T(8,128)(2,1)S(1)}, u32[]{:S(2)}, u32[]{:S(2)}) collective-permute-start(bf16[32,1024]{1,0:T(8,128)(2,1)S(1)} %get-tuple-element.48), channel_id=1, source_target_pairs={{0,3},{1,2},{2,1},{3,0},{4,7},{5,6},{6,5},{7,4},{8,11},{9,10},{10,... | collective-permute-start | bytes 196616 | tf_op jit(solution)/shard_map/ppermute | solution.py:322
  41.4 4.5 %collective-permute-start.16 = (f32[512,128]{1,0:T(8,128)S(1)}, f32[512,128]{1,0:T(8,128)S(1)}, u32[]{:S(2)}, u32[]{:S(2)}) collective-permute-start(f32[512,128]{1,0:T(8,128)S(1)} %get-tuple-element.63), channel_id=1, source_target_pairs={{0,4},{4,0},{8,12},{12,8},{16,20},{20,16},{24,28},{28,24},{1,5},{5... | collective-permute-start | bytes 786440 | tf_op jit(solution)/shard_map/ppermute | solution.py:322
  41.5 15.5 %collective-permute-start.13 = (bf16[544,128]{1,0:T(8,128)(2,1)S(1)}, bf16[544,128]{1,0:T(8,128)(2,1)S(1)}, u32[]{:S(2)}, u32[]{:S(2)}) collective-permute-start(bf16[544,128]{1,0:T(8,128)(2,1)S(1)} %get-tuple-element.58), channel_id=1, source_target_pairs={{0,1},{1,0},{2,3},{3,2},{4,5},{5,4},{6,7},{7,6},{8,9},{9,8},{10,11... | collective-permute-start | bytes 417800 | tf_op jit(solution)/shard_map/ppermute | solution.py:322
  43.1 16.1 %collective-permute-start.14 = (bf16[544,128]{1,0:T(8,128)(2,1)S(1)}, bf16[544,128]{1,0:T(8,128)(2,1)S(1)}, u32[]{:S(2)}, u32[]{:S(2)}) collective-permute-start(bf16[544,128]{1,0:T(8,128)(2,1)S(1)} %get-tuple-element.59), channel_id=1, source_target_pairs={{0,2},{1,3},{2,0},{3,1},{4,6},{5,7},{6,4},{7,5},{8,10},{9,11},{10,... | collective-permute-start | bytes 417800 | tf_op jit(solution)/shard_map/ppermute | solution.py:322
  43.9 15.4 %collective-permute-start.15 = (bf16[544,128]{1,0:T(8,128)(2,1)S(1)}, bf16[544,128]{1,0:T(8,128)(2,1)S(1)}, u32[]{:S(2)}, u32[]{:S(2)}) collective-permute-start(bf16[544,128]{1,0:T(8,128)(2,1)S(1)} %get-tuple-element.60), channel_id=1, source_target_pairs={{0,3},{1,2},{2,1},{3,0},{4,7},{5,6},{6,5},{7,4},{8,11},{9,10},{10,... | collective-permute-start | bytes 417800 | tf_op jit(solution)/shard_map/ppermute | solution.py:322
  46.0 4.0 %collective-permute-start.17 = (bf16[128,128]{1,0:T(8,128)(2,1)S(1)}, bf16[128,128]{1,0:T(8,128)(2,1)S(1)}, u32[]{:S(2)}, u32[]{:S(2)}) collective-permute-start(bf16[128,128]{1,0:T(8,128)(2,1)S(1)} %get-tuple-element.65), channel_id=1, source_target_pairs={{0,8},{4,12},{8,0},{12,4},{16,24},{20,28},{24,16},{28,20},{1,9},{5... | collective-permute-start | bytes 98312 | tf_op jit(solution)/shard_map/ppermute | solution.py:322
  47.5 4.9 %collective-permute-start.18 = (bf16[128,128]{1,0:T(8,128)(2,1)S(1)}, bf16[128,128]{1,0:T(8,128)(2,1)S(1)}, u32[]{:S(2)}, u32[]{:S(2)}) collective-permute-start(bf16[128,128]{1,0:T(8,128)(2,1)S(1)} %get-tuple-element.66), channel_id=1, source_target_pairs={{0,16},{4,20},{8,24},{12,28},{16,0},{20,4},{24,8},{28,12},{1,17},{... | collective-permute-start | bytes 98312 | tf_op jit(solution)/shard_map/ppermute | solution.py:322
  49.9 4.8 %collective-permute-start.19 = (bf16[128,128]{1,0:T(8,128)(2,1)S(1)}, bf16[128,128]{1,0:T(8,128)(2,1)S(1)}, u32[]{:S(2)}, u32[]{:S(2)}) collective-permute-start(bf16[128,128]{1,0:T(8,128)(2,1)S(1)} %get-tuple-element.67), channel_id=1, source_target_pairs={{0,24},{4,28},{8,16},{12,20},{16,8},{20,12},{24,0},{28,4},{1,25},{... | collective-permute-start | bytes 98312 | tf_op jit(solution)/shard_map/ppermute | solution.py:322
  54.8 5.9 %collective-permute-start.22 = (bf16[128,128]{1,0:T(8,128)(2,1)S(1)}, bf16[128,128]{1,0:T(8,128)(2,1)S(1)}, u32[]{:S(2)}, u32[]{:S(2)}) collective-permute-start(bf16[128,128]{1,0:T(8,128)(2,1)S(1)} %shard_map.103.refs_0_), channel_id=1, source_target_pairs={{0,3},{1,2},{2,1},{3,0},{4,7},{5,6},{6,5},{7,4},{8,11},{9,10},{10,... | collective-permute-start | bytes 98312 | tf_op jit(solution)/shard_map/ppermute | solution.py:322
  56.6 4.9 %collective-permute-start.21 = (bf16[128,128]{1,0:T(8,128)(2,1)S(1)}, bf16[128,128]{1,0:T(8,128)(2,1)S(1)}, u32[]{:S(2)}, u32[]{:S(2)}) collective-permute-start(bf16[128,128]{1,0:T(8,128)(2,1)S(1)} %shard_map.103.refs_0_), channel_id=1, source_target_pairs={{0,2},{1,3},{2,0},{3,1},{4,6},{5,7},{6,4},{7,5},{8,10},{9,11},{10,... | collective-permute-start | bytes 98312 | tf_op jit(solution)/shard_map/ppermute | solution.py:322
  57.0 4.6 %collective-permute-start.20 = (bf16[128,128]{1,0:T(8,128)(2,1)S(1)}, bf16[128,128]{1,0:T(8,128)(2,1)S(1)}, u32[]{:S(2)}, u32[]{:S(2)}) collective-permute-start(bf16[128,128]{1,0:T(8,128)(2,1)S(1)} %shard_map.103.refs_0_), channel_id=1, source_target_pairs={{0,1},{1,0},{2,3},{3,2},{4,5},{5,4},{6,7},{7,6},{8,9},{9,8},{10,11... | collective-permute-start | bytes 98312 | tf_op jit(solution)/shard_map/ppermute | solution.py:322
  (8 other events, 12.9 us)

commit v9 on v8

--- a/solution.py
+++ b/solution.py
@@ -433,7 +433,9 @@
     half = shape((rows, index_width), bf16)
     mine, *others = call(pair_kernel, [term] + [half] * (blocks // 2 - 1), (even, odd))
     others = [swap(value, "pb", 2 * (i + 1)) for i, value in enumerate(others)]
-    mine = call(sum_kernel, half, [mine] + others)
+    mine, answers[1] = lax.optimization_barrier(
+        (call(sum_kernel, half, [mine] + others), answers[1])
+    )
     key_grad = call(sum_kernel, half, [mine] + [swap(mine, "ha", r) for r in range(1, parts)])
 
     answers = [answers[0]] + [swap(answers[r], "ha", r) for r in range(1, parts)]

time: 62.6 us -> 68.2 us (1.089)
  waiting for transfers between devices: 7.91 us -> 13.1 us
    ppermute x23, waiting for transfers between devices: 7.91 us -> 13.1 us  [swap(): return lax.ppermute(value, axis, [(i, i ^ rel) for i in range(size)])]
  transfers between devices with their start and end apart: 23 -> 23, of which waited for: 6 -> 6; matrix products, arithmetic and copies ran while one was open for 0% -> 0% of each run, Pallas kernels for 17% -> 15%
where the time goes in v9:
time: 68.2 us; the launch traced here: 67.8 us
  starting transfers between devices  31.7 us (46%)
  Pallas kernels  15.1 us (22%)
  waiting for transfers between devices  13.1 us (19%)
  local copies, waits for them, and re-layouts  7.11 us (10%)
  between operations  0.79 us (1%)
    ppermute x23, starting transfers between devices, swap(): return lax.ppermute(value, axis, [(i, i ^ rel) for i in range(size)])  31.7 us
    pallas_call x11, Pallas kernels, call(): pl.pallas_call(kernel, grid=(1,), out_shape=outs, in_specs=specs or [whol...  15.1 us
    ppermute x23, waiting for transfers between devices, swap(): return lax.ppermute(value, axis, [(i, i ^ rel) for i in range(size)])  13.1 us
    unnamed x18, local copies, waits for them, and re-layouts  7.11 us
  transfers between devices with their start and end apart: 23, of which 6 were waited for; matrix products, arithmetic and copies ran while one was open for 0% of the time, Pallas kernels for 15%

profile of v9, /device:TPU:0, one launch (start us, length us, event | category | flops | bytes accessed | tf_op | source)
XLA Modules:
  0.0 67.8 jit_solution(14935314602654153506)
XLA Ops:
  2.9 3.5 %collective-permute-start.3 = (bf16[128,704]{1,0:T(8,128)(2,1)S(1)}, bf16[128,704]{1,0:T(8,128)(2,1)S(1)}, u32[]{:S(2)}, u32[]{:S(2)}) collective-permute-start(bf16[128,704]{1,0:T(8,128)(2,1)S(1)} %shard_map.94.refs_0_.refs_4_), channel_id=1, source_target_pairs={{0,24},{4,28},{8,16},{12,20},{16,8},{20,12},{24,0},{28,4},{1,25},{... | collective-permute-start | bytes 540680 | tf_op jit(solution)/shard_map/ppermute | solution.py:322
  7.1 1.0 %copy-done.2 = bf16[128,16,128]{2,1,0:T(8,128)(2,1)S(1)} copy-done((bf16[128,16,128]{2,1,0:T(8,128)(2,1)S(1)}, bf16[128,16,128]{2,1,0:T(8,128)(2,1)}, u32[]{:S(2)}) %copy-start.2) | copy-done | bytes 524312
  8.9 2.0 %collective-permute-start.4 = (bf16[560,128]{1,0:T(8,128)(2,1)S(1)}, bf16[560,128]{1,0:T(8,128)(2,1)S(1)}, u32[]{:S(2)}, u32[]{:S(2)}) collective-permute-start(bf16[560,128]{1,0:T(8,128)(2,1)S(1)} %get-tuple-element.40), channel_id=1, source_target_pairs={{0,1},{1,0},{2,3},{3,2},{4,5},{5,4},{6,7},{7,6},{8,9},{9,8},{10,11... | collective-permute-start | bytes 430088 | tf_op jit(solution)/shard_map/ppermute | solution.py:322
  10.9 2.6 %collective-permute-start.5 = (bf16[560,128]{1,0:T(8,128)(2,1)S(1)}, bf16[560,128]{1,0:T(8,128)(2,1)S(1)}, u32[]{:S(2)}, u32[]{:S(2)}) collective-permute-start(bf16[560,128]{1,0:T(8,128)(2,1)S(1)} %get-tuple-element.41), channel_id=1, source_target_pairs={{0,2},{1,3},{2,0},{3,1},{4,6},{5,7},{6,4},{7,5},{8,10},{9,11},{10,... | collective-permute-start | bytes 430088 | tf_op jit(solution)/shard_map/ppermute | solution.py:322
  13.5 2.3 %copy-done = bf16[128,32,576]{0,2,1:T(8,128)(2,1)S(1)} copy-done((bf16[128,32,576]{0,2,1:T(8,128)(2,1)S(1)}, bf16[128,32,576]{0,2,1:T(8,128)(2,1)}, u32[]{:S(2)}) %copy-start) | copy-done | bytes 4718616
  17.2 1.9 %shard_map.96.refs_5_ = bf16[128,256]{1,0:T(8,128)(2,1)S(1)} custom-call(bf16[128,704]{1,0:T(8,128)(2,1)S(1)} %shard_map.94.refs_0_.refs_4_, bf16[128,704]{1,0:T(8,128)(2,1)S(1)} %collective-permute-done.refs_1_.refs_5_, bf16[32,576,128]{2,1,0:T(8,128)(2,1)S(1)} %bitcast.8, f32[32,128]{1,0:T(8,128)S(1)} %bitcast.13, s32[1,128]{1,0:T(1,128)S(1)} %bitcast.17), custom_call_target="tpu_custom_call" | custom-call | flops 12079595520 | bytes 4718592 | tf_op jit(solution)/shard_map/pallas_call | solution.py:30
  20.5 2.5 %collective-permute-start.12 = (bf16[560,128]{1,0:T(8,128)(2,1)S(1)}, bf16[560,128]{1,0:T(8,128)(2,1)S(1)}, u32[]{:S(2)}, u32[]{:S(2)}) collective-permute-start(bf16[560,128]{1,0:T(8,128)(2,1)S(1)} %get-tuple-element.55), channel_id=1, source_target_pairs={{0,3},{1,2},{2,1},{3,0},{4,7},{5,6},{6,5},{7,4},{8,11},{9,10},{10,... | collective-permute-start | bytes 430088 | tf_op jit(solution)/shard_map/ppermute | solution.py:322
  23.0 3.6 %shard_map.97.refs_6_ = bf16[128,512]{1,0:T(8,128)(2,1)S(1)} custom-call(bf16[128,704]{1,0:T(8,128)(2,1)S(1)} %collective-permute-done.1.refs_0_.refs_2_.refs_6_, bf16[128,704]{1,0:T(8,128)(2,1)S(1)} %collective-permute-done.7.refs_1_.refs_3_.refs_7_, bf16[128,704]{1,0:T(8,128)(2,1)S(1)} %collective-permute-done.2.refs_2_.refs_4_.refs_8_, ...), custom_call_target="tpu_custom_call" | custom-call | flops 2415919104 | bytes 4718592 | tf_op jit(solution)/shard_map/pallas_call | solution.py:30
  26.6 1.9 %shard_map.98 = (bf16[32,1024]{1,0:T(8,128)(2,1)S(1)}, bf16[32,1024]{1,0:T(8,128)(2,1)S(1)}, bf16[32,1024]{1,0:T(8,128)(2,1)S(1)}, bf16[32,1024]{1,0:T(8,128)(2,1)S(1)}) custom-call(bf16[128,704]{1,0:T(8,128)(2,1)S(1)} %collective-permute-done.3.refs_0_.refs_6_.refs_10_, bf16[128,704]{1,0:T(8,128)(2,1)S(1)} %collective-permute-done.6.refs_1_.refs_7_.refs_11_, ...), custom_call_target="tpu_custom_call" | custom-call | flops 1207959552 | bytes 4718592 | tf_op jit(solution)/shard_map/pallas_call | solution.py:30
  28.7 1.9 %collective-permute-start.10 = (bf16[32,1024]{1,0:T(8,128)(2,1)S(1)}, bf16[32,1024]{1,0:T(8,128)(2,1)S(1)}, u32[]{:S(2)}, u32[]{:S(2)}) collective-permute-start(bf16[32,1024]{1,0:T(8,128)(2,1)S(1)} %get-tuple-element.49), channel_id=1, source_target_pairs={{0,2},{1,3},{2,0},{3,1},{4,6},{5,7},{6,4},{7,5},{8,10},{9,11},{10,... | collective-permute-start | bytes 196616 | tf_op jit(solution)/shard_map/ppermute | solution.py:322
  30.6 2.5 %collective-permute-start.11 = (bf16[32,1024]{1,0:T(8,128)(2,1)S(1)}, bf16[32,1024]{1,0:T(8,128)(2,1)S(1)}, u32[]{:S(2)}, u32[]{:S(2)}) collective-permute-start(bf16[32,1024]{1,0:T(8,128)(2,1)S(1)} %get-tuple-element.50), channel_id=1, source_target_pairs={{0,3},{1,2},{2,1},{3,0},{4,7},{5,6},{6,5},{7,4},{8,11},{9,10},{10,... | collective-permute-start | bytes 196616 | tf_op jit(solution)/shard_map/ppermute | solution.py:322
  33.0 1.9 %shard_map.99 = (f32[1024,128]{1,0:T(8,128)S(1)}, bf16[2048,128]{1,0:T(8,128)(2,1)S(1)}, f32[16,128]{1,0:T(8,128)S(1)}) custom-call(bf16[128,704]{1,0:T(8,128)(2,1)S(1)} %shard_map.94.refs_0_.refs_4_, bf16[128,704]{1,0:T(8,128)(2,1)S(1)} %collective-permute-done.refs_1_.refs_5_, bf16[128,704]{1,0:T(8,128)(2,1)S(1)} %collective-permute-done.1.refs_0_.refs_2_.refs_6_, ...), custom_call_target="tpu_custom_call" | custom-call | flops 536870912 | bytes 524288 | tf_op jit(solution)/shard_map/pallas_call | solution.py:30
  35.0 2.4 %collective-permute-done.10.refs_2_ = bf16[32,1024]{1,0:T(8,128)(2,1)S(1)} collective-permute-done((bf16[32,1024]{1,0:T(8,128)(2,1)S(1)}, bf16[32,1024]{1,0:T(8,128)(2,1)S(1)}, u32[]{:S(2)}, u32[]{:S(2)}) %collective-permute-start.10) | collective-permute-done | bytes 65568 | tf_op jit(solution)/shard_map/ppermute | solution.py:322
  37.4 4.0 %shard_map.100 = (f32[512,128]{1,0:T(8,128)S(1)}, f32[512,128]{1,0:T(8,128)S(1)}, bf16[544,128]{1,0:T(8,128)(2,1)S(1)}, bf16[544,128]{1,0:T(8,128)(2,1)S(1)}, bf...) custom-call(bf16[32,1024]{1,0:T(8,128)(2,1)S(1)} %get-tuple-element.47.refs_0_, ...), custom_call_target="tpu_custom_call" | custom-call | flops 1610612736 | bytes 524288 | tf_op jit(solution)/shard_map/pallas_call | solution.py:30
  41.5 1.5 %collective-permute-done.13.other_ref = f32[512,128]{1,0:T(8,128)S(1)} collective-permute-done((f32[512,128]{1,0:T(8,128)S(1)}, f32[512,128]{1,0:T(8,128)S(1)}, u32[]{:S(2)}, u32[]{:S(2)}) %collective-permute-start.13) | collective-permute-done | bytes 262176 | tf_op jit(solution)/shard_map/ppermute | solution.py:322
  43.0 1.6 %collective-permute-start.14 = (bf16[128,128]{1,0:T(8,128)(2,1)S(1)}, bf16[128,128]{1,0:T(8,128)(2,1)S(1)}, u32[]{:S(2)}, u32[]{:S(2)}) collective-permute-start(bf16[128,128]{1,0:T(8,128)(2,1)S(1)} %get-tuple-element.63), channel_id=1, source_target_pairs={{0,8},{4,12},{8,0},{12,4},{16,24},{20,28},{24,16},{28,20},{1,9},{5... | collective-permute-start | bytes 98312 | tf_op jit(solution)/shard_map/ppermute | solution.py:322
  44.6 1.5 %collective-permute-start.15 = (bf16[128,128]{1,0:T(8,128)(2,1)S(1)}, bf16[128,128]{1,0:T(8,128)(2,1)S(1)}, u32[]{:S(2)}, u32[]{:S(2)}) collective-permute-start(bf16[128,128]{1,0:T(8,128)(2,1)S(1)} %get-tuple-element.64), channel_id=1, source_target_pairs={{0,16},{4,20},{8,24},{12,28},{16,0},{20,4},{24,8},{28,12},{1,17},{... | collective-permute-start | bytes 98312 | tf_op jit(solution)/shard_map/ppermute | solution.py:322
  46.6 1.5 %collective-permute-start.18 = (bf16[544,128]{1,0:T(8,128)(2,1)S(1)}, bf16[544,128]{1,0:T(8,128)(2,1)S(1)}, u32[]{:S(2)}, u32[]{:S(2)}) collective-permute-start(bf16[544,128]{1,0:T(8,128)(2,1)S(1)} %get-tuple-element.68), channel_id=1, source_target_pairs={{0,2},{1,3},{2,0},{3,1},{4,6},{5,7},{6,4},{7,5},{8,10},{9,11},{10,... | collective-permute-start | bytes 417800 | tf_op jit(solution)/shard_map/ppermute | solution.py:322
  48.1 2.4 %collective-permute-start.19 = (bf16[544,128]{1,0:T(8,128)(2,1)S(1)}, bf16[544,128]{1,0:T(8,128)(2,1)S(1)}, u32[]{:S(2)}, u32[]{:S(2)}) collective-permute-start(bf16[544,128]{1,0:T(8,128)(2,1)S(1)} %get-tuple-element.69), channel_id=1, source_target_pairs={{0,3},{1,2},{2,1},{3,0},{4,7},{5,6},{6,5},{7,4},{8,11},{9,10},{10,... | collective-permute-start | bytes 417800 | tf_op jit(solution)/shard_map/ppermute | solution.py:322
  50.9 1.6 %collective-permute-start.17 = (bf16[544,128]{1,0:T(8,128)(2,1)S(1)}, bf16[544,128]{1,0:T(8,128)(2,1)S(1)}, u32[]{:S(2)}, u32[]{:S(2)}) collective-permute-start(bf16[544,128]{1,0:T(8,128)(2,1)S(1)} %get-tuple-element.67), channel_id=1, source_target_pairs={{0,1},{1,0},{2,3},{3,2},{4,5},{5,4},{6,7},{7,6},{8,9},{9,8},{10,11... | collective-permute-start | bytes 417800 | tf_op jit(solution)/shard_map/ppermute | solution.py:322
  52.6 1.4 %collective-permute-start.22 = (bf16[128,128]{1,0:T(8,128)(2,1)S(1)}, bf16[128,128]{1,0:T(8,128)(2,1)S(1)}, u32[]{:S(2)}, u32[]{:S(2)}) collective-permute-start(bf16[128,128]{1,0:T(8,128)(2,1)S(1)} %shard_map.102.refs_0_), channel_id=1, source_target_pairs={{0,3},{1,2},{2,1},{3,0},{4,7},{5,6},{6,5},{7,4},{8,11},{9,10},{10,... | collective-permute-start | bytes 98312 | tf_op jit(solution)/shard_map/ppermute | solution.py:322
  54.5 6.0 %collective-permute-done.22.refs_3_ = bf16[128,128]{1,0:T(8,128)(2,1)S(1)} collective-permute-done((bf16[128,128]{1,0:T(8,128)(2,1)S(1)}, bf16[128,128]{1,0:T(8,128)(2,1)S(1)}, u32[]{:S(2)}, u32[]{:S(2)}) %collective-permute-start.22) | collective-permute-done | bytes 32800 | tf_op jit(solution)/shard_map/ppermute | solution.py:322
  60.5 3.8 %collective-permute-start.20 = (bf16[128,128]{1,0:T(8,128)(2,1)S(1)}, bf16[128,128]{1,0:T(8,128)(2,1)S(1)}, u32[]{:S(2)}, u32[]{:S(2)}) collective-permute-start(bf16[128,128]{1,0:T(8,128)(2,1)S(1)} %shard_map.102.refs_0_), channel_id=1, source_target_pairs={{0,1},{1,0},{2,3},{3,2},{4,5},{5,4},{6,7},{7,6},{8,9},{9,8},{10,11... | collective-permute-start | bytes 98312 | tf_op jit(solution)/shard_map/ppermute | solution.py:322
  64.3 1.9 %collective-permute-done.20.refs_1_ = bf16[128,128]{1,0:T(8,128)(2,1)S(1)} collective-permute-done((bf16[128,128]{1,0:T(8,128)(2,1)S(1)}, bf16[128,128]{1,0:T(8,128)(2,1)S(1)}, u32[]{:S(2)}, u32[]{:S(2)}) %collective-permute-start.20) | collective-permute-done | bytes 32800 | tf_op jit(solution)/shard_map/ppermute | solution.py:322
  (51 shorter events, 9.6 us)
Async XLA Ops:
  2.4 8.5 %collective-permute-start = (bf16[128,704]{1,0:T(8,128)(2,1)S(1)}, bf16[128,704]{1,0:T(8,128)(2,1)S(1)}, u32[]{:S(2)}, u32[]{:S(2)}) collective-permute-start(bf16[128,704]{1,0:T(8,128)(2,1)S(1)} %shard_map.94.refs_0_.refs_4_), channel_id=1, source_target_pairs={{0,4},{4,0},{8,12},{12,8},{16,20},{20,16},{24,28},{28,24},{1,5},{5... | collective-permute-start | bytes 540680 | tf_op jit(solution)/shard_map/ppermute | solution.py:322
  2.9 17.0 %collective-permute-start.3 = (bf16[128,704]{1,0:T(8,128)(2,1)S(1)}, bf16[128,704]{1,0:T(8,128)(2,1)S(1)}, u32[]{:S(2)}, u32[]{:S(2)}) collective-permute-start(bf16[128,704]{1,0:T(8,128)(2,1)S(1)} %shard_map.94.refs_0_.refs_4_), channel_id=1, source_target_pairs={{0,24},{4,28},{8,16},{12,20},{16,8},{20,12},{24,0},{28,4},{1,25},{... | collective-permute-start | bytes 540680 | tf_op jit(solution)/shard_map/ppermute | solution.py:322
  6.4 13.5 %collective-permute-start.2 = (bf16[128,704]{1,0:T(8,128)(2,1)S(1)}, bf16[128,704]{1,0:T(8,128)(2,1)S(1)}, u32[]{:S(2)}, u32[]{:S(2)}) collective-permute-start(bf16[128,704]{1,0:T(8,128)(2,1)S(1)} %shard_map.94.refs_0_.refs_4_), channel_id=1, source_target_pairs={{0,16},{4,20},{8,24},{12,28},{16,0},{20,4},{24,8},{28,12},{1,17},{... | collective-permute-start | bytes 540680 | tf_op jit(solution)/shard_map/ppermute | solution.py:322
  7.0 13.0 %collective-permute-start.1 = (bf16[128,704]{1,0:T(8,128)(2,1)S(1)}, bf16[128,704]{1,0:T(8,128)(2,1)S(1)}, u32[]{:S(2)}, u32[]{:S(2)}) collective-permute-start(bf16[128,704]{1,0:T(8,128)(2,1)S(1)} %shard_map.94.refs_0_.refs_4_), channel_id=1, source_target_pairs={{0,8},{4,12},{8,0},{12,4},{16,24},{20,28},{24,16},{28,20},{1,9},{5... | collective-permute-start | bytes 540680 | tf_op jit(solution)/shard_map/ppermute | solution.py:322
  8.9 10.3 %collective-permute-start.4 = (bf16[560,128]{1,0:T(8,128)(2,1)S(1)}, bf16[560,128]{1,0:T(8,128)(2,1)S(1)}, u32[]{:S(2)}, u32[]{:S(2)}) collective-permute-start(bf16[560,128]{1,0:T(8,128)(2,1)S(1)} %get-tuple-element.40), channel_id=1, source_target_pairs={{0,1},{1,0},{2,3},{3,2},{4,5},{5,4},{6,7},{7,6},{8,9},{9,8},{10,11... | collective-permute-start | bytes 430088 | tf_op jit(solution)/shard_map/ppermute | solution.py:322
  10.9 9.0 %collective-permute-start.5 = (bf16[560,128]{1,0:T(8,128)(2,1)S(1)}, bf16[560,128]{1,0:T(8,128)(2,1)S(1)}, u32[]{:S(2)}, u32[]{:S(2)}) collective-permute-start(bf16[560,128]{1,0:T(8,128)(2,1)S(1)} %get-tuple-element.41), channel_id=1, source_target_pairs={{0,2},{1,3},{2,0},{3,1},{4,6},{5,7},{6,4},{7,5},{8,10},{9,11},{10,... | collective-permute-start | bytes 430088 | tf_op jit(solution)/shard_map/ppermute | solution.py:322
  17.2 5.8 %copy-start.6 = (f32[128,32]{0,1:T(8,128)S(1)}, f32[128,32]{0,1:T(8,128)}, u32[]{:S(2)}) copy-start(f32[128,32]{0,1:T(8,128)} %param.9) | copy-start | bytes 49156
  19.9 3.1 %collective-permute-start.7 = (bf16[128,704]{1,0:T(8,128)(2,1)S(1)}, bf16[128,704]{1,0:T(8,128)(2,1)S(1)}, u32[]{:S(2)}, u32[]{:S(2)}) collective-permute-start(bf16[128,704]{1,0:T(8,128)(2,1)S(1)} %collective-permute-done.1.refs_0_.refs_2_.refs_6_), channel_id=1, source_target_pairs={{0,4},{4,0},{8,12},{12,8},{16,20},{20,16},{24,28},{28,24},{1,5},{5... | collective-permute-start | bytes 540680 | tf_op jit(solution)/shard_map/ppermute | solution.py:322
  20.0 3.0 %collective-permute-start.8 = (bf16[128,704]{1,0:T(8,128)(2,1)S(1)}, bf16[128,704]{1,0:T(8,128)(2,1)S(1)}, u32[]{:S(2)}, u32[]{:S(2)}) collective-permute-start(bf16[128,704]{1,0:T(8,128)(2,1)S(1)} %collective-permute-done.2.refs_2_.refs_4_.refs_8_), channel_id=1, source_target_pairs={{0,4},{4,0},{8,12},{12,8},{16,20},{20,16},{24,28},{28,24},{1,5},{5... | collective-permute-start | bytes 540680 | tf_op jit(solution)/shard_map/ppermute | solution.py:322
  20.5 12.5 %collective-permute-start.12 = (bf16[560,128]{1,0:T(8,128)(2,1)S(1)}, bf16[560,128]{1,0:T(8,128)(2,1)S(1)}, u32[]{:S(2)}, u32[]{:S(2)}) collective-permute-start(bf16[560,128]{1,0:T(8,128)(2,1)S(1)} %get-tuple-element.55), channel_id=1, source_target_pairs={{0,3},{1,2},{2,1},{3,0},{4,7},{5,6},{6,5},{7,4},{8,11},{9,10},{10,... | collective-permute-start | bytes 430088 | tf_op jit(solution)/shard_map/ppermute | solution.py:322
  23.0 3.6 %collective-permute-start.6 = (bf16[128,704]{1,0:T(8,128)(2,1)S(1)}, bf16[128,704]{1,0:T(8,128)(2,1)S(1)}, u32[]{:S(2)}, u32[]{:S(2)}) collective-permute-start(bf16[128,704]{1,0:T(8,128)(2,1)S(1)} %collective-permute-done.3.refs_0_.refs_6_.refs_10_), channel_id=1, source_target_pairs={{0,4},{4,0},{8,12},{12,8},{16,20},{20,16},{24,28},{28,24},{1,5},{5... | collective-permute-start | bytes 540680 | tf_op jit(solution)/shard_map/ppermute | solution.py:322
  28.6 6.4 %collective-permute-start.9 = (bf16[32,1024]{1,0:T(8,128)(2,1)S(1)}, bf16[32,1024]{1,0:T(8,128)(2,1)S(1)}, u32[]{:S(2)}, u32[]{:S(2)}) collective-permute-start(bf16[32,1024]{1,0:T(8,128)(2,1)S(1)} %get-tuple-element.48), channel_id=1, source_target_pairs={{0,1},{1,0},{2,3},{3,2},{4,5},{5,4},{6,7},{7,6},{8,9},{9,8},{10,11... | collective-permute-start | bytes 196616 | tf_op jit(solution)/shard_map/ppermute | solution.py:322
  28.7 8.7 %collective-permute-start.10 = (bf16[32,1024]{1,0:T(8,128)(2,1)S(1)}, bf16[32,1024]{1,0:T(8,128)(2,1)S(1)}, u32[]{:S(2)}, u32[]{:S(2)}) collective-permute-start(bf16[32,1024]{1,0:T(8,128)(2,1)S(1)} %get-tuple-element.49), channel_id=1, source_target_pairs={{0,2},{1,3},{2,0},{3,1},{4,6},{5,7},{6,4},{7,5},{8,10},{9,11},{10,... | collective-permute-start | bytes 196616 | tf_op jit(solution)/shard_map/ppermute | solution.py:322
  30.6 6.8 %collective-permute-start.11 = (bf16[32,1024]{1,0:T(8,128)(2,1)S(1)}, bf16[32,1024]{1,0:T(8,128)(2,1)S(1)}, u32[]{:S(2)}, u32[]{:S(2)}) collective-permute-start(bf16[32,1024]{1,0:T(8,128)(2,1)S(1)} %get-tuple-element.50), channel_id=1, source_target_pairs={{0,3},{1,2},{2,1},{3,0},{4,7},{5,6},{6,5},{7,4},{8,11},{9,10},{10,... | collective-permute-start | bytes 196616 | tf_op jit(solution)/shard_map/ppermute | solution.py:322
  41.4 1.6 %collective-permute-start.13 = (f32[512,128]{1,0:T(8,128)S(1)}, f32[512,128]{1,0:T(8,128)S(1)}, u32[]{:S(2)}, u32[]{:S(2)}) collective-permute-start(f32[512,128]{1,0:T(8,128)S(1)} %get-tuple-element.61), channel_id=1, source_target_pairs={{0,4},{4,0},{8,12},{12,8},{16,20},{20,16},{24,28},{28,24},{1,5},{5... | collective-permute-start | bytes 786440 | tf_op jit(solution)/shard_map/ppermute | solution.py:322
  43.0 7.5 %collective-permute-start.14 = (bf16[128,128]{1,0:T(8,128)(2,1)S(1)}, bf16[128,128]{1,0:T(8,128)(2,1)S(1)}, u32[]{:S(2)}, u32[]{:S(2)}) collective-permute-start(bf16[128,128]{1,0:T(8,128)(2,1)S(1)} %get-tuple-element.63), channel_id=1, source_target_pairs={{0,8},{4,12},{8,0},{12,4},{16,24},{20,28},{24,16},{28,20},{1,9},{5... | collective-permute-start | bytes 98312 | tf_op jit(solution)/shard_map/ppermute | solution.py:322
  44.6 5.9 %collective-permute-start.15 = (bf16[128,128]{1,0:T(8,128)(2,1)S(1)}, bf16[128,128]{1,0:T(8,128)(2,1)S(1)}, u32[]{:S(2)}, u32[]{:S(2)}) collective-permute-start(bf16[128,128]{1,0:T(8,128)(2,1)S(1)} %get-tuple-element.64), channel_id=1, source_target_pairs={{0,16},{4,20},{8,24},{12,28},{16,0},{20,4},{24,8},{28,12},{1,17},{... | collective-permute-start | bytes 98312 | tf_op jit(solution)/shard_map/ppermute | solution.py:322
  46.1 4.8 %collective-permute-start.16 = (bf16[128,128]{1,0:T(8,128)(2,1)S(1)}, bf16[128,128]{1,0:T(8,128)(2,1)S(1)}, u32[]{:S(2)}, u32[]{:S(2)}) collective-permute-start(bf16[128,128]{1,0:T(8,128)(2,1)S(1)} %get-tuple-element.65), channel_id=1, source_target_pairs={{0,24},{4,28},{8,16},{12,20},{16,8},{20,12},{24,0},{28,4},{1,25},{... | collective-permute-start | bytes 98312 | tf_op jit(solution)/shard_map/ppermute | solution.py:322
  46.6 20.3 %collective-permute-start.18 = (bf16[544,128]{1,0:T(8,128)(2,1)S(1)}, bf16[544,128]{1,0:T(8,128)(2,1)S(1)}, u32[]{:S(2)}, u32[]{:S(2)}) collective-permute-start(bf16[544,128]{1,0:T(8,128)(2,1)S(1)} %get-tuple-element.68), channel_id=1, source_target_pairs={{0,2},{1,3},{2,0},{3,1},{4,6},{5,7},{6,4},{7,5},{8,10},{9,11},{10,... | collective-permute-start | bytes 417800 | tf_op jit(solution)/shard_map/ppermute | solution.py:322
  48.1 18.8 %collective-permute-start.19 = (bf16[544,128]{1,0:T(8,128)(2,1)S(1)}, bf16[544,128]{1,0:T(8,128)(2,1)S(1)}, u32[]{:S(2)}, u32[]{:S(2)}) collective-permute-start(bf16[544,128]{1,0:T(8,128)(2,1)S(1)} %get-tuple-element.69), channel_id=1, source_target_pairs={{0,3},{1,2},{2,1},{3,0},{4,7},{5,6},{6,5},{7,4},{8,11},{9,10},{10,... | collective-permute-start | bytes 417800 | tf_op jit(solution)/shard_map/ppermute | solution.py:322
  50.9 15.9 %collective-permute-start.17 = (bf16[544,128]{1,0:T(8,128)(2,1)S(1)}, bf16[544,128]{1,0:T(8,128)(2,1)S(1)}, u32[]{:S(2)}, u32[]{:S(2)}) collective-permute-start(bf16[544,128]{1,0:T(8,128)(2,1)S(1)} %get-tuple-element.67), channel_id=1, source_target_pairs={{0,1},{1,0},{2,3},{3,2},{4,5},{5,4},{6,7},{7,6},{8,9},{9,8},{10,11... | collective-permute-start | bytes 417800 | tf_op jit(solution)/shard_map/ppermute | solution.py:322
  52.6 8.0 %collective-permute-start.22 = (bf16[128,128]{1,0:T(8,128)(2,1)S(1)}, bf16[128,128]{1,0:T(8,128)(2,1)S(1)}, u32[]{:S(2)}, u32[]{:S(2)}) collective-permute-start(bf16[128,128]{1,0:T(8,128)(2,1)S(1)} %shard_map.102.refs_0_), channel_id=1, source_target_pairs={{0,3},{1,2},{2,1},{3,0},{4,7},{5,6},{6,5},{7,4},{8,11},{9,10},{10,... | collective-permute-start | bytes 98312 | tf_op jit(solution)/shard_map/ppermute | solution.py:322
  54.0 10.4 %collective-permute-start.21 = (bf16[128,128]{1,0:T(8,128)(2,1)S(1)}, bf16[128,128]{1,0:T(8,128)(2,1)S(1)}, u32[]{:S(2)}, u32[]{:S(2)}) collective-permute-start(bf16[128,128]{1,0:T(8,128)(2,1)S(1)} %shard_map.102.refs_0_), channel_id=1, source_target_pairs={{0,2},{1,3},{2,0},{3,1},{4,6},{5,7},{6,4},{7,5},{8,10},{9,11},{10,... | collective-permute-start | bytes 98312 | tf_op jit(solution)/shard_map/ppermute | solution.py:322
  60.5 5.7 %collective-permute-start.20 = (bf16[128,128]{1,0:T(8,128)(2,1)S(1)}, bf16[128,128]{1,0:T(8,128)(2,1)S(1)}, u32[]{:S(2)}, u32[]{:S(2)}) collective-permute-start(bf16[128,128]{1,0:T(8,128)(2,1)S(1)} %shard_map.102.refs_0_), channel_id=1, source_target_pairs={{0,1},{1,0},{2,3},{3,2},{4,5},{5,4},{6,7},{7,6},{8,9},{9,8},{10,11... | collective-permute-start | bytes 98312 | tf_op jit(solution)/shard_map/ppermute | solution.py:322
  (8 other events, 12.9 us)

commit v10 on v9

--- a/solution.py
+++ b/solution.py
@@ -433,12 +433,15 @@
     half = shape((rows, index_width), bf16)
     mine, *others = call(pair_kernel, [term] + [half] * (blocks // 2 - 1), (even, odd))
     others = [swap(value, "pb", 2 * (i + 1)) for i, value in enumerate(others)]
-    mine, answers[1] = lax.optimization_barrier(
-        (call(sum_kernel, half, [mine] + others), answers[1])
+    answers[2] = swap(answers[2], "ha", 2)
+    mine, answers[1:3] = lax.optimization_barrier(
+        (call(sum_kernel, half, [mine] + others), answers[1:3])
     )
     key_grad = call(sum_kernel, half, [mine] + [swap(mine, "ha", r) for r in range(1, parts)])
 
-    answers = [answers[0]] + [swap(answers[r], "ha", r) for r in range(1, parts)]
+    answers = [
+        value if r in (0, 2) else swap(value, "ha", r) for r, value in enumerate(answers)
+    ]
     query_grad, weight_grad = call(
         functools.partial(finish_kernel, share, heads),
         [shape((rows * heads, index_width), bf16), shape((heads, rows), f32)],

time: 68.2 us -> 64.2 us (0.941)
  starting transfers between devices: 31.7 us -> 28.8 us
  waiting for transfers between devices: 13.1 us -> 12 us
    ppermute x23, starting transfers between devices: 31.7 us -> 28.8 us  [swap(): return lax.ppermute(value, axis, [(i, i ^ rel) for i in range(size)])]
    ppermute x23, waiting for transfers between devices: 13.1 us -> 12 us  [swap(): return lax.ppermute(value, axis, [(i, i ^ rel) for i in range(size)])]
  transfers between devices with their start and end apart: 23 -> 23, of which waited for: 6 -> 7; matrix products, arithmetic and copies ran while one was open for 0% -> 0% of each run, Pallas kernels for 15% -> 16%
where the time goes in v10:
time: 64.2 us; the launch traced here: 63.8 us
  starting transfers between devices  28.8 us (45%)
  Pallas kernels  15.1 us (24%)
  waiting for transfers between devices  12 us (19%)
  local copies, waits for them, and re-layouts  7.11 us (11%)
  between operations  0.78 us (1%)
    ppermute x23, starting transfers between devices, swap(): return lax.ppermute(value, axis, [(i, i ^ rel) for i in range(size)])  28.8 us
    pallas_call x11, Pallas kernels, call(): pl.pallas_call(kernel, grid=(1,), out_shape=outs, in_specs=specs or [whol...  15.1 us
    ppermute x23, waiting for transfers between devices, swap(): return lax.ppermute(value, axis, [(i, i ^ rel) for i in range(size)])  12 us
    unnamed x18, local copies, waits for them, and re-layouts  7.11 us
  transfers between devices with their start and end apart: 23, of which 7 were waited for; matrix products, arithmetic and copies ran while one was open for 0% of the time, Pallas kernels for 16%

profile of v10, /device:TPU:0, one launch (start us, length us, event | category | flops | bytes accessed | tf_op | source)
XLA Modules:
  0.0 63.8 jit_solution(15170225744566918132)
XLA Ops:
  2.9 3.5 %collective-permute-start.3 = (bf16[128,704]{1,0:T(8,128)(2,1)S(1)}, bf16[128,704]{1,0:T(8,128)(2,1)S(1)}, u32[]{:S(2)}, u32[]{:S(2)}) collective-permute-start(bf16[128,704]{1,0:T(8,128)(2,1)S(1)} %shard_map.94.refs_0_.refs_4_), channel_id=1, source_target_pairs={{0,24},{4,28},{8,16},{12,20},{16,8},{20,12},{24,0},{28,4},{1,25},{... | collective-permute-start | bytes 540680 | tf_op jit(solution)/shard_map/ppermute | solution.py:322
  7.1 1.0 %copy-done.2 = bf16[128,16,128]{2,1,0:T(8,128)(2,1)S(1)} copy-done((bf16[128,16,128]{2,1,0:T(8,128)(2,1)S(1)}, bf16[128,16,128]{2,1,0:T(8,128)(2,1)}, u32[]{:S(2)}) %copy-start.2) | copy-done | bytes 524312
  8.9 2.0 %collective-permute-start.4 = (bf16[560,128]{1,0:T(8,128)(2,1)S(1)}, bf16[560,128]{1,0:T(8,128)(2,1)S(1)}, u32[]{:S(2)}, u32[]{:S(2)}) collective-permute-start(bf16[560,128]{1,0:T(8,128)(2,1)S(1)} %get-tuple-element.41), channel_id=1, source_target_pairs={{0,1},{1,0},{2,3},{3,2},{4,5},{5,4},{6,7},{7,6},{8,9},{9,8},{10,11... | collective-permute-start | bytes 430088 | tf_op jit(solution)/shard_map/ppermute | solution.py:322
  10.9 2.6 %collective-permute-start.5 = (bf16[560,128]{1,0:T(8,128)(2,1)S(1)}, bf16[560,128]{1,0:T(8,128)(2,1)S(1)}, u32[]{:S(2)}, u32[]{:S(2)}) collective-permute-start(bf16[560,128]{1,0:T(8,128)(2,1)S(1)} %get-tuple-element.42), channel_id=1, source_target_pairs={{0,2},{1,3},{2,0},{3,1},{4,6},{5,7},{6,4},{7,5},{8,10},{9,11},{10,... | collective-permute-start | bytes 430088 | tf_op jit(solution)/shard_map/ppermute | solution.py:322
  13.5 2.3 %copy-done = bf16[128,32,576]{0,2,1:T(8,128)(2,1)S(1)} copy-done((bf16[128,32,576]{0,2,1:T(8,128)(2,1)S(1)}, bf16[128,32,576]{0,2,1:T(8,128)(2,1)}, u32[]{:S(2)}) %copy-start) | copy-done | bytes 4718616
  17.2 1.9 %shard_map.96.refs_5_ = bf16[128,256]{1,0:T(8,128)(2,1)S(1)} custom-call(bf16[128,704]{1,0:T(8,128)(2,1)S(1)} %shard_map.94.refs_0_.refs_4_, bf16[128,704]{1,0:T(8,128)(2,1)S(1)} %collective-permute-done.refs_1_.refs_5_, bf16[32,576,128]{2,1,0:T(8,128)(2,1)S(1)} %bitcast.8, f32[32,128]{1,0:T(8,128)S(1)} %bitcast.13, s32[1,128]{1,0:T(1,128)S(1)} %bitcast.17), custom_call_target="tpu_custom_call" | custom-call | flops 12079595520 | bytes 4718592 | tf_op jit(solution)/shard_map/pallas_call | solution.py:30
  20.5 2.5 %collective-permute-start.12 = (bf16[560,128]{1,0:T(8,128)(2,1)S(1)}, bf16[560,128]{1,0:T(8,128)(2,1)S(1)}, u32[]{:S(2)}, u32[]{:S(2)}) collective-permute-start(bf16[560,128]{1,0:T(8,128)(2,1)S(1)} %get-tuple-element.56), channel_id=1, source_target_pairs={{0,3},{1,2},{2,1},{3,0},{4,7},{5,6},{6,5},{7,4},{8,11},{9,10},{10,... | collective-permute-start | bytes 430088 | tf_op jit(solution)/shard_map/ppermute | solution.py:322
  23.0 3.6 %shard_map.97.refs_6_ = bf16[128,512]{1,0:T(8,128)(2,1)S(1)} custom-call(bf16[128,704]{1,0:T(8,128)(2,1)S(1)} %collective-permute-done.1.refs_0_.refs_2_.refs_6_, bf16[128,704]{1,0:T(8,128)(2,1)S(1)} %collective-permute-done.7.refs_1_.refs_3_.refs_7_, bf16[128,704]{1,0:T(8,128)(2,1)S(1)} %collective-permute-done.2.refs_2_.refs_4_.refs_8_, ...), custom_call_target="tpu_custom_call" | custom-call | flops 2415919104 | bytes 4718592 | tf_op jit(solution)/shard_map/pallas_call | solution.py:30
  26.6 1.9 %shard_map.98 = (bf16[32,1024]{1,0:T(8,128)(2,1)S(1)}, bf16[32,1024]{1,0:T(8,128)(2,1)S(1)}, bf16[32,1024]{1,0:T(8,128)(2,1)S(1)}, bf16[32,1024]{1,0:T(8,128)(2,1)S(1)}) custom-call(bf16[128,704]{1,0:T(8,128)(2,1)S(1)} %collective-permute-done.3.refs_0_.refs_6_.refs_10_, bf16[128,704]{1,0:T(8,128)(2,1)S(1)} %collective-permute-done.6.refs_1_.refs_7_.refs_11_, ...), custom_call_target="tpu_custom_call" | custom-call | flops 1207959552 | bytes 4718592 | tf_op jit(solution)/shard_map/pallas_call | solution.py:30
  28.7 1.9 %collective-permute-start.10 = (bf16[32,1024]{1,0:T(8,128)(2,1)S(1)}, bf16[32,1024]{1,0:T(8,128)(2,1)S(1)}, u32[]{:S(2)}, u32[]{:S(2)}) collective-permute-start(bf16[32,1024]{1,0:T(8,128)(2,1)S(1)} %get-tuple-element.50), channel_id=1, source_target_pairs={{0,2},{1,3},{2,0},{3,1},{4,6},{5,7},{6,4},{7,5},{8,10},{9,11},{10,... | collective-permute-start | bytes 196616 | tf_op jit(solution)/shard_map/ppermute | solution.py:322
  30.6 2.5 %collective-permute-start.11 = (bf16[32,1024]{1,0:T(8,128)(2,1)S(1)}, bf16[32,1024]{1,0:T(8,128)(2,1)S(1)}, u32[]{:S(2)}, u32[]{:S(2)}) collective-permute-start(bf16[32,1024]{1,0:T(8,128)(2,1)S(1)} %get-tuple-element.51), channel_id=1, source_target_pairs={{0,3},{1,2},{2,1},{3,0},{4,7},{5,6},{6,5},{7,4},{8,11},{9,10},{10,... | collective-permute-start | bytes 196616 | tf_op jit(solution)/shard_map/ppermute | solution.py:322
  33.0 1.9 %shard_map.99 = (f32[1024,128]{1,0:T(8,128)S(1)}, bf16[2048,128]{1,0:T(8,128)(2,1)S(1)}, f32[16,128]{1,0:T(8,128)S(1)}) custom-call(bf16[128,704]{1,0:T(8,128)(2,1)S(1)} %shard_map.94.refs_0_.refs_4_, bf16[128,704]{1,0:T(8,128)(2,1)S(1)} %collective-permute-done.refs_1_.refs_5_, bf16[128,704]{1,0:T(8,128)(2,1)S(1)} %collective-permute-done.1.refs_0_.refs_2_.refs_6_, ...), custom_call_target="tpu_custom_call" | custom-call | flops 536870912 | bytes 524288 | tf_op jit(solution)/shard_map/pallas_call | solution.py:30
  35.0 2.4 %collective-permute-done.10.refs_2_ = bf16[32,1024]{1,0:T(8,128)(2,1)S(1)} collective-permute-done((bf16[32,1024]{1,0:T(8,128)(2,1)S(1)}, bf16[32,1024]{1,0:T(8,128)(2,1)S(1)}, u32[]{:S(2)}, u32[]{:S(2)}) %collective-permute-start.10) | collective-permute-done | bytes 65568 | tf_op jit(solution)/shard_map/ppermute | solution.py:322
  37.4 4.0 %shard_map.100 = (f32[512,128]{1,0:T(8,128)S(1)}, f32[512,128]{1,0:T(8,128)S(1)}, bf16[544,128]{1,0:T(8,128)(2,1)S(1)}, bf16[544,128]{1,0:T(8,128)(2,1)S(1)}, bf...) custom-call(bf16[32,1024]{1,0:T(8,128)(2,1)S(1)} %get-tuple-element.48.refs_0_, ...), custom_call_target="tpu_custom_call" | custom-call | flops 1610612736 | bytes 524288 | tf_op jit(solution)/shard_map/pallas_call | solution.py:30
  41.5 1.6 %collective-permute-start.17 = (bf16[544,128]{1,0:T(8,128)(2,1)S(1)}, bf16[544,128]{1,0:T(8,128)(2,1)S(1)}, u32[]{:S(2)}, u32[]{:S(2)}) collective-permute-start(bf16[544,128]{1,0:T(8,128)(2,1)S(1)} %get-tuple-element.68), channel_id=1, source_target_pairs={{0,2},{1,3},{2,0},{3,1},{4,6},{5,7},{6,4},{7,5},{8,10},{9,11},{10,... | collective-permute-start | bytes 417800 | tf_op jit(solution)/shard_map/ppermute | solution.py:322
  43.1 1.6 %collective-permute-start.14 = (bf16[128,128]{1,0:T(8,128)(2,1)S(1)}, bf16[128,128]{1,0:T(8,128)(2,1)S(1)}, u32[]{:S(2)}, u32[]{:S(2)}) collective-permute-start(bf16[128,128]{1,0:T(8,128)(2,1)S(1)} %get-tuple-element.64), channel_id=1, source_target_pairs={{0,8},{4,12},{8,0},{12,4},{16,24},{20,28},{24,16},{28,20},{1,9},{5... | collective-permute-start | bytes 98312 | tf_op jit(solution)/shard_map/ppermute | solution.py:322
  44.6 1.5 %collective-permute-start.15 = (bf16[128,128]{1,0:T(8,128)(2,1)S(1)}, bf16[128,128]{1,0:T(8,128)(2,1)S(1)}, u32[]{:S(2)}, u32[]{:S(2)}) collective-permute-start(bf16[128,128]{1,0:T(8,128)(2,1)S(1)} %get-tuple-element.65), channel_id=1, source_target_pairs={{0,16},{4,20},{8,24},{12,28},{16,0},{20,4},{24,8},{28,12},{1,17},{... | collective-permute-start | bytes 98312 | tf_op jit(solution)/shard_map/ppermute | solution.py:322
  46.6 2.4 %collective-permute-start.19 = (bf16[544,128]{1,0:T(8,128)(2,1)S(1)}, bf16[544,128]{1,0:T(8,128)(2,1)S(1)}, u32[]{:S(2)}, u32[]{:S(2)}) collective-permute-start(bf16[544,128]{1,0:T(8,128)(2,1)S(1)} %get-tuple-element.71), channel_id=1, source_target_pairs={{0,3},{1,2},{2,1},{3,0},{4,7},{5,6},{6,5},{7,4},{8,11},{9,10},{10,... | collective-permute-start | bytes 417800 | tf_op jit(solution)/shard_map/ppermute | solution.py:322
  49.1 1.9 %collective-permute-done.16.refs_3_ = bf16[128,128]{1,0:T(8,128)(2,1)S(1)} collective-permute-done((bf16[128,128]{1,0:T(8,128)(2,1)S(1)}, bf16[128,128]{1,0:T(8,128)(2,1)S(1)}, u32[]{:S(2)}, u32[]{:S(2)}) %collective-permute-start.16) | collective-permute-done | bytes 32800 | tf_op jit(solution)/shard_map/ppermute | solution.py:322
  51.0 3.9 %collective-permute-done.17.refs_2_ = bf16[544,128]{1,0:T(8,128)(2,1)S(1)} collective-permute-done((bf16[544,128]{1,0:T(8,128)(2,1)S(1)}, bf16[544,128]{1,0:T(8,128)(2,1)S(1)}, u32[]{:S(2)}, u32[]{:S(2)}) %collective-permute-start.17) | collective-permute-done | bytes 139296 | tf_op jit(solution)/shard_map/ppermute | solution.py:322
  54.9 1.8 %collective-permute-start.22 = (bf16[128,128]{1,0:T(8,128)(2,1)S(1)}, bf16[128,128]{1,0:T(8,128)(2,1)S(1)}, u32[]{:S(2)}, u32[]{:S(2)}) collective-permute-start(bf16[128,128]{1,0:T(8,128)(2,1)S(1)} %shard_map.102.refs_0_), channel_id=1, source_target_pairs={{0,3},{1,2},{2,1},{3,0},{4,7},{5,6},{6,5},{7,4},{8,11},{9,10},{10,... | collective-permute-start | bytes 98312 | tf_op jit(solution)/shard_map/ppermute | solution.py:322
  56.6 1.7 %collective-permute-start.21 = (bf16[128,128]{1,0:T(8,128)(2,1)S(1)}, bf16[128,128]{1,0:T(8,128)(2,1)S(1)}, u32[]{:S(2)}, u32[]{:S(2)}) collective-permute-start(bf16[128,128]{1,0:T(8,128)(2,1)S(1)} %shard_map.102.refs_0_), channel_id=1, source_target_pairs={{0,2},{1,3},{2,0},{3,1},{4,6},{5,7},{6,4},{7,5},{8,10},{9,11},{10,... | collective-permute-start | bytes 98312 | tf_op jit(solution)/shard_map/ppermute | solution.py:322
  59.3 1.8 %collective-permute-done.22.refs_3_ = bf16[128,128]{1,0:T(8,128)(2,1)S(1)} collective-permute-done((bf16[128,128]{1,0:T(8,128)(2,1)S(1)}, bf16[128,128]{1,0:T(8,128)(2,1)S(1)}, u32[]{:S(2)}, u32[]{:S(2)}) %collective-permute-start.22) | collective-permute-done | bytes 32800 | tf_op jit(solution)/shard_map/ppermute | solution.py:322
  62.9 0.9 %shard_map.103 = (bf16[2048,128]{1,0:T(8,128)(2,1)}, f32[16,128]{1,0:T(8,128)}) custom-call(bf16[544,128]{1,0:T(8,128)(2,1)S(1)} %get-tuple-element.60.refs_0_, bf16[544,128]{1,0:T(8,128)(2,1)S(1)} %collective-permute-done.18.refs_1_, bf16[544,128]{1,0:T(8,128)(2,1)S(1)} %collective-permute-done.17.refs_2_, bf16[544,128]{1,0:T(8,128)(2,1)S(1)} %collective-permute-done.19.refs_3_), custom_call_target="tpu_custom_call" | custom-call | tf_op jit(solution)/shard_map/pallas_call | solution.py:30
  (51 shorter events, 9.8 us)
Async XLA Ops:
  2.4 8.5 %collective-permute-start = (bf16[128,704]{1,0:T(8,128)(2,1)S(1)}, bf16[128,704]{1,0:T(8,128)(2,1)S(1)}, u32[]{:S(2)}, u32[]{:S(2)}) collective-permute-start(bf16[128,704]{1,0:T(8,128)(2,1)S(1)} %shard_map.94.refs_0_.refs_4_), channel_id=1, source_target_pairs={{0,4},{4,0},{8,12},{12,8},{16,20},{20,16},{24,28},{28,24},{1,5},{5... | collective-permute-start | bytes 540680 | tf_op jit(solution)/shard_map/ppermute | solution.py:322
  2.9 17.0 %collective-permute-start.3 = (bf16[128,704]{1,0:T(8,128)(2,1)S(1)}, bf16[128,704]{1,0:T(8,128)(2,1)S(1)}, u32[]{:S(2)}, u32[]{:S(2)}) collective-permute-start(bf16[128,704]{1,0:T(8,128)(2,1)S(1)} %shard_map.94.refs_0_.refs_4_), channel_id=1, source_target_pairs={{0,24},{4,28},{8,16},{12,20},{16,8},{20,12},{24,0},{28,4},{1,25},{... | collective-permute-start | bytes 540680 | tf_op jit(solution)/shard_map/ppermute | solution.py:322
  6.4 13.5 %collective-permute-start.2 = (bf16[128,704]{1,0:T(8,128)(2,1)S(1)}, bf16[128,704]{1,0:T(8,128)(2,1)S(1)}, u32[]{:S(2)}, u32[]{:S(2)}) collective-permute-start(bf16[128,704]{1,0:T(8,128)(2,1)S(1)} %shard_map.94.refs_0_.refs_4_), channel_id=1, source_target_pairs={{0,16},{4,20},{8,24},{12,28},{16,0},{20,4},{24,8},{28,12},{1,17},{... | collective-permute-start | bytes 540680 | tf_op jit(solution)/shard_map/ppermute | solution.py:322
  7.0 13.0 %collective-permute-start.1 = (bf16[128,704]{1,0:T(8,128)(2,1)S(1)}, bf16[128,704]{1,0:T(8,128)(2,1)S(1)}, u32[]{:S(2)}, u32[]{:S(2)}) collective-permute-start(bf16[128,704]{1,0:T(8,128)(2,1)S(1)} %shard_map.94.refs_0_.refs_4_), channel_id=1, source_target_pairs={{0,8},{4,12},{8,0},{12,4},{16,24},{20,28},{24,16},{28,20},{1,9},{5... | collective-permute-start | bytes 540680 | tf_op jit(solution)/shard_map/ppermute | solution.py:322
  8.9 10.3 %collective-permute-start.4 = (bf16[560,128]{1,0:T(8,128)(2,1)S(1)}, bf16[560,128]{1,0:T(8,128)(2,1)S(1)}, u32[]{:S(2)}, u32[]{:S(2)}) collective-permute-start(bf16[560,128]{1,0:T(8,128)(2,1)S(1)} %get-tuple-element.41), channel_id=1, source_target_pairs={{0,1},{1,0},{2,3},{3,2},{4,5},{5,4},{6,7},{7,6},{8,9},{9,8},{10,11... | collective-permute-start | bytes 430088 | tf_op jit(solution)/shard_map/ppermute | solution.py:322
  10.9 9.0 %collective-permute-start.5 = (bf16[560,128]{1,0:T(8,128)(2,1)S(1)}, bf16[560,128]{1,0:T(8,128)(2,1)S(1)}, u32[]{:S(2)}, u32[]{:S(2)}) collective-permute-start(bf16[560,128]{1,0:T(8,128)(2,1)S(1)} %get-tuple-element.42), channel_id=1, source_target_pairs={{0,2},{1,3},{2,0},{3,1},{4,6},{5,7},{6,4},{7,5},{8,10},{9,11},{10,... | collective-permute-start | bytes 430088 | tf_op jit(solution)/shard_map/ppermute | solution.py:322
  17.2 5.8 %copy-start.6 = (f32[128,32]{0,1:T(8,128)S(1)}, f32[128,32]{0,1:T(8,128)}, u32[]{:S(2)}) copy-start(f32[128,32]{0,1:T(8,128)} %param.9) | copy-start | bytes 49156
  19.9 3.1 %collective-permute-start.7 = (bf16[128,704]{1,0:T(8,128)(2,1)S(1)}, bf16[128,704]{1,0:T(8,128)(2,1)S(1)}, u32[]{:S(2)}, u32[]{:S(2)}) collective-permute-start(bf16[128,704]{1,0:T(8,128)(2,1)S(1)} %collective-permute-done.1.refs_0_.refs_2_.refs_6_), channel_id=1, source_target_pairs={{0,4},{4,0},{8,12},{12,8},{16,20},{20,16},{24,28},{28,24},{1,5},{5... | collective-permute-start | bytes 540680 | tf_op jit(solution)/shard_map/ppermute | solution.py:322
  20.0 3.0 %collective-permute-start.8 = (bf16[128,704]{1,0:T(8,128)(2,1)S(1)}, bf16[128,704]{1,0:T(8,128)(2,1)S(1)}, u32[]{:S(2)}, u32[]{:S(2)}) collective-permute-start(bf16[128,704]{1,0:T(8,128)(2,1)S(1)} %collective-permute-done.2.refs_2_.refs_4_.refs_8_), channel_id=1, source_target_pairs={{0,4},{4,0},{8,12},{12,8},{16,20},{20,16},{24,28},{28,24},{1,5},{5... | collective-permute-start | bytes 540680 | tf_op jit(solution)/shard_map/ppermute | solution.py:322
  20.5 12.5 %collective-permute-start.12 = (bf16[560,128]{1,0:T(8,128)(2,1)S(1)}, bf16[560,128]{1,0:T(8,128)(2,1)S(1)}, u32[]{:S(2)}, u32[]{:S(2)}) collective-permute-start(bf16[560,128]{1,0:T(8,128)(2,1)S(1)} %get-tuple-element.56), channel_id=1, source_target_pairs={{0,3},{1,2},{2,1},{3,0},{4,7},{5,6},{6,5},{7,4},{8,11},{9,10},{10,... | collective-permute-start | bytes 430088 | tf_op jit(solution)/shard_map/ppermute | solution.py:322
  23.0 3.6 %collective-permute-start.6 = (bf16[128,704]{1,0:T(8,128)(2,1)S(1)}, bf16[128,704]{1,0:T(8,128)(2,1)S(1)}, u32[]{:S(2)}, u32[]{:S(2)}) collective-permute-start(bf16[128,704]{1,0:T(8,128)(2,1)S(1)} %collective-permute-done.3.refs_0_.refs_6_.refs_10_), channel_id=1, source_target_pairs={{0,4},{4,0},{8,12},{12,8},{16,20},{20,16},{24,28},{28,24},{1,5},{5... | collective-permute-start | bytes 540680 | tf_op jit(solution)/shard_map/ppermute | solution.py:322
  28.6 6.4 %collective-permute-start.9 = (bf16[32,1024]{1,0:T(8,128)(2,1)S(1)}, bf16[32,1024]{1,0:T(8,128)(2,1)S(1)}, u32[]{:S(2)}, u32[]{:S(2)}) collective-permute-start(bf16[32,1024]{1,0:T(8,128)(2,1)S(1)} %get-tuple-element.49), channel_id=1, source_target_pairs={{0,1},{1,0},{2,3},{3,2},{4,5},{5,4},{6,7},{7,6},{8,9},{9,8},{10,11... | collective-permute-start | bytes 196616 | tf_op jit(solution)/shard_map/ppermute | solution.py:322
  28.7 8.7 %collective-permute-start.10 = (bf16[32,1024]{1,0:T(8,128)(2,1)S(1)}, bf16[32,1024]{1,0:T(8,128)(2,1)S(1)}, u32[]{:S(2)}, u32[]{:S(2)}) collective-permute-start(bf16[32,1024]{1,0:T(8,128)(2,1)S(1)} %get-tuple-element.50), channel_id=1, source_target_pairs={{0,2},{1,3},{2,0},{3,1},{4,6},{5,7},{6,4},{7,5},{8,10},{9,11},{10,... | collective-permute-start | bytes 196616 | tf_op jit(solution)/shard_map/ppermute | solution.py:322
  30.6 6.8 %collective-permute-start.11 = (bf16[32,1024]{1,0:T(8,128)(2,1)S(1)}, bf16[32,1024]{1,0:T(8,128)(2,1)S(1)}, u32[]{:S(2)}, u32[]{:S(2)}) collective-permute-start(bf16[32,1024]{1,0:T(8,128)(2,1)S(1)} %get-tuple-element.51), channel_id=1, source_target_pairs={{0,3},{1,2},{2,1},{3,0},{4,7},{5,6},{6,5},{7,4},{8,11},{9,10},{10,... | collective-permute-start | bytes 196616 | tf_op jit(solution)/shard_map/ppermute | solution.py:322
  41.4 1.6 %collective-permute-start.13 = (f32[512,128]{1,0:T(8,128)S(1)}, f32[512,128]{1,0:T(8,128)S(1)}, u32[]{:S(2)}, u32[]{:S(2)}) collective-permute-start(f32[512,128]{1,0:T(8,128)S(1)} %get-tuple-element.62), channel_id=1, source_target_pairs={{0,4},{4,0},{8,12},{12,8},{16,20},{20,16},{24,28},{28,24},{1,5},{5... | collective-permute-start | bytes 786440 | tf_op jit(solution)/shard_map/ppermute | solution.py:322
  41.5 13.4 %collective-permute-start.17 = (bf16[544,128]{1,0:T(8,128)(2,1)S(1)}, bf16[544,128]{1,0:T(8,128)(2,1)S(1)}, u32[]{:S(2)}, u32[]{:S(2)}) collective-permute-start(bf16[544,128]{1,0:T(8,128)(2,1)S(1)} %get-tuple-element.68), channel_id=1, source_target_pairs={{0,2},{1,3},{2,0},{3,1},{4,6},{5,7},{6,4},{7,5},{8,10},{9,11},{10,... | collective-permute-start | bytes 417800 | tf_op jit(solution)/shard_map/ppermute | solution.py:322
  43.1 6.0 %collective-permute-start.14 = (bf16[128,128]{1,0:T(8,128)(2,1)S(1)}, bf16[128,128]{1,0:T(8,128)(2,1)S(1)}, u32[]{:S(2)}, u32[]{:S(2)}) collective-permute-start(bf16[128,128]{1,0:T(8,128)(2,1)S(1)} %get-tuple-element.64), channel_id=1, source_target_pairs={{0,8},{4,12},{8,0},{12,4},{16,24},{20,28},{24,16},{28,20},{1,9},{5... | collective-permute-start | bytes 98312 | tf_op jit(solution)/shard_map/ppermute | solution.py:322
  44.6 4.4 %collective-permute-start.15 = (bf16[128,128]{1,0:T(8,128)(2,1)S(1)}, bf16[128,128]{1,0:T(8,128)(2,1)S(1)}, u32[]{:S(2)}, u32[]{:S(2)}) collective-permute-start(bf16[128,128]{1,0:T(8,128)(2,1)S(1)} %get-tuple-element.65), channel_id=1, source_target_pairs={{0,16},{4,20},{8,24},{12,28},{16,0},{20,4},{24,8},{28,12},{1,17},{... | collective-permute-start | bytes 98312 | tf_op jit(solution)/shard_map/ppermute | solution.py:322
  46.1 4.8 %collective-permute-start.16 = (bf16[128,128]{1,0:T(8,128)(2,1)S(1)}, bf16[128,128]{1,0:T(8,128)(2,1)S(1)}, u32[]{:S(2)}, u32[]{:S(2)}) collective-permute-start(bf16[128,128]{1,0:T(8,128)(2,1)S(1)} %get-tuple-element.66), channel_id=1, source_target_pairs={{0,24},{4,28},{8,16},{12,20},{16,8},{20,12},{24,0},{28,4},{1,25},{... | collective-permute-start | bytes 98312 | tf_op jit(solution)/shard_map/ppermute | solution.py:322
  46.6 16.3 %collective-permute-start.19 = (bf16[544,128]{1,0:T(8,128)(2,1)S(1)}, bf16[544,128]{1,0:T(8,128)(2,1)S(1)}, u32[]{:S(2)}, u32[]{:S(2)}) collective-permute-start(bf16[544,128]{1,0:T(8,128)(2,1)S(1)} %get-tuple-element.71), channel_id=1, source_target_pairs={{0,3},{1,2},{2,1},{3,0},{4,7},{5,6},{6,5},{7,4},{8,11},{9,10},{10,... | collective-permute-start | bytes 417800 | tf_op jit(solution)/shard_map/ppermute | solution.py:322
  54.9 8.0 %collective-permute-start.18 = (bf16[544,128]{1,0:T(8,128)(2,1)S(1)}, bf16[544,128]{1,0:T(8,128)(2,1)S(1)}, u32[]{:S(2)}, u32[]{:S(2)}) collective-permute-start(bf16[544,128]{1,0:T(8,128)(2,1)S(1)} %get-tuple-element.69), channel_id=1, source_target_pairs={{0,1},{1,0},{2,3},{3,2},{4,5},{5,4},{6,7},{7,6},{8,9},{9,8},{10,11... | collective-permute-start | bytes 417800 | tf_op jit(solution)/shard_map/ppermute | solution.py:322
  54.9 6.2 %collective-permute-start.22 = (bf16[128,128]{1,0:T(8,128)(2,1)S(1)}, bf16[128,128]{1,0:T(8,128)(2,1)S(1)}, u32[]{:S(2)}, u32[]{:S(2)}) collective-permute-start(bf16[128,128]{1,0:T(8,128)(2,1)S(1)} %shard_map.102.refs_0_), channel_id=1, source_target_pairs={{0,3},{1,2},{2,1},{3,0},{4,7},{5,6},{6,5},{7,4},{8,11},{9,10},{10,... | collective-permute-start | bytes 98312 | tf_op jit(solution)/shard_map/ppermute | solution.py:322
  56.6 4.8 %collective-permute-start.21 = (bf16[128,128]{1,0:T(8,128)(2,1)S(1)}, bf16[128,128]{1,0:T(8,128)(2,1)S(1)}, u32[]{:S(2)}, u32[]{:S(2)}) collective-permute-start(bf16[128,128]{1,0:T(8,128)(2,1)S(1)} %shard_map.102.refs_0_), channel_id=1, source_target_pairs={{0,2},{1,3},{2,0},{3,1},{4,6},{5,7},{6,4},{7,5},{8,10},{9,11},{10,... | collective-permute-start | bytes 98312 | tf_op jit(solution)/shard_map/ppermute | solution.py:322
  58.4 3.9 %collective-permute-start.20 = (bf16[128,128]{1,0:T(8,128)(2,1)S(1)}, bf16[128,128]{1,0:T(8,128)(2,1)S(1)}, u32[]{:S(2)}, u32[]{:S(2)}) collective-permute-start(bf16[128,128]{1,0:T(8,128)(2,1)S(1)} %shard_map.102.refs_0_), channel_id=1, source_target_pairs={{0,1},{1,0},{2,3},{3,2},{4,5},{5,4},{6,7},{7,6},{8,9},{9,8},{10,11... | collective-permute-start | bytes 98312 | tf_op jit(solution)/shard_map/ppermute | solution.py:322
  (8 other events, 12.9 us)

commit v11 on v8

--- a/solution.py
+++ b/solution.py
@@ -101,17 +101,17 @@
         keys[k * rows : (k + 1) * rows, :] = block[:, block.shape[1] - width :]
     total[...] = jnp.zeros_like(total)
 
-    for head in range(0, heads, 2):
-        two = jnp.concatenate([query[head], query[head + 1]], axis=1)
-        scores = jnp.dot(keys[...], two, preferred_element_type=f32)
+    for head in range(0, heads, 4):
+        four = jnp.concatenate([query[head + n] for n in range(4)], axis=1)
+        scores = jnp.dot(keys[...], four, preferred_element_type=f32)
         parts = [
             jnp.exp2(
-                scores[:, half * rows : (half + 1) * rows] * (main_scale * log2e)
-                - sums_ref[head + half : head + half + 1, :] * log2e
+                scores[:, n * rows : (n + 1) * rows] * (main_scale * log2e)
+                - sums_ref[head + n : head + n + 1, :] * log2e
             )
-            for half in range(2)
+            for n in range(4)
         ]
-        total[...] += parts[0] + parts[1]
+        total[...] += tree(parts)
 
     me = lax.axis_index("pb")
     kept = turned.shape[1] - count * rows

time: 62.6 us -> 62.6 us (level)
  no operation moved by 1% of the time
where the time goes in v11:
time: 62.6 us; the launch traced here: 62.2 us
  starting transfers between devices  31.3 us (50%)
  Pallas kernels  15.1 us (24%)
  waiting for transfers between devices  7.89 us (13%)
  local copies, waits for them, and re-layouts  7.11 us (11%)
  between operations  0.78 us (1%)
    ppermute x23, starting transfers between devices, swap(): return lax.ppermute(value, axis, [(i, i ^ rel) for i in range(size)])  31.3 us
    pallas_call x11, Pallas kernels, call(): pl.pallas_call(kernel, grid=(1,), out_shape=outs, in_specs=specs or [whol...  15.1 us
    ppermute x23, waiting for transfers between devices, swap(): return lax.ppermute(value, axis, [(i, i ^ rel) for i in range(size)])  7.89 us
    unnamed x18, local copies, waits for them, and re-layouts  7.11 us
  transfers between devices with their start and end apart: 23, of which 6 were waited for; matrix products, arithmetic and copies ran while one was open for 0% of the time, Pallas kernels for 17%

profile of v11, /device:TPU:0, one launch (start us, length us, event | category | flops | bytes accessed | tf_op | source)
XLA Modules:
  0.0 62.2 jit_solution(5066366868941475894)
XLA Ops:
  2.9 3.5 %collective-permute-start.3 = (bf16[128,704]{1,0:T(8,128)(2,1)S(1)}, bf16[128,704]{1,0:T(8,128)(2,1)S(1)}, u32[]{:S(2)}, u32[]{:S(2)}) collective-permute-start(bf16[128,704]{1,0:T(8,128)(2,1)S(1)} %shard_map.94.refs_0_.refs_4_), channel_id=1, source_target_pairs={{0,24},{4,28},{8,16},{12,20},{16,8},{20,12},{24,0},{28,4},{1,25},{... | collective-permute-start | bytes 540680 | tf_op jit(solution)/shard_map/ppermute | solution.py:322
  7.1 1.0 %copy-done.2 = bf16[128,16,128]{2,1,0:T(8,128)(2,1)S(1)} copy-done((bf16[128,16,128]{2,1,0:T(8,128)(2,1)S(1)}, bf16[128,16,128]{2,1,0:T(8,128)(2,1)}, u32[]{:S(2)}) %copy-start.2) | copy-done | bytes 524312
  8.9 2.0 %collective-permute-start.4 = (bf16[560,128]{1,0:T(8,128)(2,1)S(1)}, bf16[560,128]{1,0:T(8,128)(2,1)S(1)}, u32[]{:S(2)}, u32[]{:S(2)}) collective-permute-start(bf16[560,128]{1,0:T(8,128)(2,1)S(1)} %get-tuple-element.38), channel_id=1, source_target_pairs={{0,1},{1,0},{2,3},{3,2},{4,5},{5,4},{6,7},{7,6},{8,9},{9,8},{10,11... | collective-permute-start | bytes 430088 | tf_op jit(solution)/shard_map/ppermute | solution.py:322
  10.9 2.6 %collective-permute-start.5 = (bf16[560,128]{1,0:T(8,128)(2,1)S(1)}, bf16[560,128]{1,0:T(8,128)(2,1)S(1)}, u32[]{:S(2)}, u32[]{:S(2)}) collective-permute-start(bf16[560,128]{1,0:T(8,128)(2,1)S(1)} %get-tuple-element.39), channel_id=1, source_target_pairs={{0,2},{1,3},{2,0},{3,1},{4,6},{5,7},{6,4},{7,5},{8,10},{9,11},{10,... | collective-permute-start | bytes 430088 | tf_op jit(solution)/shard_map/ppermute | solution.py:322
  13.5 2.3 %copy-done = bf16[128,32,576]{0,2,1:T(8,128)(2,1)S(1)} copy-done((bf16[128,32,576]{0,2,1:T(8,128)(2,1)S(1)}, bf16[128,32,576]{0,2,1:T(8,128)(2,1)}, u32[]{:S(2)}) %copy-start) | copy-done | bytes 4718616
  17.2 1.9 %shard_map.96.refs_5_ = bf16[128,256]{1,0:T(8,128)(2,1)S(1)} custom-call(bf16[128,704]{1,0:T(8,128)(2,1)S(1)} %shard_map.94.refs_0_.refs_4_, bf16[128,704]{1,0:T(8,128)(2,1)S(1)} %collective-permute-done.refs_1_.refs_5_, bf16[32,576,128]{2,1,0:T(8,128)(2,1)S(1)} %bitcast.8, f32[32,128]{1,0:T(8,128)S(1)} %bitcast.13, s32[1,128]{1,0:T(1,128)S(1)} %bitcast.17), custom_call_target="tpu_custom_call" | custom-call | flops 12079595520 | bytes 4718592 | tf_op jit(solution)/shard_map/pallas_call | solution.py:30
  20.5 2.5 %collective-permute-start.12 = (bf16[560,128]{1,0:T(8,128)(2,1)S(1)}, bf16[560,128]{1,0:T(8,128)(2,1)S(1)}, u32[]{:S(2)}, u32[]{:S(2)}) collective-permute-start(bf16[560,128]{1,0:T(8,128)(2,1)S(1)} %get-tuple-element.53), channel_id=1, source_target_pairs={{0,3},{1,2},{2,1},{3,0},{4,7},{5,6},{6,5},{7,4},{8,11},{9,10},{10,... | collective-permute-start | bytes 430088 | tf_op jit(solution)/shard_map/ppermute | solution.py:322
  23.0 3.6 %shard_map.97.refs_6_ = bf16[128,512]{1,0:T(8,128)(2,1)S(1)} custom-call(bf16[128,704]{1,0:T(8,128)(2,1)S(1)} %collective-permute-done.1.refs_0_.refs_2_.refs_6_, bf16[128,704]{1,0:T(8,128)(2,1)S(1)} %collective-permute-done.7.refs_1_.refs_3_.refs_7_, bf16[128,704]{1,0:T(8,128)(2,1)S(1)} %collective-permute-done.2.refs_2_.refs_4_.refs_8_, ...), custom_call_target="tpu_custom_call" | custom-call | flops 2415919104 | bytes 4718592 | tf_op jit(solution)/shard_map/pallas_call | solution.py:30
  26.6 2.0 %shard_map.98 = (bf16[32,1024]{1,0:T(8,128)(2,1)S(1)}, bf16[32,1024]{1,0:T(8,128)(2,1)S(1)}, bf16[32,1024]{1,0:T(8,128)(2,1)S(1)}, bf16[32,1024]{1,0:T(8,128)(2,1)S(1)}) custom-call(bf16[128,704]{1,0:T(8,128)(2,1)S(1)} %collective-permute-done.3.refs_0_.refs_6_.refs_10_, bf16[128,704]{1,0:T(8,128)(2,1)S(1)} %collective-permute-done.6.refs_1_.refs_7_.refs_11_, ...), custom_call_target="tpu_custom_call" | custom-call | flops 1207959552 | bytes 4718592 | tf_op jit(solution)/shard_map/pallas_call | solution.py:30
  28.7 1.9 %collective-permute-start.10 = (bf16[32,1024]{1,0:T(8,128)(2,1)S(1)}, bf16[32,1024]{1,0:T(8,128)(2,1)S(1)}, u32[]{:S(2)}, u32[]{:S(2)}) collective-permute-start(bf16[32,1024]{1,0:T(8,128)(2,1)S(1)} %get-tuple-element.47), channel_id=1, source_target_pairs={{0,2},{1,3},{2,0},{3,1},{4,6},{5,7},{6,4},{7,5},{8,10},{9,11},{10,... | collective-permute-start | bytes 196616 | tf_op jit(solution)/shard_map/ppermute | solution.py:322
  30.6 2.5 %collective-permute-start.11 = (bf16[32,1024]{1,0:T(8,128)(2,1)S(1)}, bf16[32,1024]{1,0:T(8,128)(2,1)S(1)}, u32[]{:S(2)}, u32[]{:S(2)}) collective-permute-start(bf16[32,1024]{1,0:T(8,128)(2,1)S(1)} %get-tuple-element.48), channel_id=1, source_target_pairs={{0,3},{1,2},{2,1},{3,0},{4,7},{5,6},{6,5},{7,4},{8,11},{9,10},{10,... | collective-permute-start | bytes 196616 | tf_op jit(solution)/shard_map/ppermute | solution.py:322
  33.1 1.9 %shard_map.99 = (f32[1024,128]{1,0:T(8,128)S(1)}, bf16[2048,128]{1,0:T(8,128)(2,1)S(1)}, f32[16,128]{1,0:T(8,128)S(1)}) custom-call(bf16[128,704]{1,0:T(8,128)(2,1)S(1)} %shard_map.94.refs_0_.refs_4_, bf16[128,704]{1,0:T(8,128)(2,1)S(1)} %collective-permute-done.refs_1_.refs_5_, bf16[128,704]{1,0:T(8,128)(2,1)S(1)} %collective-permute-done.1.refs_0_.refs_2_.refs_6_, ...), custom_call_target="tpu_custom_call" | custom-call | flops 536870912 | bytes 524288 | tf_op jit(solution)/shard_map/pallas_call | solution.py:30
  35.0 2.4 %collective-permute-done.10.refs_2_ = bf16[32,1024]{1,0:T(8,128)(2,1)S(1)} collective-permute-done((bf16[32,1024]{1,0:T(8,128)(2,1)S(1)}, bf16[32,1024]{1,0:T(8,128)(2,1)S(1)}, u32[]{:S(2)}, u32[]{:S(2)}) %collective-permute-start.10) | collective-permute-done | bytes 65568 | tf_op jit(solution)/shard_map/ppermute | solution.py:322
  37.4 4.0 %shard_map.100 = (f32[512,128]{1,0:T(8,128)S(1)}, f32[512,128]{1,0:T(8,128)S(1)}, bf16[544,128]{1,0:T(8,128)(2,1)S(1)}, bf16[544,128]{1,0:T(8,128)(2,1)S(1)}, bf...) custom-call(bf16[32,1024]{1,0:T(8,128)(2,1)S(1)} %get-tuple-element.45.refs_0_, ...), custom_call_target="tpu_custom_call" | custom-call | flops 1610612736 | bytes 524288 | tf_op jit(solution)/shard_map/pallas_call | solution.py:30
  41.5 1.6 %collective-permute-start.13 = (bf16[544,128]{1,0:T(8,128)(2,1)S(1)}, bf16[544,128]{1,0:T(8,128)(2,1)S(1)}, u32[]{:S(2)}, u32[]{:S(2)}) collective-permute-start(bf16[544,128]{1,0:T(8,128)(2,1)S(1)} %get-tuple-element.58), channel_id=1, source_target_pairs={{0,1},{1,0},{2,3},{3,2},{4,5},{5,4},{6,7},{7,6},{8,9},{9,8},{10,11... | collective-permute-start | bytes 417800 | tf_op jit(solution)/shard_map/ppermute | solution.py:322
  43.9 2.0 %collective-permute-start.15 = (bf16[544,128]{1,0:T(8,128)(2,1)S(1)}, bf16[544,128]{1,0:T(8,128)(2,1)S(1)}, u32[]{:S(2)}, u32[]{:S(2)}) collective-permute-start(bf16[544,128]{1,0:T(8,128)(2,1)S(1)} %get-tuple-element.60), channel_id=1, source_target_pairs={{0,3},{1,2},{2,1},{3,0},{4,7},{5,6},{6,5},{7,4},{8,11},{9,10},{10,... | collective-permute-start | bytes 417800 | tf_op jit(solution)/shard_map/ppermute | solution.py:322
  46.0 1.6 %collective-permute-start.17 = (bf16[128,128]{1,0:T(8,128)(2,1)S(1)}, bf16[128,128]{1,0:T(8,128)(2,1)S(1)}, u32[]{:S(2)}, u32[]{:S(2)}) collective-permute-start(bf16[128,128]{1,0:T(8,128)(2,1)S(1)} %get-tuple-element.65), channel_id=1, source_target_pairs={{0,8},{4,12},{8,0},{12,4},{16,24},{20,28},{24,16},{28,20},{1,9},{5... | collective-permute-start | bytes 98312 | tf_op jit(solution)/shard_map/ppermute | solution.py:322
  47.5 1.5 %collective-permute-start.18 = (bf16[128,128]{1,0:T(8,128)(2,1)S(1)}, bf16[128,128]{1,0:T(8,128)(2,1)S(1)}, u32[]{:S(2)}, u32[]{:S(2)}) collective-permute-start(bf16[128,128]{1,0:T(8,128)(2,1)S(1)} %get-tuple-element.66), channel_id=1, source_target_pairs={{0,16},{4,20},{8,24},{12,28},{16,0},{20,4},{24,8},{28,12},{1,17},{... | collective-permute-start | bytes 98312 | tf_op jit(solution)/shard_map/ppermute | solution.py:322
  49.0 0.9 %collective-permute-done.17.refs_1_ = bf16[128,128]{1,0:T(8,128)(2,1)S(1)} collective-permute-done((bf16[128,128]{1,0:T(8,128)(2,1)S(1)}, bf16[128,128]{1,0:T(8,128)(2,1)S(1)}, u32[]{:S(2)}, u32[]{:S(2)}) %collective-permute-start.17) | collective-permute-done | bytes 32800 | tf_op jit(solution)/shard_map/ppermute | solution.py:322
  49.9 2.4 %collective-permute-start.19 = (bf16[128,128]{1,0:T(8,128)(2,1)S(1)}, bf16[128,128]{1,0:T(8,128)(2,1)S(1)}, u32[]{:S(2)}, u32[]{:S(2)}) collective-permute-start(bf16[128,128]{1,0:T(8,128)(2,1)S(1)} %get-tuple-element.67), channel_id=1, source_target_pairs={{0,24},{4,28},{8,16},{12,20},{16,8},{20,12},{24,0},{28,4},{1,25},{... | collective-permute-start | bytes 98312 | tf_op jit(solution)/shard_map/ppermute | solution.py:322
  52.4 2.4 %collective-permute-done.19.refs_3_ = bf16[128,128]{1,0:T(8,128)(2,1)S(1)} collective-permute-done((bf16[128,128]{1,0:T(8,128)(2,1)S(1)}, bf16[128,128]{1,0:T(8,128)(2,1)S(1)}, u32[]{:S(2)}, u32[]{:S(2)}) %collective-permute-start.19) | collective-permute-done | bytes 32800 | tf_op jit(solution)/shard_map/ppermute | solution.py:322
  54.8 1.8 %collective-permute-start.22 = (bf16[128,128]{1,0:T(8,128)(2,1)S(1)}, bf16[128,128]{1,0:T(8,128)(2,1)S(1)}, u32[]{:S(2)}, u32[]{:S(2)}) collective-permute-start(bf16[128,128]{1,0:T(8,128)(2,1)S(1)} %shard_map.103.refs_0_), channel_id=1, source_target_pairs={{0,3},{1,2},{2,1},{3,0},{4,7},{5,6},{6,5},{7,4},{8,11},{9,10},{10,... | collective-permute-start | bytes 98312 | tf_op jit(solution)/shard_map/ppermute | solution.py:322
  57.0 2.3 %collective-permute-start.20 = (bf16[128,128]{1,0:T(8,128)(2,1)S(1)}, bf16[128,128]{1,0:T(8,128)(2,1)S(1)}, u32[]{:S(2)}, u32[]{:S(2)}) collective-permute-start(bf16[128,128]{1,0:T(8,128)(2,1)S(1)} %shard_map.103.refs_0_), channel_id=1, source_target_pairs={{0,1},{1,0},{2,3},{3,2},{4,5},{5,4},{6,7},{7,6},{8,9},{9,8},{10,11... | collective-permute-start | bytes 98312 | tf_op jit(solution)/shard_map/ppermute | solution.py:322
  59.2 0.9 %shard_map.101 = (bf16[2048,128]{1,0:T(8,128)(2,1)}, f32[16,128]{1,0:T(8,128)}) custom-call(bf16[544,128]{1,0:T(8,128)(2,1)S(1)} %get-tuple-element.57.refs_0_, bf16[544,128]{1,0:T(8,128)(2,1)S(1)} %collective-permute-done.13.refs_1_, bf16[544,128]{1,0:T(8,128)(2,1)S(1)} %collective-permute-done.14.refs_2_, bf16[544,128]{1,0:T(8,128)(2,1)S(1)} %collective-permute-done.15.refs_3_), custom_call_target="tpu_custom_call" | custom-call | tf_op jit(solution)/shard_map/pallas_call | solution.py:30
  (51 shorter events, 9.8 us)
Async XLA Ops:
  2.4 8.5 %collective-permute-start = (bf16[128,704]{1,0:T(8,128)(2,1)S(1)}, bf16[128,704]{1,0:T(8,128)(2,1)S(1)}, u32[]{:S(2)}, u32[]{:S(2)}) collective-permute-start(bf16[128,704]{1,0:T(8,128)(2,1)S(1)} %shard_map.94.refs_0_.refs_4_), channel_id=1, source_target_pairs={{0,4},{4,0},{8,12},{12,8},{16,20},{20,16},{24,28},{28,24},{1,5},{5... | collective-permute-start | bytes 540680 | tf_op jit(solution)/shard_map/ppermute | solution.py:322
  2.9 17.0 %collective-permute-start.3 = (bf16[128,704]{1,0:T(8,128)(2,1)S(1)}, bf16[128,704]{1,0:T(8,128)(2,1)S(1)}, u32[]{:S(2)}, u32[]{:S(2)}) collective-permute-start(bf16[128,704]{1,0:T(8,128)(2,1)S(1)} %shard_map.94.refs_0_.refs_4_), channel_id=1, source_target_pairs={{0,24},{4,28},{8,16},{12,20},{16,8},{20,12},{24,0},{28,4},{1,25},{... | collective-permute-start | bytes 540680 | tf_op jit(solution)/shard_map/ppermute | solution.py:322
  6.4 13.5 %collective-permute-start.2 = (bf16[128,704]{1,0:T(8,128)(2,1)S(1)}, bf16[128,704]{1,0:T(8,128)(2,1)S(1)}, u32[]{:S(2)}, u32[]{:S(2)}) collective-permute-start(bf16[128,704]{1,0:T(8,128)(2,1)S(1)} %shard_map.94.refs_0_.refs_4_), channel_id=1, source_target_pairs={{0,16},{4,20},{8,24},{12,28},{16,0},{20,4},{24,8},{28,12},{1,17},{... | collective-permute-start | bytes 540680 | tf_op jit(solution)/shard_map/ppermute | solution.py:322
  7.0 13.0 %collective-permute-start.1 = (bf16[128,704]{1,0:T(8,128)(2,1)S(1)}, bf16[128,704]{1,0:T(8,128)(2,1)S(1)}, u32[]{:S(2)}, u32[]{:S(2)}) collective-permute-start(bf16[128,704]{1,0:T(8,128)(2,1)S(1)} %shard_map.94.refs_0_.refs_4_), channel_id=1, source_target_pairs={{0,8},{4,12},{8,0},{12,4},{16,24},{20,28},{24,16},{28,20},{1,9},{5... | collective-permute-start | bytes 540680 | tf_op jit(solution)/shard_map/ppermute | solution.py:322
  8.9 10.3 %collective-permute-start.4 = (bf16[560,128]{1,0:T(8,128)(2,1)S(1)}, bf16[560,128]{1,0:T(8,128)(2,1)S(1)}, u32[]{:S(2)}, u32[]{:S(2)}) collective-permute-start(bf16[560,128]{1,0:T(8,128)(2,1)S(1)} %get-tuple-element.38), channel_id=1, source_target_pairs={{0,1},{1,0},{2,3},{3,2},{4,5},{5,4},{6,7},{7,6},{8,9},{9,8},{10,11... | collective-permute-start | bytes 430088 | tf_op jit(solution)/shard_map/ppermute | solution.py:322
  10.9 9.0 %collective-permute-start.5 = (bf16[560,128]{1,0:T(8,128)(2,1)S(1)}, bf16[560,128]{1,0:T(8,128)(2,1)S(1)}, u32[]{:S(2)}, u32[]{:S(2)}) collective-permute-start(bf16[560,128]{1,0:T(8,128)(2,1)S(1)} %get-tuple-element.39), channel_id=1, source_target_pairs={{0,2},{1,3},{2,0},{3,1},{4,6},{5,7},{6,4},{7,5},{8,10},{9,11},{10,... | collective-permute-start | bytes 430088 | tf_op jit(solution)/shard_map/ppermute | solution.py:322
  17.2 5.8 %copy-start.6 = (f32[128,32]{0,1:T(8,128)S(1)}, f32[128,32]{0,1:T(8,128)}, u32[]{:S(2)}) copy-start(f32[128,32]{0,1:T(8,128)} %param.9) | copy-start | bytes 49156
  19.9 3.1 %collective-permute-start.7 = (bf16[128,704]{1,0:T(8,128)(2,1)S(1)}, bf16[128,704]{1,0:T(8,128)(2,1)S(1)}, u32[]{:S(2)}, u32[]{:S(2)}) collective-permute-start(bf16[128,704]{1,0:T(8,128)(2,1)S(1)} %collective-permute-done.1.refs_0_.refs_2_.refs_6_), channel_id=1, source_target_pairs={{0,4},{4,0},{8,12},{12,8},{16,20},{20,16},{24,28},{28,24},{1,5},{5... | collective-permute-start | bytes 540680 | tf_op jit(solution)/shard_map/ppermute | solution.py:322
  20.0 3.0 %collective-permute-start.8 = (bf16[128,704]{1,0:T(8,128)(2,1)S(1)}, bf16[128,704]{1,0:T(8,128)(2,1)S(1)}, u32[]{:S(2)}, u32[]{:S(2)}) collective-permute-start(bf16[128,704]{1,0:T(8,128)(2,1)S(1)} %collective-permute-done.2.refs_2_.refs_4_.refs_8_), channel_id=1, source_target_pairs={{0,4},{4,0},{8,12},{12,8},{16,20},{20,16},{24,28},{28,24},{1,5},{5... | collective-permute-start | bytes 540680 | tf_op jit(solution)/shard_map/ppermute | solution.py:322
  20.5 12.5 %collective-permute-start.12 = (bf16[560,128]{1,0:T(8,128)(2,1)S(1)}, bf16[560,128]{1,0:T(8,128)(2,1)S(1)}, u32[]{:S(2)}, u32[]{:S(2)}) collective-permute-start(bf16[560,128]{1,0:T(8,128)(2,1)S(1)} %get-tuple-element.53), channel_id=1, source_target_pairs={{0,3},{1,2},{2,1},{3,0},{4,7},{5,6},{6,5},{7,4},{8,11},{9,10},{10,... | collective-permute-start | bytes 430088 | tf_op jit(solution)/shard_map/ppermute | solution.py:322
  23.0 3.6 %collective-permute-start.6 = (bf16[128,704]{1,0:T(8,128)(2,1)S(1)}, bf16[128,704]{1,0:T(8,128)(2,1)S(1)}, u32[]{:S(2)}, u32[]{:S(2)}) collective-permute-start(bf16[128,704]{1,0:T(8,128)(2,1)S(1)} %collective-permute-done.3.refs_0_.refs_6_.refs_10_), channel_id=1, source_target_pairs={{0,4},{4,0},{8,12},{12,8},{16,20},{20,16},{24,28},{28,24},{1,5},{5... | collective-permute-start | bytes 540680 | tf_op jit(solution)/shard_map/ppermute | solution.py:322
  28.6 6.4 %collective-permute-start.9 = (bf16[32,1024]{1,0:T(8,128)(2,1)S(1)}, bf16[32,1024]{1,0:T(8,128)(2,1)S(1)}, u32[]{:S(2)}, u32[]{:S(2)}) collective-permute-start(bf16[32,1024]{1,0:T(8,128)(2,1)S(1)} %get-tuple-element.46), channel_id=1, source_target_pairs={{0,1},{1,0},{2,3},{3,2},{4,5},{5,4},{6,7},{7,6},{8,9},{9,8},{10,11... | collective-permute-start | bytes 196616 | tf_op jit(solution)/shard_map/ppermute | solution.py:322
  28.7 8.7 %collective-permute-start.10 = (bf16[32,1024]{1,0:T(8,128)(2,1)S(1)}, bf16[32,1024]{1,0:T(8,128)(2,1)S(1)}, u32[]{:S(2)}, u32[]{:S(2)}) collective-permute-start(bf16[32,1024]{1,0:T(8,128)(2,1)S(1)} %get-tuple-element.47), channel_id=1, source_target_pairs={{0,2},{1,3},{2,0},{3,1},{4,6},{5,7},{6,4},{7,5},{8,10},{9,11},{10,... | collective-permute-start | bytes 196616 | tf_op jit(solution)/shard_map/ppermute | solution.py:322
  30.6 6.8 %collective-permute-start.11 = (bf16[32,1024]{1,0:T(8,128)(2,1)S(1)}, bf16[32,1024]{1,0:T(8,128)(2,1)S(1)}, u32[]{:S(2)}, u32[]{:S(2)}) collective-permute-start(bf16[32,1024]{1,0:T(8,128)(2,1)S(1)} %get-tuple-element.48), channel_id=1, source_target_pairs={{0,3},{1,2},{2,1},{3,0},{4,7},{5,6},{6,5},{7,4},{8,11},{9,10},{10,... | collective-permute-start | bytes 196616 | tf_op jit(solution)/shard_map/ppermute | solution.py:322
  41.4 4.5 %collective-permute-start.16 = (f32[512,128]{1,0:T(8,128)S(1)}, f32[512,128]{1,0:T(8,128)S(1)}, u32[]{:S(2)}, u32[]{:S(2)}) collective-permute-start(f32[512,128]{1,0:T(8,128)S(1)} %get-tuple-element.63), channel_id=1, source_target_pairs={{0,4},{4,0},{8,12},{12,8},{16,20},{20,16},{24,28},{28,24},{1,5},{5... | collective-permute-start | bytes 786440 | tf_op jit(solution)/shard_map/ppermute | solution.py:322
  41.5 15.5 %collective-permute-start.13 = (bf16[544,128]{1,0:T(8,128)(2,1)S(1)}, bf16[544,128]{1,0:T(8,128)(2,1)S(1)}, u32[]{:S(2)}, u32[]{:S(2)}) collective-permute-start(bf16[544,128]{1,0:T(8,128)(2,1)S(1)} %get-tuple-element.58), channel_id=1, source_target_pairs={{0,1},{1,0},{2,3},{3,2},{4,5},{5,4},{6,7},{7,6},{8,9},{9,8},{10,11... | collective-permute-start | bytes 417800 | tf_op jit(solution)/shard_map/ppermute | solution.py:322
  43.1 16.1 %collective-permute-start.14 = (bf16[544,128]{1,0:T(8,128)(2,1)S(1)}, bf16[544,128]{1,0:T(8,128)(2,1)S(1)}, u32[]{:S(2)}, u32[]{:S(2)}) collective-permute-start(bf16[544,128]{1,0:T(8,128)(2,1)S(1)} %get-tuple-element.59), channel_id=1, source_target_pairs={{0,2},{1,3},{2,0},{3,1},{4,6},{5,7},{6,4},{7,5},{8,10},{9,11},{10,... | collective-permute-start | bytes 417800 | tf_op jit(solution)/shard_map/ppermute | solution.py:322
  43.9 15.4 %collective-permute-start.15 = (bf16[544,128]{1,0:T(8,128)(2,1)S(1)}, bf16[544,128]{1,0:T(8,128)(2,1)S(1)}, u32[]{:S(2)}, u32[]{:S(2)}) collective-permute-start(bf16[544,128]{1,0:T(8,128)(2,1)S(1)} %get-tuple-element.60), channel_id=1, source_target_pairs={{0,3},{1,2},{2,1},{3,0},{4,7},{5,6},{6,5},{7,4},{8,11},{9,10},{10,... | collective-permute-start | bytes 417800 | tf_op jit(solution)/shard_map/ppermute | solution.py:322
  46.0 4.0 %collective-permute-start.17 = (bf16[128,128]{1,0:T(8,128)(2,1)S(1)}, bf16[128,128]{1,0:T(8,128)(2,1)S(1)}, u32[]{:S(2)}, u32[]{:S(2)}) collective-permute-start(bf16[128,128]{1,0:T(8,128)(2,1)S(1)} %get-tuple-element.65), channel_id=1, source_target_pairs={{0,8},{4,12},{8,0},{12,4},{16,24},{20,28},{24,16},{28,20},{1,9},{5... | collective-permute-start | bytes 98312 | tf_op jit(solution)/shard_map/ppermute | solution.py:322
  47.5 4.9 %collective-permute-start.18 = (bf16[128,128]{1,0:T(8,128)(2,1)S(1)}, bf16[128,128]{1,0:T(8,128)(2,1)S(1)}, u32[]{:S(2)}, u32[]{:S(2)}) collective-permute-start(bf16[128,128]{1,0:T(8,128)(2,1)S(1)} %get-tuple-element.66), channel_id=1, source_target_pairs={{0,16},{4,20},{8,24},{12,28},{16,0},{20,4},{24,8},{28,12},{1,17},{... | collective-permute-start | bytes 98312 | tf_op jit(solution)/shard_map/ppermute | solution.py:322
  49.9 4.8 %collective-permute-start.19 = (bf16[128,128]{1,0:T(8,128)(2,1)S(1)}, bf16[128,128]{1,0:T(8,128)(2,1)S(1)}, u32[]{:S(2)}, u32[]{:S(2)}) collective-permute-start(bf16[128,128]{1,0:T(8,128)(2,1)S(1)} %get-tuple-element.67), channel_id=1, source_target_pairs={{0,24},{4,28},{8,16},{12,20},{16,8},{20,12},{24,0},{28,4},{1,25},{... | collective-permute-start | bytes 98312 | tf_op jit(solution)/shard_map/ppermute | solution.py:322
  54.8 5.9 %collective-permute-start.22 = (bf16[128,128]{1,0:T(8,128)(2,1)S(1)}, bf16[128,128]{1,0:T(8,128)(2,1)S(1)}, u32[]{:S(2)}, u32[]{:S(2)}) collective-permute-start(bf16[128,128]{1,0:T(8,128)(2,1)S(1)} %shard_map.103.refs_0_), channel_id=1, source_target_pairs={{0,3},{1,2},{2,1},{3,0},{4,7},{5,6},{6,5},{7,4},{8,11},{9,10},{10,... | collective-permute-start | bytes 98312 | tf_op jit(solution)/shard_map/ppermute | solution.py:322
  56.6 4.9 %collective-permute-start.21 = (bf16[128,128]{1,0:T(8,128)(2,1)S(1)}, bf16[128,128]{1,0:T(8,128)(2,1)S(1)}, u32[]{:S(2)}, u32[]{:S(2)}) collective-permute-start(bf16[128,128]{1,0:T(8,128)(2,1)S(1)} %shard_map.103.refs_0_), channel_id=1, source_target_pairs={{0,2},{1,3},{2,0},{3,1},{4,6},{5,7},{6,4},{7,5},{8,10},{9,11},{10,... | collective-permute-start | bytes 98312 | tf_op jit(solution)/shard_map/ppermute | solution.py:322
  57.0 4.6 %collective-permute-start.20 = (bf16[128,128]{1,0:T(8,128)(2,1)S(1)}, bf16[128,128]{1,0:T(8,128)(2,1)S(1)}, u32[]{:S(2)}, u32[]{:S(2)}) collective-permute-start(bf16[128,128]{1,0:T(8,128)(2,1)S(1)} %shard_map.103.refs_0_), channel_id=1, source_target_pairs={{0,1},{1,0},{2,3},{3,2},{4,5},{5,4},{6,7},{7,6},{8,9},{9,8},{10,11... | collective-permute-start | bytes 98312 | tf_op jit(solution)/shard_map/ppermute | solution.py:322
  (8 other events, 12.9 us)

commit v12 on v8

--- a/solution.py
+++ b/solution.py
@@ -91,9 +91,9 @@
 def main_kernel(rels, earlier, *refs):
     count = len(rels)
     blocks = refs[:count]
-    query, sums_ref, start_ref = refs[count : count + 3]
-    before = refs[count + 3 : count + 3 + earlier]
-    outs = refs[count + 3 + earlier : -3]
+    query, sums_ref = refs[count : count + 2]
+    before = refs[count + 2 : count + 2 + earlier]
+    outs = refs[count + 2 + earlier : -3]
     keys, total, turned = refs[-3:]
     heads, width, rows = query.shape
     for k in range(count):
@@ -122,7 +122,8 @@
     for k in range(count):
         key = (me ^ rels[k]) * rows + lax.broadcasted_iota(jnp.int32, (rows, rows), 0)
         mine = me * rows + lax.broadcasted_iota(jnp.int32, (rows, rows), 1)
-        seen = (key >= start_ref[...]) & (key <= mine)
+        start = sums_ref[heads : heads + 1, :].astype(jnp.int32)
+        seen = (key >= start) & (key <= mine)
         piece = jnp.where(seen, total[k * rows : (k + 1) * rows, :], 0.0)
         turned[:, kept + k * rows : kept + (k + 1) * rows] = piece.T
     if len(outs) == 1:
@@ -336,7 +337,7 @@
         (index_query.reshape(rows * heads, index_width), index_weight.T),
     )
     queries = jnp.transpose(main_query, (1, 2, 0))
-    sums = log_sums.T
+    sums = jnp.concatenate([log_sums.T, window_start.astype(f32)[None, :]], axis=0)
     held = [None] * blocks
     held[0] = packed
     held[1] = swap(packed, "pb", 1)
@@ -353,7 +354,7 @@
         span = len(rels) * rows
         outs = [shape((share, tokens), bf16)] * parts if last else [shape((rows, span), bf16)]
         before = mass if last else []
-        values = [held[k] for k in rels] + [queries, sums, start_row] + before
+        values = [held[k] for k in rels] + [queries, sums] + before
         specs = [whole(v) for v in values]
         specs[len(rels)] = pl.BlockSpec(memory_space=pltpu.VMEM)
         found = call(

time: 62.6 us -> 64.8 us (1.035)
  waiting for transfers between devices: 7.91 us -> 10.1 us
  other arithmetic: 0 us -> 1.38 us
  local copies, waits for them, and re-layouts: 7.11 us -> 5.74 us
    ppermute x23, waiting for transfers between devices: 7.91 us -> 10.1 us  [swap(): return lax.ppermute(value, axis, [(i, i ^ rel) for i in range(size)])]
    unnamed x18 -> x14, local copies, waits for them, and re-layouts: 7.11 us -> 5.74 us
    concatenate x0 -> x1, other arithmetic: none -> 0.72 us  [on_device(): jnp.concatenate([log_sums.T, window_start.astype(f32)[None, :]], axis=0)]
    broadcast_in_dim x0 -> x1, other arithmetic: none -> 0.66 us  [on_device(): window_start.astype(f32)[None, :]]
  transfers between devices with their start and end apart: 23 -> 23, of which waited for: 6 -> 6; matrix products, arithmetic and copies ran while one was open for 0% -> 2% of each run, Pallas kernels for 17% -> 16%
where the time goes in v12:
time: 64.8 us; the launch traced here: 64.4 us
  starting transfers between devices  31.3 us (48%)
  Pallas kernels  15.1 us (23%)
  waiting for transfers between devices  10.1 us (16%)
  local copies, waits for them, and re-layouts  5.74 us (9%)
  other arithmetic  1.38 us (2%)
  between operations  0.78 us (1%)
    ppermute x23, starting transfers between devices, swap(): return lax.ppermute(value, axis, [(i, i ^ rel) for i in range(size)])  31.3 us
    pallas_call x11, Pallas kernels, call(): pl.pallas_call(kernel, grid=(1,), out_shape=outs, in_specs=specs or [whol...  15.1 us
    ppermute x23, waiting for transfers between devices, swap(): return lax.ppermute(value, axis, [(i, i ^ rel) for i in range(size)])  10.1 us
    unnamed x14, local copies, waits for them, and re-layouts  5.74 us
  transfers between devices with their start and end apart: 23, of which 6 were waited for; matrix products, arithmetic and copies ran while one was open for 2% of the time, Pallas kernels for 16%

profile of v12, /device:TPU:0, one launch (start us, length us, event | category | flops | bytes accessed | tf_op | source)
XLA Modules:
  0.0 64.4 jit_solution(4236543894710193880)
XLA Ops:
  2.4 4.0 %collective-permute-start.3 = (bf16[128,704]{1,0:T(8,128)(2,1)S(1)}, bf16[128,704]{1,0:T(8,128)(2,1)S(1)}, u32[]{:S(2)}, u32[]{:S(2)}) collective-permute-start(bf16[128,704]{1,0:T(8,128)(2,1)S(1)} %shard_map.94.refs_0_.refs_4_), channel_id=1, source_target_pairs={{0,24},{4,28},{8,16},{12,20},{16,8},{20,12},{24,0},{28,4},{1,25},{... | collective-permute-start | bytes 540680 | tf_op jit(solution)/shard_map/ppermute | solution.py:323
  7.0 1.0 %copy-done.2 = bf16[128,16,128]{2,1,0:T(8,128)(2,1)S(1)} copy-done((bf16[128,16,128]{2,1,0:T(8,128)(2,1)S(1)}, bf16[128,16,128]{2,1,0:T(8,128)(2,1)}, u32[]{:S(2)}) %copy-start.2) | copy-done | bytes 524312
  8.8 2.0 %collective-permute-start.4 = (bf16[560,128]{1,0:T(8,128)(2,1)S(1)}, bf16[560,128]{1,0:T(8,128)(2,1)S(1)}, u32[]{:S(2)}, u32[]{:S(2)}) collective-permute-start(bf16[560,128]{1,0:T(8,128)(2,1)S(1)} %get-tuple-element.38), channel_id=1, source_target_pairs={{0,1},{1,0},{2,3},{3,2},{4,5},{5,4},{6,7},{7,6},{8,9},{9,8},{10,11... | collective-permute-start | bytes 430088 | tf_op jit(solution)/shard_map/ppermute | solution.py:323
  12.2 2.6 %collective-permute-start.5 = (bf16[560,128]{1,0:T(8,128)(2,1)S(1)}, bf16[560,128]{1,0:T(8,128)(2,1)S(1)}, u32[]{:S(2)}, u32[]{:S(2)}) collective-permute-start(bf16[560,128]{1,0:T(8,128)(2,1)S(1)} %get-tuple-element.39), channel_id=1, source_target_pairs={{0,2},{1,3},{2,0},{3,1},{4,6},{5,7},{6,4},{7,5},{8,10},{9,11},{10,... | collective-permute-start | bytes 430088 | tf_op jit(solution)/shard_map/ppermute | solution.py:323
  14.8 2.3 %copy-done = bf16[128,32,576]{0,2,1:T(8,128)(2,1)S(1)} copy-done((bf16[128,32,576]{0,2,1:T(8,128)(2,1)S(1)}, bf16[128,32,576]{0,2,1:T(8,128)(2,1)}, u32[]{:S(2)}) %copy-start) | copy-done | bytes 4718616
  17.2 1.9 %shard_map.96.refs_4_ = bf16[128,256]{1,0:T(8,128)(2,1)S(1)} custom-call(bf16[128,704]{1,0:T(8,128)(2,1)S(1)} %shard_map.94.refs_0_.refs_4_, bf16[128,704]{1,0:T(8,128)(2,1)S(1)} %collective-permute-done.refs_1_.refs_5_, bf16[32,576,128]{2,1,0:T(8,128)(2,1)S(1)} %bitcast.10, f32[33,128]{1,0:T(8,128)S(1)} %pad_maximum_fusion.refs_3_.refs_5_), custom_call_target="tpu_custom_call" | custom-call | flops 12079595520 | bytes 4718592 | tf_op jit(solution)/shard_map/pallas_call | solution.py:30
  19.1 3.0 %collective-permute-done.5.refs_10_ = bf16[560,128]{1,0:T(8,128)(2,1)S(1)} collective-permute-done((bf16[560,128]{1,0:T(8,128)(2,1)S(1)}, bf16[560,128]{1,0:T(8,128)(2,1)S(1)}, u32[]{:S(2)}, u32[]{:S(2)}) %collective-permute-start.5) | collective-permute-done | bytes 143392 | tf_op jit(solution)/shard_map/ppermute | solution.py:323
  22.7 2.5 %collective-permute-start.12 = (bf16[560,128]{1,0:T(8,128)(2,1)S(1)}, bf16[560,128]{1,0:T(8,128)(2,1)S(1)}, u32[]{:S(2)}, u32[]{:S(2)}) collective-permute-start(bf16[560,128]{1,0:T(8,128)(2,1)S(1)} %get-tuple-element.53), channel_id=1, source_target_pairs={{0,3},{1,2},{2,1},{3,0},{4,7},{5,6},{6,5},{7,4},{8,11},{9,10},{10,... | collective-permute-start | bytes 430088 | tf_op jit(solution)/shard_map/ppermute | solution.py:323
  25.2 3.6 %shard_map.97.refs_5_ = bf16[128,512]{1,0:T(8,128)(2,1)S(1)} custom-call(bf16[128,704]{1,0:T(8,128)(2,1)S(1)} %collective-permute-done.1.refs_0_.refs_2_.refs_6_, bf16[128,704]{1,0:T(8,128)(2,1)S(1)} %collective-permute-done.7.refs_1_.refs_3_.refs_7_, bf16[128,704]{1,0:T(8,128)(2,1)S(1)} %collective-permute-done.2.refs_2_.refs_4_.refs_8_, ...), custom_call_target="tpu_custom_call" | custom-call | flops 2415919104 | bytes 4718592 | tf_op jit(solution)/shard_map/pallas_call | solution.py:30
  28.8 1.9 %shard_map.98 = (bf16[32,1024]{1,0:T(8,128)(2,1)S(1)}, bf16[32,1024]{1,0:T(8,128)(2,1)S(1)}, bf16[32,1024]{1,0:T(8,128)(2,1)S(1)}, bf16[32,1024]{1,0:T(8,128)(2,1)S(1)}) custom-call(bf16[128,704]{1,0:T(8,128)(2,1)S(1)} %collective-permute-done.3.refs_0_.refs_6_.refs_10_, bf16[128,704]{1,0:T(8,128)(2,1)S(1)} %collective-permute-done.6.refs_1_.refs_7_.refs_11_, ...), custom_call_target="tpu_custom_call" | custom-call | flops 1207959552 | bytes 4718592 | tf_op jit(solution)/shard_map/pallas_call | solution.py:30
  30.9 1.9 %collective-permute-start.10 = (bf16[32,1024]{1,0:T(8,128)(2,1)S(1)}, bf16[32,1024]{1,0:T(8,128)(2,1)S(1)}, u32[]{:S(2)}, u32[]{:S(2)}) collective-permute-start(bf16[32,1024]{1,0:T(8,128)(2,1)S(1)} %get-tuple-element.47), channel_id=1, source_target_pairs={{0,2},{1,3},{2,0},{3,1},{4,6},{5,7},{6,4},{7,5},{8,10},{9,11},{10,... | collective-permute-start | bytes 196616 | tf_op jit(solution)/shard_map/ppermute | solution.py:323
  32.7 2.5 %collective-permute-start.11 = (bf16[32,1024]{1,0:T(8,128)(2,1)S(1)}, bf16[32,1024]{1,0:T(8,128)(2,1)S(1)}, u32[]{:S(2)}, u32[]{:S(2)}) collective-permute-start(bf16[32,1024]{1,0:T(8,128)(2,1)S(1)} %get-tuple-element.48), channel_id=1, source_target_pairs={{0,3},{1,2},{2,1},{3,0},{4,7},{5,6},{6,5},{7,4},{8,11},{9,10},{10,... | collective-permute-start | bytes 196616 | tf_op jit(solution)/shard_map/ppermute | solution.py:323
  35.2 1.9 %shard_map.99 = (f32[1024,128]{1,0:T(8,128)S(1)}, bf16[2048,128]{1,0:T(8,128)(2,1)S(1)}, f32[16,128]{1,0:T(8,128)S(1)}) custom-call(bf16[128,704]{1,0:T(8,128)(2,1)S(1)} %shard_map.94.refs_0_.refs_4_, bf16[128,704]{1,0:T(8,128)(2,1)S(1)} %collective-permute-done.refs_1_.refs_5_, bf16[128,704]{1,0:T(8,128)(2,1)S(1)} %collective-permute-done.1.refs_0_.refs_2_.refs_6_, ...), custom_call_target="tpu_custom_call" | custom-call | flops 536870912 | bytes 524288 | tf_op jit(solution)/shard_map/pallas_call | solution.py:30
  37.2 2.4 %collective-permute-done.10.refs_2_ = bf16[32,1024]{1,0:T(8,128)(2,1)S(1)} collective-permute-done((bf16[32,1024]{1,0:T(8,128)(2,1)S(1)}, bf16[32,1024]{1,0:T(8,128)(2,1)S(1)}, u32[]{:S(2)}, u32[]{:S(2)}) %collective-permute-start.10) | collective-permute-done | bytes 65568 | tf_op jit(solution)/shard_map/ppermute | solution.py:323
  39.6 4.0 %shard_map.100 = (f32[512,128]{1,0:T(8,128)S(1)}, f32[512,128]{1,0:T(8,128)S(1)}, bf16[544,128]{1,0:T(8,128)(2,1)S(1)}, bf16[544,128]{1,0:T(8,128)(2,1)S(1)}, bf...) custom-call(bf16[32,1024]{1,0:T(8,128)(2,1)S(1)} %get-tuple-element.45.refs_0_, ...), custom_call_target="tpu_custom_call" | custom-call | flops 1610612736 | bytes 524288 | tf_op jit(solution)/shard_map/pallas_call | solution.py:30
  43.7 1.6 %collective-permute-start.13 = (bf16[544,128]{1,0:T(8,128)(2,1)S(1)}, bf16[544,128]{1,0:T(8,128)(2,1)S(1)}, u32[]{:S(2)}, u32[]{:S(2)}) collective-permute-start(bf16[544,128]{1,0:T(8,128)(2,1)S(1)} %get-tuple-element.58), channel_id=1, source_target_pairs={{0,1},{1,0},{2,3},{3,2},{4,5},{5,4},{6,7},{7,6},{8,9},{9,8},{10,11... | collective-permute-start | bytes 417800 | tf_op jit(solution)/shard_map/ppermute | solution.py:323
  46.1 2.0 %collective-permute-start.15 = (bf16[544,128]{1,0:T(8,128)(2,1)S(1)}, bf16[544,128]{1,0:T(8,128)(2,1)S(1)}, u32[]{:S(2)}, u32[]{:S(2)}) collective-permute-start(bf16[544,128]{1,0:T(8,128)(2,1)S(1)} %get-tuple-element.60), channel_id=1, source_target_pairs={{0,3},{1,2},{2,1},{3,0},{4,7},{5,6},{6,5},{7,4},{8,11},{9,10},{10,... | collective-permute-start | bytes 417800 | tf_op jit(solution)/shard_map/ppermute | solution.py:323
  48.2 1.6 %collective-permute-start.17 = (bf16[128,128]{1,0:T(8,128)(2,1)S(1)}, bf16[128,128]{1,0:T(8,128)(2,1)S(1)}, u32[]{:S(2)}, u32[]{:S(2)}) collective-permute-start(bf16[128,128]{1,0:T(8,128)(2,1)S(1)} %get-tuple-element.65), channel_id=1, source_target_pairs={{0,8},{4,12},{8,0},{12,4},{16,24},{20,28},{24,16},{28,20},{1,9},{5... | collective-permute-start | bytes 98312 | tf_op jit(solution)/shard_map/ppermute | solution.py:323
  49.7 1.5 %collective-permute-start.18 = (bf16[128,128]{1,0:T(8,128)(2,1)S(1)}, bf16[128,128]{1,0:T(8,128)(2,1)S(1)}, u32[]{:S(2)}, u32[]{:S(2)}) collective-permute-start(bf16[128,128]{1,0:T(8,128)(2,1)S(1)} %get-tuple-element.66), channel_id=1, source_target_pairs={{0,16},{4,20},{8,24},{12,28},{16,0},{20,4},{24,8},{28,12},{1,17},{... | collective-permute-start | bytes 98312 | tf_op jit(solution)/shard_map/ppermute | solution.py:323
  52.1 2.5 %collective-permute-start.19 = (bf16[128,128]{1,0:T(8,128)(2,1)S(1)}, bf16[128,128]{1,0:T(8,128)(2,1)S(1)}, u32[]{:S(2)}, u32[]{:S(2)}) collective-permute-start(bf16[128,128]{1,0:T(8,128)(2,1)S(1)} %get-tuple-element.67), channel_id=1, source_target_pairs={{0,24},{4,28},{8,16},{12,20},{16,8},{20,12},{24,0},{28,4},{1,25},{... | collective-permute-start | bytes 98312 | tf_op jit(solution)/shard_map/ppermute | solution.py:323
  54.6 2.4 %collective-permute-done.19.refs_3_ = bf16[128,128]{1,0:T(8,128)(2,1)S(1)} collective-permute-done((bf16[128,128]{1,0:T(8,128)(2,1)S(1)}, bf16[128,128]{1,0:T(8,128)(2,1)S(1)}, u32[]{:S(2)}, u32[]{:S(2)}) %collective-permute-start.19) | collective-permute-done | bytes 32800 | tf_op jit(solution)/shard_map/ppermute | solution.py:323
  57.0 1.8 %collective-permute-start.22 = (bf16[128,128]{1,0:T(8,128)(2,1)S(1)}, bf16[128,128]{1,0:T(8,128)(2,1)S(1)}, u32[]{:S(2)}, u32[]{:S(2)}) collective-permute-start(bf16[128,128]{1,0:T(8,128)(2,1)S(1)} %shard_map.103.refs_0_), channel_id=1, source_target_pairs={{0,3},{1,2},{2,1},{3,0},{4,7},{5,6},{6,5},{7,4},{8,11},{9,10},{10,... | collective-permute-start | bytes 98312 | tf_op jit(solution)/shard_map/ppermute | solution.py:323
  59.2 2.2 %collective-permute-start.20 = (bf16[128,128]{1,0:T(8,128)(2,1)S(1)}, bf16[128,128]{1,0:T(8,128)(2,1)S(1)}, u32[]{:S(2)}, u32[]{:S(2)}) collective-permute-start(bf16[128,128]{1,0:T(8,128)(2,1)S(1)} %shard_map.103.refs_0_), channel_id=1, source_target_pairs={{0,1},{1,0},{2,3},{3,2},{4,5},{5,4},{6,7},{7,6},{8,9},{9,8},{10,11... | collective-permute-start | bytes 98312 | tf_op jit(solution)/shard_map/ppermute | solution.py:323
  61.4 0.9 %shard_map.101 = (bf16[2048,128]{1,0:T(8,128)(2,1)}, f32[16,128]{1,0:T(8,128)}) custom-call(bf16[544,128]{1,0:T(8,128)(2,1)S(1)} %get-tuple-element.57.refs_0_, bf16[544,128]{1,0:T(8,128)(2,1)S(1)} %collective-permute-done.13.refs_1_, bf16[544,128]{1,0:T(8,128)(2,1)S(1)} %collective-permute-done.14.refs_2_, bf16[544,128]{1,0:T(8,128)(2,1)S(1)} %collective-permute-done.15.refs_3_), custom_call_target="tpu_custom_call" | custom-call | tf_op jit(solution)/shard_map/pallas_call | solution.py:30
  (49 shorter events, 9.4 us)
Async XLA Ops:
  2.4 19.7 %collective-permute-start.3 = (bf16[128,704]{1,0:T(8,128)(2,1)S(1)}, bf16[128,704]{1,0:T(8,128)(2,1)S(1)}, u32[]{:S(2)}, u32[]{:S(2)}) collective-permute-start(bf16[128,704]{1,0:T(8,128)(2,1)S(1)} %shard_map.94.refs_0_.refs_4_), channel_id=1, source_target_pairs={{0,24},{4,28},{8,16},{12,20},{16,8},{20,12},{24,0},{28,4},{1,25},{... | collective-permute-start | bytes 540680 | tf_op jit(solution)/shard_map/ppermute | solution.py:323
  6.4 15.7 %collective-permute-start.2 = (bf16[128,704]{1,0:T(8,128)(2,1)S(1)}, bf16[128,704]{1,0:T(8,128)(2,1)S(1)}, u32[]{:S(2)}, u32[]{:S(2)}) collective-permute-start(bf16[128,704]{1,0:T(8,128)(2,1)S(1)} %shard_map.94.refs_0_.refs_4_), channel_id=1, source_target_pairs={{0,16},{4,20},{8,24},{12,28},{16,0},{20,4},{24,8},{28,12},{1,17},{... | collective-permute-start | bytes 540680 | tf_op jit(solution)/shard_map/ppermute | solution.py:323
  6.9 15.2 %collective-permute-start.1 = (bf16[128,704]{1,0:T(8,128)(2,1)S(1)}, bf16[128,704]{1,0:T(8,128)(2,1)S(1)}, u32[]{:S(2)}, u32[]{:S(2)}) collective-permute-start(bf16[128,704]{1,0:T(8,128)(2,1)S(1)} %shard_map.94.refs_0_.refs_4_), channel_id=1, source_target_pairs={{0,8},{4,12},{8,0},{12,4},{16,24},{20,28},{24,16},{28,20},{1,9},{5... | collective-permute-start | bytes 540680 | tf_op jit(solution)/shard_map/ppermute | solution.py:323
  7.0 5.2 %collective-permute-start = (bf16[128,704]{1,0:T(8,128)(2,1)S(1)}, bf16[128,704]{1,0:T(8,128)(2,1)S(1)}, u32[]{:S(2)}, u32[]{:S(2)}) collective-permute-start(bf16[128,704]{1,0:T(8,128)(2,1)S(1)} %shard_map.94.refs_0_.refs_4_), channel_id=1, source_target_pairs={{0,4},{4,0},{8,12},{12,8},{16,20},{20,16},{24,28},{28,24},{1,5},{5... | collective-permute-start | bytes 540680 | tf_op jit(solution)/shard_map/ppermute | solution.py:323
  8.8 10.3 %collective-permute-start.4 = (bf16[560,128]{1,0:T(8,128)(2,1)S(1)}, bf16[560,128]{1,0:T(8,128)(2,1)S(1)}, u32[]{:S(2)}, u32[]{:S(2)}) collective-permute-start(bf16[560,128]{1,0:T(8,128)(2,1)S(1)} %get-tuple-element.38), channel_id=1, source_target_pairs={{0,1},{1,0},{2,3},{3,2},{4,5},{5,4},{6,7},{7,6},{8,9},{9,8},{10,11... | collective-permute-start | bytes 430088 | tf_op jit(solution)/shard_map/ppermute | solution.py:323
  12.2 9.9 %collective-permute-start.5 = (bf16[560,128]{1,0:T(8,128)(2,1)S(1)}, bf16[560,128]{1,0:T(8,128)(2,1)S(1)}, u32[]{:S(2)}, u32[]{:S(2)}) collective-permute-start(bf16[560,128]{1,0:T(8,128)(2,1)S(1)} %get-tuple-element.39), channel_id=1, source_target_pairs={{0,2},{1,3},{2,0},{3,1},{4,6},{5,7},{6,4},{7,5},{8,10},{9,11},{10,... | collective-permute-start | bytes 430088 | tf_op jit(solution)/shard_map/ppermute | solution.py:323
  17.2 8.1 %copy-start.1 = (bf16[128,32,576]{0,2,1:T(8,128)(2,1)S(1)}, bf16[128,32,576]{0,2,1:T(8,128)(2,1)}, u32[]{:S(2)}) copy-start(bf16[128,32,576]{0,2,1:T(8,128)(2,1)} %param.7) | copy-start | bytes 14155780
  22.1 3.1 %collective-permute-start.7 = (bf16[128,704]{1,0:T(8,128)(2,1)S(1)}, bf16[128,704]{1,0:T(8,128)(2,1)S(1)}, u32[]{:S(2)}, u32[]{:S(2)}) collective-permute-start(bf16[128,704]{1,0:T(8,128)(2,1)S(1)} %collective-permute-done.1.refs_0_.refs_2_.refs_6_), channel_id=1, source_target_pairs={{0,4},{4,0},{8,12},{12,8},{16,20},{20,16},{24,28},{28,24},{1,5},{5... | collective-permute-start | bytes 540680 | tf_op jit(solution)/shard_map/ppermute | solution.py:323
  22.2 3.0 %collective-permute-start.8 = (bf16[128,704]{1,0:T(8,128)(2,1)S(1)}, bf16[128,704]{1,0:T(8,128)(2,1)S(1)}, u32[]{:S(2)}, u32[]{:S(2)}) collective-permute-start(bf16[128,704]{1,0:T(8,128)(2,1)S(1)} %collective-permute-done.2.refs_2_.refs_4_.refs_8_), channel_id=1, source_target_pairs={{0,4},{4,0},{8,12},{12,8},{16,20},{20,16},{24,28},{28,24},{1,5},{5... | collective-permute-start | bytes 540680 | tf_op jit(solution)/shard_map/ppermute | solution.py:323
  22.7 12.6 %collective-permute-start.12 = (bf16[560,128]{1,0:T(8,128)(2,1)S(1)}, bf16[560,128]{1,0:T(8,128)(2,1)S(1)}, u32[]{:S(2)}, u32[]{:S(2)}) collective-permute-start(bf16[560,128]{1,0:T(8,128)(2,1)S(1)} %get-tuple-element.53), channel_id=1, source_target_pairs={{0,3},{1,2},{2,1},{3,0},{4,7},{5,6},{6,5},{7,4},{8,11},{9,10},{10,... | collective-permute-start | bytes 430088 | tf_op jit(solution)/shard_map/ppermute | solution.py:323
  25.2 3.6 %collective-permute-start.6 = (bf16[128,704]{1,0:T(8,128)(2,1)S(1)}, bf16[128,704]{1,0:T(8,128)(2,1)S(1)}, u32[]{:S(2)}, u32[]{:S(2)}) collective-permute-start(bf16[128,704]{1,0:T(8,128)(2,1)S(1)} %collective-permute-done.3.refs_0_.refs_6_.refs_10_), channel_id=1, source_target_pairs={{0,4},{4,0},{8,12},{12,8},{16,20},{20,16},{24,28},{28,24},{1,5},{5... | collective-permute-start | bytes 540680 | tf_op jit(solution)/shard_map/ppermute | solution.py:323
  30.8 6.4 %collective-permute-start.9 = (bf16[32,1024]{1,0:T(8,128)(2,1)S(1)}, bf16[32,1024]{1,0:T(8,128)(2,1)S(1)}, u32[]{:S(2)}, u32[]{:S(2)}) collective-permute-start(bf16[32,1024]{1,0:T(8,128)(2,1)S(1)} %get-tuple-element.46), channel_id=1, source_target_pairs={{0,1},{1,0},{2,3},{3,2},{4,5},{5,4},{6,7},{7,6},{8,9},{9,8},{10,11... | collective-permute-start | bytes 196616 | tf_op jit(solution)/shard_map/ppermute | solution.py:323
  30.9 8.7 %collective-permute-start.10 = (bf16[32,1024]{1,0:T(8,128)(2,1)S(1)}, bf16[32,1024]{1,0:T(8,128)(2,1)S(1)}, u32[]{:S(2)}, u32[]{:S(2)}) collective-permute-start(bf16[32,1024]{1,0:T(8,128)(2,1)S(1)} %get-tuple-element.47), channel_id=1, source_target_pairs={{0,2},{1,3},{2,0},{3,1},{4,6},{5,7},{6,4},{7,5},{8,10},{9,11},{10,... | collective-permute-start | bytes 196616 | tf_op jit(solution)/shard_map/ppermute | solution.py:323
  32.7 6.9 %collective-permute-start.11 = (bf16[32,1024]{1,0:T(8,128)(2,1)S(1)}, bf16[32,1024]{1,0:T(8,128)(2,1)S(1)}, u32[]{:S(2)}, u32[]{:S(2)}) collective-permute-start(bf16[32,1024]{1,0:T(8,128)(2,1)S(1)} %get-tuple-element.48), channel_id=1, source_target_pairs={{0,3},{1,2},{2,1},{3,0},{4,7},{5,6},{6,5},{7,4},{8,11},{9,10},{10,... | collective-permute-start | bytes 196616 | tf_op jit(solution)/shard_map/ppermute | solution.py:323
  43.6 4.5 %collective-permute-start.16 = (f32[512,128]{1,0:T(8,128)S(1)}, f32[512,128]{1,0:T(8,128)S(1)}, u32[]{:S(2)}, u32[]{:S(2)}) collective-permute-start(f32[512,128]{1,0:T(8,128)S(1)} %get-tuple-element.63), channel_id=1, source_target_pairs={{0,4},{4,0},{8,12},{12,8},{16,20},{20,16},{24,28},{28,24},{1,5},{5... | collective-permute-start | bytes 786440 | tf_op jit(solution)/shard_map/ppermute | solution.py:323
  43.7 15.5 %collective-permute-start.13 = (bf16[544,128]{1,0:T(8,128)(2,1)S(1)}, bf16[544,128]{1,0:T(8,128)(2,1)S(1)}, u32[]{:S(2)}, u32[]{:S(2)}) collective-permute-start(bf16[544,128]{1,0:T(8,128)(2,1)S(1)} %get-tuple-element.58), channel_id=1, source_target_pairs={{0,1},{1,0},{2,3},{3,2},{4,5},{5,4},{6,7},{7,6},{8,9},{9,8},{10,11... | collective-permute-start | bytes 417800 | tf_op jit(solution)/shard_map/ppermute | solution.py:323
  45.3 16.1 %collective-permute-start.14 = (bf16[544,128]{1,0:T(8,128)(2,1)S(1)}, bf16[544,128]{1,0:T(8,128)(2,1)S(1)}, u32[]{:S(2)}, u32[]{:S(2)}) collective-permute-start(bf16[544,128]{1,0:T(8,128)(2,1)S(1)} %get-tuple-element.59), channel_id=1, source_target_pairs={{0,2},{1,3},{2,0},{3,1},{4,6},{5,7},{6,4},{7,5},{8,10},{9,11},{10,... | collective-permute-start | bytes 417800 | tf_op jit(solution)/shard_map/ppermute | solution.py:323
  46.1 15.4 %collective-permute-start.15 = (bf16[544,128]{1,0:T(8,128)(2,1)S(1)}, bf16[544,128]{1,0:T(8,128)(2,1)S(1)}, u32[]{:S(2)}, u32[]{:S(2)}) collective-permute-start(bf16[544,128]{1,0:T(8,128)(2,1)S(1)} %get-tuple-element.60), channel_id=1, source_target_pairs={{0,3},{1,2},{2,1},{3,0},{4,7},{5,6},{6,5},{7,4},{8,11},{9,10},{10,... | collective-permute-start | bytes 417800 | tf_op jit(solution)/shard_map/ppermute | solution.py:323
  48.2 4.0 %collective-permute-start.17 = (bf16[128,128]{1,0:T(8,128)(2,1)S(1)}, bf16[128,128]{1,0:T(8,128)(2,1)S(1)}, u32[]{:S(2)}, u32[]{:S(2)}) collective-permute-start(bf16[128,128]{1,0:T(8,128)(2,1)S(1)} %get-tuple-element.65), channel_id=1, source_target_pairs={{0,8},{4,12},{8,0},{12,4},{16,24},{20,28},{24,16},{28,20},{1,9},{5... | collective-permute-start | bytes 98312 | tf_op jit(solution)/shard_map/ppermute | solution.py:323
  49.7 4.9 %collective-permute-start.18 = (bf16[128,128]{1,0:T(8,128)(2,1)S(1)}, bf16[128,128]{1,0:T(8,128)(2,1)S(1)}, u32[]{:S(2)}, u32[]{:S(2)}) collective-permute-start(bf16[128,128]{1,0:T(8,128)(2,1)S(1)} %get-tuple-element.66), channel_id=1, source_target_pairs={{0,16},{4,20},{8,24},{12,28},{16,0},{20,4},{24,8},{28,12},{1,17},{... | collective-permute-start | bytes 98312 | tf_op jit(solution)/shard_map/ppermute | solution.py:323
  52.1 4.8 %collective-permute-start.19 = (bf16[128,128]{1,0:T(8,128)(2,1)S(1)}, bf16[128,128]{1,0:T(8,128)(2,1)S(1)}, u32[]{:S(2)}, u32[]{:S(2)}) collective-permute-start(bf16[128,128]{1,0:T(8,128)(2,1)S(1)} %get-tuple-element.67), channel_id=1, source_target_pairs={{0,24},{4,28},{8,16},{12,20},{16,8},{20,12},{24,0},{28,4},{1,25},{... | collective-permute-start | bytes 98312 | tf_op jit(solution)/shard_map/ppermute | solution.py:323
  57.0 5.9 %collective-permute-start.22 = (bf16[128,128]{1,0:T(8,128)(2,1)S(1)}, bf16[128,128]{1,0:T(8,128)(2,1)S(1)}, u32[]{:S(2)}, u32[]{:S(2)}) collective-permute-start(bf16[128,128]{1,0:T(8,128)(2,1)S(1)} %shard_map.103.refs_0_), channel_id=1, source_target_pairs={{0,3},{1,2},{2,1},{3,0},{4,7},{5,6},{6,5},{7,4},{8,11},{9,10},{10,... | collective-permute-start | bytes 98312 | tf_op jit(solution)/shard_map/ppermute | solution.py:323
  58.8 4.9 %collective-permute-start.21 = (bf16[128,128]{1,0:T(8,128)(2,1)S(1)}, bf16[128,128]{1,0:T(8,128)(2,1)S(1)}, u32[]{:S(2)}, u32[]{:S(2)}) collective-permute-start(bf16[128,128]{1,0:T(8,128)(2,1)S(1)} %shard_map.103.refs_0_), channel_id=1, source_target_pairs={{0,2},{1,3},{2,0},{3,1},{4,6},{5,7},{6,4},{7,5},{8,10},{9,11},{10,... | collective-permute-start | bytes 98312 | tf_op jit(solution)/shard_map/ppermute | solution.py:323
  59.2 4.6 %collective-permute-start.20 = (bf16[128,128]{1,0:T(8,128)(2,1)S(1)}, bf16[128,128]{1,0:T(8,128)(2,1)S(1)}, u32[]{:S(2)}, u32[]{:S(2)}) collective-permute-start(bf16[128,128]{1,0:T(8,128)(2,1)S(1)} %shard_map.103.refs_0_), channel_id=1, source_target_pairs={{0,1},{1,0},{2,3},{3,2},{4,5},{5,4},{6,7},{7,6},{8,9},{9,8},{10,11... | collective-permute-start | bytes 98312 | tf_op jit(solution)/shard_map/ppermute | solution.py:323
  (6 other events, 12.2 us)
